TPU v7x, 512 devices: a whole 4x4x16 slice. The times are simulated.
512 devices in a mesh: dp: 8 (over y, x_hi), expert: 64 (over z, x_lo, core).
Axes of the slice: x: 4 (x_hi: 2, x_lo: 2; x = x_hi * 2 + x_lo), y: 4, z: 16, core: 2. Of those that a mesh axis runs over, the one named last changes fastest.
Arguments:
- activations: bfloat16 [65536, 2048], P(('dp', 'expert')), may hold values from -6 to 6
- routes: int32 [65536, 8], P(('dp', 'expert')), may hold values from 0 to 63, all different within a row; in each aligned block of 128 rows (0 to 127, 128 to 255, ...) at most 18 rows name the same one
- gate_probs: float32 [65536, 8], P(('dp', 'expert')), may hold values from 0.1 to 1
- advantage: float32 [65536], P(('dp', 'expert')), may hold values from -6 to 6
- readout: bfloat16 [64, 768], replicated, may hold values from -6 to 6
- weights: bfloat16 [64, 2048, 768], P('expert', 'dp'), may hold values from -6 to 6
- moment_one: float32 [64, 2048, 768], P('expert', 'dp'), may hold values from -4 to 4
- moment_two: float32 [64, 2048, 768], P('expert', 'dp'), may hold values from 0.05 to 2
- swap_flags: int32 [64], replicated, may hold values from 0 to 1, as said below
Outputs:
- new_weights: bfloat16 [64, 2048, 768], P('expert', 'dp')
- new_moment_one: float32 [64, 2048, 768], P('expert', 'dp')
- new_moment_two: float32 [64, 2048, 768], P('expert', 'dp')
Inputs may be any that keep to these rules, and one draw needn't show every extreme that they name: `routes`: each row names 8 different experts, and the rows of one device name any expert at most 18 times. swap_flags[j] equals swap_flags[(j + 32) mod 64]: partners trade together.
All inputs are finite; a program needn't handle non-finite values.
Results may differ from a plain program's by a relative error of at most 0.0085.
Values may be sent and summed in bfloat16 or wider, within the bound.
No kernel may reach another device: no remote copies, remote signals or barrier semaphores. Data moves between devices by JAX's collectives and lax.ppermute only.
A program may use at most 64 MiB of HBM per device.

v0:
```python
import math

import jax
import jax.numpy as jnp
from jax import lax
from jax.sharding import PartitionSpec as P

beta_one = 0.9
beta_two = 0.95
learn_rate = 0.02
epsilon = 1e-08
decay_rate = 0.1
adam_step = 10.0


def from_behind(block, axis, distance):
    devices = range(lax.axis_size(axis))
    route = [((i - distance) % len(devices), i) for i in devices]
    return lax.ppermute(block, axis, route)


def silu_slope(preact):
    sigmoid_val = jax.nn.sigmoid(preact)
    return sigmoid_val * (1.0 + preact * (1.0 - sigmoid_val))


def adam_update(weight_now, first_now, second_now, gradient):
    first = beta_one * first_now + (1.0 - beta_one) * gradient
    second = beta_two * second_now + (1.0 - beta_two) * gradient * gradient
    first_hat = first / (1.0 - beta_one**adam_step)
    second_hat = second / (1.0 - beta_two**adam_step)
    old_weight = weight_now.astype(jnp.float32)
    updated = (
        old_weight
        - learn_rate * (first_hat / (jnp.sqrt(second_hat) + epsilon) + decay_rate * old_weight)
    ).astype(jnp.bfloat16)
    return (updated, first, second)


def body(
    activations, routes, gate_probs, advantage, readout, weights, moment_one, moment_two, swap_flags
):
    experts = lax.axis_size("expert")
    half_way = experts // 2
    position = lax.axis_index("expert")
    tok_rows, width_d = activations.shape
    route_count = routes.shape[1]
    capacity = max(2, tok_rows * route_count * 9 // (8 * experts))
    inv_root = 1.0 / math.sqrt(width_d)
    my_flag = lax.dynamic_index_in_dim(swap_flags, position, 0, keepdims=False)
    expert_ids = jnp.arange(experts, dtype=jnp.int32)
    route_hot = routes[:, :, None] == expert_ids
    stacked = jnp.stack([weights.astype(jnp.float32), moment_one, moment_two])
    shifted = from_behind(stacked.astype(jnp.bfloat16), "expert", half_way).astype(stacked.dtype)
    chosen_state = jnp.where(my_flag == 1, shifted, stacked)
    weight_now = chosen_state[0].astype(jnp.bfloat16)
    first_now = chosen_state[1]
    second_now = chosen_state[2]
    resident = (position + my_flag * half_way) % experts
    target = (routes + jnp.sum(jnp.where(route_hot, swap_flags, 0), axis=2) * half_way) % experts
    flat_hot = route_hot.reshape(tok_rows * route_count, experts).astype(jnp.int32)
    earlier = jnp.cumsum(flat_hot, axis=0) - flat_hot
    slot_rank = jnp.sum(jnp.where(flat_hot == 1, earlier, 0), axis=1).reshape(tok_rows, route_count)
    slot_ids = target * capacity + slot_rank
    slot_hot = slot_ids[:, :, None] == jnp.arange(experts * capacity, dtype=jnp.int32)
    select = jnp.sum(slot_hot, axis=1).astype(jnp.bfloat16)
    outgoing = lax.dot_general(
        select, activations, (((0,), (0,)), ((), ())), preferred_element_type=jnp.float32
    ).astype(jnp.bfloat16)
    factor = (advantage[:, None] * gate_probs).astype(jnp.bfloat16)
    slot_factor = jnp.sum(
        jnp.where(slot_hot, factor.astype(jnp.float32)[:, :, None], 0.0), axis=(0, 1)
    ).astype(jnp.bfloat16)
    received, recv_factor = (
        lax.all_to_all(
            outgoing.reshape(experts, capacity, width_d),
            "expert",
            split_axis=0,
            concat_axis=0,
            tiled=True,
        ),
        lax.all_to_all(
            slot_factor.reshape(experts, capacity),
            "expert",
            split_axis=0,
            concat_axis=0,
            tiled=True,
        ),
    )
    slot_rows = received.reshape(experts * capacity, width_d)
    factors = recv_factor.reshape(experts * capacity).astype(jnp.float32)
    preact = (
        jnp.dot(
            slot_rows,
            lax.all_gather(weight_now[0], "dp", axis=0, tiled=True),
            preferred_element_type=jnp.float32,
        )
        * inv_root
    )
    readout_row = lax.dynamic_index_in_dim(readout, resident, 0, keepdims=False).astype(jnp.float32)
    slopes = (factors[:, None] * readout_row[None, :] * silu_slope(preact)).astype(jnp.bfloat16)
    shard_rows = weight_now.shape[1]
    full_grad = (
        lax.dot_general(
            slot_rows, slopes, (((0,), (0,)), ((), ())), preferred_element_type=jnp.float32
        )
        * inv_root
    )
    summed = lax.psum(full_grad.astype(jnp.bfloat16), "dp").astype(jnp.float32)
    gradient = lax.dynamic_slice_in_dim(summed, lax.axis_index("dp") * shard_rows, shard_rows, 0)
    updated, first, second = adam_update(weight_now, first_now, second_now, gradient[None])
    return (updated, first, second)


def solution(mesh):
    placed = (
        P(("dp", "expert"), None),
        P(("dp", "expert"), None),
        P(("dp", "expert"), None),
        P(("dp", "expert")),
        P(),
        P("expert", "dp", None),
        P("expert", "dp", None),
        P("expert", "dp", None),
        P(),
    )
    return jax.shard_map(
        body,
        mesh=mesh,
        in_specs=placed,
        out_specs=(P("expert", "dp", None), P("expert", "dp", None), P("expert", "dp", None)),
        check_vma=False,
    )
```

profile of v0, /device:TPU:1, one launch (start us, length us, event | category | flops | bytes accessed | tf_op | source)
XLA Modules:
  0.0 716.3 jit_solution(15473665716397595918)
XLA Ops:
  7.2 0.0 copy-start
  7.2 0.8 copy.30
  8.0 0.1 eq.72
  8.1 0.1 eq.66
  8.2 18.0 %reduce-window.6 = s32[64,8,128]{2,1,0:T(8,128)S(1)} reduce-window(s32[64,8,128]{2,1,0:T(8,128)S(1)} %fusion.15, s32[]{:T(128)} %constant.28.clone.1), window={size=1x1x128 pad=0_0x0_0x127_0}, to_apply=%region_1.2 | reduce-window | flops 8323072 | bytes 524292 | tf_op jit(solution)/shard_map/reduce-window
  26.2 0.1 slice.23
  26.4 0.1 copy.32
  26.6 0.1 copy.33
  26.7 0.1 broadcast_add_fusion
  26.8 0.1 fusion.14
  26.9 0.1 reshape.146
  27.0 0.8 select_reduce_fusion.1
  27.8 0.7 fusion.18
  28.5 0.1 copy.35
  28.7 0.7 fusion.19
  29.3 0.1 copy.36
  29.4 0.6 select_reduce_fusion
  30.1 0.8 convert_element_type.111
  30.8 18.1 %all-to-all-start.1 = ((bf16[64,1,18]{2,1,0:T(2,128)(2,1)}), bf16[64,1,18]{2,1,0:T(2,128)(2,1)S(1)}, u32[]{:S(2)}, u32[]{:S(2)}) async-start(bf16[64,1,18]{2,1,0:T(2,128)(2,1)} %convert_element_type.111), calls=%async_computation.1 | async-start | bytes 65536 | tf_op jit(solution)/shard_map/all_to_all | solution.py:82
  48.9 1.4 convert_reduce_fusion
  50.4 0.0 copy-done
  50.4 3.5 convolution_convert_fusion
  53.9 7.6 %reshape.147 = bf16[64,18,2048]{2,1,0:T(8,128)(2,1)} reshape(bf16[1152,2048]{1,0:T(8,128)(2,1)} %convolution_convert_fusion) | data formatting | bytes 9437184 | tf_op jit(solution)/shard_map/reshape | solution.py:76
  61.5 0.0 copy-start.5
  61.5 0.0 copy-start.2
  61.5 0.0 copy-start.3
  61.5 0.6 all-to-all-done.1
  62.1 13.3 %all-to-all-start = ((bf16[64,18,2048]{2,1,0:T(8,128)(2,1)}), bf16[64,18,2048]{2,1,0:T(8,128)(2,1)}, u32[]{:S(2)}, u32[]{:S(2)}) async-start(bf16[64,18,2048]{2,1,0:T(8,128)(2,1)} %reshape.147), calls=%async_computation | async-start | bytes 12582912 | tf_op jit(solution)/shard_map/all_to_all | solution.py:75
  75.4 0.0 copy-start.6
  75.4 0.0 all-gather.3.cloned.1.call-start
  75.5 0.0 copy-done.5
  75.5 0.1 bitcast_convert_fusion
  75.5 0.0 copy-start.1
  75.6 0.9 copy-done.1
  76.4 0.0 copy-done.2
  76.4 0.0 copy-done.3
  76.4 0.3 fusion.1
  76.7 12.1 %collective-permute-start = (bf16[3,1,256,768]{3,2,1,0:T(8,128)(2,1)S(1)}, bf16[3,1,256,768]{3,2,1,0:T(8,128)(2,1)S(1)}, u32[]{:S(2)}, u32[]{:S(2)}) collective-permute-start(bf16[3,1,256,768]{3,2,1,0:T(8,128)(2,1)S(1)} %fusion.1), channel_id=1, source_target_pairs={{32,0},{33,1},{34,2},{35,3},{36,4},{37,5},{38,6},{39,7},{40,8},{41... | collective-permute-start | bytes 3538952 | tf_op jit(solution)/shard_map/ppermute | solution.py:19
  88.8 0.0 copy-done.6
  88.8 0.6 dynamic_slice.11
  90.1 331.0 %collective-permute-done = bf16[3,1,256,768]{3,2,1,0:T(8,128)(2,1)S(1)} collective-permute-done((bf16[3,1,256,768]{3,2,1,0:T(8,128)(2,1)S(1)}, bf16[3,1,256,768]{3,2,1,0:T(8,128)(2,1)S(1)}, u32[]{:S(2)}, u32[]{:S(2)}) %collective-permute-start) | collective-permute-done | bytes 1179680 | tf_op jit(solution)/shard_map/ppermute | solution.py:19
  421.0 0.0 copy-start.4
  421.0 1.1 copy-done.4
  422.1 2.2 convert_select_fusion
  424.3 0.8 slice.49
  425.1 0.0 all-gather.3.cloned.1.call-update
  425.1 0.2 all-reduce.2.cloned.1.call-start
  426.0 0.7 convert_reduce_fusion.2
  426.8 0.1 convert_reduce_fusion.1
  426.9 0.1 reshape.150
  427.0 0.0 all-to-all-done
  427.0 7.8 %reshape.148 = bf16[1152,2048]{1,0:T(8,128)(2,1)} reshape(bf16[64,18,2048]{2,1,0:T(8,128)(2,1)} %all-to-all-done) | data formatting | bytes 9437184 | tf_op jit(solution)/shard_map/reshape | solution.py:90
  434.8 95.2 %all-gather.3.cloned.1.call-done = bf16[1,1,2048,768]{3,2,1,0:T(8,128)(2,1)} async-done(((bf16[1,1,256,768]{3,2,1,0:T(8,128)(2,1)}), bf16[1,1,2048,768]{3,2,1,0:T(8,128)(2,1)}) %all-gather.3.cloned.1.call-update) | async-done | bytes 3145744 | tf_op jit(solution)/shard_map/all_gather | solution.py:95
  530.0 17.2 %multiply_convert_fusion = bf16[2048,768]{1,0:T(8,128)(2,1)} fusion(bf16[1152,2048]{1,0:T(8,128)(2,1)} %reshape.148, bf16[1,1,2048,768]{3,2,1,0:T(8,128)(2,1)} %all-gather.3.cloned.1.call-done, f32[768]{0:T(1024)S(1)} %convert_reduce_fusion.2, f32[1152]{0:T(1024)S(1)} %reshape.150), kind=kOutput, calls=%fused_computation.1 | convolution fusion | flops 7260635136 | bytes 11017728 | tf_op jit(solution)/shard_map/dot_general | solution.py:104
  547.2 0.0 all-reduce.2.cloned.1.call-update
  547.3 159.5 %all-reduce.2.cloned.1.call-done = bf16[2048,768]{1,0:T(8,128)(2,1)} async-done(((bf16[2048,768]{1,0:T(8,128)(2,1)}), bf16[2048,768]{1,0:T(8,128)(2,1)}) %all-reduce.2.cloned.1.call-update) | async-done | bytes 3145744 | tf_op jit(solution)/shard_map/psum | solution.py:109
  706.8 2.7 fusion.10
  (4 shorter events, 0.1 us)
Async XLA Ops:
  7.2 43.2 %copy-start = (bf16[128,2048]{1,0:T(8,128)(2,1)S(1)}, bf16[128,2048]{1,0:T(8,128)(2,1)}, u32[]{:S(2)}) copy-start(bf16[128,2048]{1,0:T(8,128)(2,1)} %param.9) | copy-start | bytes 1572868
  30.8 31.2 %all-to-all-start.1 = ((bf16[64,1,18]{2,1,0:T(2,128)(2,1)}), bf16[64,1,18]{2,1,0:T(2,128)(2,1)S(1)}, u32[]{:S(2)}, u32[]{:S(2)}) async-start(bf16[64,1,18]{2,1,0:T(2,128)(2,1)} %convert_element_type.111), calls=%async_computation.1 | async-start | bytes 65536 | tf_op jit(solution)/shard_map/all_to_all | solution.py:82
  61.5 14.0 %copy-start.5 = (bf16[1,256,768]{2,1,0:T(8,128)(2,1)S(1)}, bf16[1,256,768]{2,1,0:T(8,128)(2,1)}, u32[]{:S(2)}) copy-start(bf16[1,256,768]{2,1,0:T(8,128)(2,1)} %param.14) | copy-start | bytes 1179652
  61.5 14.9 %copy-start.2 = (f32[1,256,768]{2,1,0:T(8,128)S(1)}, f32[1,256,768]{2,1,0:T(8,128)}, u32[]{:S(2)}) copy-start(f32[1,256,768]{2,1,0:T(8,128)} %param.16) | copy-start | bytes 2359300
  61.5 14.9 %copy-start.3 = (f32[1,256,768]{2,1,0:T(8,128)S(1)}, f32[1,256,768]{2,1,0:T(8,128)}, u32[]{:S(2)}) copy-start(f32[1,256,768]{2,1,0:T(8,128)} %param.15) | copy-start | bytes 2359300
  62.1 364.9 %all-to-all-start = ((bf16[64,18,2048]{2,1,0:T(8,128)(2,1)}), bf16[64,18,2048]{2,1,0:T(8,128)(2,1)}, u32[]{:S(2)}, u32[]{:S(2)}) async-start(bf16[64,18,2048]{2,1,0:T(8,128)(2,1)} %reshape.147), calls=%async_computation | async-start | bytes 12582912 | tf_op jit(solution)/shard_map/all_to_all | solution.py:75
  75.4 13.4 %copy-start.6 = (s32[64]{0:T(128)S(1)}, s32[64]{0:T(128)}, u32[]{:S(2)}) copy-start(s32[64]{0:T(128)} %param.17) | copy-start | bytes 772
  75.4 454.6 %all-gather.3.cloned.1.call-start = ((), (), s32[]{:S(2)}) async-start(), calls=%async_computation.3 | async-start | bytes 3538944 | tf_op jit(solution)/shard_map/all_gather | solution.py:95
  75.5 0.9 copy-start.1
  76.7 344.3 %collective-permute-start = (bf16[3,1,256,768]{3,2,1,0:T(8,128)(2,1)S(1)}, bf16[3,1,256,768]{3,2,1,0:T(8,128)(2,1)S(1)}, u32[]{:S(2)}, u32[]{:S(2)}) collective-permute-start(bf16[3,1,256,768]{3,2,1,0:T(8,128)(2,1)S(1)} %fusion.1), channel_id=1, source_target_pairs={{32,0},{33,1},{34,2},{35,3},{36,4},{37,5},{38,6},{39,7},{40,8},{41... | collective-permute-start | bytes 3538952 | tf_op jit(solution)/shard_map/ppermute | solution.py:19
  421.0 1.1 copy-start.4
  425.1 281.6 %all-reduce.2.cloned.1.call-start = ((), (), s32[]{:S(2)}) async-start(), calls=%async_computation.2 | async-start | bytes 6291456 | tf_op jit(solution)/shard_map/psum | solution.py:109
Sparse Core Ops, SparseCore 0:
  425.3 104.6 all-gather.2
  547.4 159.3 all-reduce.1
where the time goes:
time: 717 us; the launch traced here: 716 us
  waiting for transfers between devices  586 us (82%)
  starting transfers between devices  43.8 us (6%)
  other arithmetic  28.6 us (4%)
  local copies, waits for them, and re-layouts  21.3 us (3%)
  matrix products  20.8 us (3%)
  between operations  15.6 us (2%)
    ppermute x1, waiting for transfers between devices, from_behind(): return lax.ppermute(block, axis, route)  331 us
    psum x1, waiting for transfers between devices, body(): summed = lax.psum(full_grad.astype(jnp.bfloat16), 'dp').astype(jnp.float32)  160 us
    all_gather x1, waiting for transfers between devices, body(): lax.all_gather(weight_now[0], 'dp', axis=0, tiled=True)  95.2 us
    another operation x3, other arithmetic  18.2 us
    all_to_all x1, starting transfers between devices, body(): lax.all_to_all(slot_factor.reshape(experts, capacity), 'expert', split_ax...  18.1 us
    dot_general x1, matrix products, body(): lax.dot_general(slot_rows, slopes, (((0,), (0,)), ((), ())), preferred_el...  17.2 us
  transfers between devices with their start and end apart: 5, of which 4 were waited for; matrix products, arithmetic and copies ran while one was open for 4% of the time, Pallas kernels for 0%

commit v1 on v0

v1 whole, which is shorter than its diff:
```python
import math

import jax
import jax.numpy as jnp
from jax import lax
from jax.sharding import Mesh, PartitionSpec as P

beta_one = 0.9
beta_two = 0.95
learn_rate = 0.02
epsilon = 1e-08
decay_rate = 0.1
adam_step = 10.0

NY, NH, NZ, NX, NC = 4, 2, 16, 2, 2
CAP = 18
RELS = ((0, 0), (0, 1), (1, 0), (1, 1))
GROUPS = ((0, 1, -1, 2, -2), (3, -3, 4, -4), (5, -5, 6, -6), (7, -7, 8))


def shift_z(block, distance):
    return lax.ppermute(block, "z", [(i, (i + distance) % NZ) for i in range(NZ)])


def swap_xc(block, dx, dc):
    pairs = [
        (x * NC + c, (x ^ dx) * NC + (c ^ dc)) for x in range(NX) for c in range(NC)
    ]
    return lax.ppermute(block, ("x", "c"), pairs)


def shift_dp(block, dy, dh):
    pairs = [
        (y * NH + h, ((y + dy) % NY) * NH + (h + dh) % NH)
        for y in range(NY)
        for h in range(NH)
    ]
    return lax.ppermute(block, ("y", "h"), pairs)


def silu_slope(preact):
    sigmoid_val = jax.nn.sigmoid(preact)
    return sigmoid_val * (1.0 + preact * (1.0 - sigmoid_val))


def adam_update(weight_now, first_now, second_now, gradient):
    first = beta_one * first_now + (1.0 - beta_one) * gradient
    second = beta_two * second_now + (1.0 - beta_two) * gradient * gradient
    first_hat = first / (1.0 - beta_one**adam_step)
    second_hat = second / (1.0 - beta_two**adam_step)
    old_weight = weight_now.astype(jnp.float32)
    updated = (
        old_weight
        - learn_rate * (first_hat / (jnp.sqrt(second_hat) + epsilon) + decay_rate * old_weight)
    ).astype(jnp.bfloat16)
    return (updated, first, second)


def body(
    activations, routes, gate_probs, advantage, readout, weights, moment_one, moment_two, swap_flags
):
    tok_rows, width_d = activations.shape
    experts = NZ * NX * NC
    half = experts // 2
    inv_root = 1.0 / math.sqrt(width_d)
    z, x, c = lax.axis_index("z"), lax.axis_index("x"), lax.axis_index("c")
    y, h = lax.axis_index("y"), lax.axis_index("h")
    position = (z * NX + x) * NC + c

    def home(index):
        flag = lax.dynamic_index_in_dim(swap_flags, index, 0, keepdims=False)
        return (index + flag * half) % experts, flag

    resident, my_flag = home(position)

    weight_own = weights[0]
    weight_far = shift_z(weight_own, NZ // 2)
    weight_now = jnp.where(my_flag == 1, weight_far, weight_own)
    weight_full = lax.all_gather(weight_now, ("y", "h"), axis=0, tiled=True)

    blocks = {0: activations}
    fwd = bwd = activations
    for k in range(1, NZ // 2):
        fwd = shift_z(fwd, 1)
        bwd = shift_z(bwd, -1)
        blocks[-k] = fwd
        blocks[k] = bwd
    half_rows = tok_rows // 2
    blocks[8] = jnp.concatenate(
        [shift_z(fwd[:half_rows], 1), shift_z(bwd[half_rows:], -1)], axis=0
    )

    factor = (advantage[:, None] * gate_probs).astype(jnp.bfloat16)
    meta = jnp.concatenate([routes.astype(jnp.bfloat16).T, factor.T], axis=0)
    meta_all = lax.all_gather(meta, ("z", "x", "c"), axis=0, tiled=False)
    meta_all = meta_all.reshape(NZ, NX, NC, 2, 8, tok_rows)
    meta_all = jnp.concatenate([meta_all, meta_all], axis=0)
    offsets = [o % NZ for group in GROUPS for o in group]
    meta_z = lax.dynamic_slice_in_dim(meta_all, z, NZ, 0)
    meta_z = jnp.stack([meta_z[o] for o in offsets])
    by_rel = []
    for dx, dc in RELS:
        part = lax.dynamic_index_in_dim(meta_z, x ^ dx, 1, keepdims=False)
        by_rel.append(lax.dynamic_index_in_dim(part, c ^ dc, 1, keepdims=False))
    routes_rel = jnp.stack([m[:, 0] for m in by_rel], axis=1)
    factor_rel = jnp.stack([m[:, 1] for m in by_rel], axis=1).astype(jnp.float32)
    dest_home = jnp.stack(
        [home((z * NX + (x ^ dx)) * NC + (c ^ dc))[0] for dx, dc in RELS]
    ).astype(jnp.bfloat16)
    tri = (
        jnp.arange(tok_rows)[:, None] < jnp.arange(tok_rows)[None, :]
    ).astype(jnp.bfloat16)

    def ranked(mask):
        rank = lax.dot_general(
            mask.astype(jnp.bfloat16),
            tri,
            (((2,), (0,)), ((), ())),
            preferred_element_type=jnp.float32,
        )
        return jnp.where(mask, rank.astype(jnp.int32), -1000)

    out_mask = jnp.any(
        routes_rel[:, 0, None] == dest_home[None, :, None, None], axis=2
    )
    out_rank = ranked(out_mask)
    in_hot = routes_rel == resident.astype(jnp.bfloat16)
    in_rank = ranked(jnp.any(in_hot, axis=2))
    in_factor = jnp.sum(jnp.where(in_hot, factor_rel, 0.0), axis=2)

    readout_row = lax.dynamic_index_in_dim(readout, resident, 0, keepdims=False).astype(jnp.float32)

    all_rows, all_slopes = [], []
    start = 0
    for group in GROUPS:
        count = len(group)
        rows = -(-count * CAP // 8) * 8
        base = (jnp.arange(count, dtype=jnp.int32) * CAP)[:, None, None]
        slots = jnp.arange(rows, dtype=jnp.int32)
        mine = out_rank[start : start + count] + base
        select = (
            mine.transpose(1, 0, 2)[:, None] == slots[None, :, None, None]
        ).astype(jnp.bfloat16)
        theirs = in_rank[start : start + count] + base
        slot_factor = jnp.sum(
            jnp.where(
                theirs.transpose(1, 0, 2)[:, None] == slots[None, :, None, None],
                in_factor[start : start + count].transpose(1, 0, 2)[:, None],
                0.0,
            ),
            axis=(2, 3),
        ).reshape(4 * rows, 1)
        source = jnp.concatenate([blocks[o] for o in group], axis=0)
        picked = jnp.dot(
            select.reshape(4 * rows, count * tok_rows),
            source,
            preferred_element_type=jnp.float32,
        ).astype(jnp.bfloat16)
        pieces = [
            picked[i * rows : (i + 1) * rows]
            if rel == (0, 0)
            else swap_xc(picked[i * rows : (i + 1) * rows], *rel)
            for i, rel in enumerate(RELS)
        ]
        slot_rows = jnp.concatenate(pieces, axis=0)
        preact = (
            jnp.dot(slot_rows, weight_full, preferred_element_type=jnp.float32) * inv_root
        )
        slopes = (slot_factor * readout_row[None, :] * silu_slope(preact)).astype(jnp.bfloat16)
        all_rows.append(slot_rows)
        all_slopes.append(slopes)
        start += count

    moments = jnp.stack([moment_one[0], moment_two[0]]).astype(jnp.bfloat16)
    moments, _ = lax.optimization_barrier((moments, blocks[8]))
    moments_far = shift_z(moments, NZ // 2)

    full_grad = (
        lax.dot_general(
            jnp.concatenate(all_rows, axis=0),
            jnp.concatenate(all_slopes, axis=0),
            (((0,), (0,)), ((), ())),
            preferred_element_type=jnp.float32,
        )
        * inv_root
    ).astype(jnp.bfloat16)
    shard = weight_own.shape[0]

    def part(dy, dh):
        index = ((y + dy) % NY) * NH + (h + dh) % NH
        return lax.dynamic_slice_in_dim(full_grad, index * shard, shard, 0)

    gradient = part(0, 0).astype(jnp.float32)
    for dy, dh in ((2, 1), (1, 1), (3, 1), (2, 0), (1, 0), (3, 0), (0, 1)):
        gradient = gradient + shift_dp(part(dy, dh), dy, dh).astype(jnp.float32)

    first_now = jnp.where(my_flag == 1, moments_far[0].astype(jnp.float32), moment_one[0])
    second_now = jnp.where(my_flag == 1, moments_far[1].astype(jnp.float32), moment_two[0])
    updated, first, second = adam_update(weight_now, first_now, second_now, gradient)
    return (updated[None], first[None], second[None])


def solution(mesh):
    inner = Mesh(mesh.devices.reshape(NY, NH, NZ, NX, NC), ("y", "h", "z", "x", "c"))
    dp, expert = ("y", "h"), ("z", "x", "c")
    placed = (
        P(dp + expert, None),
        P(dp + expert, None),
        P(dp + expert, None),
        P(dp + expert),
        P(),
        P(expert, dp, None),
        P(expert, dp, None),
        P(expert, dp, None),
        P(),
    )
    return jax.shard_map(
        body,
        mesh=inner,
        in_specs=placed,
        out_specs=(P(expert, dp, None),) * 3,
        check_vma=False,
    )
```

time: 717 us -> 436 us (0.61)
  waiting for transfers between devices: 586 us -> 59.5 us
  blocking collectives: 0 us -> 149 us
  starting transfers between devices: 43.8 us -> 132 us
  other arithmetic: 28.6 us -> 14.1 us
  local copies, waits for them, and re-layouts: 21.3 us -> 32.3 us
    ppermute x1 -> x37, waiting for transfers between devices: 331 us -> 59.5 us  [the longest x18 23 us: shift_z(): lax.ppermute(block, 'z', [(i, (i + distance) % NZ) for i in range(NZ)])]
    psum x1 -> x0, waiting for transfers between devices: 160 us -> none  [body(): summed = lax.psum(full_grad.astype(jnp.bfloat16), 'dp').astype(jnp.float32)]
    all_gather x0 -> x1, blocking collectives: none -> 149 us  [body(): meta_all = lax.all_gather(meta, ('z', 'x', 'c'), axis=0, tiled=False)]
    ppermute x1 -> x37, starting transfers between devices: 12.1 us -> 132 us  [the longest x18 68.7 us: shift_z(): lax.ppermute(block, 'z', [(i, (i + distance) % NZ) for i in range(NZ)])]
    all_gather x1, waiting for transfers between devices: 95.2 us -> 0.01 us  [body(): weight_full = lax.all_gather(weight_now, ('y', 'h'), axis=0, tiled=True)]
    all_to_all x2 -> x0, starting transfers between devices: 31.4 us -> none  [the longest x1 18.1 us: body(): lax.all_to_all(slot_factor.reshape(experts, capacity), 'expert', split_ax...]
    unnamed x15 -> x75, local copies, waits for them, and re-layouts: 2.84 us -> 19.4 us
    reshape x4 -> x0, local copies, waits for them, and re-layouts: 15.5 us -> none  [the longest x1 7.77 us: body(): slot_rows = received.reshape(experts * capacity, width_d)]
  transfers between devices with their start and end apart: 5 -> 38, of which waited for: 4 -> 16; matrix products, arithmetic and copies ran while one was open for 4% -> 15% of each run, Pallas kernels for 0% -> 0%
where the time goes in v1:
time: 436 us; the launch traced here: 429 us
  blocking collectives  149 us (34%)
  starting transfers between devices  132 us (30%)
  waiting for transfers between devices  59.5 us (14%)
  local copies, waits for them, and re-layouts  32.3 us (7%)
  matrix products  23.9 us (5%)
  between operations  18.6 us (4%)
  other arithmetic  14.1 us (3%)
    all_gather x1, blocking collectives, body(): meta_all = lax.all_gather(meta, ('z', 'x', 'c'), axis=0, tiled=False)  149 us
    ppermute x18, starting transfers between devices, shift_z(): lax.ppermute(block, 'z', [(i, (i + distance) % NZ) for i in range(NZ)])  68.7 us
    ppermute x12, starting transfers between devices, swap_xc(): return lax.ppermute(block, ('x', 'c'), pairs)  36.9 us
    ppermute x7, starting transfers between devices, shift_dp(): return lax.ppermute(block, ('y', 'h'), pairs)  26 us
    ppermute x18, waiting for transfers between devices, shift_z(): lax.ppermute(block, 'z', [(i, (i + distance) % NZ) for i in range(NZ)])  23 us
    unnamed x75, local copies, waits for them, and re-layouts  19.4 us
    ppermute x7, waiting for transfers between devices, shift_dp(): return lax.ppermute(block, ('y', 'h'), pairs)  18.8 us
    ppermute x12, waiting for transfers between devices, swap_xc(): return lax.ppermute(block, ('x', 'c'), pairs)  17.7 us
  transfers between devices with their start and end apart: 38, of which 16 were waited for; matrix products, arithmetic and copies ran while one was open for 15% of the time, Pallas kernels for 0%

profile of v1, /device:TPU:1, one launch (start us, length us, event | category | flops | bytes accessed | tf_op | source)
XLA Modules:
  0.0 428.6 jit_solution(10552756987489268373)
XLA Ops:
  7.3 12.0 %collective-permute-start.2 = (bf16[128,2048]{1,0:T(8,128)(2,1)}, bf16[128,2048]{1,0:T(8,128)(2,1)}, u32[]{:S(2)}, u32[]{:S(2)}) collective-permute-start(bf16[128,2048]{1,0:T(8,128)(2,1)} %param.9), channel_id=1, source_target_pairs={{0,60},{4,0},{8,4},{12,8},{16,12},{20,16},{24,20},{28,24},{32,28},... | collective-permute-start | bytes 1572872 | tf_op jit(solution)/shard_map/ppermute | solution.py:22
  19.2 1.9 collective-permute-start.3
  24.5 7.7 %collective-permute-start.1 = (bf16[2,256,768]{2,1,0:T(8,128)(2,1)}, bf16[2,256,768]{2,1,0:T(8,128)(2,1)S(1)}, u32[]{:S(2)}, u32[]{:S(2)}) collective-permute-start(bf16[2,256,768]{2,1,0:T(8,128)(2,1)} %pad_maximum_fusion), channel_id=1, source_target_pairs={{0,32},{4,36},{8,40},{12,44},{16,48},{20,52},{24,56},{28,60},{32,0... | collective-permute-start | bytes 2359304 | tf_op jit(solution)/shard_map/ppermute | solution.py:22
  32.1 6.3 %collective-permute-start = (bf16[256,768]{1,0:T(8,128)(2,1)}, bf16[256,768]{1,0:T(8,128)(2,1)}, u32[]{:S(2)}, u32[]{:S(2)}) collective-permute-start(bf16[256,768]{1,0:T(8,128)(2,1)} %bitcast.1), channel_id=1, source_target_pairs={{0,32},{4,36},{8,40},{12,44},{16,48},{20,52},{24,56},{28,60},{32,0... | collective-permute-start | bytes 1179656 | tf_op jit(solution)/shard_map/ppermute | solution.py:22
  42.0 148.6 %all-gather = bf16[1024,128]{1,0:T(8,128)(2,1)S(1)} all-gather(bf16[16,128]{1,0:T(8,128)(2,1)S(1)} %pad_maximum_fusion.1), channel_id=2, replica_groups=mesh['y'=4,'h'=2,'z'=16,'x'=2,'c'=2] {'z','x','c'}, dimensions={0}, use_global_device_ids=true | all-gather | bytes 266240 | tf_op jit(solution)/shard_map/all_gather | solution.py:95
  193.3 1.9 collective-permute-start.4
  197.2 3.4 collective-permute-start.5
  200.5 1.9 constant_dynamic-update-slice_fusion.18
  202.4 1.9 constant_dynamic-update-slice_fusion.17
  204.3 4.6 %collective-permute-done.4 = bf16[128,2048]{1,0:T(8,128)(2,1)} collective-permute-done((bf16[128,2048]{1,0:T(8,128)(2,1)}, bf16[128,2048]{1,0:T(8,128)(2,1)}, u32[]{:S(2)}, u32[]{:S(2)}) %collective-permute-start.4) | collective-permute-done | bytes 524320 | tf_op jit(solution)/shard_map/ppermute | solution.py:22
  208.9 1.9 constant_dynamic-update-slice_fusion.16
  210.8 3.1 collective-permute-done.5
  214.7 3.2 convolution_convert_fusion
  218.8 2.9 collective-permute-start.6
  221.7 2.0 collective-permute-start.9
  223.8 3.2 collective-permute-start.10
  229.3 3.1 collective-permute-start.7
  232.4 1.8 broadcast_select_fusion
  234.2 3.1 collective-permute-start.8
  237.5 3.9 collective-permute-start.11
  241.3 1.9 collective-permute-start.12
  244.1 1.8 constant_dynamic-update-slice_fusion.33
  245.8 4.9 %collective-permute-done.8 = bf16[96,2048]{1,0:T(8,128)(2,1)S(1)} collective-permute-done((bf16[96,2048]{1,0:T(8,128)(2,1)S(1)}, bf16[96,2048]{1,0:T(8,128)(2,1)S(1)}, u32[]{:S(2)}, u32[]{:S(2)}) %collective-permute-start.8) | collective-permute-done | bytes 393248 | tf_op jit(solution)/shard_map/ppermute | solution.py:29
  252.5 5.2 %collective-permute-start.16 = (bf16[128,2048]{1,0:T(8,128)(2,1)S(1)}, bf16[128,2048]{1,0:T(8,128)(2,1)S(1)}, u32[]{:S(2)}, u32[]{:S(2)}) collective-permute-start(bf16[128,2048]{1,0:T(8,128)(2,1)S(1)} %collective-permute-done.11), channel_id=1, source_target_pairs={{0,60},{4,0},{8,4},{12,8},{16,12},{20,16},{24,20},{28,24},{32,28},... | collective-permute-start | bytes 1572872 | tf_op jit(solution)/shard_map/ppermute | solution.py:22
  257.8 1.9 collective-permute-start.17
  260.5 2.0 convolution_convert_fusion.2
  263.5 3.4 collective-permute-start.13
  266.9 3.8 collective-permute-start.14
  270.8 1.9 collective-permute-start.15
  272.7 4.9 %collective-permute-start.18 = (bf16[128,2048]{1,0:T(8,128)(2,1)S(1)}, bf16[128,2048]{1,0:T(8,128)(2,1)}, u32[]{:S(2)}, u32[]{:S(2)}) collective-permute-start(bf16[128,2048]{1,0:T(8,128)(2,1)S(1)} %collective-permute-done.16), channel_id=1, source_target_pairs={{0,60},{4,0},{8,4},{12,8},{16,12},{20,16},{24,20},{28,24},{32,28},... | collective-permute-start | bytes 1572872 | tf_op jit(solution)/shard_map/ppermute | solution.py:22
  277.6 1.9 collective-permute-start.19
  281.0 5.3 %collective-permute-done.15 = bf16[72,2048]{1,0:T(8,128)(2,1)S(1)} collective-permute-done((bf16[72,2048]{1,0:T(8,128)(2,1)S(1)}, bf16[72,2048]{1,0:T(8,128)(2,1)S(1)}, u32[]{:S(2)}, u32[]{:S(2)}) %collective-permute-start.15) | collective-permute-done | bytes 294944 | tf_op jit(solution)/shard_map/ppermute | solution.py:29
  288.5 5.1 %collective-permute-done.19 = bf16[128,2048]{1,0:T(8,128)(2,1)} collective-permute-done((bf16[128,2048]{1,0:T(8,128)(2,1)S(1)}, bf16[128,2048]{1,0:T(8,128)(2,1)}, u32[]{:S(2)}, u32[]{:S(2)}) %collective-permute-start.19) | collective-permute-done | bytes 524320 | tf_op jit(solution)/shard_map/ppermute | solution.py:22
  293.7 2.0 convolution_convert_fusion.1
  297.0 3.4 collective-permute-start.20
  300.4 1.9 collective-permute-start.23
  302.3 3.4 collective-permute-start.24
  306.1 3.5 collective-permute-start.21
  309.9 2.5 collective-permute-start.22
  314.1 2.0 collective-permute-done.23
  317.1 3.3 collective-permute-start.26
  321.5 1.9 collective-permute-start.25
  326.1 5.4 %collective-permute-done.25 = bf16[64,2048]{1,0:T(8,128)(2,1)S(1)} collective-permute-done((bf16[64,2048]{1,0:T(8,128)(2,1)S(1)}, bf16[64,2048]{1,0:T(8,128)(2,1)S(1)}, u32[]{:S(2)}, u32[]{:S(2)}) %collective-permute-start.25) | collective-permute-done | bytes 262176 | tf_op jit(solution)/shard_map/ppermute | solution.py:22
  331.6 1.9 convolution_convert_fusion.3
  334.6 3.7 collective-permute-start.27
  339.5 3.5 collective-permute-start.28
  343.1 2.1 collective-permute-start.29
  345.9 3.2 collective-permute-done.28
  349.8 4.2 collective-permute-done.29
  355.5 3.3 multiply_convert_fusion.4
  358.8 2.4 multiply_convert_fusion.2
  362.5 2.7 multiply_convert_fusion.1
  365.3 4.8 %multiply_convert_fusion = bf16[2048,768]{1,0:T(8,128)(2,1)S(1)} fusion(bf16[1184,2048]{1,0:T(8,128)(2,1)S(1)} %bitcast.100, bf16[224,768]{1,0:T(8,128)(2,1)S(1)} %multiply_convert_fusion.4, bf16[288,768]{1,0:T(8,128)(2,1)S(1)} %multiply_convert_fusion.2, bf16[288,768]{1,0:T(8,128)(2,1)S(1)} %multiply_convert_fusion.3, ...), kind=kOutput, calls=%fused_computation | convolution fusion | flops 3734962176 | bytes 9814016 | tf_op jit(solution)/shard_map/dot_general | solution.py:179
  371.9 4.3 %collective-permute-start.36 = (bf16[256,768]{1,0:T(8,128)(2,1)S(1)}, bf16[256,768]{1,0:T(8,128)(2,1)S(1)}, u32[]{:S(2)}, u32[]{:S(2)}) collective-permute-start(bf16[256,768]{1,0:T(8,128)(2,1)S(1)} %get-tuple-element.8), channel_id=1, source_target_pairs={{0,64},{64,0},{128,192},{192,128},{256,320},{320,256},{384,448},{4... | collective-permute-start | bytes 1179656 | tf_op jit(solution)/shard_map/ppermute | solution.py:38
  376.3 4.6 %collective-permute-start.35 = (bf16[256,768]{1,0:T(8,128)(2,1)S(1)}, bf16[256,768]{1,0:T(8,128)(2,1)}, u32[]{:S(2)}, u32[]{:S(2)}) collective-permute-start(bf16[256,768]{1,0:T(8,128)(2,1)S(1)} %get-tuple-element.9), channel_id=1, source_target_pairs={{0,384},{64,448},{128,0},{192,64},{256,128},{320,192},{384,256},{4... | collective-permute-start | bytes 1179656 | tf_op jit(solution)/shard_map/ppermute | solution.py:38
  380.9 1.9 collective-permute-start.34
  382.8 3.5 collective-permute-start.33
  386.4 3.2 collective-permute-start.32
  389.6 4.5 %collective-permute-start.31 = (bf16[256,768]{1,0:T(8,128)(2,1)S(1)}, bf16[256,768]{1,0:T(8,128)(2,1)}, u32[]{:S(2)}, u32[]{:S(2)}) collective-permute-start(bf16[256,768]{1,0:T(8,128)(2,1)S(1)} %get-tuple-element.13), channel_id=1, source_target_pairs={{0,192},{64,128},{128,320},{192,256},{256,448},{320,384},{384,64},... | collective-permute-start | bytes 1179656 | tf_op jit(solution)/shard_map/ppermute | solution.py:38
  394.1 3.9 collective-permute-start.30
  398.0 3.7 collective-permute-done.33
  401.8 7.7 %collective-permute-done.31 = bf16[256,768]{1,0:T(8,128)(2,1)} collective-permute-done((bf16[256,768]{1,0:T(8,128)(2,1)S(1)}, bf16[256,768]{1,0:T(8,128)(2,1)}, u32[]{:S(2)}, u32[]{:S(2)}) %collective-permute-start.31) | collective-permute-done | bytes 393248 | tf_op jit(solution)/shard_map/ppermute | solution.py:38
  409.5 7.3 %collective-permute-done.30 = bf16[256,768]{1,0:T(8,128)(2,1)} collective-permute-done((bf16[256,768]{1,0:T(8,128)(2,1)S(1)}, bf16[256,768]{1,0:T(8,128)(2,1)}, u32[]{:S(2)}, u32[]{:S(2)}) %collective-permute-start.30) | collective-permute-done | bytes 393248 | tf_op jit(solution)/shard_map/ppermute | solution.py:38
  416.8 3.1 fusion.106
  (163 shorter events, 38.5 us)
Async XLA Ops:
  7.2 31.3 %copy-start.16 = (s32[64]{0:T(128)S(1)}, s32[64]{0:T(128)}, u32[]{:S(2)}) copy-start(s32[64]{0:T(128)} %param.17) | copy-start | bytes 772
  7.2 34.8 %copy-start.17 = (s32[128,8]{0,1:T(8,128)S(1)}, s32[128,8]{0,1:T(8,128)}, u32[]{:S(2)}) copy-start(s32[128,8]{0,1:T(8,128)} %param.10) | copy-start | bytes 12292
  7.2 34.8 %copy-start.18 = (f32[128,8]{0,1:T(8,128)S(1)}, f32[128,8]{0,1:T(8,128)}, u32[]{:S(2)}) copy-start(f32[128,8]{0,1:T(8,128)} %param.11) | copy-start | bytes 12292
  7.2 34.8 %copy-start.19 = (f32[128]{0:T(128)S(1)}, f32[128]{0:T(128)}, u32[]{:S(2)}) copy-start(f32[128]{0:T(128)} %param.12) | copy-start | bytes 1540
  7.2 348.2 %all-gather.3.cloned.1.call-start = ((), (), s32[]{:S(2)}) async-start(), calls=%async_computation | async-start | bytes 3538944 | tf_op jit(solution)/shard_map/all_gather | solution.py:79
  7.3 186.1 %collective-permute-start.2 = (bf16[128,2048]{1,0:T(8,128)(2,1)}, bf16[128,2048]{1,0:T(8,128)(2,1)}, u32[]{:S(2)}, u32[]{:S(2)}) collective-permute-start(bf16[128,2048]{1,0:T(8,128)(2,1)} %param.9), channel_id=1, source_target_pairs={{0,60},{4,0},{8,4},{12,8},{16,12},{20,16},{24,20},{28,24},{32,28},... | collective-permute-start | bytes 1572872 | tf_op jit(solution)/shard_map/ppermute | solution.py:22
  19.2 178.0 %collective-permute-start.3 = (bf16[128,2048]{1,0:T(8,128)(2,1)}, bf16[128,2048]{1,0:T(8,128)(2,1)}, u32[]{:S(2)}, u32[]{:S(2)}) collective-permute-start(bf16[128,2048]{1,0:T(8,128)(2,1)} %param.9), channel_id=1, source_target_pairs={{0,4},{4,8},{8,12},{12,16},{16,20},{20,24},{24,28},{28,32},{32,36}... | collective-permute-start | bytes 1572872 | tf_op jit(solution)/shard_map/ppermute | solution.py:22
  23.5 169.0 %copy-start.4 = (bf16[128,2048]{1,0:T(8,128)(2,1)S(1)}, bf16[128,2048]{1,0:T(8,128)(2,1)}, u32[]{:S(2)}) copy-start(bf16[128,2048]{1,0:T(8,128)(2,1)} %param.9) | copy-start | bytes 1572868
  24.5 361.9 %collective-permute-start.1 = (bf16[2,256,768]{2,1,0:T(8,128)(2,1)}, bf16[2,256,768]{2,1,0:T(8,128)(2,1)S(1)}, u32[]{:S(2)}, u32[]{:S(2)}) collective-permute-start(bf16[2,256,768]{2,1,0:T(8,128)(2,1)} %pad_maximum_fusion), channel_id=1, source_target_pairs={{0,32},{4,36},{8,40},{12,44},{16,48},{20,52},{24,56},{28,60},{32,0... | collective-permute-start | bytes 2359304 | tf_op jit(solution)/shard_map/ppermute | solution.py:22
  32.1 197.2 %collective-permute-start = (bf16[256,768]{1,0:T(8,128)(2,1)}, bf16[256,768]{1,0:T(8,128)(2,1)}, u32[]{:S(2)}, u32[]{:S(2)}) collective-permute-start(bf16[256,768]{1,0:T(8,128)(2,1)} %bitcast.1), channel_id=1, source_target_pairs={{0,32},{4,36},{8,40},{12,44},{16,48},{20,52},{24,56},{28,60},{32,0... | collective-permute-start | bytes 1179656 | tf_op jit(solution)/shard_map/ppermute | solution.py:22
  191.7 3.6 copy-start.10
  193.3 15.6 %collective-permute-start.4 = (bf16[128,2048]{1,0:T(8,128)(2,1)}, bf16[128,2048]{1,0:T(8,128)(2,1)}, u32[]{:S(2)}, u32[]{:S(2)}) collective-permute-start(bf16[128,2048]{1,0:T(8,128)(2,1)} %collective-permute-done.2), channel_id=1, source_target_pairs={{0,60},{4,0},{8,4},{12,8},{16,12},{20,16},{24,20},{28,24},{32,28},... | collective-permute-start | bytes 1572872 | tf_op jit(solution)/shard_map/ppermute | solution.py:22
  197.2 16.7 %collective-permute-start.5 = (bf16[128,2048]{1,0:T(8,128)(2,1)}, bf16[128,2048]{1,0:T(8,128)(2,1)S(1)}, u32[]{:S(2)}, u32[]{:S(2)}) collective-permute-start(bf16[128,2048]{1,0:T(8,128)(2,1)} %collective-permute-done.3), channel_id=1, source_target_pairs={{0,4},{4,8},{8,12},{12,16},{16,20},{20,24},{24,28},{28,32},{32,36}... | collective-permute-start | bytes 1572872 | tf_op jit(solution)/shard_map/ppermute | solution.py:22
  218.8 15.4 %collective-permute-start.6 = (bf16[96,2048]{1,0:T(8,128)(2,1)S(1)}, bf16[96,2048]{1,0:T(8,128)(2,1)S(1)}, u32[]{:S(2)}, u32[]{:S(2)}) collective-permute-start(bf16[96,2048]{1,0:T(8,128)(2,1)S(1)} %get-tuple-element.20), channel_id=1, source_target_pairs={{0,1},{1,0},{2,3},{3,2},{4,5},{5,4},{6,7},{7,6},{8,9},{9,8},{10,11... | collective-permute-start | bytes 1179656 | tf_op jit(solution)/shard_map/ppermute | solution.py:29
  221.7 15.8 %collective-permute-start.9 = (bf16[128,2048]{1,0:T(8,128)(2,1)}, bf16[128,2048]{1,0:T(8,128)(2,1)}, u32[]{:S(2)}, u32[]{:S(2)}) collective-permute-start(bf16[128,2048]{1,0:T(8,128)(2,1)} %collective-permute-done.4), channel_id=1, source_target_pairs={{0,60},{4,0},{8,4},{12,8},{16,12},{20,16},{24,20},{28,24},{32,28},... | collective-permute-start | bytes 1572872 | tf_op jit(solution)/shard_map/ppermute | solution.py:22
  223.8 17.6 %collective-permute-start.10 = (bf16[128,2048]{1,0:T(8,128)(2,1)S(1)}, bf16[128,2048]{1,0:T(8,128)(2,1)}, u32[]{:S(2)}, u32[]{:S(2)}) collective-permute-start(bf16[128,2048]{1,0:T(8,128)(2,1)S(1)} %collective-permute-done.5), channel_id=1, source_target_pairs={{0,4},{4,8},{8,12},{12,16},{16,20},{20,24},{24,28},{28,32},{32,36}... | collective-permute-start | bytes 1572872 | tf_op jit(solution)/shard_map/ppermute | solution.py:22
  229.3 14.8 %collective-permute-start.7 = (bf16[96,2048]{1,0:T(8,128)(2,1)S(1)}, bf16[96,2048]{1,0:T(8,128)(2,1)}, u32[]{:S(2)}, u32[]{:S(2)}) collective-permute-start(bf16[96,2048]{1,0:T(8,128)(2,1)S(1)} %get-tuple-element.19), channel_id=1, source_target_pairs={{0,2},{1,3},{2,0},{3,1},{4,6},{5,7},{6,4},{7,5},{8,10},{9,11},{10,... | collective-permute-start | bytes 1179656 | tf_op jit(solution)/shard_map/ppermute | solution.py:29
  234.2 16.5 %collective-permute-start.8 = (bf16[96,2048]{1,0:T(8,128)(2,1)S(1)}, bf16[96,2048]{1,0:T(8,128)(2,1)S(1)}, u32[]{:S(2)}, u32[]{:S(2)}) collective-permute-start(bf16[96,2048]{1,0:T(8,128)(2,1)S(1)} %get-tuple-element.18), channel_id=1, source_target_pairs={{0,3},{1,2},{2,1},{3,0},{4,7},{5,6},{6,5},{7,4},{8,11},{9,10},{10,... | collective-permute-start | bytes 1179656 | tf_op jit(solution)/shard_map/ppermute | solution.py:29
  237.5 15.1 %collective-permute-start.11 = (bf16[128,2048]{1,0:T(8,128)(2,1)}, bf16[128,2048]{1,0:T(8,128)(2,1)S(1)}, u32[]{:S(2)}, u32[]{:S(2)}) collective-permute-start(bf16[128,2048]{1,0:T(8,128)(2,1)} %collective-permute-done.9), channel_id=1, source_target_pairs={{0,60},{4,0},{8,4},{12,8},{16,12},{20,16},{24,20},{28,24},{32,28},... | collective-permute-start | bytes 1572872 | tf_op jit(solution)/shard_map/ppermute | solution.py:22
  241.3 16.4 %collective-permute-start.12 = (bf16[128,2048]{1,0:T(8,128)(2,1)}, bf16[128,2048]{1,0:T(8,128)(2,1)S(1)}, u32[]{:S(2)}, u32[]{:S(2)}) collective-permute-start(bf16[128,2048]{1,0:T(8,128)(2,1)} %collective-permute-done.10), channel_id=1, source_target_pairs={{0,4},{4,8},{8,12},{12,16},{16,20},{20,24},{24,28},{28,32},{32,36}... | collective-permute-start | bytes 1572872 | tf_op jit(solution)/shard_map/ppermute | solution.py:22
  252.5 20.2 %collective-permute-start.16 = (bf16[128,2048]{1,0:T(8,128)(2,1)S(1)}, bf16[128,2048]{1,0:T(8,128)(2,1)S(1)}, u32[]{:S(2)}, u32[]{:S(2)}) collective-permute-start(bf16[128,2048]{1,0:T(8,128)(2,1)S(1)} %collective-permute-done.11), channel_id=1, source_target_pairs={{0,60},{4,0},{8,4},{12,8},{16,12},{20,16},{24,20},{28,24},{32,28},... | collective-permute-start | bytes 1572872 | tf_op jit(solution)/shard_map/ppermute | solution.py:22
  257.8 19.8 %collective-permute-start.17 = (bf16[128,2048]{1,0:T(8,128)(2,1)S(1)}, bf16[128,2048]{1,0:T(8,128)(2,1)S(1)}, u32[]{:S(2)}, u32[]{:S(2)}) collective-permute-start(bf16[128,2048]{1,0:T(8,128)(2,1)S(1)} %collective-permute-done.12), channel_id=1, source_target_pairs={{0,4},{4,8},{8,12},{12,16},{16,20},{20,24},{24,28},{28,32},{32,36}... | collective-permute-start | bytes 1572872 | tf_op jit(solution)/shard_map/ppermute | solution.py:22
  262.5 31.1 %copy-start.12 = (s32[4,4,128]{2,1,0:T(4,128)S(1)}, s32[4,4,128]{2,1,0:T(4,128)}, u32[]{:S(2)}) copy-start(s32[4,4,128]{2,1,0:T(4,128)} %get-tuple-element.58) | copy-start | bytes 24580
  263.5 7.2 %collective-permute-start.13 = (bf16[72,2048]{1,0:T(8,128)(2,1)S(1)}, bf16[72,2048]{1,0:T(8,128)(2,1)S(1)}, u32[]{:S(2)}, u32[]{:S(2)}) collective-permute-start(bf16[72,2048]{1,0:T(8,128)(2,1)S(1)} %get-tuple-element.25), channel_id=1, source_target_pairs={{0,1},{1,0},{2,3},{3,2},{4,5},{5,4},{6,7},{7,6},{8,9},{9,8},{10,11... | collective-permute-start | bytes 884744 | tf_op jit(solution)/shard_map/ppermute | solution.py:29
  266.9 13.3 %collective-permute-start.14 = (bf16[72,2048]{1,0:T(8,128)(2,1)S(1)}, bf16[72,2048]{1,0:T(8,128)(2,1)S(1)}, u32[]{:S(2)}, u32[]{:S(2)}) collective-permute-start(bf16[72,2048]{1,0:T(8,128)(2,1)S(1)} %get-tuple-element.24), channel_id=1, source_target_pairs={{0,2},{1,3},{2,0},{3,1},{4,6},{5,7},{6,4},{7,5},{8,10},{9,11},{10,... | collective-permute-start | bytes 884744 | tf_op jit(solution)/shard_map/ppermute | solution.py:29
  270.8 15.5 %collective-permute-start.15 = (bf16[72,2048]{1,0:T(8,128)(2,1)S(1)}, bf16[72,2048]{1,0:T(8,128)(2,1)S(1)}, u32[]{:S(2)}, u32[]{:S(2)}) collective-permute-start(bf16[72,2048]{1,0:T(8,128)(2,1)S(1)} %get-tuple-element.23), channel_id=1, source_target_pairs={{0,3},{1,2},{2,1},{3,0},{4,7},{5,6},{6,5},{7,4},{8,11},{9,10},{10,... | collective-permute-start | bytes 884744 | tf_op jit(solution)/shard_map/ppermute | solution.py:29
  272.7 15.8 %collective-permute-start.18 = (bf16[128,2048]{1,0:T(8,128)(2,1)S(1)}, bf16[128,2048]{1,0:T(8,128)(2,1)}, u32[]{:S(2)}, u32[]{:S(2)}) collective-permute-start(bf16[128,2048]{1,0:T(8,128)(2,1)S(1)} %collective-permute-done.16), channel_id=1, source_target_pairs={{0,60},{4,0},{8,4},{12,8},{16,12},{20,16},{24,20},{28,24},{32,28},... | collective-permute-start | bytes 1572872 | tf_op jit(solution)/shard_map/ppermute | solution.py:22
  277.6 16.0 %collective-permute-start.19 = (bf16[128,2048]{1,0:T(8,128)(2,1)S(1)}, bf16[128,2048]{1,0:T(8,128)(2,1)}, u32[]{:S(2)}, u32[]{:S(2)}) collective-permute-start(bf16[128,2048]{1,0:T(8,128)(2,1)S(1)} %collective-permute-done.17), channel_id=1, source_target_pairs={{0,4},{4,8},{8,12},{12,16},{16,20},{20,24},{24,28},{28,32},{32,36}... | collective-permute-start | bytes 1572872 | tf_op jit(solution)/shard_map/ppermute | solution.py:22
  295.7 10.2 %copy-start.15 = (s32[4,4,128]{2,1,0:T(4,128)S(1)}, s32[4,4,128]{2,1,0:T(4,128)}, u32[]{:S(2)}) copy-start(s32[4,4,128]{2,1,0:T(4,128)} %get-tuple-element.50) | copy-start | bytes 24580
  295.7 13.9 %copy-start.13 = (s32[4,3,128]{2,1,0:T(4,128)S(1)}, s32[4,3,128]{2,1,0:T(4,128)}, u32[]{:S(2)}) copy-start(s32[4,3,128]{2,1,0:T(4,128)} %get-tuple-element.59) | copy-start | bytes 18436
  295.7 35.8 %copy-start.11 = (s32[4,3,128]{2,1,0:T(4,128)S(1)}, s32[4,3,128]{2,1,0:T(4,128)}, u32[]{:S(2)}) copy-start(s32[4,3,128]{2,1,0:T(4,128)} %get-tuple-element.60) | copy-start | bytes 18436
  297.0 13.0 %collective-permute-start.20 = (bf16[72,2048]{1,0:T(8,128)(2,1)}, bf16[72,2048]{1,0:T(8,128)(2,1)}, u32[]{:S(2)}, u32[]{:S(2)}) collective-permute-start(bf16[72,2048]{1,0:T(8,128)(2,1)} %get-tuple-element.30), channel_id=1, source_target_pairs={{0,1},{1,0},{2,3},{3,2},{4,5},{5,4},{6,7},{7,6},{8,9},{9,8},{10,11... | collective-permute-start | bytes 884744 | tf_op jit(solution)/shard_map/ppermute | solution.py:29
  300.4 15.8 %collective-permute-start.23 = (bf16[128,2048]{1,0:T(8,128)(2,1)}, bf16[128,2048]{1,0:T(8,128)(2,1)}, u32[]{:S(2)}, u32[]{:S(2)}) collective-permute-start(bf16[128,2048]{1,0:T(8,128)(2,1)} %collective-permute-done.18), channel_id=1, source_target_pairs={{0,60},{4,0},{8,4},{12,8},{16,12},{20,16},{24,20},{28,24},{32,28},... | collective-permute-start | bytes 1572872 | tf_op jit(solution)/shard_map/ppermute | solution.py:22
  302.3 18.1 %collective-permute-start.24 = (bf16[128,2048]{1,0:T(8,128)(2,1)}, bf16[128,2048]{1,0:T(8,128)(2,1)}, u32[]{:S(2)}, u32[]{:S(2)}) collective-permute-start(bf16[128,2048]{1,0:T(8,128)(2,1)} %collective-permute-done.19), channel_id=1, source_target_pairs={{0,4},{4,8},{8,12},{12,16},{16,20},{20,24},{24,28},{28,32},{32,36}... | collective-permute-start | bytes 1572872 | tf_op jit(solution)/shard_map/ppermute | solution.py:22
  306.1 17.3 %collective-permute-start.21 = (bf16[72,2048]{1,0:T(8,128)(2,1)}, bf16[72,2048]{1,0:T(8,128)(2,1)}, u32[]{:S(2)}, u32[]{:S(2)}) collective-permute-start(bf16[72,2048]{1,0:T(8,128)(2,1)} %get-tuple-element.29), channel_id=1, source_target_pairs={{0,2},{1,3},{2,0},{3,1},{4,6},{5,7},{6,4},{7,5},{8,10},{9,11},{10,... | collective-permute-start | bytes 884744 | tf_op jit(solution)/shard_map/ppermute | solution.py:29
  309.9 15.2 %collective-permute-start.22 = (bf16[72,2048]{1,0:T(8,128)(2,1)}, bf16[72,2048]{1,0:T(8,128)(2,1)S(1)}, u32[]{:S(2)}, u32[]{:S(2)}) collective-permute-start(bf16[72,2048]{1,0:T(8,128)(2,1)} %get-tuple-element.28), channel_id=1, source_target_pairs={{0,3},{1,2},{2,1},{3,0},{4,7},{5,6},{6,5},{7,4},{8,11},{9,10},{10,... | collective-permute-start | bytes 884744 | tf_op jit(solution)/shard_map/ppermute | solution.py:29
  317.1 8.9 %collective-permute-start.26 = (bf16[64,2048]{1,0:T(8,128)(2,1)S(1)}, bf16[64,2048]{1,0:T(8,128)(2,1)S(1)}, u32[]{:S(2)}, u32[]{:S(2)}) collective-permute-start(bf16[64,2048]{1,0:T(8,128)(2,1)S(1)} %slice.256), channel_id=1, source_target_pairs={{0,60},{4,0},{8,4},{12,8},{16,12},{20,16},{24,20},{28,24},{32,28},... | collective-permute-start | bytes 786440 | tf_op jit(solution)/shard_map/ppermute | solution.py:22
  321.5 10.1 %collective-permute-start.25 = (bf16[64,2048]{1,0:T(8,128)(2,1)S(1)}, bf16[64,2048]{1,0:T(8,128)(2,1)S(1)}, u32[]{:S(2)}, u32[]{:S(2)}) collective-permute-start(bf16[64,2048]{1,0:T(8,128)(2,1)S(1)} %slice.255), channel_id=1, source_target_pairs={{0,4},{4,8},{8,12},{12,16},{16,20},{20,24},{24,28},{28,32},{32,36}... | collective-permute-start | bytes 786440 | tf_op jit(solution)/shard_map/ppermute | solution.py:22
  325.1 6.5 %copy-start.5 = (bf16[72,2048]{1,0:T(8,128)(2,1)}, bf16[72,2048]{1,0:T(8,128)(2,1)S(1)}, u32[]{:S(2)}) copy-start(bf16[72,2048]{1,0:T(8,128)(2,1)S(1)} %collective-permute-done.22) | copy-start | bytes 884740
  331.6 6.6 %copy-start.14 = (s32[4,4,128]{2,1,0:T(4,128)S(1)}, s32[4,4,128]{2,1,0:T(4,128)}, u32[]{:S(2)}) copy-start(s32[4,4,128]{2,1,0:T(4,128)} %get-tuple-element.49) | copy-start | bytes 24580
  334.6 10.6 %collective-permute-start.27 = (bf16[56,2048]{1,0:T(8,128)(2,1)}, bf16[56,2048]{1,0:T(8,128)(2,1)S(1)}, u32[]{:S(2)}, u32[]{:S(2)}) collective-permute-start(bf16[56,2048]{1,0:T(8,128)(2,1)} %get-tuple-element.35), channel_id=1, source_target_pairs={{0,1},{1,0},{2,3},{3,2},{4,5},{5,4},{6,7},{7,6},{8,9},{9,8},{10,11... | collective-permute-start | bytes 688136 | tf_op jit(solution)/shard_map/ppermute | solution.py:29
  339.5 9.6 %collective-permute-start.28 = (bf16[56,2048]{1,0:T(8,128)(2,1)}, bf16[56,2048]{1,0:T(8,128)(2,1)S(1)}, u32[]{:S(2)}, u32[]{:S(2)}) collective-permute-start(bf16[56,2048]{1,0:T(8,128)(2,1)} %get-tuple-element.34), channel_id=1, source_target_pairs={{0,2},{1,3},{2,0},{3,1},{4,6},{5,7},{6,4},{7,5},{8,10},{9,11},{10,... | collective-permute-start | bytes 688136 | tf_op jit(solution)/shard_map/ppermute | solution.py:29
  343.1 11.0 %collective-permute-start.29 = (bf16[56,2048]{1,0:T(8,128)(2,1)}, bf16[56,2048]{1,0:T(8,128)(2,1)S(1)}, u32[]{:S(2)}, u32[]{:S(2)}) collective-permute-start(bf16[56,2048]{1,0:T(8,128)(2,1)} %get-tuple-element.33), channel_id=1, source_target_pairs={{0,3},{1,2},{2,1},{3,0},{4,7},{5,6},{6,5},{7,4},{8,11},{9,10},{10,... | collective-permute-start | bytes 688136 | tf_op jit(solution)/shard_map/ppermute | solution.py:29
  354.0 0.7 copy-start.9
  355.4 3.3 copy-start.6
  355.4 3.3 copy-start.8
  355.5 3.3 copy-start.20
  358.8 2.4 copy-start.7
  361.2 4.1 slice-start
  362.5 2.8 slice-start.1
  370.0 1.9 copy-start.3
  370.0 46.8 %copy-start = (f32[1,256,768]{2,1,0:T(8,128)S(1)}, f32[1,256,768]{2,1,0:T(8,128)}, u32[]{:S(2)}) copy-start(f32[1,256,768]{2,1,0:T(8,128)} %param.16) | copy-start | bytes 2359300
  371.9 17.7 %collective-permute-start.36 = (bf16[256,768]{1,0:T(8,128)(2,1)S(1)}, bf16[256,768]{1,0:T(8,128)(2,1)S(1)}, u32[]{:S(2)}, u32[]{:S(2)}) collective-permute-start(bf16[256,768]{1,0:T(8,128)(2,1)S(1)} %get-tuple-element.8), channel_id=1, source_target_pairs={{0,64},{64,0},{128,192},{192,128},{256,320},{320,256},{384,448},{4... | collective-permute-start | bytes 1179656 | tf_op jit(solution)/shard_map/ppermute | solution.py:38
  376.3 17.9 %collective-permute-start.35 = (bf16[256,768]{1,0:T(8,128)(2,1)S(1)}, bf16[256,768]{1,0:T(8,128)(2,1)}, u32[]{:S(2)}, u32[]{:S(2)}) collective-permute-start(bf16[256,768]{1,0:T(8,128)(2,1)S(1)} %get-tuple-element.9), channel_id=1, source_target_pairs={{0,384},{64,448},{128,0},{192,64},{256,128},{320,192},{384,256},{4... | collective-permute-start | bytes 1179656 | tf_op jit(solution)/shard_map/ppermute | solution.py:38
  380.9 17.1 %collective-permute-start.34 = (bf16[256,768]{1,0:T(8,128)(2,1)}, bf16[256,768]{1,0:T(8,128)(2,1)}, u32[]{:S(2)}, u32[]{:S(2)}) collective-permute-start(bf16[256,768]{1,0:T(8,128)(2,1)} %get-tuple-element.10), channel_id=1, source_target_pairs={{0,128},{64,192},{128,256},{192,320},{256,384},{320,448},{384,0},{... | collective-permute-start | bytes 1179656 | tf_op jit(solution)/shard_map/ppermute | solution.py:38
  382.8 18.9 %collective-permute-start.33 = (bf16[256,768]{1,0:T(8,128)(2,1)}, bf16[256,768]{1,0:T(8,128)(2,1)}, u32[]{:S(2)}, u32[]{:S(2)}) collective-permute-start(bf16[256,768]{1,0:T(8,128)(2,1)} %get-tuple-element.11), channel_id=1, source_target_pairs={{0,256},{64,320},{128,384},{192,448},{256,0},{320,64},{384,128},{4... | collective-permute-start | bytes 1179656 | tf_op jit(solution)/shard_map/ppermute | solution.py:38
  386.4 15.4 %collective-permute-start.32 = (bf16[256,768]{1,0:T(8,128)(2,1)S(1)}, bf16[256,768]{1,0:T(8,128)(2,1)}, u32[]{:S(2)}, u32[]{:S(2)}) collective-permute-start(bf16[256,768]{1,0:T(8,128)(2,1)S(1)} %get-tuple-element.12), channel_id=1, source_target_pairs={{0,448},{64,384},{128,64},{192,0},{256,192},{320,128},{384,320},{4... | collective-permute-start | bytes 1179656 | tf_op jit(solution)/shard_map/ppermute | solution.py:38
  389.6 19.9 %collective-permute-start.31 = (bf16[256,768]{1,0:T(8,128)(2,1)S(1)}, bf16[256,768]{1,0:T(8,128)(2,1)}, u32[]{:S(2)}, u32[]{:S(2)}) collective-permute-start(bf16[256,768]{1,0:T(8,128)(2,1)S(1)} %get-tuple-element.13), channel_id=1, source_target_pairs={{0,192},{64,128},{128,320},{192,256},{256,448},{320,384},{384,64},... | collective-permute-start | bytes 1179656 | tf_op jit(solution)/shard_map/ppermute | solution.py:38
  394.1 22.7 %collective-permute-start.30 = (bf16[256,768]{1,0:T(8,128)(2,1)S(1)}, bf16[256,768]{1,0:T(8,128)(2,1)}, u32[]{:S(2)}, u32[]{:S(2)}) collective-permute-start(bf16[256,768]{1,0:T(8,128)(2,1)S(1)} %get-tuple-element.7), channel_id=1, source_target_pairs={{0,320},{64,256},{128,448},{192,384},{256,64},{320,0},{384,192},{4... | collective-permute-start | bytes 1179656 | tf_op jit(solution)/shard_map/ppermute | solution.py:38
  398.0 22.0 %copy-start.1 = (bf16[256,768]{1,0:T(8,128)(2,1)S(1)}, bf16[256,768]{1,0:T(8,128)(2,1)}, u32[]{:S(2)}) copy-start(bf16[256,768]{1,0:T(8,128)(2,1)} %broadcast_select_fusion) | copy-start | bytes 1179652
  398.0 21.9 %copy-start.2 = (f32[1,256,768]{2,1,0:T(8,128)S(1)}, f32[1,256,768]{2,1,0:T(8,128)}, u32[]{:S(2)}) copy-start(f32[1,256,768]{2,1,0:T(8,128)} %param.15) | copy-start | bytes 2359300
Sparse Core Ops, SparseCore 0:
  234.3 78.1 all-gather.2

commit v2 on v1

v2 whole, which is shorter than its diff:
```python
import functools
import math

import jax
import jax.numpy as jnp
from jax import lax
from jax.experimental import pallas as pl
from jax.experimental.pallas import tpu as pltpu
from jax.sharding import Mesh, PartitionSpec as P

beta_one = 0.9
beta_two = 0.95
learn_rate = 0.02
epsilon = 1e-08
decay_rate = 0.1
adam_step = 10.0

NY, NH, NZ, NX, NC = 4, 2, 16, 2, 2
CAP = 18
TOK, D, FF = 128, 2048, 768
SHARD = D // (NY * NH)
META = 8
WIDE = D + 128
RELS = ((0, 0), (0, 1), (1, 0), (1, 1))
GROUPS = ((0, 1, -1, 2, -2, 3, -3), (4, -4, 5, -5, 6, -6), (7, -7, 8))
INV_ROOT = 1.0 / math.sqrt(D)
SENDS = ((2, 1), (1, 1), (3, 1), (2, 0), (1, 0), (3, 0), (0, 1), (0, 0))
VMEM_LIMIT = 50 * 1024 * 1024


def rows_of(count):
    return -(-count * CAP // 16) * 16


def shift_z(block, distance):
    return lax.ppermute(block, "z", [(i, (i + distance) % NZ) for i in range(NZ)])


def swap_xc(block, dx, dc):
    pairs = [
        (x * NC + c, (x ^ dx) * NC + (c ^ dc)) for x in range(NX) for c in range(NC)
    ]
    return lax.ppermute(block, ("x", "c"), pairs)


def shift_dp(block, dy, dh):
    pairs = [
        (y * NH + h, ((y + dy) % NY) * NH + (h + dh) % NH)
        for y in range(NY)
        for h in range(NH)
    ]
    return lax.ppermute(block, ("y", "h"), pairs)


def silu_slope(preact):
    sigmoid_val = jax.nn.sigmoid(preact)
    return sigmoid_val * (1.0 + preact * (1.0 - sigmoid_val))


def adam_update(weight_now, first_now, second_now, gradient):
    first = beta_one * first_now + (1.0 - beta_one) * gradient
    second = beta_two * second_now + (1.0 - beta_two) * gradient * gradient
    first_hat = first / (1.0 - beta_one**adam_step)
    second_hat = second / (1.0 - beta_two**adam_step)
    old_weight = weight_now.astype(jnp.float32)
    updated = (
        old_weight
        - learn_rate * (first_hat / (jnp.sqrt(second_hat) + epsilon) + decay_rate * old_weight)
    ).astype(jnp.bfloat16)
    return (updated, first, second)


def select_kernel(cuts, rows, home_ref, *refs):
    outs = refs[-4:]
    count = len(cuts)
    parts, routes, factors, at = [], [], [], 0
    for cut in cuts:
        mine = refs[at : at + cut]
        at += cut
        parts += [(r, min(r.shape[0], TOK if cut == 1 else TOK // cut)) for r in mine]
        tail = mine[-1]
        facts = tail[tail.shape[0] - META :, 0 : 2 * TOK].astype(jnp.float32)
        routes.append(facts[:, :TOK])
        factors.append(facts[:, TOK:])
    masks, gains = [], []
    for i in range(4):
        home = home_ref[i].astype(jnp.float32)
        for b in range(count):
            hot = routes[b] == home
            masks.append(jnp.max(jnp.where(hot, 1.0, 0.0), axis=0, keepdims=True))
            gains.append(jnp.sum(jnp.where(hot, factors[b], 0.0), axis=0, keepdims=True))
    mask = jnp.concatenate(masks, axis=0)
    earlier = (
        lax.broadcasted_iota(jnp.int32, (TOK, TOK), 0)
        < lax.broadcasted_iota(jnp.int32, (TOK, TOK), 1)
    )
    rank = jnp.dot(
        mask.astype(jnp.bfloat16),
        jnp.where(earlier, 1.0, 0.0).astype(jnp.bfloat16),
        preferred_element_type=jnp.float32,
    )
    slots = lax.broadcasted_iota(jnp.int32, (rows, TOK), 0).astype(jnp.float32)
    selects = []
    for i in range(4):
        lanes, total = [], jnp.zeros((rows, 1), jnp.float32)
        for b in range(count):
            at = i * count + b
            slot = jnp.where(mask[at : at + 1] > 0.0, rank[at : at + 1] + float(b * CAP), -1.0)
            one = jnp.where(slots == slot, 1.0, 0.0)
            total = total + jnp.sum(one * gains[at], axis=1, keepdims=True)
            lanes.append(one.astype(jnp.bfloat16))
        selects.append(jnp.concatenate(lanes, axis=1))
        outs[i][:, D:] = jnp.broadcast_to(total, (rows, WIDE - D)).astype(jnp.bfloat16)
    select = jnp.concatenate(selects, axis=0)
    step = 512
    for j in range(0, D, step):
        source = jnp.concatenate([r[0:n, j : j + step] for r, n in parts], axis=0)
        picked = jnp.dot(select, source, preferred_element_type=jnp.float32).astype(jnp.bfloat16)
        for i in range(4):
            outs[i][:, j : j + step] = picked[i * rows : (i + 1) * rows]


def select(blocks, homes):
    cuts = tuple(len(b) for b in blocks)
    rows = rows_of(len(blocks))
    flat = [a for b in blocks for a in b]
    return pl.pallas_call(
        functools.partial(select_kernel, cuts, rows),
        out_shape=[jax.ShapeDtypeStruct((rows, WIDE), jnp.bfloat16)] * 4,
        in_specs=[pl.BlockSpec(memory_space=pltpu.SMEM)]
        + [pl.BlockSpec(memory_space=pltpu.VMEM)] * len(flat),
        out_specs=[pl.BlockSpec(memory_space=pltpu.VMEM)] * 4,
        compiler_params=pltpu.CompilerParams(vmem_limit_bytes=VMEM_LIMIT),
        cost_estimate=pl.CostEstimate(
            flops=2 * 4 * rows * len(blocks) * TOK * D,
            bytes_accessed=2 * D * (len(blocks) * TOK + 4 * rows),
            transcendentals=0,
        ),
        name="select",
    )(homes, *flat)


def slopes_kernel(*refs):
    pieces, weight_ref, readout_ref, out_ref = refs[:4], refs[4], refs[5], refs[6]
    rows = jnp.concatenate([p[:, :D] for p in pieces], axis=0)
    factor = jnp.concatenate([p[:, D : D + 1] for p in pieces], axis=0).astype(jnp.float32)
    step = 256
    for j in range(0, FF, step):
        preact = (
            jnp.dot(rows, weight_ref[:, j : j + step], preferred_element_type=jnp.float32)
            * INV_ROOT
        )
        out_ref[:, j : j + step] = (
            factor * readout_ref[:, j : j + step] * silu_slope(preact)
        ).astype(jnp.bfloat16)


def slopes_of(pieces, weight_full, readout_row):
    rows = 4 * pieces[0].shape[0]
    return pl.pallas_call(
        slopes_kernel,
        out_shape=jax.ShapeDtypeStruct((rows, FF), jnp.bfloat16),
        in_specs=[pl.BlockSpec(memory_space=pltpu.VMEM)] * 6,
        out_specs=pl.BlockSpec(memory_space=pltpu.VMEM),
        compiler_params=pltpu.CompilerParams(vmem_limit_bytes=VMEM_LIMIT),
        cost_estimate=pl.CostEstimate(
            flops=2 * rows * D * FF,
            bytes_accessed=2 * (D * FF + rows * (D + FF)),
            transcendentals=rows * FF,
        ),
        name="slopes",
    )(*pieces, weight_full, readout_row)


def gradient_kernel(n_pieces, order_ref, *refs):
    pieces, slopes, out_ref = refs[:n_pieces], refs[n_pieces:-1], refs[-1]
    rows = jnp.concatenate([p[...] for p in pieces], axis=0)
    down = jnp.concatenate([s[...] for s in slopes], axis=0)
    total = lax.dot_general(
        rows, down, (((0,), (0,)), ((), ())), preferred_element_type=jnp.float32
    )
    out_ref[0] = (total * INV_ROOT).astype(jnp.bfloat16)


def gradient_parts(pieces, slopes, order):
    parts = order.shape[0]
    rows = sum(p.shape[0] for p in pieces)
    return pl.pallas_call(
        functools.partial(gradient_kernel, len(pieces)),
        out_shape=jax.ShapeDtypeStruct((parts, SHARD, FF), jnp.bfloat16),
        grid_spec=pltpu.PrefetchScalarGridSpec(
            num_scalar_prefetch=1,
            grid=(parts,),
            in_specs=[
                pl.BlockSpec((p.shape[0], SHARD), lambda i, order: (0, order[i])) for p in pieces
            ]
            + [pl.BlockSpec(s.shape, lambda i, order: (0, 0)) for s in slopes],
            out_specs=pl.BlockSpec((1, SHARD, FF), lambda i, order: (i, 0, 0)),
        ),
        compiler_params=pltpu.CompilerParams(
            vmem_limit_bytes=VMEM_LIMIT, dimension_semantics=("arbitrary",)
        ),
        cost_estimate=pl.CostEstimate(
            flops=2 * rows * parts * SHARD * FF,
            bytes_accessed=2 * (rows * (parts * SHARD + FF) + parts * SHARD * FF),
            transcendentals=0,
        ),
        name="gradient",
    )(order, *pieces, *slopes)


def body(
    activations, routes, gate_probs, advantage, readout, weights, moment_one, moment_two, swap_flags
):
    experts = NZ * NX * NC
    half = experts // 2
    z, x, c = lax.axis_index("z"), lax.axis_index("x"), lax.axis_index("c")
    y, h = lax.axis_index("y"), lax.axis_index("h")

    def home(dx, dc):
        index = (z * NX + (x ^ dx)) * NC + (c ^ dc)
        flag = lax.dynamic_index_in_dim(swap_flags, index, 0, keepdims=False)
        return (index + flag * half) % experts, flag

    resident, my_flag = home(0, 0)
    homes = jnp.stack([home(dx, dc)[0] for dx, dc in RELS])

    weight_own = weights[0]
    weight_far = shift_z(weight_own, NZ // 2)
    weight_now = jnp.where(my_flag == 1, weight_far, weight_own)
    weight_full = lax.all_gather(weight_now, ("y", "h"), axis=0, tiled=True)

    factor = (advantage[:, None] * gate_probs).astype(jnp.bfloat16)
    facts = jnp.concatenate([routes.astype(jnp.bfloat16).T, factor.T], axis=1)
    facts = jnp.pad(facts, ((0, 0), (0, D - 2 * TOK)))
    block = jnp.concatenate([activations, facts], axis=0)
    blocks = {0: (block,)}
    fwd = bwd = block
    for k in range(1, NZ // 2):
        fwd = shift_z(fwd, 1)
        bwd = shift_z(bwd, -1)
        blocks[-k] = (fwd,)
        blocks[k] = (bwd,)
    last = (shift_z(fwd[: TOK // 2], 1), shift_z(bwd[TOK // 2 :], -1))
    moments = jnp.stack([moment_one[0], moment_two[0]]).astype(jnp.bfloat16)

    readout_row = lax.dynamic_index_in_dim(readout, resident, 0).astype(jnp.float32)

    all_pieces, all_slopes = [], []
    for number, group in enumerate(GROUPS):
        if number == len(GROUPS) - 1:
            last, moments, all_slopes = lax.optimization_barrier((last, moments, all_slopes))
            blocks[8] = last
        picked = select([blocks[o] for o in group], homes)
        pieces = [
            piece if rel == (0, 0) else swap_xc(piece, *rel) for piece, rel in zip(picked, RELS)
        ]
        all_slopes.append(slopes_of(pieces, weight_full, readout_row))
        all_pieces += pieces

    moments_far = shift_z(moments, NZ // 2)

    order = jnp.stack([((y + dy) % NY) * NH + (h + dh) % NH for dy, dh in SENDS])
    parts = gradient_parts(all_pieces, all_slopes, order)
    gradient = parts[len(SENDS) - 1].astype(jnp.float32)
    for i, (dy, dh) in enumerate(SENDS[:-1]):
        gradient = gradient + shift_dp(parts[i], dy, dh).astype(jnp.float32)

    first_now = jnp.where(my_flag == 1, moments_far[0].astype(jnp.float32), moment_one[0])
    second_now = jnp.where(my_flag == 1, moments_far[1].astype(jnp.float32), moment_two[0])
    updated, first, second = adam_update(weight_now, first_now, second_now, gradient)
    return (updated[None], first[None], second[None])


def solution(mesh):
    inner = Mesh(mesh.devices.reshape(NY, NH, NZ, NX, NC), ("y", "h", "z", "x", "c"))
    dp, expert = ("y", "h"), ("z", "x", "c")
    placed = (
        P(dp + expert, None),
        P(dp + expert, None),
        P(dp + expert, None),
        P(dp + expert),
        P(),
        P(expert, dp, None),
        P(expert, dp, None),
        P(expert, dp, None),
        P(),
    )
    return jax.shard_map(
        body,
        mesh=inner,
        in_specs=placed,
        out_specs=(P(expert, dp, None),) * 3,
        check_vma=False,
    )
```

time: 436 us -> 362 us (0.83)
  the two profiles are of different devices: /device:TPU:1 before, /device:TPU:129 now
where the time goes in v2:
time: 362 us; the launch traced here: 360 us
  waiting for transfers between devices  148 us (41%)
  starting transfers between devices  126 us (35%)
  Pallas kernels  34.8 us (10%)
  local copies, waits for them, and re-layouts  18.1 us (5%)
  between operations  18 us (5%)
  other arithmetic  15.1 us (4%)
    ppermute x18, waiting for transfers between devices, shift_z(): lax.ppermute(block, 'z', [(i, (i + distance) % NZ) for i in range(NZ)])  116 us
    ppermute x18, starting transfers between devices, shift_z(): lax.ppermute(block, 'z', [(i, (i + distance) % NZ) for i in range(NZ)])  71.6 us
    ppermute x9, starting transfers between devices, swap_xc(): return lax.ppermute(block, ('x', 'c'), pairs)  28.7 us
    ppermute x7, starting transfers between devices, shift_dp(): return lax.ppermute(block, ('y', 'h'), pairs)  25.3 us
    ppermute x7, waiting for transfers between devices, shift_dp(): return lax.ppermute(block, ('y', 'h'), pairs)  17.7 us
    ppermute x9, waiting for transfers between devices, swap_xc(): return lax.ppermute(block, ('x', 'c'), pairs)  14.6 us
    unnamed x54, local copies, waits for them, and re-layouts  13.1 us
    pallas_call x3, Pallas kernels, select(): pl.pallas_call(functools.partial(select_kernel, cuts, rows), out_shape=[j...  12.1 us
  transfers between devices with their start and end apart: 35, of which 16 were waited for; matrix products, arithmetic and copies ran while one was open for 3% of the time, Pallas kernels for 5%

profile of v2, /device:TPU:129, one launch (start us, length us, event | category | flops | bytes accessed | tf_op | source)
XLA Modules:
  0.0 359.6 jit_solution(14078295044037731885)
XLA Ops:
  7.2 10.6 %collective-permute-start = (bf16[256,768]{1,0:T(8,128)(2,1)}, bf16[256,768]{1,0:T(8,128)(2,1)S(1)}, u32[]{:S(2)}, u32[]{:S(2)}) collective-permute-start(bf16[256,768]{1,0:T(8,128)(2,1)} %bitcast.61), channel_id=1, source_target_pairs={{0,32},{4,36},{8,40},{12,44},{16,48},{20,52},{24,56},{28,60},{32,0... | collective-permute-start | bytes 1179656 | tf_op jit(solution)/shard_map/ppermute | solution.py:36
  17.9 1.5 fusion.18
  20.1 27.5 %collective-permute-done = bf16[256,768]{1,0:T(8,128)(2,1)S(1)} collective-permute-done((bf16[256,768]{1,0:T(8,128)(2,1)}, bf16[256,768]{1,0:T(8,128)(2,1)S(1)}, u32[]{:S(2)}, u32[]{:S(2)}) %collective-permute-start) | collective-permute-done | bytes 393248 | tf_op jit(solution)/shard_map/ppermute | solution.py:36
  47.6 1.8 broadcast_select_fusion
  51.9 1.9 collective-permute-start.9
  53.8 3.4 collective-permute-start.1
  57.2 9.2 %collective-permute-done.9.refs_1_ = bf16[136,2048]{1,0:T(8,128)(2,1)S(1)} collective-permute-done((bf16[136,2048]{1,0:T(8,128)(2,1)S(1)}, bf16[136,2048]{1,0:T(8,128)(2,1)S(1)}, u32[]{:S(2)}, u32[]{:S(2)}) %collective-permute-start.9) | collective-permute-done | bytes 557088 | tf_op jit(solution)/shard_map/ppermute | solution.py:36
  66.4 3.4 collective-permute-start.10
  69.9 9.2 %collective-permute-start.2 = (bf16[136,2048]{1,0:T(8,128)(2,1)S(1)}, bf16[136,2048]{1,0:T(8,128)(2,1)S(1)}, u32[]{:S(2)}, u32[]{:S(2)}) collective-permute-start(bf16[136,2048]{1,0:T(8,128)(2,1)S(1)} %collective-permute-done.1.refs_2_), channel_id=1, source_target_pairs={{0,4},{4,8},{8,12},{12,16},{16,20},{20,24},{24,28},{28,32},{32,36}... | collective-permute-start | bytes 1671176 | tf_op jit(solution)/shard_map/ppermute | solution.py:36
  79.0 9.7 %collective-permute-done.10.refs_3_ = bf16[136,2048]{1,0:T(8,128)(2,1)S(1)} collective-permute-done((bf16[136,2048]{1,0:T(8,128)(2,1)S(1)}, bf16[136,2048]{1,0:T(8,128)(2,1)S(1)}, u32[]{:S(2)}, u32[]{:S(2)}) %collective-permute-start.10) | collective-permute-done | bytes 557088 | tf_op jit(solution)/shard_map/ppermute | solution.py:36
  88.7 1.9 collective-permute-start.11
  90.7 3.4 collective-permute-start.3
  94.0 8.8 %collective-permute-done.11.refs_5_ = bf16[136,2048]{1,0:T(8,128)(2,1)S(1)} collective-permute-done((bf16[136,2048]{1,0:T(8,128)(2,1)S(1)}, bf16[136,2048]{1,0:T(8,128)(2,1)S(1)}, u32[]{:S(2)}, u32[]{:S(2)}) %collective-permute-start.11) | collective-permute-done | bytes 557088 | tf_op jit(solution)/shard_map/ppermute | solution.py:36
  102.8 3.4 collective-permute-start.12
  106.2 1.9 collective-permute-start.4
  108.2 7.9 %collective-permute-done.12.refs_0_ = bf16[136,2048]{1,0:T(8,128)(2,1)S(1)} collective-permute-done((bf16[136,2048]{1,0:T(8,128)(2,1)S(1)}, bf16[136,2048]{1,0:T(8,128)(2,1)S(1)}, u32[]{:S(2)}, u32[]{:S(2)}) %collective-permute-start.12) | collective-permute-done | bytes 557088 | tf_op jit(solution)/shard_map/ppermute | solution.py:36
  116.1 4.9 %collective-permute-start.13 = (bf16[136,2048]{1,0:T(8,128)(2,1)S(1)}, bf16[136,2048]{1,0:T(8,128)(2,1)S(1)}, u32[]{:S(2)}, u32[]{:S(2)}) collective-permute-start(bf16[136,2048]{1,0:T(8,128)(2,1)S(1)} %collective-permute-done.12.refs_0_), channel_id=1, source_target_pairs={{0,60},{4,0},{8,4},{12,8},{16,12},{20,16},{24,20},{28,24},{32,28},... | collective-permute-start | bytes 1671176 | tf_op jit(solution)/shard_map/ppermute | solution.py:36
  121.0 1.9 collective-permute-start.5
  122.9 6.6 %collective-permute-done.13.refs_2_ = bf16[136,2048]{1,0:T(8,128)(2,1)S(1)} collective-permute-done((bf16[136,2048]{1,0:T(8,128)(2,1)S(1)}, bf16[136,2048]{1,0:T(8,128)(2,1)S(1)}, u32[]{:S(2)}, u32[]{:S(2)}) %collective-permute-start.13) | collective-permute-done | bytes 557088 | tf_op jit(solution)/shard_map/ppermute | solution.py:36
  129.5 5.3 %collective-permute-start.14 = (bf16[136,2048]{1,0:T(8,128)(2,1)S(1)}, bf16[136,2048]{1,0:T(8,128)(2,1)}, u32[]{:S(2)}, u32[]{:S(2)}) collective-permute-start(bf16[136,2048]{1,0:T(8,128)(2,1)S(1)} %collective-permute-done.13.refs_2_), channel_id=1, source_target_pairs={{0,60},{4,0},{8,4},{12,8},{16,12},{20,16},{24,20},{28,24},{32,28},... | collective-permute-start | bytes 1671176 | tf_op jit(solution)/shard_map/ppermute | solution.py:36
  135.7 1.9 collective-permute-start.6
  140.3 2.1 collective-permute-done.14.refs_4_
  142.4 5.4 %collective-permute-start.15 = (bf16[136,2048]{1,0:T(8,128)(2,1)}, bf16[136,2048]{1,0:T(8,128)(2,1)S(1)}, u32[]{:S(2)}, u32[]{:S(2)}) collective-permute-start(bf16[136,2048]{1,0:T(8,128)(2,1)} %collective-permute-done.14.refs_4_), channel_id=1, source_target_pairs={{0,60},{4,0},{8,4},{12,8},{16,12},{20,16},{24,20},{28,24},{32,28},... | collective-permute-start | bytes 1671176 | tf_op jit(solution)/shard_map/ppermute | solution.py:36
  149.7 4.0 %select.33 = (bf16[112,2176]{1,0:T(8,128)(2,1)S(1)}, bf16[112,2176]{1,0:T(8,128)(2,1)S(1)}, bf16[112,2176]{1,0:T(8,128)(2,1)S(1)}, bf16[112,2176]{1,0:T(8,128)(2,1)}) custom-call(s32[4]{0:T(128)S(1)} %pad_add_fusion.home_ref, bf16[136,2048]{1,0:T(8,128)(2,1)S(1)} %collective-permute-done.12.refs_0_, bf16[136,2048]{1,0:T(8,128)(2,1)S(1)} %collective-permute-done.4.refs_1_, ...), custom_call_target="tpu_custom_call" | custom-call | flops 1409286144 | bytes 4980736 | tf_op jit(solution)/shard_map/select/pallas_call | solution.py:127
  153.6 7.4 %collective-permute-start.20 = (bf16[112,2176]{1,0:T(8,128)(2,1)S(1)}, bf16[112,2176]{1,0:T(8,128)(2,1)S(1)}, u32[]{:S(2)}, u32[]{:S(2)}) collective-permute-start(bf16[112,2176]{1,0:T(8,128)(2,1)S(1)} %get-tuple-element.25), channel_id=1, source_target_pairs={{0,1},{1,0},{2,3},{3,2},{4,5},{5,4},{6,7},{7,6},{8,9},{9,8},{10,11... | collective-permute-start | bytes 1462280 | tf_op jit(solution)/shard_map/ppermute | solution.py:43
  161.0 3.3 collective-permute-start.21
  164.3 1.9 collective-permute-start.7
  166.3 2.2 collective-permute-start.22
  168.4 5.3 %select.32 = (bf16[128,2176]{1,0:T(8,128)(2,1)S(1)}, bf16[128,2176]{1,0:T(8,128)(2,1)}, bf16[128,2176]{1,0:T(8,128)(2,1)}, bf16[128,2176]{1,0:T(8,128)(2,1)}) custom-call(s32[4]{0:T(128)S(1)} %pad_add_fusion.home_ref, bf16[136,2048]{1,0:T(8,128)(2,1)S(1)} %pad_maximum_fusion.1.refs_0_, bf16[136,2048]{1,0:T(8,128)(2,1)S(1)} %collective-permute-done.9.refs_1_, ...), custom_call_target="tpu_custom_call" | custom-call | flops 1879048192 | bytes 5767168 | tf_op jit(solution)/shard_map/select/pallas_call | solution.py:127
  174.6 2.1 collective-permute-start.17
  177.5 3.3 collective-permute-start.18
  180.8 2.4 collective-permute-start.19
  183.2 1.9 convert.7
  185.2 1.9 convert.8
  187.1 2.1 pad_maximum_fusion
  189.9 4.8 %collective-permute-start.16 = (bf16[72,2048]{1,0:T(8,128)(2,1)}, bf16[72,2048]{1,0:T(8,128)(2,1)}, u32[]{:S(2)}, u32[]{:S(2)}) collective-permute-start(bf16[72,2048]{1,0:T(8,128)(2,1)} %slice.49), channel_id=1, source_target_pairs={{0,60},{4,0},{8,4},{12,8},{16,12},{20,16},{24,20},{28,24},{32,28},... | collective-permute-start | bytes 884744 | tf_op jit(solution)/shard_map/ppermute | solution.py:36
  196.2 1.9 collective-permute-start.8
  201.2 3.8 %slopes.4.refs_13_ = bf16[448,768]{1,0:T(8,128)(2,1)S(1)} custom-call(bf16[112,2176]{1,0:T(8,128)(2,1)S(1)} %copy-done.6, bf16[112,2176]{1,0:T(8,128)(2,1)S(1)} %copy-done.9, bf16[112,2176]{1,0:T(8,128)(2,1)S(1)} %copy-done.12, bf16[112,2176]{1,0:T(8,128)(2,1)} %collective-permute-done.22.refs_3_.refs_7_, ...), custom_call_target="tpu_custom_call" | custom-call | flops 1409286144 | bytes 5668864 | tf_op jit(solution)/shard_map/slopes/pallas_call | solution.py:160
  206.0 4.1 %collective-permute-done.19.refs_3_ = bf16[128,2176]{1,0:T(8,128)(2,1)S(1)} collective-permute-done((bf16[128,2176]{1,0:T(8,128)(2,1)}, bf16[128,2176]{1,0:T(8,128)(2,1)S(1)}, u32[]{:S(2)}, u32[]{:S(2)}) %collective-permute-start.19) | collective-permute-done | bytes 557088 | tf_op jit(solution)/shard_map/ppermute | solution.py:43
  210.1 4.1 %slopes.3.refs_12_ = bf16[512,768]{1,0:T(8,128)(2,1)S(1)} custom-call(bf16[128,2176]{1,0:T(8,128)(2,1)S(1)} %get-tuple-element.20.refs_0_, bf16[128,2176]{1,0:T(8,128)(2,1)S(1)} %collective-permute-done.17.refs_1_, bf16[128,2176]{1,0:T(8,128)(2,1)S(1)} %collective-permute-done.18.refs_2_, bf16[128,2176]{1,0:T(8,128)(2,1)S(1)} %collective-permute-done.19.refs_3_, ...), custom_call_target="tpu_custom_call" | custom-call | flops 1610612736 | bytes 6029312 | tf_op jit(solution)/shard_map/slopes/pallas_call | solution.py:160
  215.1 2.8 select.34
  218.6 2.2 collective-permute-start.24
  220.8 3.3 collective-permute-start.25
  224.1 2.5 collective-permute-start.26
  226.8 4.1 %collective-permute-done.25.refs_2_.refs_10_ = bf16[64,2176]{1,0:T(8,128)(2,1)S(1)} collective-permute-done((bf16[64,2176]{1,0:T(8,128)(2,1)}, bf16[64,2176]{1,0:T(8,128)(2,1)S(1)}, u32[]{:S(2)}, u32[]{:S(2)}) %collective-permute-start.25) | collective-permute-done | bytes 278560 | tf_op jit(solution)/shard_map/ppermute | solution.py:43
  230.9 6.3 %collective-permute-done.26.refs_3_.refs_11_ = bf16[64,2176]{1,0:T(8,128)(2,1)S(1)} collective-permute-done((bf16[64,2176]{1,0:T(8,128)(2,1)}, bf16[64,2176]{1,0:T(8,128)(2,1)S(1)}, u32[]{:S(2)}, u32[]{:S(2)}) %collective-permute-start.26) | collective-permute-done | bytes 278560 | tf_op jit(solution)/shard_map/ppermute | solution.py:43
  238.2 3.0 slopes.5.refs_14_
  244.3 11.8 %gradient.1 = bf16[8,256,768]{2,1,0:T(8,128)(2,1)} custom-call(s32[8]{0:T(128)S(1)} %stack.60.order_ref, bf16[128,2176]{1,0:T(8,128)(2,1)S(1)} %get-tuple-element.20.refs_0_, bf16[128,2176]{1,0:T(8,128)(2,1)} %copy-done.2, bf16[128,2176]{1,0:T(8,128)(2,1)} %copy-done.3, bf16[128,2176]{1,0:T(8,128)(2,1)} %copy-done.4, bf16[112,2176]{1,0:T(8,128)(2,1)S(1)} %copy-done.7, ...), custom_call_target="tpu_custom_call" | custom-call | flops 3825205248 | bytes 9994240 | tf_op jit(solution)/shard_map/gradient/pallas_call | solution.py:188
  256.1 2.0 slice_bitcast_fusion.6
  258.1 7.4 %collective-permute-start.27 = (bf16[256,768]{1,0:T(8,128)(2,1)S(1)}, bf16[256,768]{1,0:T(8,128)(2,1)S(1)}, u32[]{:S(2)}, u32[]{:S(2)}) collective-permute-start(bf16[256,768]{1,0:T(8,128)(2,1)S(1)} %get-tuple-element.39), channel_id=1, source_target_pairs={{0,320},{64,256},{128,448},{192,384},{256,64},{320,0},{384,192},{4... | collective-permute-start | bytes 1179656 | tf_op jit(solution)/shard_map/ppermute | solution.py:52
  265.6 2.3 collective-permute-start.33
  267.9 2.7 collective-permute-start.32
  270.6 4.4 %collective-permute-start.23 = (bf16[2,256,768]{2,1,0:T(8,128)(2,1)S(1)}, bf16[2,256,768]{2,1,0:T(8,128)(2,1)S(1)}, u32[]{:S(2)}, u32[]{:S(2)}) collective-permute-start(bf16[2,256,768]{2,1,0:T(8,128)(2,1)S(1)} %copy-done.22), channel_id=1, source_target_pairs={{0,32},{4,36},{8,40},{12,44},{16,48},{20,52},{24,56},{28,60},{32,0... | collective-permute-start | bytes 2359304 | tf_op jit(solution)/shard_map/ppermute | solution.py:36
  275.0 2.6 collective-permute-start.31
  277.6 2.6 collective-permute-start.30
  280.3 3.4 collective-permute-done.33
  283.6 5.0 %collective-permute-start.29 = (bf16[256,768]{1,0:T(8,128)(2,1)S(1)}, bf16[256,768]{1,0:T(8,128)(2,1)S(1)}, u32[]{:S(2)}, u32[]{:S(2)}) collective-permute-start(bf16[256,768]{1,0:T(8,128)(2,1)S(1)} %get-tuple-element.44), channel_id=1, source_target_pairs={{0,448},{64,384},{128,64},{192,0},{256,192},{320,128},{384,320},{4... | collective-permute-start | bytes 1179656 | tf_op jit(solution)/shard_map/ppermute | solution.py:52
  288.6 2.7 collective-permute-start.28
  291.3 3.7 %collective-permute-done.30 = bf16[256,768]{1,0:T(8,128)(2,1)S(1)} collective-permute-done((bf16[256,768]{1,0:T(8,128)(2,1)S(1)}, bf16[256,768]{1,0:T(8,128)(2,1)S(1)}, u32[]{:S(2)}, u32[]{:S(2)}) %collective-permute-start.30) | collective-permute-done | bytes 393248 | tf_op jit(solution)/shard_map/ppermute | solution.py:52
  295.0 2.7 collective-permute-done.29
  297.7 8.0 %collective-permute-done.28 = bf16[256,768]{1,0:T(8,128)(2,1)S(1)} collective-permute-done((bf16[256,768]{1,0:T(8,128)(2,1)S(1)}, bf16[256,768]{1,0:T(8,128)(2,1)S(1)}, u32[]{:S(2)}, u32[]{:S(2)}) %collective-permute-start.28) | collective-permute-done | bytes 393248 | tf_op jit(solution)/shard_map/ppermute | solution.py:52
  305.7 43.0 %collective-permute-done.23 = bf16[2,256,768]{2,1,0:T(8,128)(2,1)S(1)} collective-permute-done((bf16[2,256,768]{2,1,0:T(8,128)(2,1)S(1)}, bf16[2,256,768]{2,1,0:T(8,128)(2,1)S(1)}, u32[]{:S(2)}, u32[]{:S(2)}) %collective-permute-start.23) | collective-permute-done | bytes 786464 | tf_op jit(solution)/shard_map/ppermute | solution.py:36
  348.6 2.4 fusion.16
  351.0 1.7 fusion.15
  (85 shorter events, 18.8 us)
Async XLA Ops:
  7.2 191.0 %all-gather.2.cloned.1.call-start = ((), (), s32[]{:S(2)}) async-start(), calls=%async_computation | async-start | bytes 3538944 | tf_op jit(solution)/shard_map/all_gather | solution.py:231
  7.2 40.4 %collective-permute-start = (bf16[256,768]{1,0:T(8,128)(2,1)}, bf16[256,768]{1,0:T(8,128)(2,1)S(1)}, u32[]{:S(2)}, u32[]{:S(2)}) collective-permute-start(bf16[256,768]{1,0:T(8,128)(2,1)} %bitcast.61), channel_id=1, source_target_pairs={{0,32},{4,36},{8,40},{12,44},{16,48},{20,52},{24,56},{28,60},{32,0... | collective-permute-start | bytes 1179656 | tf_op jit(solution)/shard_map/ppermute | solution.py:36
  51.9 14.5 %collective-permute-start.9 = (bf16[136,2048]{1,0:T(8,128)(2,1)S(1)}, bf16[136,2048]{1,0:T(8,128)(2,1)S(1)}, u32[]{:S(2)}, u32[]{:S(2)}) collective-permute-start(bf16[136,2048]{1,0:T(8,128)(2,1)S(1)} %pad_maximum_fusion.1.refs_0_), channel_id=1, source_target_pairs={{0,60},{4,0},{8,4},{12,8},{16,12},{20,16},{24,20},{28,24},{32,28},... | collective-permute-start | bytes 1671176 | tf_op jit(solution)/shard_map/ppermute | solution.py:36
  53.8 16.0 %collective-permute-start.1 = (bf16[136,2048]{1,0:T(8,128)(2,1)S(1)}, bf16[136,2048]{1,0:T(8,128)(2,1)S(1)}, u32[]{:S(2)}, u32[]{:S(2)}) collective-permute-start(bf16[136,2048]{1,0:T(8,128)(2,1)S(1)} %pad_maximum_fusion.1.refs_0_), channel_id=1, source_target_pairs={{0,4},{4,8},{8,12},{12,16},{16,20},{20,24},{24,28},{28,32},{32,36}... | collective-permute-start | bytes 1671176 | tf_op jit(solution)/shard_map/ppermute | solution.py:36
  66.4 22.3 %collective-permute-start.10 = (bf16[136,2048]{1,0:T(8,128)(2,1)S(1)}, bf16[136,2048]{1,0:T(8,128)(2,1)S(1)}, u32[]{:S(2)}, u32[]{:S(2)}) collective-permute-start(bf16[136,2048]{1,0:T(8,128)(2,1)S(1)} %collective-permute-done.9.refs_1_), channel_id=1, source_target_pairs={{0,60},{4,0},{8,4},{12,8},{16,12},{20,16},{24,20},{28,24},{32,28},... | collective-permute-start | bytes 1671176 | tf_op jit(solution)/shard_map/ppermute | solution.py:36
  69.9 20.8 %collective-permute-start.2 = (bf16[136,2048]{1,0:T(8,128)(2,1)S(1)}, bf16[136,2048]{1,0:T(8,128)(2,1)S(1)}, u32[]{:S(2)}, u32[]{:S(2)}) collective-permute-start(bf16[136,2048]{1,0:T(8,128)(2,1)S(1)} %collective-permute-done.1.refs_2_), channel_id=1, source_target_pairs={{0,4},{4,8},{8,12},{12,16},{16,20},{20,24},{24,28},{28,32},{32,36}... | collective-permute-start | bytes 1671176 | tf_op jit(solution)/shard_map/ppermute | solution.py:36
  88.7 46.9 %copy-start.23 = (bf16[136,2048]{1,0:T(8,128)(2,1)}, bf16[136,2048]{1,0:T(8,128)(2,1)S(1)}, u32[]{:S(2)}) copy-start(bf16[136,2048]{1,0:T(8,128)(2,1)S(1)} %collective-permute-done.10.refs_3_) | copy-start | bytes 1671172
  88.7 14.1 %collective-permute-start.11 = (bf16[136,2048]{1,0:T(8,128)(2,1)S(1)}, bf16[136,2048]{1,0:T(8,128)(2,1)S(1)}, u32[]{:S(2)}, u32[]{:S(2)}) collective-permute-start(bf16[136,2048]{1,0:T(8,128)(2,1)S(1)} %collective-permute-done.10.refs_3_), channel_id=1, source_target_pairs={{0,60},{4,0},{8,4},{12,8},{16,12},{20,16},{24,20},{28,24},{32,28},... | collective-permute-start | bytes 1671176 | tf_op jit(solution)/shard_map/ppermute | solution.py:36
  90.7 15.6 %copy-start.24 = (bf16[136,2048]{1,0:T(8,128)(2,1)}, bf16[136,2048]{1,0:T(8,128)(2,1)S(1)}, u32[]{:S(2)}) copy-start(bf16[136,2048]{1,0:T(8,128)(2,1)S(1)} %collective-permute-done.2.refs_4_) | copy-start | bytes 1671172
  90.7 15.6 %collective-permute-start.3 = (bf16[136,2048]{1,0:T(8,128)(2,1)S(1)}, bf16[136,2048]{1,0:T(8,128)(2,1)S(1)}, u32[]{:S(2)}, u32[]{:S(2)}) collective-permute-start(bf16[136,2048]{1,0:T(8,128)(2,1)S(1)} %collective-permute-done.2.refs_4_), channel_id=1, source_target_pairs={{0,4},{4,8},{8,12},{12,16},{16,20},{20,24},{24,28},{28,32},{32,36}... | collective-permute-start | bytes 1671176 | tf_op jit(solution)/shard_map/ppermute | solution.py:36
  102.8 34.8 %copy-start.25 = (bf16[136,2048]{1,0:T(8,128)(2,1)}, bf16[136,2048]{1,0:T(8,128)(2,1)S(1)}, u32[]{:S(2)}) copy-start(bf16[136,2048]{1,0:T(8,128)(2,1)S(1)} %collective-permute-done.11.refs_5_) | copy-start | bytes 1671172
  102.8 13.3 %collective-permute-start.12 = (bf16[136,2048]{1,0:T(8,128)(2,1)S(1)}, bf16[136,2048]{1,0:T(8,128)(2,1)S(1)}, u32[]{:S(2)}, u32[]{:S(2)}) collective-permute-start(bf16[136,2048]{1,0:T(8,128)(2,1)S(1)} %collective-permute-done.11.refs_5_), channel_id=1, source_target_pairs={{0,60},{4,0},{8,4},{12,8},{16,12},{20,16},{24,20},{28,24},{32,28},... | collective-permute-start | bytes 1671176 | tf_op jit(solution)/shard_map/ppermute | solution.py:36
  106.2 31.4 %copy-start.26 = (bf16[136,2048]{1,0:T(8,128)(2,1)}, bf16[136,2048]{1,0:T(8,128)(2,1)S(1)}, u32[]{:S(2)}) copy-start(bf16[136,2048]{1,0:T(8,128)(2,1)S(1)} %collective-permute-done.3.refs_6_) | copy-start | bytes 1671172
  106.2 14.7 %collective-permute-start.4 = (bf16[136,2048]{1,0:T(8,128)(2,1)S(1)}, bf16[136,2048]{1,0:T(8,128)(2,1)S(1)}, u32[]{:S(2)}, u32[]{:S(2)}) collective-permute-start(bf16[136,2048]{1,0:T(8,128)(2,1)S(1)} %collective-permute-done.3.refs_6_), channel_id=1, source_target_pairs={{0,4},{4,8},{8,12},{12,16},{16,20},{20,24},{24,28},{28,32},{32,36}... | collective-permute-start | bytes 1671176 | tf_op jit(solution)/shard_map/ppermute | solution.py:36
  116.1 13.4 %collective-permute-start.13 = (bf16[136,2048]{1,0:T(8,128)(2,1)S(1)}, bf16[136,2048]{1,0:T(8,128)(2,1)S(1)}, u32[]{:S(2)}, u32[]{:S(2)}) collective-permute-start(bf16[136,2048]{1,0:T(8,128)(2,1)S(1)} %collective-permute-done.12.refs_0_), channel_id=1, source_target_pairs={{0,60},{4,0},{8,4},{12,8},{16,12},{20,16},{24,20},{28,24},{32,28},... | collective-permute-start | bytes 1671176 | tf_op jit(solution)/shard_map/ppermute | solution.py:36
  121.0 14.7 %collective-permute-start.5 = (bf16[136,2048]{1,0:T(8,128)(2,1)S(1)}, bf16[136,2048]{1,0:T(8,128)(2,1)}, u32[]{:S(2)}, u32[]{:S(2)}) collective-permute-start(bf16[136,2048]{1,0:T(8,128)(2,1)S(1)} %collective-permute-done.4.refs_1_), channel_id=1, source_target_pairs={{0,4},{4,8},{8,12},{12,16},{16,20},{20,24},{24,28},{28,32},{32,36}... | collective-permute-start | bytes 1671176 | tf_op jit(solution)/shard_map/ppermute | solution.py:36
  129.5 12.9 %collective-permute-start.14 = (bf16[136,2048]{1,0:T(8,128)(2,1)S(1)}, bf16[136,2048]{1,0:T(8,128)(2,1)}, u32[]{:S(2)}, u32[]{:S(2)}) collective-permute-start(bf16[136,2048]{1,0:T(8,128)(2,1)S(1)} %collective-permute-done.13.refs_2_), channel_id=1, source_target_pairs={{0,60},{4,0},{8,4},{12,8},{16,12},{20,16},{24,20},{28,24},{32,28},... | collective-permute-start | bytes 1671176 | tf_op jit(solution)/shard_map/ppermute | solution.py:36
  134.8 0.9 copy-start.17
  135.7 12.9 %collective-permute-start.6 = (bf16[136,2048]{1,0:T(8,128)(2,1)}, bf16[136,2048]{1,0:T(8,128)(2,1)}, u32[]{:S(2)}, u32[]{:S(2)}) collective-permute-start(bf16[136,2048]{1,0:T(8,128)(2,1)} %collective-permute-done.5.refs_3_), channel_id=1, source_target_pairs={{0,4},{4,8},{8,12},{12,16},{16,20},{20,24},{24,28},{28,32},{32,36}... | collective-permute-start | bytes 1671176 | tf_op jit(solution)/shard_map/ppermute | solution.py:36
  142.4 38.4 %collective-permute-start.15 = (bf16[136,2048]{1,0:T(8,128)(2,1)}, bf16[136,2048]{1,0:T(8,128)(2,1)S(1)}, u32[]{:S(2)}, u32[]{:S(2)}) collective-permute-start(bf16[136,2048]{1,0:T(8,128)(2,1)} %collective-permute-done.14.refs_4_), channel_id=1, source_target_pairs={{0,60},{4,0},{8,4},{12,8},{16,12},{20,16},{24,20},{28,24},{32,28},... | collective-permute-start | bytes 1671176 | tf_op jit(solution)/shard_map/ppermute | solution.py:36
  148.6 1.1 copy-start.18
  153.6 20.1 %copy-start.5 = (bf16[112,2176]{1,0:T(8,128)(2,1)}, bf16[112,2176]{1,0:T(8,128)(2,1)S(1)}, u32[]{:S(2)}) copy-start(bf16[112,2176]{1,0:T(8,128)(2,1)S(1)} %get-tuple-element.24.refs_0_.refs_4_) | copy-start | bytes 1462276
  153.6 20.1 %collective-permute-start.20 = (bf16[112,2176]{1,0:T(8,128)(2,1)S(1)}, bf16[112,2176]{1,0:T(8,128)(2,1)S(1)}, u32[]{:S(2)}, u32[]{:S(2)}) collective-permute-start(bf16[112,2176]{1,0:T(8,128)(2,1)S(1)} %get-tuple-element.25), channel_id=1, source_target_pairs={{0,1},{1,0},{2,3},{3,2},{4,5},{5,4},{6,7},{7,6},{8,9},{9,8},{10,11... | collective-permute-start | bytes 1462280 | tf_op jit(solution)/shard_map/ppermute | solution.py:43
  161.0 15.6 %collective-permute-start.21 = (bf16[112,2176]{1,0:T(8,128)(2,1)S(1)}, bf16[112,2176]{1,0:T(8,128)(2,1)S(1)}, u32[]{:S(2)}, u32[]{:S(2)}) collective-permute-start(bf16[112,2176]{1,0:T(8,128)(2,1)S(1)} %get-tuple-element.26), channel_id=1, source_target_pairs={{0,2},{1,3},{2,0},{3,1},{4,6},{5,7},{6,4},{7,5},{8,10},{9,11},{10,... | collective-permute-start | bytes 1462280 | tf_op jit(solution)/shard_map/ppermute | solution.py:43
  164.3 25.5 %collective-permute-start.7 = (bf16[136,2048]{1,0:T(8,128)(2,1)}, bf16[136,2048]{1,0:T(8,128)(2,1)S(1)}, u32[]{:S(2)}, u32[]{:S(2)}) collective-permute-start(bf16[136,2048]{1,0:T(8,128)(2,1)} %collective-permute-done.6.refs_5_), channel_id=1, source_target_pairs={{0,4},{4,8},{8,12},{12,16},{16,20},{20,24},{24,28},{28,32},{32,36}... | collective-permute-start | bytes 1671176 | tf_op jit(solution)/shard_map/ppermute | solution.py:36
  166.3 29.9 %collective-permute-start.22 = (bf16[112,2176]{1,0:T(8,128)(2,1)}, bf16[112,2176]{1,0:T(8,128)(2,1)}, u32[]{:S(2)}, u32[]{:S(2)}) collective-permute-start(bf16[112,2176]{1,0:T(8,128)(2,1)} %get-tuple-element.27), channel_id=1, source_target_pairs={{0,3},{1,2},{2,1},{3,0},{4,7},{5,6},{6,5},{7,4},{8,11},{9,10},{10,... | collective-permute-start | bytes 1462280 | tf_op jit(solution)/shard_map/ppermute | solution.py:43
  173.8 0.8 copy-start.8
  174.6 31.4 %collective-permute-start.17 = (bf16[128,2176]{1,0:T(8,128)(2,1)}, bf16[128,2176]{1,0:T(8,128)(2,1)S(1)}, u32[]{:S(2)}, u32[]{:S(2)}) collective-permute-start(bf16[128,2176]{1,0:T(8,128)(2,1)} %get-tuple-element.21), channel_id=1, source_target_pairs={{0,1},{1,0},{2,3},{3,2},{4,5},{5,4},{6,7},{7,6},{8,9},{9,8},{10,11... | collective-permute-start | bytes 1671176 | tf_op jit(solution)/shard_map/ppermute | solution.py:43
  176.7 0.8 copy-start.11
  177.5 28.5 %collective-permute-start.18 = (bf16[128,2176]{1,0:T(8,128)(2,1)}, bf16[128,2176]{1,0:T(8,128)(2,1)S(1)}, u32[]{:S(2)}, u32[]{:S(2)}) collective-permute-start(bf16[128,2176]{1,0:T(8,128)(2,1)} %get-tuple-element.22), channel_id=1, source_target_pairs={{0,2},{1,3},{2,0},{3,1},{4,6},{5,7},{6,4},{7,5},{8,10},{9,11},{10,... | collective-permute-start | bytes 1671176 | tf_op jit(solution)/shard_map/ppermute | solution.py:43
  180.8 29.3 %collective-permute-start.19 = (bf16[128,2176]{1,0:T(8,128)(2,1)}, bf16[128,2176]{1,0:T(8,128)(2,1)S(1)}, u32[]{:S(2)}, u32[]{:S(2)}) collective-permute-start(bf16[128,2176]{1,0:T(8,128)(2,1)} %get-tuple-element.23), channel_id=1, source_target_pairs={{0,3},{1,2},{2,1},{3,0},{4,7},{5,6},{6,5},{7,4},{8,11},{9,10},{10,... | collective-permute-start | bytes 1671176 | tf_op jit(solution)/shard_map/ppermute | solution.py:43
  189.9 25.2 %collective-permute-start.16 = (bf16[72,2048]{1,0:T(8,128)(2,1)}, bf16[72,2048]{1,0:T(8,128)(2,1)}, u32[]{:S(2)}, u32[]{:S(2)}) collective-permute-start(bf16[72,2048]{1,0:T(8,128)(2,1)} %slice.49), channel_id=1, source_target_pairs={{0,60},{4,0},{8,4},{12,8},{16,12},{20,16},{24,20},{28,24},{32,28},... | collective-permute-start | bytes 884744 | tf_op jit(solution)/shard_map/ppermute | solution.py:36
  196.2 18.9 %collective-permute-start.8 = (bf16[64,2048]{1,0:T(8,128)(2,1)}, bf16[64,2048]{1,0:T(8,128)(2,1)}, u32[]{:S(2)}, u32[]{:S(2)}) collective-permute-start(bf16[64,2048]{1,0:T(8,128)(2,1)} %slice.48), channel_id=1, source_target_pairs={{0,4},{4,8},{8,12},{12,16},{16,20},{20,24},{24,28},{28,32},{32,36}... | collective-permute-start | bytes 786440 | tf_op jit(solution)/shard_map/ppermute | solution.py:36
  198.1 1.0 copy-start.6
  199.2 1.0 copy-start.9
  200.2 1.0 copy-start.12
  205.1 0.9 copy-start.1
  206.0 11.9 %copy-start.2 = (bf16[128,2176]{1,0:T(8,128)(2,1)}, bf16[128,2176]{1,0:T(8,128)(2,1)S(1)}, u32[]{:S(2)}) copy-start(bf16[128,2176]{1,0:T(8,128)(2,1)S(1)} %collective-permute-done.17.refs_1_) | copy-start | bytes 1671172
  206.0 11.9 %copy-start.3 = (bf16[128,2176]{1,0:T(8,128)(2,1)}, bf16[128,2176]{1,0:T(8,128)(2,1)S(1)}, u32[]{:S(2)}) copy-start(bf16[128,2176]{1,0:T(8,128)(2,1)S(1)} %collective-permute-done.18.refs_2_) | copy-start | bytes 1671172
  210.1 7.8 %copy-start.4 = (bf16[128,2176]{1,0:T(8,128)(2,1)}, bf16[128,2176]{1,0:T(8,128)(2,1)S(1)}, u32[]{:S(2)}) copy-start(bf16[128,2176]{1,0:T(8,128)(2,1)S(1)} %collective-permute-done.19.refs_3_) | copy-start | bytes 1671172
  214.2 0.9 copy-start
  217.9 0.7 copy-start.14
  218.6 8.2 %collective-permute-start.24 = (bf16[64,2176]{1,0:T(8,128)(2,1)}, bf16[64,2176]{1,0:T(8,128)(2,1)S(1)}, u32[]{:S(2)}, u32[]{:S(2)}) collective-permute-start(bf16[64,2176]{1,0:T(8,128)(2,1)} %get-tuple-element.32), channel_id=1, source_target_pairs={{0,1},{1,0},{2,3},{3,2},{4,5},{5,4},{6,7},{7,6},{8,9},{9,8},{10,11... | collective-permute-start | bytes 835592 | tf_op jit(solution)/shard_map/ppermute | solution.py:43
  220.8 10.1 %collective-permute-start.25 = (bf16[64,2176]{1,0:T(8,128)(2,1)}, bf16[64,2176]{1,0:T(8,128)(2,1)S(1)}, u32[]{:S(2)}, u32[]{:S(2)}) collective-permute-start(bf16[64,2176]{1,0:T(8,128)(2,1)} %get-tuple-element.33), channel_id=1, source_target_pairs={{0,2},{1,3},{2,0},{3,1},{4,6},{5,7},{6,4},{7,5},{8,10},{9,11},{10,... | collective-permute-start | bytes 835592 | tf_op jit(solution)/shard_map/ppermute | solution.py:43
  224.1 13.1 %collective-permute-start.26 = (bf16[64,2176]{1,0:T(8,128)(2,1)}, bf16[64,2176]{1,0:T(8,128)(2,1)S(1)}, u32[]{:S(2)}, u32[]{:S(2)}) collective-permute-start(bf16[64,2176]{1,0:T(8,128)(2,1)} %get-tuple-element.34), channel_id=1, source_target_pairs={{0,3},{1,2},{2,1},{3,0},{4,7},{5,6},{6,5},{7,4},{8,11},{9,10},{10,... | collective-permute-start | bytes 835592 | tf_op jit(solution)/shard_map/ppermute | solution.py:43
  237.3 1.0 copy-start.15
  238.2 3.0 copy-start.16
  241.3 1.0 copy-start.7
  242.3 1.0 copy-start.10
  243.3 1.0 copy-start.13
  256.1 14.5 %copy-start.22 = (bf16[2,256,768]{2,1,0:T(8,128)(2,1)S(1)}, bf16[2,256,768]{2,1,0:T(8,128)(2,1)}, u32[]{:S(2)}) copy-start(bf16[2,256,768]{2,1,0:T(8,128)(2,1)} %pad_maximum_fusion) | copy-start | bytes 2359300
  256.1 92.5 %copy-start.19 = (f32[1,256,768]{2,1,0:T(8,128)S(1)}, f32[1,256,768]{2,1,0:T(8,128)}, u32[]{:S(2)}) copy-start(f32[1,256,768]{2,1,0:T(8,128)} %param.16) | copy-start | bytes 2359300
  258.1 92.9 %copy-start.20 = (bf16[256,768]{1,0:T(8,128)(2,1)S(1)}, bf16[256,768]{1,0:T(8,128)(2,1)}, u32[]{:S(2)}) copy-start(bf16[256,768]{1,0:T(8,128)(2,1)} %broadcast_select_fusion) | copy-start | bytes 1179652
  258.1 92.9 %copy-start.21 = (f32[1,256,768]{2,1,0:T(8,128)S(1)}, f32[1,256,768]{2,1,0:T(8,128)}, u32[]{:S(2)}) copy-start(f32[1,256,768]{2,1,0:T(8,128)} %param.15) | copy-start | bytes 2359300
  258.1 19.5 %collective-permute-start.27 = (bf16[256,768]{1,0:T(8,128)(2,1)S(1)}, bf16[256,768]{1,0:T(8,128)(2,1)S(1)}, u32[]{:S(2)}, u32[]{:S(2)}) collective-permute-start(bf16[256,768]{1,0:T(8,128)(2,1)S(1)} %get-tuple-element.39), channel_id=1, source_target_pairs={{0,320},{64,256},{128,448},{192,384},{256,64},{320,0},{384,192},{4... | collective-permute-start | bytes 1179656 | tf_op jit(solution)/shard_map/ppermute | solution.py:52
  265.6 18.0 %collective-permute-start.33 = (bf16[256,768]{1,0:T(8,128)(2,1)S(1)}, bf16[256,768]{1,0:T(8,128)(2,1)S(1)}, u32[]{:S(2)}, u32[]{:S(2)}) collective-permute-start(bf16[256,768]{1,0:T(8,128)(2,1)S(1)} %get-tuple-element.40), channel_id=1, source_target_pairs={{0,64},{64,0},{128,192},{192,128},{256,320},{320,256},{384,448},{4... | collective-permute-start | bytes 1179656 | tf_op jit(solution)/shard_map/ppermute | solution.py:52
  267.9 20.7 %collective-permute-start.32 = (bf16[256,768]{1,0:T(8,128)(2,1)S(1)}, bf16[256,768]{1,0:T(8,128)(2,1)S(1)}, u32[]{:S(2)}, u32[]{:S(2)}) collective-permute-start(bf16[256,768]{1,0:T(8,128)(2,1)S(1)} %get-tuple-element.41), channel_id=1, source_target_pairs={{0,384},{64,448},{128,0},{192,64},{256,128},{320,192},{384,256},{4... | collective-permute-start | bytes 1179656 | tf_op jit(solution)/shard_map/ppermute | solution.py:52
  270.6 78.0 %collective-permute-start.23 = (bf16[2,256,768]{2,1,0:T(8,128)(2,1)S(1)}, bf16[2,256,768]{2,1,0:T(8,128)(2,1)S(1)}, u32[]{:S(2)}, u32[]{:S(2)}) collective-permute-start(bf16[2,256,768]{2,1,0:T(8,128)(2,1)S(1)} %copy-done.22), channel_id=1, source_target_pairs={{0,32},{4,36},{8,40},{12,44},{16,48},{20,52},{24,56},{28,60},{32,0... | collective-permute-start | bytes 2359304 | tf_op jit(solution)/shard_map/ppermute | solution.py:36
  275.0 16.3 %collective-permute-start.31 = (bf16[256,768]{1,0:T(8,128)(2,1)S(1)}, bf16[256,768]{1,0:T(8,128)(2,1)S(1)}, u32[]{:S(2)}, u32[]{:S(2)}) collective-permute-start(bf16[256,768]{1,0:T(8,128)(2,1)S(1)} %get-tuple-element.42), channel_id=1, source_target_pairs={{0,128},{64,192},{128,256},{192,320},{256,384},{320,448},{384,0},{... | collective-permute-start | bytes 1179656 | tf_op jit(solution)/shard_map/ppermute | solution.py:52
  277.6 17.4 %collective-permute-start.30 = (bf16[256,768]{1,0:T(8,128)(2,1)S(1)}, bf16[256,768]{1,0:T(8,128)(2,1)S(1)}, u32[]{:S(2)}, u32[]{:S(2)}) collective-permute-start(bf16[256,768]{1,0:T(8,128)(2,1)S(1)} %get-tuple-element.43), channel_id=1, source_target_pairs={{0,256},{64,320},{128,384},{192,448},{256,0},{320,64},{384,128},{4... | collective-permute-start | bytes 1179656 | tf_op jit(solution)/shard_map/ppermute | solution.py:52
  283.6 14.1 %collective-permute-start.29 = (bf16[256,768]{1,0:T(8,128)(2,1)S(1)}, bf16[256,768]{1,0:T(8,128)(2,1)S(1)}, u32[]{:S(2)}, u32[]{:S(2)}) collective-permute-start(bf16[256,768]{1,0:T(8,128)(2,1)S(1)} %get-tuple-element.44), channel_id=1, source_target_pairs={{0,448},{64,384},{128,64},{192,0},{256,192},{320,128},{384,320},{4... | collective-permute-start | bytes 1179656 | tf_op jit(solution)/shard_map/ppermute | solution.py:52
  288.6 17.0 %collective-permute-start.28 = (bf16[256,768]{1,0:T(8,128)(2,1)S(1)}, bf16[256,768]{1,0:T(8,128)(2,1)S(1)}, u32[]{:S(2)}, u32[]{:S(2)}) collective-permute-start(bf16[256,768]{1,0:T(8,128)(2,1)S(1)} %get-tuple-element.45), channel_id=1, source_target_pairs={{0,192},{64,128},{128,320},{192,256},{256,448},{320,384},{384,64},... | collective-permute-start | bytes 1179656 | tf_op jit(solution)/shard_map/ppermute | solution.py:52
Sparse Core Ops, SparseCore 0:
  49.5 86.9 all-gather.1

commit v3 on v2

v3 whole, which is shorter than its diff:
```python
import functools
import math

import jax
import jax.numpy as jnp
from jax import lax
from jax.experimental import pallas as pl
from jax.experimental.pallas import tpu as pltpu
from jax.sharding import Mesh, PartitionSpec as P

beta_one = 0.9
beta_two = 0.95
learn_rate = 0.02
epsilon = 1e-08
decay_rate = 0.1
adam_step = 10.0

NY, NH, NZ, NX, NC = 4, 2, 16, 2, 2
CAP = 18
TOK, D, FF = 128, 2048, 768
SHARD = D // (NY * NH)
META = 8
WIDE = D + 128
RELS = ((0, 0), (0, 1), (1, 0), (1, 1))
GROUPS = (((0, 1, -1, 2, -2, 3), (-3, 4, -4, 5, -5)), ((6, -6, 7, -7, 8),))
TILE = 512
INV_ROOT = 1.0 / math.sqrt(D)
SENDS = ((2, 1), (1, 1), (3, 1), (2, 0), (1, 0), (3, 0), (0, 1))
CUTS = (SHARD // 8, 7 * SHARD // 8)
VMEM_LIMIT = 56 * 1024 * 1024


def rows_of(count):
    return -(-count * CAP // 16) * 16


def shift_z(block, distance):
    return lax.ppermute(block, "z", [(i, (i + distance) % NZ) for i in range(NZ)])


def swap_xc(block, dx, dc):
    pairs = [
        (x * NC + c, (x ^ dx) * NC + (c ^ dc)) for x in range(NX) for c in range(NC)
    ]
    return lax.ppermute(block, ("x", "c"), pairs)


def shift_dp(block, dy, dh):
    pairs = [
        (y * NH + h, ((y + dy) % NY) * NH + (h + dh) % NH)
        for y in range(NY)
        for h in range(NH)
    ]
    return lax.ppermute(block, ("y", "h"), pairs)


def silu_slope(preact):
    sigmoid_val = jax.nn.sigmoid(preact)
    return sigmoid_val * (1.0 + preact * (1.0 - sigmoid_val))


def cast_kernel(one_ref, two_ref, *outs):
    at = 0
    for out in outs:
        rows = out.shape[1]
        out[0] = one_ref[at : at + rows, :].astype(jnp.bfloat16)
        out[1] = two_ref[at : at + rows, :].astype(jnp.bfloat16)
        at += rows


def cast_moments(one, two):
    step = FF // 2
    return pl.pallas_call(
        cast_kernel,
        out_shape=[jax.ShapeDtypeStruct((2, rows, FF), jnp.bfloat16) for rows in CUTS],
        grid=(FF // step,),
        in_specs=[pl.BlockSpec((SHARD, step), lambda i: (0, i))] * 2,
        out_specs=[pl.BlockSpec((2, rows, step), lambda i: (0, 0, i)) for rows in CUTS],
        compiler_params=pltpu.CompilerParams(vmem_limit_bytes=VMEM_LIMIT),
        cost_estimate=pl.CostEstimate(
            flops=2 * SHARD * FF, bytes_accessed=12 * SHARD * FF, transcendentals=0
        ),
        name="cast",
    )(one, two)


def adam_kernel(n_parts, flag_ref, *refs):
    parts = refs[:n_parts]
    own_ref, weight_ref, one_ref, two_ref = refs[n_parts : n_parts + 4]
    far_a, far_b = refs[n_parts + 4 : n_parts + 6]
    updated_ref, first_ref, second_ref = refs[n_parts + 6 :]
    total = own_ref[0].astype(jnp.float32)
    for part in parts:
        total = total + part[...].astype(jnp.float32)
    gradient = total.T
    swapped = flag_ref[0] == 1
    rows = gradient.shape[0]
    rest = rows - far_a.shape[1]
    low = jnp.concatenate([far_a[...], far_b[:, :rest]], axis=1).astype(jnp.float32)
    high = far_b[:, rest:].astype(jnp.float32)
    far = jnp.where(pl.program_id(0) == 0, low, high)
    first_now = jnp.where(swapped, far[0], one_ref[...])
    second_now = jnp.where(swapped, far[1], two_ref[...])
    first = beta_one * first_now + (1.0 - beta_one) * gradient
    second = beta_two * second_now + (1.0 - beta_two) * gradient * gradient
    first_hat = first / (1.0 - beta_one**adam_step)
    second_hat = second / (1.0 - beta_two**adam_step)
    old_weight = weight_ref[...].astype(jnp.float32)
    updated_ref[...] = (
        old_weight
        - learn_rate * (first_hat / (jnp.sqrt(second_hat) + epsilon) + decay_rate * old_weight)
    ).astype(jnp.bfloat16)
    first_ref[...] = first
    second_ref[...] = second


def adam(flag, own, received, weight, one, two, far):
    step = SHARD // 2
    plain = pl.BlockSpec((step, FF), lambda i: (i, 0))
    whole = [pl.BlockSpec(f.shape, lambda i: (0, 0, 0)) for f in far]
    return pl.pallas_call(
        functools.partial(adam_kernel, len(received)),
        out_shape=[
            jax.ShapeDtypeStruct((SHARD, FF), jnp.bfloat16),
            jax.ShapeDtypeStruct((SHARD, FF), jnp.float32),
            jax.ShapeDtypeStruct((SHARD, FF), jnp.float32),
        ],
        grid=(SHARD // step,),
        in_specs=[pl.BlockSpec(memory_space=pltpu.SMEM)]
        + [pl.BlockSpec((FF, step), lambda i: (0, i))] * len(received)
        + [pl.BlockSpec((1, FF, step), lambda i: (0, 0, i))]
        + [plain, plain, plain]
        + whole,
        out_specs=[plain] * 3,
        compiler_params=pltpu.CompilerParams(vmem_limit_bytes=VMEM_LIMIT),
        cost_estimate=pl.CostEstimate(
            flops=30 * SHARD * FF, bytes_accessed=40 * SHARD * FF, transcendentals=SHARD * FF
        ),
        name="adam",
    )(flag, *received, own, weight, one, two, *far)


def pick_plan(homes, facts, rows):
    count = len(facts)
    masks, gains = [], []
    for home in homes:
        for routes, factors in facts:
            hot = routes == home
            masks.append(jnp.max(jnp.where(hot, 1.0, 0.0), axis=0, keepdims=True))
            gains.append(jnp.sum(jnp.where(hot, factors, 0.0), axis=0, keepdims=True))
    mask = jnp.concatenate(masks, axis=0)
    earlier = (
        lax.broadcasted_iota(jnp.int32, (TOK, TOK), 0)
        < lax.broadcasted_iota(jnp.int32, (TOK, TOK), 1)
    )
    rank = jnp.dot(
        mask.astype(jnp.bfloat16),
        jnp.where(earlier, 1.0, 0.0).astype(jnp.bfloat16),
        preferred_element_type=jnp.float32,
    )
    slots = lax.broadcasted_iota(jnp.int32, (rows, TOK), 0).astype(jnp.float32)
    selects, totals = [], []
    for i in range(len(homes)):
        lanes, total = [], jnp.zeros((rows, 1), jnp.float32)
        for b in range(count):
            at = i * count + b
            slot = jnp.where(mask[at : at + 1] > 0.0, rank[at : at + 1] + float(b * CAP), -1.0)
            one = jnp.where(slots == slot, 1.0, 0.0)
            total = total + jnp.sum(one * gains[at], axis=1, keepdims=True)
            lanes.append(one.astype(jnp.bfloat16))
        selects.append(jnp.concatenate(lanes, axis=1))
        totals.append(total)
    return jnp.concatenate(selects, axis=0), totals


def select_kernel(cuts, home_ref, *refs):
    n_in = sum(sum(cut) for cut in cuts)
    ins, outs, plans = refs[:n_in], refs[n_in : n_in + 4], refs[n_in + 4 : -1]
    gain_ref = refs[-1]
    step = pl.program_id(0)

    @pl.when(step == 0)
    def _():
        homes = [home_ref[i].astype(jnp.float32) for i in range(4)]
        at = row = 0
        for cut, plan in zip(cuts, plans):
            facts = []
            for n in cut:
                tail = ins[at + n - 1]
                found = tail[tail.shape[0] - META :, 0 : 2 * TOK].astype(jnp.float32)
                facts.append((found[:, :TOK], found[:, TOK:]))
                at += n
            rows = rows_of(len(cut))
            chosen, totals = pick_plan(homes, facts, rows)
            plan[...] = chosen
            for i in range(4):
                gain_ref[i, row : row + rows, :] = jnp.broadcast_to(
                    totals[i], (rows, WIDE - D)
                ).astype(jnp.bfloat16)
            row += rows

    @pl.when(step < D // TILE)
    def _():
        at = row = 0
        for cut, plan in zip(cuts, plans):
            parts = []
            for n in cut:
                parts += [r[0 : TOK // n, :] for r in ins[at : at + n]]
                at += n
            rows = rows_of(len(cut))
            picked = jnp.dot(
                plan[...], jnp.concatenate(parts, axis=0), preferred_element_type=jnp.float32
            ).astype(jnp.bfloat16)
            for i in range(4):
                outs[i][row : row + rows, :] = picked[i * rows : (i + 1) * rows]
            row += rows

    @pl.when(step == D // TILE)
    def _():
        for i in range(4):
            outs[i][:, 0 : WIDE - D] = gain_ref[i]


def select(products, homes):
    cuts = tuple(tuple(len(b) for b in blocks) for blocks in products)
    sizes = [rows_of(len(blocks)) for blocks in products]
    rows = sum(sizes)
    flat = [a for blocks in products for b in blocks for a in b]
    last = D // TILE - 1
    return pl.pallas_call(
        functools.partial(select_kernel, cuts),
        out_shape=[jax.ShapeDtypeStruct((rows, WIDE), jnp.bfloat16)] * 4,
        grid=(D // TILE + 1,),
        in_specs=[pl.BlockSpec(memory_space=pltpu.SMEM)]
        + [
            pl.BlockSpec((a.shape[0], TILE), lambda j: (0, jnp.minimum(j, last))) for a in flat
        ],
        out_specs=[pl.BlockSpec((rows, TILE), lambda j: (0, j))] * 4,
        scratch_shapes=[
            pltpu.VMEM((4 * size, len(blocks) * TOK), jnp.bfloat16)
            for size, blocks in zip(sizes, products)
        ]
        + [pltpu.VMEM((4, rows, WIDE - D), jnp.bfloat16)],
        compiler_params=pltpu.CompilerParams(
            vmem_limit_bytes=VMEM_LIMIT, dimension_semantics=("arbitrary",)
        ),
        cost_estimate=pl.CostEstimate(
            flops=sum(8 * s * len(b) * TOK * D for s, b in zip(sizes, products)),
            bytes_accessed=2 * D * (sum(a.shape[0] for a in flat) + 4 * rows),
            transcendentals=0,
        ),
        name="select",
    )(homes, *flat)


def slopes_kernel(*refs):
    pieces, weight_ref, readout_ref, out_ref = refs[:4], refs[4], refs[5], refs[6]
    rows = jnp.concatenate([p[:, :D] for p in pieces], axis=0)
    factor = jnp.concatenate([p[:, D : D + 1] for p in pieces], axis=0).astype(jnp.float32)
    preact = jnp.dot(rows, weight_ref[...], preferred_element_type=jnp.float32) * INV_ROOT
    slope = factor * readout_ref[...] * silu_slope(preact)
    out_ref[...] = slope.T.astype(jnp.bfloat16)


def slopes_of(pieces, weight_full, readout_row):
    rows = 4 * pieces[0].shape[0]
    step = 256
    return pl.pallas_call(
        slopes_kernel,
        out_shape=jax.ShapeDtypeStruct((FF, rows), jnp.bfloat16),
        grid=(FF // step,),
        in_specs=[pl.BlockSpec(p.shape, lambda j: (0, 0)) for p in pieces]
        + [pl.BlockSpec((D, step), lambda j: (0, j)), pl.BlockSpec((1, step), lambda j: (0, j))],
        out_specs=pl.BlockSpec((step, rows), lambda j: (j, 0)),
        compiler_params=pltpu.CompilerParams(vmem_limit_bytes=VMEM_LIMIT),
        cost_estimate=pl.CostEstimate(
            flops=2 * rows * D * FF,
            bytes_accessed=2 * (D * FF + rows * (D + FF)),
            transcendentals=rows * FF,
        ),
        name="slopes",
    )(*pieces, weight_full, readout_row)


def gradient_kernel(n_pieces, *refs):
    pieces, slopes, out_ref = refs[:n_pieces], refs[n_pieces:-1], refs[-1]
    down = jnp.concatenate([s[...] for s in slopes], axis=1)
    rows = jnp.concatenate([p[...] for p in pieces], axis=0)
    total = jnp.dot(down, rows, preferred_element_type=jnp.float32)
    total = (total * INV_ROOT).astype(jnp.bfloat16)
    for i in range(TILE // SHARD):
        out_ref[i] = total[:, i * SHARD : (i + 1) * SHARD]


def gradient_parts(pieces, slopes):
    rows = sum(p.shape[0] for p in pieces)
    return pl.pallas_call(
        functools.partial(gradient_kernel, len(pieces)),
        out_shape=jax.ShapeDtypeStruct((D // SHARD, FF, SHARD), jnp.bfloat16),
        grid=(D // TILE,),
        in_specs=[pl.BlockSpec((p.shape[0], TILE), lambda j: (0, j)) for p in pieces]
        + [pl.BlockSpec(s.shape, lambda j: (0, 0)) for s in slopes],
        out_specs=pl.BlockSpec((TILE // SHARD, FF, SHARD), lambda j: (j, 0, 0)),
        compiler_params=pltpu.CompilerParams(vmem_limit_bytes=VMEM_LIMIT),
        cost_estimate=pl.CostEstimate(
            flops=2 * rows * D * FF,
            bytes_accessed=2 * (rows * (D + FF) + D * FF),
            transcendentals=0,
        ),
        name="gradient",
    )(*pieces, *slopes)


def body(
    activations, routes, gate_probs, advantage, readout, weights, moment_one, moment_two, swap_flags
):
    experts = NZ * NX * NC
    half = experts // 2
    z, x, c = lax.axis_index("z"), lax.axis_index("x"), lax.axis_index("c")
    y, h = lax.axis_index("y"), lax.axis_index("h")

    def home(dx, dc):
        index = (z * NX + (x ^ dx)) * NC + (c ^ dc)
        flag = lax.dynamic_index_in_dim(swap_flags, index, 0, keepdims=False)
        return (index + flag * half) % experts, flag

    resident, my_flag = home(0, 0)
    homes = jnp.stack([home(dx, dc)[0] for dx, dc in RELS])

    factor = (advantage[:, None] * gate_probs).astype(jnp.bfloat16)
    facts = jnp.concatenate([routes.astype(jnp.bfloat16).T, factor.T], axis=1)
    facts = jnp.pad(facts, ((0, 0), (0, D - 2 * TOK)))
    block = jnp.concatenate([activations, facts], axis=0)
    weight_own = weights[0]
    weight_far = shift_z(weight_own, NZ // 2)
    moments = cast_moments(moment_one[0], moment_two[0])
    readout_row = lax.dynamic_index_in_dim(readout, resident, 0).astype(jnp.float32)

    blocks = {0: (block,)}
    fwd = bwd = block
    picked, pieces, slopes, far = [], [], [], []

    def pick(group):
        picked.append(select([[blocks[o] for o in part] for part in group], homes))

    def exchange():
        pieces.append(
            [p if rel == (0, 0) else swap_xc(p, *rel) for p, rel in zip(picked[-1], RELS)]
        )

    for k in range(1, NZ // 2):
        fwd = shift_z(fwd, 1)
        bwd = shift_z(bwd, -1)
        beside = {1: (moments, weight_far), 6: picked[-1:]}.get(k, ())
        fwd, bwd, beside = lax.optimization_barrier((fwd, bwd, beside))
        blocks[-k] = (fwd,)
        blocks[k] = (bwd,)
        if k == 1:
            moments, weight_far = beside
            weight_now = jnp.where(my_flag == 1, weight_far, weight_own)
            weight_full = lax.all_gather(weight_now, ("y", "h"), axis=0, tiled=True)
        elif k == 5:
            pick(GROUPS[0])
        elif k == 6:
            picked[-1] = beside[0]
            exchange()
    last = (shift_z(fwd[: TOK // 2], 1), shift_z(bwd[TOK // 2 :], -1))
    last, moments = lax.optimization_barrier((last, moments))
    blocks[8] = last
    far = [shift_z(m, NZ // 2) for m in moments]
    pick(GROUPS[1])
    exchange()
    slopes = [slopes_of(p, weight_full, readout_row) for p in pieces]
    slopes, far[0] = lax.optimization_barrier((slopes, far[0]))

    parts = gradient_parts([p for group in pieces for p in group], slopes)

    def part(dy, dh):
        index = ((y + dy) % NY) * NH + (h + dh) % NH
        return lax.dynamic_index_in_dim(parts, index, 0)

    received = [shift_dp(part(dy, dh)[0], dy, dh) for dy, dh in SENDS]
    updated, first, second = adam(
        my_flag.reshape(1),
        part(0, 0),
        received,
        weight_now,
        moment_one[0],
        moment_two[0],
        far,
    )
    return (updated[None], first[None], second[None])


def solution(mesh):
    inner = Mesh(mesh.devices.reshape(NY, NH, NZ, NX, NC), ("y", "h", "z", "x", "c"))
    dp, expert = ("y", "h"), ("z", "x", "c")
    placed = (
        P(dp + expert, None),
        P(dp + expert, None),
        P(dp + expert, None),
        P(dp + expert),
        P(),
        P(expert, dp, None),
        P(expert, dp, None),
        P(expert, dp, None),
        P(),
    )
    return jax.shard_map(
        body,
        mesh=inner,
        in_specs=placed,
        out_specs=(P(expert, dp, None),) * 3,
        check_vma=False,
    )
```

time: 362 us -> 325 us (0.90)
  the two profiles are of different devices: /device:TPU:129 before, /device:TPU:1 now
where the time goes in v3:
time: 325 us; the launch traced here: 323 us
  starting transfers between devices  142 us (44%)
  waiting for transfers between devices  110 us (34%)
  Pallas kernels  41.2 us (13%)
  between operations  17.9 us (6%)
  local copies, waits for them, and re-layouts  6.47 us (2%)
  other arithmetic  5.38 us (2%)
    ppermute x19, waiting for transfers between devices, shift_z(): lax.ppermute(block, 'z', [(i, (i + distance) % NZ) for i in range(NZ)])  96.1 us
    ppermute x19, starting transfers between devices, shift_z(): lax.ppermute(block, 'z', [(i, (i + distance) % NZ) for i in range(NZ)])  83 us
    ppermute x7, starting transfers between devices, shift_dp(): return lax.ppermute(block, ('y', 'h'), pairs)  32.5 us
    ppermute x6, starting transfers between devices, swap_xc(): return lax.ppermute(block, ('x', 'c'), pairs)  26.3 us
    pallas_call x2, Pallas kernels, select(): pl.pallas_call(functools.partial(select_kernel, cuts), out_shape=[jax.Sha...  13.3 us
    pallas_call x2, Pallas kernels, slopes_of(): pl.pallas_call(slopes_kernel, out_shape=jax.ShapeDtypeStruct((FF, rows),...  12.2 us
    pallas_call x1, Pallas kernels, gradient_parts(): pl.pallas_call(functools.partial(gradient_kernel, len(pieces)), out_shape...  8.21 us
    ppermute x7, waiting for transfers between devices, shift_dp(): return lax.ppermute(block, ('y', 'h'), pairs)  8.18 us
  transfers between devices with their start and end apart: 33, of which 15 were waited for; matrix products, arithmetic and copies ran while one was open for 2% of the time, Pallas kernels for 11%

profile of v3, /device:TPU:1, one launch (start us, length us, event | category | flops | bytes accessed | tf_op | source)
XLA Modules:
  0.0 322.6 jit_solution(13875492296341681682)
XLA Ops:
  7.2 0.7 convert_bitcast_fusion
  7.9 0.7 fusion.3
  8.6 1.1 pad_maximum_fusion.refs_0_
  9.8 4.4 %collective-permute-start = (bf16[136,2048]{1,0:T(8,128)(2,1)S(1)}, bf16[136,2048]{1,0:T(8,128)(2,1)S(1)}, u32[]{:S(2)}, u32[]{:S(2)}) collective-permute-start(bf16[136,2048]{1,0:T(8,128)(2,1)S(1)} %pad_maximum_fusion.refs_0_), channel_id=1, source_target_pairs={{0,4},{4,8},{8,12},{12,16},{16,20},{20,24},{24,28},{28,32},{32,36}... | collective-permute-start | bytes 1671176 | tf_op jit(solution)/shard_map/ppermute | solution.py:38
  14.1 9.5 %collective-permute-start.1 = (bf16[136,2048]{1,0:T(8,128)(2,1)S(1)}, bf16[136,2048]{1,0:T(8,128)(2,1)S(1)}, u32[]{:S(2)}, u32[]{:S(2)}) collective-permute-start(bf16[136,2048]{1,0:T(8,128)(2,1)S(1)} %pad_maximum_fusion.refs_0_), channel_id=1, source_target_pairs={{0,60},{4,0},{8,4},{12,8},{16,12},{20,16},{24,20},{28,24},{32,28},... | collective-permute-start | bytes 1671176 | tf_op jit(solution)/shard_map/ppermute | solution.py:38
  23.7 8.9 %collective-permute-start.2 = (bf16[256,768]{1,0:T(8,128)(2,1)}, bf16[256,768]{1,0:T(8,128)(2,1)S(1)}, u32[]{:S(2)}, u32[]{:S(2)}) collective-permute-start(bf16[256,768]{1,0:T(8,128)(2,1)} %bitcast.38), channel_id=1, source_target_pairs={{0,32},{4,36},{8,40},{12,44},{16,48},{20,52},{24,56},{28,60},{32,0... | collective-permute-start | bytes 1179656 | tf_op jit(solution)/shard_map/ppermute | solution.py:38
  32.6 2.2 cast.1
  34.7 0.6 fusion.4
  36.0 36.5 %collective-permute-done.2 = bf16[256,768]{1,0:T(8,128)(2,1)S(1)} collective-permute-done((bf16[256,768]{1,0:T(8,128)(2,1)}, bf16[256,768]{1,0:T(8,128)(2,1)S(1)}, u32[]{:S(2)}, u32[]{:S(2)}) %collective-permute-start.2) | collective-permute-done | bytes 393248 | tf_op jit(solution)/shard_map/ppermute | solution.py:38
  72.5 0.9 broadcast_select_fusion.refs_8_
  73.5 1.9 collective-permute-start.3
  75.4 5.8 %collective-permute-start.4 = (bf16[136,2048]{1,0:T(8,128)(2,1)S(1)}, bf16[136,2048]{1,0:T(8,128)(2,1)S(1)}, u32[]{:S(2)}, u32[]{:S(2)}) collective-permute-start(bf16[136,2048]{1,0:T(8,128)(2,1)S(1)} %collective-permute-done.1.refs_1_), channel_id=1, source_target_pairs={{0,60},{4,0},{8,4},{12,8},{16,12},{20,16},{24,20},{28,24},{32,28},... | collective-permute-start | bytes 1671176 | tf_op jit(solution)/shard_map/ppermute | solution.py:38
  81.2 9.2 %collective-permute-done.3.refs_4_ = bf16[136,2048]{1,0:T(8,128)(2,1)S(1)} collective-permute-done((bf16[136,2048]{1,0:T(8,128)(2,1)S(1)}, bf16[136,2048]{1,0:T(8,128)(2,1)S(1)}, u32[]{:S(2)}, u32[]{:S(2)}) %collective-permute-start.3) | collective-permute-done | bytes 557088 | tf_op jit(solution)/shard_map/ppermute | solution.py:38
  90.4 0.9 collective-permute-done.4.refs_3_
  91.3 1.9 collective-permute-start.5
  93.2 5.3 %collective-permute-start.6 = (bf16[136,2048]{1,0:T(8,128)(2,1)S(1)}, bf16[136,2048]{1,0:T(8,128)(2,1)S(1)}, u32[]{:S(2)}, u32[]{:S(2)}) collective-permute-start(bf16[136,2048]{1,0:T(8,128)(2,1)S(1)} %collective-permute-done.4.refs_3_), channel_id=1, source_target_pairs={{0,60},{4,0},{8,4},{12,8},{16,12},{20,16},{24,20},{28,24},{32,28},... | collective-permute-start | bytes 1671176 | tf_op jit(solution)/shard_map/ppermute | solution.py:38
  98.5 8.3 %collective-permute-done.5.refs_6_ = bf16[136,2048]{1,0:T(8,128)(2,1)S(1)} collective-permute-done((bf16[136,2048]{1,0:T(8,128)(2,1)S(1)}, bf16[136,2048]{1,0:T(8,128)(2,1)S(1)}, u32[]{:S(2)}, u32[]{:S(2)}) %collective-permute-start.5) | collective-permute-done | bytes 557088 | tf_op jit(solution)/shard_map/ppermute | solution.py:38
  106.8 0.9 collective-permute-done.6.refs_5_
  107.7 1.9 collective-permute-start.7
  109.6 5.3 %collective-permute-start.8 = (bf16[136,2048]{1,0:T(8,128)(2,1)S(1)}, bf16[136,2048]{1,0:T(8,128)(2,1)S(1)}, u32[]{:S(2)}, u32[]{:S(2)}) collective-permute-start(bf16[136,2048]{1,0:T(8,128)(2,1)S(1)} %collective-permute-done.6.refs_5_), channel_id=1, source_target_pairs={{0,60},{4,0},{8,4},{12,8},{16,12},{20,16},{24,20},{28,24},{32,28},... | collective-permute-start | bytes 1671176 | tf_op jit(solution)/shard_map/ppermute | solution.py:38
  114.9 7.3 %collective-permute-done.7.refs_8_ = bf16[136,2048]{1,0:T(8,128)(2,1)S(1)} collective-permute-done((bf16[136,2048]{1,0:T(8,128)(2,1)S(1)}, bf16[136,2048]{1,0:T(8,128)(2,1)S(1)}, u32[]{:S(2)}, u32[]{:S(2)}) %collective-permute-start.7) | collective-permute-done | bytes 557088 | tf_op jit(solution)/shard_map/ppermute | solution.py:38
  122.3 0.9 collective-permute-done.8.refs_7_
  123.2 5.3 %collective-permute-start.10 = (bf16[136,2048]{1,0:T(8,128)(2,1)S(1)}, bf16[136,2048]{1,0:T(8,128)(2,1)}, u32[]{:S(2)}, u32[]{:S(2)}) collective-permute-start(bf16[136,2048]{1,0:T(8,128)(2,1)S(1)} %collective-permute-done.8.refs_7_), channel_id=1, source_target_pairs={{0,60},{4,0},{8,4},{12,8},{16,12},{20,16},{24,20},{28,24},{32,28},... | collective-permute-start | bytes 1671176 | tf_op jit(solution)/shard_map/ppermute | solution.py:38
  128.5 1.9 collective-permute-start.9
  130.4 5.4 %collective-permute-done.10.refs_9_ = bf16[136,2048]{1,0:T(8,128)(2,1)} collective-permute-done((bf16[136,2048]{1,0:T(8,128)(2,1)S(1)}, bf16[136,2048]{1,0:T(8,128)(2,1)}, u32[]{:S(2)}, u32[]{:S(2)}) %collective-permute-start.10) | collective-permute-done | bytes 557088 | tf_op jit(solution)/shard_map/ppermute | solution.py:38
  135.8 5.2 %collective-permute-done.9.refs_10_ = bf16[136,2048]{1,0:T(8,128)(2,1)} collective-permute-done((bf16[136,2048]{1,0:T(8,128)(2,1)S(1)}, bf16[136,2048]{1,0:T(8,128)(2,1)}, u32[]{:S(2)}, u32[]{:S(2)}) %collective-permute-start.9) | collective-permute-done | bytes 557088 | tf_op jit(solution)/shard_map/ppermute | solution.py:38
  141.0 1.9 collective-permute-start.11
  142.9 4.6 %collective-permute-start.12 = (bf16[136,2048]{1,0:T(8,128)(2,1)}, bf16[136,2048]{1,0:T(8,128)(2,1)}, u32[]{:S(2)}, u32[]{:S(2)}) collective-permute-start(bf16[136,2048]{1,0:T(8,128)(2,1)} %collective-permute-done.10.refs_9_), channel_id=1, source_target_pairs={{0,60},{4,0},{8,4},{12,8},{16,12},{20,16},{24,20},{28,24},{32,28},... | collective-permute-start | bytes 1671176 | tf_op jit(solution)/shard_map/ppermute | solution.py:38
  150.7 7.8 %select.31 = (bf16[208,2176]{1,0:T(8,128)(2,1)}, bf16[208,2176]{1,0:T(8,128)(2,1)}, bf16[208,2176]{1,0:T(8,128)(2,1)}, bf16[208,2176]{1,0:T(8,128)(2,1)}) custom-call(s32[4]{0:T(128)} %pad_add_fusion.home_ref, bf16[136,2048]{1,0:T(8,128)(2,1)} %copy-done.1, bf16[136,2048]{1,0:T(8,128)(2,1)} %copy-done.19, bf16[136,2048]{1,0:T(8,128)(2,1)} %copy-done.18, ...), custom_call_target="tpu_custom_call" | custom-call | flops 2415919104 | bytes 9535488 | tf_op jit(solution)/shard_map/select/pallas_call | solution.py:230
  158.6 1.9 collective-permute-start.16
  160.5 4.6 %collective-permute-start.17 = (bf16[136,2048]{1,0:T(8,128)(2,1)}, bf16[136,2048]{1,0:T(8,128)(2,1)S(1)}, u32[]{:S(2)}, u32[]{:S(2)}) collective-permute-start(bf16[136,2048]{1,0:T(8,128)(2,1)} %collective-permute-done.12.refs_0_), channel_id=1, source_target_pairs={{0,60},{4,0},{8,4},{12,8},{16,12},{20,16},{24,20},{28,24},{32,28},... | collective-permute-start | bytes 1671176 | tf_op jit(solution)/shard_map/ppermute | solution.py:38
  165.1 8.8 %collective-permute-start.13 = (bf16[208,2176]{1,0:T(8,128)(2,1)}, bf16[208,2176]{1,0:T(8,128)(2,1)S(1)}, u32[]{:S(2)}, u32[]{:S(2)}) collective-permute-start(bf16[208,2176]{1,0:T(8,128)(2,1)} %get-tuple-element.61), channel_id=1, source_target_pairs={{0,1},{1,0},{2,3},{3,2},{4,5},{5,4},{6,7},{7,6},{8,9},{9,8},{10,11... | collective-permute-start | bytes 2715656 | tf_op jit(solution)/shard_map/ppermute | solution.py:45
  173.9 3.1 collective-permute-start.14
  177.0 2.3 collective-permute-start.15
  179.4 1.9 collective-permute-start.19
  181.4 3.5 %collective-permute-start.18 = (bf16[64,2048]{1,0:T(8,128)(2,1)S(1)}, bf16[64,2048]{1,0:T(8,128)(2,1)S(1)}, u32[]{:S(2)}, u32[]{:S(2)}) collective-permute-start(bf16[64,2048]{1,0:T(8,128)(2,1)S(1)} %slice.6), channel_id=1, source_target_pairs={{0,4},{4,8},{8,12},{12,16},{16,20},{20,24},{24,28},{28,32},{32,36}... | collective-permute-start | bytes 786440 | tf_op jit(solution)/shard_map/ppermute | solution.py:38
  184.9 5.0 %collective-permute-done.18.refs_4_ = bf16[64,2048]{1,0:T(8,128)(2,1)S(1)} collective-permute-done((bf16[64,2048]{1,0:T(8,128)(2,1)S(1)}, bf16[64,2048]{1,0:T(8,128)(2,1)S(1)}, u32[]{:S(2)}, u32[]{:S(2)}) %collective-permute-start.18) | collective-permute-done | bytes 262176 | tf_op jit(solution)/shard_map/ppermute | solution.py:38
  189.9 0.7 copy-done.28
  190.6 0.7 copy-done.27
  191.3 5.5 %select.32 = (bf16[96,2176]{1,0:T(8,128)(2,1)}, bf16[96,2176]{1,0:T(8,128)(2,1)}, bf16[96,2176]{1,0:T(8,128)(2,1)}, bf16[96,2176]{1,0:T(8,128)(2,1)}) custom-call(s32[4]{0:T(128)} %pad_add_fusion.home_ref, bf16[136,2048]{1,0:T(8,128)(2,1)} %collective-permute-done.12.refs_0_, bf16[136,2048]{1,0:T(8,128)(2,1)} %copy-done.20, bf16[136,2048]{1,0:T(8,128)(2,1)} %copy-done.13, ...), custom_call_target="tpu_custom_call" | custom-call | flops 1006632960 | bytes 4358144 | tf_op jit(solution)/shard_map/select/pallas_call | solution.py:230
  196.8 6.5 %collective-permute-start.20 = (bf16[96,2176]{1,0:T(8,128)(2,1)}, bf16[96,2176]{1,0:T(8,128)(2,1)S(1)}, u32[]{:S(2)}, u32[]{:S(2)}) collective-permute-start(bf16[96,2176]{1,0:T(8,128)(2,1)} %get-tuple-element.73), channel_id=1, source_target_pairs={{0,1},{1,0},{2,3},{3,2},{4,5},{5,4},{6,7},{7,6},{8,9},{9,8},{10,11... | collective-permute-start | bytes 1253384 | tf_op jit(solution)/shard_map/ppermute | solution.py:45
  203.3 3.1 collective-permute-start.21
  206.5 2.3 collective-permute-start.22
  208.9 1.3 dynamic-slice_convert_fusion.refs_5_
  210.2 5.9 %collective-permute-start.23 = (bf16[2,32,768]{2,1,0:T(8,128)(2,1)S(1)}, bf16[2,32,768]{2,1,0:T(8,128)(2,1)S(1)}, u32[]{:S(2)}, u32[]{:S(2)}) collective-permute-start(bf16[2,32,768]{2,1,0:T(8,128)(2,1)S(1)} %copy-done.29), channel_id=1, source_target_pairs={{0,32},{4,36},{8,40},{12,44},{16,48},{20,52},{24,56},{28,60},{32,0... | collective-permute-start | bytes 294920 | tf_op jit(solution)/shard_map/ppermute | solution.py:38
  216.1 1.6 collective-permute-done.15.refs_3_
  217.7 6.5 %collective-permute-start.31 = (bf16[2,224,768]{2,1,0:T(8,128)(2,1)}, bf16[2,224,768]{2,1,0:T(8,128)(2,1)S(1)}, u32[]{:S(2)}, u32[]{:S(2)}) collective-permute-start(bf16[2,224,768]{2,1,0:T(8,128)(2,1)} %get-tuple-element.81), channel_id=1, source_target_pairs={{0,32},{4,36},{8,40},{12,44},{16,48},{20,52},{24,56},{28,60},{32,0... | collective-permute-start | bytes 2064392 | tf_op jit(solution)/shard_map/ppermute | solution.py:38
  224.3 7.1 %slopes.2.refs_8_ = bf16[768,832]{1,0:T(8,128)(2,1)} custom-call(bf16[208,2176]{1,0:T(8,128)(2,1)} %get-tuple-element.60.refs_0_, bf16[208,2176]{1,0:T(8,128)(2,1)} %copy-done.17, bf16[208,2176]{1,0:T(8,128)(2,1)} %collective-permute-done.14.refs_2_, bf16[208,2176]{1,0:T(8,128)(2,1)} %collective-permute-done.15.refs_3_, ...), custom_call_target="tpu_custom_call" | custom-call | flops 2617245696 | bytes 7831552 | tf_op jit(solution)/shard_map/slopes/pallas_call | solution.py:268
  231.4 4.0 %collective-permute-done.22.refs_3_.refs_7_ = bf16[96,2176]{1,0:T(8,128)(2,1)S(1)} collective-permute-done((bf16[96,2176]{1,0:T(8,128)(2,1)}, bf16[96,2176]{1,0:T(8,128)(2,1)S(1)}, u32[]{:S(2)}, u32[]{:S(2)}) %collective-permute-start.22) | collective-permute-done | bytes 417824 | tf_op jit(solution)/shard_map/ppermute | solution.py:45
  235.4 0.8 copy-done.4
  236.2 5.1 %slopes.3.refs_9_ = bf16[768,384]{1,0:T(8,128)(2,1)} custom-call(bf16[96,2176]{1,0:T(8,128)(2,1)} %get-tuple-element.72.refs_0_.refs_4_, bf16[96,2176]{1,0:T(8,128)(2,1)} %copy-done.2, bf16[96,2176]{1,0:T(8,128)(2,1)} %copy-done.3, bf16[96,2176]{1,0:T(8,128)(2,1)} %copy-done.4, bf16[2048,768]{1,0:T(8,128)(2,1)} %all-gather.2.cloned.1.call-done.refs_4_, ...), custom_call_target="tpu_custom_call" | custom-call | flops 1207959552 | bytes 5308416 | tf_op jit(solution)/shard_map/slopes/pallas_call | solution.py:268
  241.3 8.2 %gradient.1 = bf16[8,768,256]{2,1,0:T(8,128)(2,1)} custom-call(bf16[208,2176]{1,0:T(8,128)(2,1)} %get-tuple-element.60.refs_0_, bf16[208,2176]{1,0:T(8,128)(2,1)} %copy-done.17, bf16[208,2176]{1,0:T(8,128)(2,1)} %collective-permute-done.14.refs_2_, bf16[208,2176]{1,0:T(8,128)(2,1)} %collective-permute-done.15.refs_3_, ...), custom_call_target="tpu_custom_call" | custom-call | flops 3825205248 | bytes 9994240 | tf_op jit(solution)/shard_map/gradient/pallas_call | solution.py:297
  249.5 2.8 constant_dynamic-slice_fusion
  252.3 7.3 %collective-permute-start.24 = (bf16[768,256]{1,0:T(8,128)(2,1)S(1)}, bf16[768,256]{1,0:T(8,128)(2,1)S(1)}, u32[]{:S(2)}, u32[]{:S(2)}) collective-permute-start(bf16[768,256]{1,0:T(8,128)(2,1)S(1)} %get-tuple-element.92), channel_id=1, source_target_pairs={{0,320},{64,256},{128,448},{192,384},{256,64},{320,0},{384,192},{4... | collective-permute-start | bytes 1179656 | tf_op jit(solution)/shard_map/ppermute | solution.py:54
  259.6 2.3 collective-permute-start.25
  261.9 6.6 %collective-permute-start.26 = (bf16[768,256]{1,0:T(8,128)(2,1)S(1)}, bf16[768,256]{1,0:T(8,128)(2,1)S(1)}, u32[]{:S(2)}, u32[]{:S(2)}) collective-permute-start(bf16[768,256]{1,0:T(8,128)(2,1)S(1)} %get-tuple-element.90), channel_id=1, source_target_pairs={{0,448},{64,384},{128,64},{192,0},{256,192},{320,128},{384,320},{4... | collective-permute-start | bytes 1179656 | tf_op jit(solution)/shard_map/ppermute | solution.py:54
  268.5 1.9 collective-permute-start.27
  270.4 16.6 %collective-permute-done.31.refs_12_ = bf16[2,224,768]{2,1,0:T(8,128)(2,1)S(1)} collective-permute-done((bf16[2,224,768]{2,1,0:T(8,128)(2,1)}, bf16[2,224,768]{2,1,0:T(8,128)(2,1)S(1)}, u32[]{:S(2)}, u32[]{:S(2)}) %collective-permute-start.31) | collective-permute-done | bytes 688160 | tf_op jit(solution)/shard_map/ppermute | solution.py:38
  287.0 2.0 collective-permute-start.28
  289.1 4.5 %collective-permute-start.29 = (bf16[768,256]{1,0:T(8,128)(2,1)S(1)}, bf16[768,256]{1,0:T(8,128)(2,1)S(1)}, u32[]{:S(2)}, u32[]{:S(2)}) collective-permute-start(bf16[768,256]{1,0:T(8,128)(2,1)S(1)} %get-tuple-element.87), channel_id=1, source_target_pairs={{0,384},{64,448},{128,0},{192,64},{256,128},{320,192},{384,256},{4... | collective-permute-start | bytes 1179656 | tf_op jit(solution)/shard_map/ppermute | solution.py:54
  293.6 7.9 %collective-permute-start.30 = (bf16[768,256]{1,0:T(8,128)(2,1)S(1)}, bf16[768,256]{1,0:T(8,128)(2,1)S(1)}, u32[]{:S(2)}, u32[]{:S(2)}) collective-permute-start(bf16[768,256]{1,0:T(8,128)(2,1)S(1)} %get-tuple-element.86), channel_id=1, source_target_pairs={{0,64},{64,0},{128,192},{192,128},{256,320},{320,256},{384,448},{4... | collective-permute-start | bytes 1179656 | tf_op jit(solution)/shard_map/ppermute | solution.py:54
  301.6 8.1 %collective-permute-done.30.refs_6_ = bf16[768,256]{1,0:T(8,128)(2,1)S(1)} collective-permute-done((bf16[768,256]{1,0:T(8,128)(2,1)S(1)}, bf16[768,256]{1,0:T(8,128)(2,1)S(1)}, u32[]{:S(2)}, u32[]{:S(2)}) %collective-permute-start.30) | collective-permute-done | bytes 393248 | tf_op jit(solution)/shard_map/ppermute | solution.py:54
  309.7 0.7 copy-done.11
  310.5 5.3 %adam.1 = (bf16[256,768]{1,0:T(8,128)(2,1)}, f32[256,768]{1,0:T(8,128)}, f32[256,768]{1,0:T(8,128)}) custom-call(s32[1]{0:T(128)} %get-tuple-element.94.flag_ref, bf16[768,256]{1,0:T(8,128)(2,1)} %copy-done.5, bf16[768,256]{1,0:T(8,128)(2,1)} %copy-done.6, bf16[768,256]{1,0:T(8,128)(2,1)} %copy-done.7, bf16[768,256]{1,0:T(8,128)(2,1)} %copy-done.8, ...), custom_call_target="tpu_custom_call" | custom-call | flops 5898240 | bytes 7864320 | tf_op jit(solution)/shard_map/adam/pallas_call | solution.py:121
  (81 shorter events, 1.0 us)
Async XLA Ops:
  7.2 217.1 %all-gather.2.cloned.1.call-start = ((), (), s32[]{:S(2)}) async-start(), calls=%async_computation | async-start | bytes 3538944 | tf_op jit(solution)/shard_map/all_gather | solution.py:361
  8.6 26.1 %copy-start.16 = (s32[64]{0:T(128)S(1)}, s32[64]{0:T(128)}, u32[]{:S(2)}) copy-start(s32[64]{0:T(128)} %param.17) | copy-start | bytes 772
  8.6 63.9 %copy-start.12 = (bf16[1,256,768]{2,1,0:T(8,128)(2,1)S(1)}, bf16[1,256,768]{2,1,0:T(8,128)(2,1)}, u32[]{:S(2)}) copy-start(bf16[1,256,768]{2,1,0:T(8,128)(2,1)} %param.14) | copy-start | bytes 1179652
  9.8 63.7 %copy-start.1 = (bf16[136,2048]{1,0:T(8,128)(2,1)}, bf16[136,2048]{1,0:T(8,128)(2,1)S(1)}, u32[]{:S(2)}) copy-start(bf16[136,2048]{1,0:T(8,128)(2,1)S(1)} %pad_maximum_fusion.refs_0_) | copy-start | bytes 1671172
  9.8 62.7 %collective-permute-start = (bf16[136,2048]{1,0:T(8,128)(2,1)S(1)}, bf16[136,2048]{1,0:T(8,128)(2,1)S(1)}, u32[]{:S(2)}, u32[]{:S(2)}) collective-permute-start(bf16[136,2048]{1,0:T(8,128)(2,1)S(1)} %pad_maximum_fusion.refs_0_), channel_id=1, source_target_pairs={{0,4},{4,8},{8,12},{12,16},{16,20},{20,24},{24,28},{28,32},{32,36}... | collective-permute-start | bytes 1671176 | tf_op jit(solution)/shard_map/ppermute | solution.py:38
  14.1 58.4 %collective-permute-start.1 = (bf16[136,2048]{1,0:T(8,128)(2,1)S(1)}, bf16[136,2048]{1,0:T(8,128)(2,1)S(1)}, u32[]{:S(2)}, u32[]{:S(2)}) collective-permute-start(bf16[136,2048]{1,0:T(8,128)(2,1)S(1)} %pad_maximum_fusion.refs_0_), channel_id=1, source_target_pairs={{0,60},{4,0},{8,4},{12,8},{16,12},{20,16},{24,20},{28,24},{32,28},... | collective-permute-start | bytes 1671176 | tf_op jit(solution)/shard_map/ppermute | solution.py:38
  23.7 48.8 %collective-permute-start.2 = (bf16[256,768]{1,0:T(8,128)(2,1)}, bf16[256,768]{1,0:T(8,128)(2,1)S(1)}, u32[]{:S(2)}, u32[]{:S(2)}) collective-permute-start(bf16[256,768]{1,0:T(8,128)(2,1)} %bitcast.38), channel_id=1, source_target_pairs={{0,32},{4,36},{8,40},{12,44},{16,48},{20,52},{24,56},{28,60},{32,0... | collective-permute-start | bytes 1179656 | tf_op jit(solution)/shard_map/ppermute | solution.py:38
  72.5 78.2 %copy-start.18 = (bf16[136,2048]{1,0:T(8,128)(2,1)}, bf16[136,2048]{1,0:T(8,128)(2,1)S(1)}, u32[]{:S(2)}) copy-start(bf16[136,2048]{1,0:T(8,128)(2,1)S(1)} %collective-permute-done.refs_2_) | copy-start | bytes 1671172
  72.5 78.2 %copy-start.19 = (bf16[136,2048]{1,0:T(8,128)(2,1)}, bf16[136,2048]{1,0:T(8,128)(2,1)S(1)}, u32[]{:S(2)}) copy-start(bf16[136,2048]{1,0:T(8,128)(2,1)S(1)} %collective-permute-done.1.refs_1_) | copy-start | bytes 1671172
  73.5 16.9 %collective-permute-start.3 = (bf16[136,2048]{1,0:T(8,128)(2,1)S(1)}, bf16[136,2048]{1,0:T(8,128)(2,1)S(1)}, u32[]{:S(2)}, u32[]{:S(2)}) collective-permute-start(bf16[136,2048]{1,0:T(8,128)(2,1)S(1)} %collective-permute-done.refs_2_), channel_id=1, source_target_pairs={{0,4},{4,8},{8,12},{12,16},{16,20},{20,24},{24,28},{28,32},{32,36}... | collective-permute-start | bytes 1671176 | tf_op jit(solution)/shard_map/ppermute | solution.py:38
  75.4 15.9 %collective-permute-start.4 = (bf16[136,2048]{1,0:T(8,128)(2,1)S(1)}, bf16[136,2048]{1,0:T(8,128)(2,1)S(1)}, u32[]{:S(2)}, u32[]{:S(2)}) collective-permute-start(bf16[136,2048]{1,0:T(8,128)(2,1)S(1)} %collective-permute-done.1.refs_1_), channel_id=1, source_target_pairs={{0,60},{4,0},{8,4},{12,8},{16,12},{20,16},{24,20},{28,24},{32,28},... | collective-permute-start | bytes 1671176 | tf_op jit(solution)/shard_map/ppermute | solution.py:38
  90.4 60.3 %copy-start.21 = (bf16[136,2048]{1,0:T(8,128)(2,1)}, bf16[136,2048]{1,0:T(8,128)(2,1)S(1)}, u32[]{:S(2)}) copy-start(bf16[136,2048]{1,0:T(8,128)(2,1)S(1)} %collective-permute-done.3.refs_4_) | copy-start | bytes 1671172
  91.3 59.4 %copy-start.22 = (bf16[136,2048]{1,0:T(8,128)(2,1)}, bf16[136,2048]{1,0:T(8,128)(2,1)S(1)}, u32[]{:S(2)}) copy-start(bf16[136,2048]{1,0:T(8,128)(2,1)S(1)} %collective-permute-done.4.refs_3_) | copy-start | bytes 1671172
  91.3 15.5 %collective-permute-start.5 = (bf16[136,2048]{1,0:T(8,128)(2,1)S(1)}, bf16[136,2048]{1,0:T(8,128)(2,1)S(1)}, u32[]{:S(2)}, u32[]{:S(2)}) collective-permute-start(bf16[136,2048]{1,0:T(8,128)(2,1)S(1)} %collective-permute-done.3.refs_4_), channel_id=1, source_target_pairs={{0,4},{4,8},{8,12},{12,16},{16,20},{20,24},{24,28},{28,32},{32,36}... | collective-permute-start | bytes 1671176 | tf_op jit(solution)/shard_map/ppermute | solution.py:38
  93.2 14.5 %collective-permute-start.6 = (bf16[136,2048]{1,0:T(8,128)(2,1)S(1)}, bf16[136,2048]{1,0:T(8,128)(2,1)S(1)}, u32[]{:S(2)}, u32[]{:S(2)}) collective-permute-start(bf16[136,2048]{1,0:T(8,128)(2,1)S(1)} %collective-permute-done.4.refs_3_), channel_id=1, source_target_pairs={{0,60},{4,0},{8,4},{12,8},{16,12},{20,16},{24,20},{28,24},{32,28},... | collective-permute-start | bytes 1671176 | tf_op jit(solution)/shard_map/ppermute | solution.py:38
  106.8 29.0 %copy-start.23 = (bf16[136,2048]{1,0:T(8,128)(2,1)}, bf16[136,2048]{1,0:T(8,128)(2,1)S(1)}, u32[]{:S(2)}) copy-start(bf16[136,2048]{1,0:T(8,128)(2,1)S(1)} %collective-permute-done.5.refs_6_) | copy-start | bytes 1671172
  107.7 33.3 %copy-start.24 = (bf16[136,2048]{1,0:T(8,128)(2,1)}, bf16[136,2048]{1,0:T(8,128)(2,1)S(1)}, u32[]{:S(2)}) copy-start(bf16[136,2048]{1,0:T(8,128)(2,1)S(1)} %collective-permute-done.6.refs_5_) | copy-start | bytes 1671172
  107.7 14.6 %collective-permute-start.7 = (bf16[136,2048]{1,0:T(8,128)(2,1)S(1)}, bf16[136,2048]{1,0:T(8,128)(2,1)S(1)}, u32[]{:S(2)}, u32[]{:S(2)}) collective-permute-start(bf16[136,2048]{1,0:T(8,128)(2,1)S(1)} %collective-permute-done.5.refs_6_), channel_id=1, source_target_pairs={{0,4},{4,8},{8,12},{12,16},{16,20},{20,24},{24,28},{28,32},{32,36}... | collective-permute-start | bytes 1671176 | tf_op jit(solution)/shard_map/ppermute | solution.py:38
  109.6 13.6 %collective-permute-start.8 = (bf16[136,2048]{1,0:T(8,128)(2,1)S(1)}, bf16[136,2048]{1,0:T(8,128)(2,1)S(1)}, u32[]{:S(2)}, u32[]{:S(2)}) collective-permute-start(bf16[136,2048]{1,0:T(8,128)(2,1)S(1)} %collective-permute-done.6.refs_5_), channel_id=1, source_target_pairs={{0,60},{4,0},{8,4},{12,8},{16,12},{20,16},{24,20},{28,24},{32,28},... | collective-permute-start | bytes 1671176 | tf_op jit(solution)/shard_map/ppermute | solution.py:38
  122.3 20.6 %copy-start.25 = (bf16[136,2048]{1,0:T(8,128)(2,1)}, bf16[136,2048]{1,0:T(8,128)(2,1)S(1)}, u32[]{:S(2)}) copy-start(bf16[136,2048]{1,0:T(8,128)(2,1)S(1)} %collective-permute-done.7.refs_8_) | copy-start | bytes 1671172
  123.2 24.3 %copy-start.26 = (bf16[136,2048]{1,0:T(8,128)(2,1)}, bf16[136,2048]{1,0:T(8,128)(2,1)S(1)}, u32[]{:S(2)}) copy-start(bf16[136,2048]{1,0:T(8,128)(2,1)S(1)} %collective-permute-done.8.refs_7_) | copy-start | bytes 1671172
  123.2 12.6 %collective-permute-start.10 = (bf16[136,2048]{1,0:T(8,128)(2,1)S(1)}, bf16[136,2048]{1,0:T(8,128)(2,1)}, u32[]{:S(2)}, u32[]{:S(2)}) collective-permute-start(bf16[136,2048]{1,0:T(8,128)(2,1)S(1)} %collective-permute-done.8.refs_7_), channel_id=1, source_target_pairs={{0,60},{4,0},{8,4},{12,8},{16,12},{20,16},{24,20},{28,24},{32,28},... | collective-permute-start | bytes 1671176 | tf_op jit(solution)/shard_map/ppermute | solution.py:38
  128.5 12.5 %collective-permute-start.9 = (bf16[136,2048]{1,0:T(8,128)(2,1)S(1)}, bf16[136,2048]{1,0:T(8,128)(2,1)}, u32[]{:S(2)}, u32[]{:S(2)}) collective-permute-start(bf16[136,2048]{1,0:T(8,128)(2,1)S(1)} %collective-permute-done.7.refs_8_), channel_id=1, source_target_pairs={{0,4},{4,8},{8,12},{12,16},{16,20},{20,24},{24,28},{28,32},{32,36}... | collective-permute-start | bytes 1671176 | tf_op jit(solution)/shard_map/ppermute | solution.py:38
  141.0 17.5 %collective-permute-start.11 = (bf16[136,2048]{1,0:T(8,128)(2,1)}, bf16[136,2048]{1,0:T(8,128)(2,1)S(1)}, u32[]{:S(2)}, u32[]{:S(2)}) collective-permute-start(bf16[136,2048]{1,0:T(8,128)(2,1)} %collective-permute-done.9.refs_10_), channel_id=1, source_target_pairs={{0,4},{4,8},{8,12},{12,16},{16,20},{20,24},{24,28},{28,32},{32,36}... | collective-permute-start | bytes 1671176 | tf_op jit(solution)/shard_map/ppermute | solution.py:38
  142.9 15.6 %collective-permute-start.12 = (bf16[136,2048]{1,0:T(8,128)(2,1)}, bf16[136,2048]{1,0:T(8,128)(2,1)}, u32[]{:S(2)}, u32[]{:S(2)}) collective-permute-start(bf16[136,2048]{1,0:T(8,128)(2,1)} %collective-permute-done.10.refs_9_), channel_id=1, source_target_pairs={{0,60},{4,0},{8,4},{12,8},{16,12},{20,16},{24,20},{28,24},{32,28},... | collective-permute-start | bytes 1671176 | tf_op jit(solution)/shard_map/ppermute | solution.py:38
  158.5 31.3 %copy-start.20 = (bf16[136,2048]{1,0:T(8,128)(2,1)}, bf16[136,2048]{1,0:T(8,128)(2,1)S(1)}, u32[]{:S(2)}) copy-start(bf16[136,2048]{1,0:T(8,128)(2,1)S(1)} %collective-permute-done.11.refs_1_) | copy-start | bytes 1671172
  158.6 20.8 %collective-permute-start.16 = (bf16[136,2048]{1,0:T(8,128)(2,1)S(1)}, bf16[136,2048]{1,0:T(8,128)(2,1)S(1)}, u32[]{:S(2)}, u32[]{:S(2)}) collective-permute-start(bf16[136,2048]{1,0:T(8,128)(2,1)S(1)} %collective-permute-done.11.refs_1_), channel_id=1, source_target_pairs={{0,4},{4,8},{8,12},{12,16},{16,20},{20,24},{24,28},{28,32},{32,36}... | collective-permute-start | bytes 1671176 | tf_op jit(solution)/shard_map/ppermute | solution.py:38
  160.5 18.9 %collective-permute-start.17 = (bf16[136,2048]{1,0:T(8,128)(2,1)}, bf16[136,2048]{1,0:T(8,128)(2,1)S(1)}, u32[]{:S(2)}, u32[]{:S(2)}) collective-permute-start(bf16[136,2048]{1,0:T(8,128)(2,1)} %collective-permute-done.12.refs_0_), channel_id=1, source_target_pairs={{0,60},{4,0},{8,4},{12,8},{16,12},{20,16},{24,20},{28,24},{32,28},... | collective-permute-start | bytes 1671176 | tf_op jit(solution)/shard_map/ppermute | solution.py:38
  165.1 41.4 %collective-permute-start.13 = (bf16[208,2176]{1,0:T(8,128)(2,1)}, bf16[208,2176]{1,0:T(8,128)(2,1)S(1)}, u32[]{:S(2)}, u32[]{:S(2)}) collective-permute-start(bf16[208,2176]{1,0:T(8,128)(2,1)} %get-tuple-element.61), channel_id=1, source_target_pairs={{0,1},{1,0},{2,3},{3,2},{4,5},{5,4},{6,7},{7,6},{8,9},{9,8},{10,11... | collective-permute-start | bytes 2715656 | tf_op jit(solution)/shard_map/ppermute | solution.py:45
  173.9 36.3 %collective-permute-start.14 = (bf16[208,2176]{1,0:T(8,128)(2,1)}, bf16[208,2176]{1,0:T(8,128)(2,1)}, u32[]{:S(2)}, u32[]{:S(2)}) collective-permute-start(bf16[208,2176]{1,0:T(8,128)(2,1)} %get-tuple-element.62), channel_id=1, source_target_pairs={{0,2},{1,3},{2,0},{3,1},{4,6},{5,7},{6,4},{7,5},{8,10},{9,11},{10,... | collective-permute-start | bytes 2715656 | tf_op jit(solution)/shard_map/ppermute | solution.py:45
  177.0 40.7 %collective-permute-start.15 = (bf16[208,2176]{1,0:T(8,128)(2,1)}, bf16[208,2176]{1,0:T(8,128)(2,1)}, u32[]{:S(2)}, u32[]{:S(2)}) collective-permute-start(bf16[208,2176]{1,0:T(8,128)(2,1)} %get-tuple-element.63), channel_id=1, source_target_pairs={{0,3},{1,2},{2,1},{3,0},{4,7},{5,6},{6,5},{7,4},{8,11},{9,10},{10,... | collective-permute-start | bytes 2715656 | tf_op jit(solution)/shard_map/ppermute | solution.py:45
  179.4 10.5 %copy-start.14 = (bf16[136,2048]{1,0:T(8,128)(2,1)}, bf16[136,2048]{1,0:T(8,128)(2,1)S(1)}, u32[]{:S(2)}) copy-start(bf16[136,2048]{1,0:T(8,128)(2,1)S(1)} %collective-permute-done.16.refs_3_) | copy-start | bytes 1671172
  179.4 10.5 %copy-start.13 = (bf16[136,2048]{1,0:T(8,128)(2,1)}, bf16[136,2048]{1,0:T(8,128)(2,1)S(1)}, u32[]{:S(2)}) copy-start(bf16[136,2048]{1,0:T(8,128)(2,1)S(1)} %collective-permute-done.17.refs_2_) | copy-start | bytes 1671172
  179.4 10.4 %collective-permute-start.19 = (bf16[72,2048]{1,0:T(8,128)(2,1)S(1)}, bf16[72,2048]{1,0:T(8,128)(2,1)S(1)}, u32[]{:S(2)}, u32[]{:S(2)}) collective-permute-start(bf16[72,2048]{1,0:T(8,128)(2,1)S(1)} %slice.7), channel_id=1, source_target_pairs={{0,60},{4,0},{8,4},{12,8},{16,12},{20,16},{24,20},{28,24},{32,28},... | collective-permute-start | bytes 884744 | tf_op jit(solution)/shard_map/ppermute | solution.py:38
  181.4 28.8 %copy-start.29 = (bf16[2,32,768]{2,1,0:T(8,128)(2,1)S(1)}, bf16[2,32,768]{2,1,0:T(8,128)(2,1)}, u32[]{:S(2)}) copy-start(bf16[2,32,768]{2,1,0:T(8,128)(2,1)} %get-tuple-element.77) | copy-start | bytes 294916
  181.4 8.5 %collective-permute-start.18 = (bf16[64,2048]{1,0:T(8,128)(2,1)S(1)}, bf16[64,2048]{1,0:T(8,128)(2,1)S(1)}, u32[]{:S(2)}, u32[]{:S(2)}) collective-permute-start(bf16[64,2048]{1,0:T(8,128)(2,1)S(1)} %slice.6), channel_id=1, source_target_pairs={{0,4},{4,8},{8,12},{12,16},{16,20},{20,24},{24,28},{28,32},{32,36}... | collective-permute-start | bytes 786440 | tf_op jit(solution)/shard_map/ppermute | solution.py:38
  189.8 0.7 copy-start.28
  190.6 0.7 copy-start.27
  196.8 34.6 %collective-permute-start.20 = (bf16[96,2176]{1,0:T(8,128)(2,1)}, bf16[96,2176]{1,0:T(8,128)(2,1)S(1)}, u32[]{:S(2)}, u32[]{:S(2)}) collective-permute-start(bf16[96,2176]{1,0:T(8,128)(2,1)} %get-tuple-element.73), channel_id=1, source_target_pairs={{0,1},{1,0},{2,3},{3,2},{4,5},{5,4},{6,7},{7,6},{8,9},{9,8},{10,11... | collective-permute-start | bytes 1253384 | tf_op jit(solution)/shard_map/ppermute | solution.py:45
  203.3 28.0 %collective-permute-start.21 = (bf16[96,2176]{1,0:T(8,128)(2,1)}, bf16[96,2176]{1,0:T(8,128)(2,1)S(1)}, u32[]{:S(2)}, u32[]{:S(2)}) collective-permute-start(bf16[96,2176]{1,0:T(8,128)(2,1)} %get-tuple-element.74), channel_id=1, source_target_pairs={{0,2},{1,3},{2,0},{3,1},{4,6},{5,7},{6,4},{7,5},{8,10},{9,11},{10,... | collective-permute-start | bytes 1253384 | tf_op jit(solution)/shard_map/ppermute | solution.py:45
  206.5 17.8 %copy-start.17 = (bf16[208,2176]{1,0:T(8,128)(2,1)}, bf16[208,2176]{1,0:T(8,128)(2,1)S(1)}, u32[]{:S(2)}) copy-start(bf16[208,2176]{1,0:T(8,128)(2,1)S(1)} %collective-permute-done.13.refs_1_) | copy-start | bytes 2715652
  206.5 28.9 %collective-permute-start.22 = (bf16[96,2176]{1,0:T(8,128)(2,1)}, bf16[96,2176]{1,0:T(8,128)(2,1)S(1)}, u32[]{:S(2)}, u32[]{:S(2)}) collective-permute-start(bf16[96,2176]{1,0:T(8,128)(2,1)} %get-tuple-element.75), channel_id=1, source_target_pairs={{0,3},{1,2},{2,1},{3,0},{4,7},{5,6},{6,5},{7,4},{8,11},{9,10},{10,... | collective-permute-start | bytes 1253384 | tf_op jit(solution)/shard_map/ppermute | solution.py:45
  210.2 31.0 %collective-permute-start.23 = (bf16[2,32,768]{2,1,0:T(8,128)(2,1)S(1)}, bf16[2,32,768]{2,1,0:T(8,128)(2,1)S(1)}, u32[]{:S(2)}, u32[]{:S(2)}) collective-permute-start(bf16[2,32,768]{2,1,0:T(8,128)(2,1)S(1)} %copy-done.29), channel_id=1, source_target_pairs={{0,32},{4,36},{8,40},{12,44},{16,48},{20,52},{24,56},{28,60},{32,0... | collective-permute-start | bytes 294920 | tf_op jit(solution)/shard_map/ppermute | solution.py:38
  217.7 69.4 %collective-permute-start.31 = (bf16[2,224,768]{2,1,0:T(8,128)(2,1)}, bf16[2,224,768]{2,1,0:T(8,128)(2,1)S(1)}, u32[]{:S(2)}, u32[]{:S(2)}) collective-permute-start(bf16[2,224,768]{2,1,0:T(8,128)(2,1)} %get-tuple-element.81), channel_id=1, source_target_pairs={{0,32},{4,36},{8,40},{12,44},{16,48},{20,52},{24,56},{28,60},{32,0... | collective-permute-start | bytes 2064392 | tf_op jit(solution)/shard_map/ppermute | solution.py:38
  231.4 4.0 %copy-start.2 = (bf16[96,2176]{1,0:T(8,128)(2,1)}, bf16[96,2176]{1,0:T(8,128)(2,1)S(1)}, u32[]{:S(2)}) copy-start(bf16[96,2176]{1,0:T(8,128)(2,1)S(1)} %collective-permute-done.20.refs_1_.refs_5_) | copy-start | bytes 1253380
  231.4 4.0 %copy-start.3 = (bf16[96,2176]{1,0:T(8,128)(2,1)}, bf16[96,2176]{1,0:T(8,128)(2,1)S(1)}, u32[]{:S(2)}) copy-start(bf16[96,2176]{1,0:T(8,128)(2,1)S(1)} %collective-permute-done.21.refs_2_.refs_6_) | copy-start | bytes 1253380
  235.4 0.8 copy-start.4
  241.3 8.2 %copy-start.15 = (bf16[2,32,768]{2,1,0:T(8,128)(2,1)}, bf16[2,32,768]{2,1,0:T(8,128)(2,1)S(1)}, u32[]{:S(2)}) copy-start(bf16[2,32,768]{2,1,0:T(8,128)(2,1)S(1)} %collective-permute-done.23.refs_11_) | copy-start | bytes 294916
  252.3 36.8 %collective-permute-start.24 = (bf16[768,256]{1,0:T(8,128)(2,1)S(1)}, bf16[768,256]{1,0:T(8,128)(2,1)S(1)}, u32[]{:S(2)}, u32[]{:S(2)}) collective-permute-start(bf16[768,256]{1,0:T(8,128)(2,1)S(1)} %get-tuple-element.92), channel_id=1, source_target_pairs={{0,320},{64,256},{128,448},{192,384},{256,64},{320,0},{384,192},{4... | collective-permute-start | bytes 1179656 | tf_op jit(solution)/shard_map/ppermute | solution.py:54
  259.6 34.0 %collective-permute-start.25 = (bf16[768,256]{1,0:T(8,128)(2,1)S(1)}, bf16[768,256]{1,0:T(8,128)(2,1)S(1)}, u32[]{:S(2)}, u32[]{:S(2)}) collective-permute-start(bf16[768,256]{1,0:T(8,128)(2,1)S(1)} %get-tuple-element.91), channel_id=1, source_target_pairs={{0,192},{64,128},{128,320},{192,256},{256,448},{320,384},{384,64},... | collective-permute-start | bytes 1179656 | tf_op jit(solution)/shard_map/ppermute | solution.py:54
  261.9 39.5 %collective-permute-start.26 = (bf16[768,256]{1,0:T(8,128)(2,1)S(1)}, bf16[768,256]{1,0:T(8,128)(2,1)S(1)}, u32[]{:S(2)}, u32[]{:S(2)}) collective-permute-start(bf16[768,256]{1,0:T(8,128)(2,1)S(1)} %get-tuple-element.90), channel_id=1, source_target_pairs={{0,448},{64,384},{128,64},{192,0},{256,192},{320,128},{384,320},{4... | collective-permute-start | bytes 1179656 | tf_op jit(solution)/shard_map/ppermute | solution.py:54
  268.5 33.0 %collective-permute-start.27 = (bf16[768,256]{1,0:T(8,128)(2,1)S(1)}, bf16[768,256]{1,0:T(8,128)(2,1)S(1)}, u32[]{:S(2)}, u32[]{:S(2)}) collective-permute-start(bf16[768,256]{1,0:T(8,128)(2,1)S(1)} %get-tuple-element.89), channel_id=1, source_target_pairs={{0,256},{64,320},{128,384},{192,448},{256,0},{320,64},{384,128},{4... | collective-permute-start | bytes 1179656 | tf_op jit(solution)/shard_map/ppermute | solution.py:54
  287.0 22.6 %copy-start = (bf16[2,224,768]{2,1,0:T(8,128)(2,1)}, bf16[2,224,768]{2,1,0:T(8,128)(2,1)S(1)}, u32[]{:S(2)}) copy-start(bf16[2,224,768]{2,1,0:T(8,128)(2,1)S(1)} %collective-permute-done.31.refs_12_) | copy-start | bytes 2064388
  287.0 14.5 %collective-permute-start.28 = (bf16[768,256]{1,0:T(8,128)(2,1)S(1)}, bf16[768,256]{1,0:T(8,128)(2,1)S(1)}, u32[]{:S(2)}, u32[]{:S(2)}) collective-permute-start(bf16[768,256]{1,0:T(8,128)(2,1)S(1)} %get-tuple-element.88), channel_id=1, source_target_pairs={{0,128},{64,192},{128,256},{192,320},{256,384},{320,448},{384,0},{... | collective-permute-start | bytes 1179656 | tf_op jit(solution)/shard_map/ppermute | solution.py:54
  289.1 20.6 %copy-start.5 = (bf16[768,256]{1,0:T(8,128)(2,1)}, bf16[768,256]{1,0:T(8,128)(2,1)S(1)}, u32[]{:S(2)}) copy-start(bf16[768,256]{1,0:T(8,128)(2,1)S(1)} %collective-permute-done.24.refs_0_) | copy-start | bytes 1179652
  289.1 12.5 %collective-permute-start.29 = (bf16[768,256]{1,0:T(8,128)(2,1)S(1)}, bf16[768,256]{1,0:T(8,128)(2,1)S(1)}, u32[]{:S(2)}, u32[]{:S(2)}) collective-permute-start(bf16[768,256]{1,0:T(8,128)(2,1)S(1)} %get-tuple-element.87), channel_id=1, source_target_pairs={{0,384},{64,448},{128,0},{192,64},{256,128},{320,192},{384,256},{4... | collective-permute-start | bytes 1179656 | tf_op jit(solution)/shard_map/ppermute | solution.py:54
  293.6 16.1 %copy-start.6 = (bf16[768,256]{1,0:T(8,128)(2,1)}, bf16[768,256]{1,0:T(8,128)(2,1)S(1)}, u32[]{:S(2)}) copy-start(bf16[768,256]{1,0:T(8,128)(2,1)S(1)} %collective-permute-done.25.refs_1_) | copy-start | bytes 1179652
  293.6 16.1 %collective-permute-start.30 = (bf16[768,256]{1,0:T(8,128)(2,1)S(1)}, bf16[768,256]{1,0:T(8,128)(2,1)S(1)}, u32[]{:S(2)}, u32[]{:S(2)}) collective-permute-start(bf16[768,256]{1,0:T(8,128)(2,1)S(1)} %get-tuple-element.86), channel_id=1, source_target_pairs={{0,64},{64,0},{128,192},{192,128},{256,320},{320,256},{384,448},{4... | collective-permute-start | bytes 1179656 | tf_op jit(solution)/shard_map/ppermute | solution.py:54
  301.5 8.2 %copy-start.7 = (bf16[768,256]{1,0:T(8,128)(2,1)}, bf16[768,256]{1,0:T(8,128)(2,1)S(1)}, u32[]{:S(2)}) copy-start(bf16[768,256]{1,0:T(8,128)(2,1)S(1)} %collective-permute-done.26.refs_2_) | copy-start | bytes 1179652
  301.5 8.2 %copy-start.8 = (bf16[768,256]{1,0:T(8,128)(2,1)}, bf16[768,256]{1,0:T(8,128)(2,1)S(1)}, u32[]{:S(2)}) copy-start(bf16[768,256]{1,0:T(8,128)(2,1)S(1)} %collective-permute-done.27.refs_3_) | copy-start | bytes 1179652
  301.5 8.2 %copy-start.9 = (bf16[768,256]{1,0:T(8,128)(2,1)}, bf16[768,256]{1,0:T(8,128)(2,1)S(1)}, u32[]{:S(2)}) copy-start(bf16[768,256]{1,0:T(8,128)(2,1)S(1)} %collective-permute-done.28.refs_4_) | copy-start | bytes 1179652
  301.6 8.1 %copy-start.10 = (bf16[768,256]{1,0:T(8,128)(2,1)}, bf16[768,256]{1,0:T(8,128)(2,1)S(1)}, u32[]{:S(2)}) copy-start(bf16[768,256]{1,0:T(8,128)(2,1)S(1)} %collective-permute-done.29.refs_5_) | copy-start | bytes 1179652
  309.7 0.8 copy-start.11
Sparse Core Ops, SparseCore 0:
  73.6 75.6 all-gather.1

commit v4 on v3

--- a/solution.py
+++ b/solution.py
@@ -22,11 +22,11 @@
 META = 8
 WIDE = D + 128
 RELS = ((0, 0), (0, 1), (1, 0), (1, 1))
-GROUPS = (((0, 1, -1, 2, -2, 3), (-3, 4, -4, 5, -5)), ((6, -6, 7, -7, 8),))
+GROUPS = (((0, 1, -1, 2, -2, 3, -3),), ((4, -4, 5, -5),), ((6, -6, 7, -7, 8),))
 TILE = 512
+PICK_TILE = 1024
 INV_ROOT = 1.0 / math.sqrt(D)
-SENDS = ((2, 1), (1, 1), (3, 1), (2, 0), (1, 0), (3, 0), (0, 1))
-CUTS = (SHARD // 8, 7 * SHARD // 8)
+CUTS = (7 * SHARD // 16, 9 * SHARD // 16)
 VMEM_LIMIT = 56 * 1024 * 1024
 
 
@@ -43,15 +43,6 @@
         (x * NC + c, (x ^ dx) * NC + (c ^ dc)) for x in range(NX) for c in range(NC)
     ]
     return lax.ppermute(block, ("x", "c"), pairs)
-
-
-def shift_dp(block, dy, dh):
-    pairs = [
-        (y * NH + h, ((y + dy) % NY) * NH + (h + dh) % NH)
-        for y in range(NY)
-        for h in range(NH)
-    ]
-    return lax.ppermute(block, ("y", "h"), pairs)
 
 
 def silu_slope(preact):
@@ -84,14 +75,11 @@
     )(one, two)
 
 
-def adam_kernel(n_parts, flag_ref, *refs):
-    parts = refs[:n_parts]
-    own_ref, weight_ref, one_ref, two_ref = refs[n_parts : n_parts + 4]
-    far_a, far_b = refs[n_parts + 4 : n_parts + 6]
-    updated_ref, first_ref, second_ref = refs[n_parts + 6 :]
-    total = own_ref[0].astype(jnp.float32)
-    for part in parts:
-        total = total + part[...].astype(jnp.float32)
+def adam_kernel(flag_ref, parts_ref, weight_ref, one_ref, two_ref, far_a, far_b, *outs):
+    updated_ref, first_ref, second_ref = outs
+    total = parts_ref[0].astype(jnp.float32)
+    for i in range(1, parts_ref.shape[0]):
+        total = total + parts_ref[i].astype(jnp.float32)
     gradient = total.T
     swapped = flag_ref[0] == 1
     rows = gradient.shape[0]
@@ -114,12 +102,12 @@
     second_ref[...] = second
 
 
-def adam(flag, own, received, weight, one, two, far):
+def adam(flag, parts, weight, one, two, far):
     step = SHARD // 2
     plain = pl.BlockSpec((step, FF), lambda i: (i, 0))
     whole = [pl.BlockSpec(f.shape, lambda i: (0, 0, 0)) for f in far]
     return pl.pallas_call(
-        functools.partial(adam_kernel, len(received)),
+        adam_kernel,
         out_shape=[
             jax.ShapeDtypeStruct((SHARD, FF), jnp.bfloat16),
             jax.ShapeDtypeStruct((SHARD, FF), jnp.float32),
@@ -127,8 +115,7 @@
         ],
         grid=(SHARD // step,),
         in_specs=[pl.BlockSpec(memory_space=pltpu.SMEM)]
-        + [pl.BlockSpec((FF, step), lambda i: (0, i))] * len(received)
-        + [pl.BlockSpec((1, FF, step), lambda i: (0, 0, i))]
+        + [pl.BlockSpec((parts.shape[0], FF, step), lambda i: (0, 0, i))]
         + [plain, plain, plain]
         + whole,
         out_specs=[plain] * 3,
@@ -137,7 +124,7 @@
             flops=30 * SHARD * FF, bytes_accessed=40 * SHARD * FF, transcendentals=SHARD * FF
         ),
         name="adam",
-    )(flag, *received, own, weight, one, two, *far)
+    )(flag, parts, weight, one, two, *far)
 
 
 def pick_plan(homes, facts, rows):
@@ -199,7 +186,7 @@
                 ).astype(jnp.bfloat16)
             row += rows
 
-    @pl.when(step < D // TILE)
+    @pl.when(step < D // PICK_TILE)
     def _():
         at = row = 0
         for cut, plan in zip(cuts, plans):
@@ -215,7 +202,7 @@
                 outs[i][row : row + rows, :] = picked[i * rows : (i + 1) * rows]
             row += rows
 
-    @pl.when(step == D // TILE)
+    @pl.when(step == D // PICK_TILE)
     def _():
         for i in range(4):
             outs[i][:, 0 : WIDE - D] = gain_ref[i]
@@ -226,16 +213,16 @@
     sizes = [rows_of(len(blocks)) for blocks in products]
     rows = sum(sizes)
     flat = [a for blocks in products for b in blocks for a in b]
-    last = D // TILE - 1
+    last = D // PICK_TILE - 1
     return pl.pallas_call(
         functools.partial(select_kernel, cuts),
         out_shape=[jax.ShapeDtypeStruct((rows, WIDE), jnp.bfloat16)] * 4,
-        grid=(D // TILE + 1,),
+        grid=(D // PICK_TILE + 1,),
         in_specs=[pl.BlockSpec(memory_space=pltpu.SMEM)]
         + [
-            pl.BlockSpec((a.shape[0], TILE), lambda j: (0, jnp.minimum(j, last))) for a in flat
+            pl.BlockSpec((a.shape[0], PICK_TILE), lambda j: (0, jnp.minimum(j, last))) for a in flat
         ],
-        out_specs=[pl.BlockSpec((rows, TILE), lambda j: (0, j))] * 4,
+        out_specs=[pl.BlockSpec((rows, PICK_TILE), lambda j: (0, j))] * 4,
         scratch_shapes=[
             pltpu.VMEM((4 * size, len(blocks) * TOK), jnp.bfloat16)
             for size, blocks in zip(sizes, products)
@@ -254,49 +241,60 @@
 
 
 def slopes_kernel(*refs):
-    pieces, weight_ref, readout_ref, out_ref = refs[:4], refs[4], refs[5], refs[6]
-    rows = jnp.concatenate([p[:, :D] for p in pieces], axis=0)
-    factor = jnp.concatenate([p[:, D : D + 1] for p in pieces], axis=0).astype(jnp.float32)
-    preact = jnp.dot(rows, weight_ref[...], preferred_element_type=jnp.float32) * INV_ROOT
-    slope = factor * readout_ref[...] * silu_slope(preact)
-    out_ref[...] = slope.T.astype(jnp.bfloat16)
+    pieces, gains, weight_ref, readout_ref, out_ref, total = refs[:4], refs[4:8], *refs[8:]
+    step, steps = pl.program_id(0), pl.num_programs(0)
+    rows = jnp.concatenate([p[...] for p in pieces], axis=0)
+    product = jnp.dot(rows, weight_ref[...], preferred_element_type=jnp.float32)
+
+    @pl.when(step == 0)
+    def _():
+        total[...] = product
+
+    @pl.when(step == steps - 1)
+    def _():
+        factor = jnp.concatenate([g[:, 0:1] for g in gains], axis=0).astype(jnp.float32)
+        slope = factor * readout_ref[...] * silu_slope((total[...] + product) * INV_ROOT)
+        out_ref[...] = slope.T.astype(jnp.bfloat16)
 
 
 def slopes_of(pieces, weight_full, readout_row):
     rows = 4 * pieces[0].shape[0]
-    step = 256
+    step = D // 2
     return pl.pallas_call(
         slopes_kernel,
         out_shape=jax.ShapeDtypeStruct((FF, rows), jnp.bfloat16),
-        grid=(FF // step,),
-        in_specs=[pl.BlockSpec(p.shape, lambda j: (0, 0)) for p in pieces]
-        + [pl.BlockSpec((D, step), lambda j: (0, j)), pl.BlockSpec((1, step), lambda j: (0, j))],
-        out_specs=pl.BlockSpec((step, rows), lambda j: (j, 0)),
-        compiler_params=pltpu.CompilerParams(vmem_limit_bytes=VMEM_LIMIT),
+        grid=(2,),
+        in_specs=[pl.BlockSpec((p.shape[0], step), lambda j: (0, j)) for p in pieces]
+        + [pl.BlockSpec((p.shape[0], WIDE - D), lambda j: (0, D // (WIDE - D))) for p in pieces]
+        + [pl.BlockSpec((step, FF), lambda j: (j, 0)), pl.BlockSpec((1, FF), lambda j: (0, 0))],
+        out_specs=pl.BlockSpec((FF, rows), lambda j: (0, 0)),
+        scratch_shapes=[pltpu.VMEM((rows, FF), jnp.float32)],
+        compiler_params=pltpu.CompilerParams(
+            vmem_limit_bytes=VMEM_LIMIT, dimension_semantics=("arbitrary",)
+        ),
         cost_estimate=pl.CostEstimate(
             flops=2 * rows * D * FF,
             bytes_accessed=2 * (D * FF + rows * (D + FF)),
             transcendentals=rows * FF,
         ),
         name="slopes",
-    )(*pieces, weight_full, readout_row)
-
-
-def gradient_kernel(n_pieces, *refs):
+    )(*pieces, *pieces, weight_full, readout_row)
+
+
+def partial_kernel(n_pieces, *refs):
     pieces, slopes, out_ref = refs[:n_pieces], refs[n_pieces:-1], refs[-1]
     down = jnp.concatenate([s[...] for s in slopes], axis=1)
     rows = jnp.concatenate([p[...] for p in pieces], axis=0)
     total = jnp.dot(down, rows, preferred_element_type=jnp.float32)
-    total = (total * INV_ROOT).astype(jnp.bfloat16)
     for i in range(TILE // SHARD):
         out_ref[i] = total[:, i * SHARD : (i + 1) * SHARD]
 
 
-def gradient_parts(pieces, slopes):
+def partial_gradient(pieces, slopes):
     rows = sum(p.shape[0] for p in pieces)
     return pl.pallas_call(
-        functools.partial(gradient_kernel, len(pieces)),
-        out_shape=jax.ShapeDtypeStruct((D // SHARD, FF, SHARD), jnp.bfloat16),
+        functools.partial(partial_kernel, len(pieces)),
+        out_shape=jax.ShapeDtypeStruct((D // SHARD, FF, SHARD), jnp.float32),
         grid=(D // TILE,),
         in_specs=[pl.BlockSpec((p.shape[0], TILE), lambda j: (0, j)) for p in pieces]
         + [pl.BlockSpec(s.shape, lambda j: (0, 0)) for s in slopes],
@@ -304,11 +302,40 @@
         compiler_params=pltpu.CompilerParams(vmem_limit_bytes=VMEM_LIMIT),
         cost_estimate=pl.CostEstimate(
             flops=2 * rows * D * FF,
-            bytes_accessed=2 * (rows * (D + FF) + D * FF),
+            bytes_accessed=2 * rows * (D + FF) + 4 * D * FF,
             transcendentals=0,
         ),
+        name="partial",
+    )(*pieces, *slopes)
+
+
+def gradient_kernel(n_pieces, early_ref, slopes_ref, *refs):
+    pieces, out_ref = refs[:n_pieces], refs[n_pieces]
+    rows = jnp.concatenate([p[...] for p in pieces], axis=0)
+    late = jnp.dot(slopes_ref[...], rows, preferred_element_type=jnp.float32)
+    for i in range(TILE // SHARD):
+        part = late[:, i * SHARD : (i + 1) * SHARD] + early_ref[i]
+        out_ref[i] = (part * INV_ROOT).astype(jnp.bfloat16)
+
+
+def gradient_parts(early, pieces, slopes):
+    rows = slopes.shape[1]
+    shards = pl.BlockSpec((TILE // SHARD, FF, SHARD), lambda j: (j, 0, 0))
+    return pl.pallas_call(
+        functools.partial(gradient_kernel, len(pieces)),
+        out_shape=jax.ShapeDtypeStruct((D // SHARD, FF, SHARD), jnp.bfloat16),
+        grid=(D // TILE,),
+        in_specs=[shards, pl.BlockSpec(slopes.shape, lambda j: (0, 0))]
+        + [pl.BlockSpec((p.shape[0], TILE), lambda j: (0, j)) for p in pieces],
+        out_specs=shards,
+        compiler_params=pltpu.CompilerParams(vmem_limit_bytes=VMEM_LIMIT),
+        cost_estimate=pl.CostEstimate(
+            flops=2 * rows * D * FF,
+            bytes_accessed=2 * rows * (D + FF) + 6 * D * FF,
+            transcendentals=0,
+        ),
         name="gradient",
-    )(*pieces, *slopes)
+    )(early, slopes, *pieces)
 
 
 def body(
@@ -351,38 +378,52 @@
     for k in range(1, NZ // 2):
         fwd = shift_z(fwd, 1)
         bwd = shift_z(bwd, -1)
-        beside = {1: (moments, weight_far), 6: picked[-1:]}.get(k, ())
+        beside = {
+            1: (moments, weight_far, readout_row),
+            4: picked[-1:],
+            6: pieces[0][2:3] if pieces else (),
+            7: pieces[0][1:2] + pieces[0][3:] + pieces[1][2:3] if len(pieces) > 1 else (),
+        }.get(k, ())
+        if k == 6:
+            beside = (beside, picked[1])
         fwd, bwd, beside = lax.optimization_barrier((fwd, bwd, beside))
         blocks[-k] = (fwd,)
         blocks[k] = (bwd,)
         if k == 1:
-            moments, weight_far = beside
+            moments, weight_far, readout_row = beside
             weight_now = jnp.where(my_flag == 1, weight_far, weight_own)
             weight_full = lax.all_gather(weight_now, ("y", "h"), axis=0, tiled=True)
-        elif k == 5:
+        elif k == 3:
             pick(GROUPS[0])
-        elif k == 6:
+        elif k == 4:
             picked[-1] = beside[0]
             exchange()
+        elif k == 5:
+            pick(GROUPS[1])
+        elif k == 6:
+            (pieces[0][2],), picked[1] = beside
+            exchange()
+        elif k == 7:
+            pieces[0][1], pieces[0][3], pieces[1][2] = beside
     last = (shift_z(fwd[: TOK // 2], 1), shift_z(bwd[TOK // 2 :], -1))
-    last, moments = lax.optimization_barrier((last, moments))
+    slopes = [slopes_of(pieces[0], weight_full, readout_row)]
+    rest = [pieces[1][1], pieces[1][3]]
+    last, moments, slopes, rest = lax.optimization_barrier((last, moments, slopes, rest))
+    pieces[1][1], pieces[1][3] = rest
     blocks[8] = last
     far = [shift_z(m, NZ // 2) for m in moments]
-    pick(GROUPS[1])
+    pick(GROUPS[2])
     exchange()
-    slopes = [slopes_of(p, weight_full, readout_row) for p in pieces]
-    slopes, far[0] = lax.optimization_barrier((slopes, far[0]))
-
-    parts = gradient_parts([p for group in pieces for p in group], slopes)
-
-    def part(dy, dh):
-        index = ((y + dy) % NY) * NH + (h + dh) % NH
-        return lax.dynamic_index_in_dim(parts, index, 0)
-
-    received = [shift_dp(part(dy, dh)[0], dy, dh) for dy, dh in SENDS]
+    slopes.append(slopes_of(pieces[1], weight_full, readout_row))
+    early = partial_gradient(pieces[0] + pieces[1], slopes)
+    late = slopes_of(pieces[2], weight_full, readout_row)
+    late, early = lax.optimization_barrier((late, early))
+
+    parts = gradient_parts(early, pieces[2], late)
+    parts, far[0] = lax.optimization_barrier((parts, far[0]))
+    received = lax.all_to_all(parts, ("y", "h"), split_axis=0, concat_axis=0, tiled=True)
     updated, first, second = adam(
         my_flag.reshape(1),
-        part(0, 0),
         received,
         weight_now,
         moment_one[0],

time: 325 us -> 315 us (0.969)
  starting transfers between devices: 142 us -> 121 us
  Pallas kernels: 41.2 us -> 50.1 us
    ppermute x7 -> x0, starting transfers between devices: 32.5 us -> none  [shift_dp(): return lax.ppermute(block, ('y', 'h'), pairs)]
    ppermute x19, waiting for transfers between devices: 96.1 us -> 107 us  [shift_z(): lax.ppermute(block, 'z', [(i, (i + distance) % NZ) for i in range(NZ)])]
    ppermute x7 -> x0, waiting for transfers between devices: 8.18 us -> none  [shift_dp(): return lax.ppermute(block, ('y', 'h'), pairs)]
    pallas_call x1 -> x2, Pallas kernels: 5.32 us -> 12.6 us  [the longest x1 7.68 us: partial_gradient(): pl.pallas_call(functools.partial(partial_kernel, len(pieces)), out_shape=...]
    ppermute x6 -> x9, starting transfers between devices: 26.3 us -> 32.9 us  [swap_xc(): return lax.ppermute(block, ('x', 'c'), pairs)]
    all_to_all x0 -> x1, starting transfers between devices: none -> 6.47 us  [body(): lax.all_to_all(parts, ('y', 'h'), split_axis=0, concat_axis=0, tiled=True)]
    pallas_call x2 -> x3, Pallas kernels: 12.2 us -> 14.9 us  [slopes_of(): pl.pallas_call(slopes_kernel, out_shape=jax.ShapeDtypeStruct((FF, rows),...]
    pallas_call x2 -> x3, Pallas kernels: 13.3 us -> 14 us  [select(): pl.pallas_call(functools.partial(select_kernel, cuts), out_shape=[jax.Sha...]
  transfers between devices with their start and end apart: 33 -> 30, of which waited for: 15 -> 11; matrix products, arithmetic and copies ran while one was open for 2% -> 1% of each run, Pallas kernels for 11% -> 13%
where the time goes in v4:
time: 315 us; the launch traced here: 311 us
  starting transfers between devices  121 us (38%)
  waiting for transfers between devices  110 us (35%)
  Pallas kernels  50.1 us (16%)
  between operations  17.9 us (6%)
  other arithmetic  6.55 us (2%)
  local copies, waits for them, and re-layouts  5.66 us (2%)
    ppermute x19, waiting for transfers between devices, shift_z(): lax.ppermute(block, 'z', [(i, (i + distance) % NZ) for i in range(NZ)])  107 us
    ppermute x19, starting transfers between devices, shift_z(): lax.ppermute(block, 'z', [(i, (i + distance) % NZ) for i in range(NZ)])  81.1 us
    ppermute x9, starting transfers between devices, swap_xc(): return lax.ppermute(block, ('x', 'c'), pairs)  32.9 us
    pallas_call x3, Pallas kernels, slopes_of(): pl.pallas_call(slopes_kernel, out_shape=jax.ShapeDtypeStruct((FF, rows),...  14.9 us
    pallas_call x3, Pallas kernels, select(): pl.pallas_call(functools.partial(select_kernel, cuts), out_shape=[jax.Sha...  14 us
    pallas_call x1, Pallas kernels, partial_gradient(): pl.pallas_call(functools.partial(partial_kernel, len(pieces)), out_shape=...  7.68 us
    all_to_all x1, starting transfers between devices, body(): lax.all_to_all(parts, ('y', 'h'), split_axis=0, concat_axis=0, tiled=True)  6.47 us
    pallas_call x1, Pallas kernels, gradient_parts(): pl.pallas_call(functools.partial(gradient_kernel, len(pieces)), out_shape...  6.43 us
  transfers between devices with their start and end apart: 30, of which 11 were waited for; matrix products, arithmetic and copies ran while one was open for 1% of the time, Pallas kernels for 13%

profile of v4, /device:TPU:1, one launch (start us, length us, event | category | flops | bytes accessed | tf_op | source)
XLA Modules:
  0.0 310.6 jit_solution(12307978837424612922)
XLA Ops:
  7.2 0.0 all-gather.2.cloned.1.call-start
  7.2 0.7 convert_bitcast_fusion
  7.9 0.7 fusion.3
  8.6 1.1 pad_maximum_fusion.refs_0_
  9.7 12.0 %collective-permute-start.1 = (bf16[136,2048]{1,0:T(8,128)(2,1)S(1)}, bf16[136,2048]{1,0:T(8,128)(2,1)S(1)}, u32[]{:S(2)}, u32[]{:S(2)}) collective-permute-start(bf16[136,2048]{1,0:T(8,128)(2,1)S(1)} %pad_maximum_fusion.refs_0_), channel_id=1, source_target_pairs={{0,60},{4,0},{8,4},{12,8},{16,12},{20,16},{24,20},{28,24},{32,28},... | collective-permute-start | bytes 1671176 | tf_op jit(solution)/shard_map/ppermute | solution.py:38
  21.7 1.9 collective-permute-start
  23.6 7.7 %collective-permute-start.2 = (bf16[256,768]{1,0:T(8,128)(2,1)}, bf16[256,768]{1,0:T(8,128)(2,1)S(1)}, u32[]{:S(2)}, u32[]{:S(2)}) collective-permute-start(bf16[256,768]{1,0:T(8,128)(2,1)} %bitcast.24), channel_id=1, source_target_pairs={{0,32},{4,36},{8,40},{12,44},{16,48},{20,52},{24,56},{28,60},{32,0... | collective-permute-start | bytes 1179656 | tf_op jit(solution)/shard_map/ppermute | solution.py:38
  31.3 2.2 cast.1
  33.5 1.5 fusion.4
  36.2 1.3 dynamic-slice_convert_fusion.refs_9_
  37.5 37.2 %collective-permute-done.2 = bf16[256,768]{1,0:T(8,128)(2,1)S(1)} collective-permute-done((bf16[256,768]{1,0:T(8,128)(2,1)}, bf16[256,768]{1,0:T(8,128)(2,1)S(1)}, u32[]{:S(2)}, u32[]{:S(2)}) %collective-permute-start.2) | collective-permute-done | bytes 393248 | tf_op jit(solution)/shard_map/ppermute | solution.py:38
  74.8 2.1 broadcast_select_fusion.weight_ref
  76.9 1.9 collective-permute-start.3
  78.8 4.6 %collective-permute-start.4 = (bf16[136,2048]{1,0:T(8,128)(2,1)S(1)}, bf16[136,2048]{1,0:T(8,128)(2,1)S(1)}, u32[]{:S(2)}, u32[]{:S(2)}) collective-permute-start(bf16[136,2048]{1,0:T(8,128)(2,1)S(1)} %collective-permute-done.1.refs_1_), channel_id=1, source_target_pairs={{0,60},{4,0},{8,4},{12,8},{16,12},{20,16},{24,20},{28,24},{32,28},... | collective-permute-start | bytes 1671176 | tf_op jit(solution)/shard_map/ppermute | solution.py:38
  83.4 8.6 %collective-permute-done.3.refs_4_ = bf16[136,2048]{1,0:T(8,128)(2,1)S(1)} collective-permute-done((bf16[136,2048]{1,0:T(8,128)(2,1)S(1)}, bf16[136,2048]{1,0:T(8,128)(2,1)S(1)}, u32[]{:S(2)}, u32[]{:S(2)}) %collective-permute-start.3) | collective-permute-done | bytes 557088 | tf_op jit(solution)/shard_map/ppermute | solution.py:38
  92.1 0.9 collective-permute-done.4.refs_3_
  93.0 1.9 collective-permute-start.5
  94.9 5.3 %collective-permute-start.6 = (bf16[136,2048]{1,0:T(8,128)(2,1)S(1)}, bf16[136,2048]{1,0:T(8,128)(2,1)}, u32[]{:S(2)}, u32[]{:S(2)}) collective-permute-start(bf16[136,2048]{1,0:T(8,128)(2,1)S(1)} %collective-permute-done.4.refs_3_), channel_id=1, source_target_pairs={{0,60},{4,0},{8,4},{12,8},{16,12},{20,16},{24,20},{28,24},{32,28},... | collective-permute-start | bytes 1671176 | tf_op jit(solution)/shard_map/ppermute | solution.py:38
  100.2 7.8 %collective-permute-done.5.refs_6_ = bf16[136,2048]{1,0:T(8,128)(2,1)} collective-permute-done((bf16[136,2048]{1,0:T(8,128)(2,1)S(1)}, bf16[136,2048]{1,0:T(8,128)(2,1)}, u32[]{:S(2)}, u32[]{:S(2)}) %collective-permute-start.5) | collective-permute-done | bytes 557088 | tf_op jit(solution)/shard_map/ppermute | solution.py:38
  108.0 0.8 collective-permute-done.6.refs_5_
  108.8 1.9 collective-permute-start.7
  110.7 5.4 %collective-permute-start.8 = (bf16[136,2048]{1,0:T(8,128)(2,1)}, bf16[136,2048]{1,0:T(8,128)(2,1)S(1)}, u32[]{:S(2)}, u32[]{:S(2)}) collective-permute-start(bf16[136,2048]{1,0:T(8,128)(2,1)} %collective-permute-done.6.refs_5_), channel_id=1, source_target_pairs={{0,60},{4,0},{8,4},{12,8},{16,12},{20,16},{24,20},{28,24},{32,28},... | collective-permute-start | bytes 1671176 | tf_op jit(solution)/shard_map/ppermute | solution.py:38
  118.2 0.7 pad_add_fusion.home_ref
  118.8 5.9 %select.20 = (bf16[128,2176]{1,0:T(8,128)(2,1)}, bf16[128,2176]{1,0:T(8,128)(2,1)}, bf16[128,2176]{1,0:T(8,128)(2,1)}, bf16[128,2176]{1,0:T(8,128)(2,1)}) custom-call(s32[4]{0:T(128)} %pad_add_fusion.home_ref, bf16[136,2048]{1,0:T(8,128)(2,1)} %copy-done.10, bf16[136,2048]{1,0:T(8,128)(2,1)} %copy-done.14, bf16[136,2048]{1,0:T(8,128)(2,1)} %copy-done.15, ...), custom_call_target="tpu_custom_call" | custom-call | flops 1879048192 | bytes 5996544 | tf_op jit(solution)/shard_map/select/pallas_call | solution.py:217
  124.8 1.9 collective-permute-start.9
  126.7 4.6 %collective-permute-start.10 = (bf16[136,2048]{1,0:T(8,128)(2,1)S(1)}, bf16[136,2048]{1,0:T(8,128)(2,1)S(1)}, u32[]{:S(2)}, u32[]{:S(2)}) collective-permute-start(bf16[136,2048]{1,0:T(8,128)(2,1)S(1)} %collective-permute-done.8.refs_0_), channel_id=1, source_target_pairs={{0,60},{4,0},{8,4},{12,8},{16,12},{20,16},{24,20},{28,24},{32,28},... | collective-permute-start | bytes 1671176 | tf_op jit(solution)/shard_map/ppermute | solution.py:38
  131.3 3.1 %collective-permute-start.13 = (bf16[128,2176]{1,0:T(8,128)(2,1)}, bf16[128,2176]{1,0:T(8,128)(2,1)S(1)}, u32[]{:S(2)}, u32[]{:S(2)}) collective-permute-start(bf16[128,2176]{1,0:T(8,128)(2,1)} %get-tuple-element.77), channel_id=1, source_target_pairs={{0,2},{1,3},{2,0},{3,1},{4,6},{5,7},{6,4},{7,5},{8,10},{9,11},{10,... | collective-permute-start | bytes 1671176 | tf_op jit(solution)/shard_map/ppermute | solution.py:45
  134.5 2.8 collective-permute-done.9.refs_3_
  137.3 1.0 collective-permute-done.10.refs_2_
  138.3 2.9 collective-permute-start.11
  141.3 4.1 %collective-permute-start.12 = (bf16[136,2048]{1,0:T(8,128)(2,1)S(1)}, bf16[136,2048]{1,0:T(8,128)(2,1)S(1)}, u32[]{:S(2)}, u32[]{:S(2)}) collective-permute-start(bf16[136,2048]{1,0:T(8,128)(2,1)S(1)} %collective-permute-done.10.refs_2_), channel_id=1, source_target_pairs={{0,60},{4,0},{8,4},{12,8},{16,12},{20,16},{24,20},{28,24},{32,28},... | collective-permute-start | bytes 1671176 | tf_op jit(solution)/shard_map/ppermute | solution.py:38
  145.5 8.1 %collective-permute-start.16 = (bf16[128,2176]{1,0:T(8,128)(2,1)}, bf16[128,2176]{1,0:T(8,128)(2,1)S(1)}, u32[]{:S(2)}, u32[]{:S(2)}) collective-permute-start(bf16[128,2176]{1,0:T(8,128)(2,1)} %get-tuple-element.84), channel_id=1, source_target_pairs={{0,1},{1,0},{2,3},{3,2},{4,5},{5,4},{6,7},{7,6},{8,9},{9,8},{10,11... | collective-permute-start | bytes 1671176 | tf_op jit(solution)/shard_map/ppermute | solution.py:45
  153.6 3.0 collective-permute-start.17
  156.7 3.7 %select.21 = (bf16[80,2176]{1,0:T(8,128)(2,1)}, bf16[80,2176]{1,0:T(8,128)(2,1)}, bf16[80,2176]{1,0:T(8,128)(2,1)}, bf16[80,2176]{1,0:T(8,128)(2,1)}) custom-call(s32[4]{0:T(128)} %pad_add_fusion.home_ref, bf16[136,2048]{1,0:T(8,128)(2,1)} %copy-done.17, bf16[136,2048]{1,0:T(8,128)(2,1)} %copy-done.16, bf16[136,2048]{1,0:T(8,128)(2,1)} %copy-done.23, ...), custom_call_target="tpu_custom_call" | custom-call | flops 671088640 | bytes 3538944 | tf_op jit(solution)/shard_map/select/pallas_call | solution.py:217
  160.4 3.6 %collective-permute-start.15 = (bf16[136,2048]{1,0:T(8,128)(2,1)S(1)}, bf16[136,2048]{1,0:T(8,128)(2,1)S(1)}, u32[]{:S(2)}, u32[]{:S(2)}) collective-permute-start(bf16[136,2048]{1,0:T(8,128)(2,1)S(1)} %collective-permute-done.12.refs_0_), channel_id=1, source_target_pairs={{0,60},{4,0},{8,4},{12,8},{16,12},{20,16},{24,20},{28,24},{32,28},... | collective-permute-start | bytes 1671176 | tf_op jit(solution)/shard_map/ppermute | solution.py:38
  164.0 1.9 collective-permute-start.14
  166.0 2.2 collective-permute-start.18
  168.2 3.4 %collective-permute-start.21 = (bf16[80,2176]{1,0:T(8,128)(2,1)}, bf16[80,2176]{1,0:T(8,128)(2,1)S(1)}, u32[]{:S(2)}, u32[]{:S(2)}) collective-permute-start(bf16[80,2176]{1,0:T(8,128)(2,1)} %get-tuple-element.97), channel_id=1, source_target_pairs={{0,1},{1,0},{2,3},{3,2},{4,5},{5,4},{6,7},{7,6},{8,9},{9,8},{10,11... | collective-permute-start | bytes 1044488 | tf_op jit(solution)/shard_map/ppermute | solution.py:45
  171.6 2.6 collective-permute-start.22
  174.2 2.8 collective-permute-done.18.refs_2_.refs_6_
  177.0 3.5 %collective-permute-done.14.refs_3_ = bf16[136,2048]{1,0:T(8,128)(2,1)S(1)} collective-permute-done((bf16[136,2048]{1,0:T(8,128)(2,1)S(1)}, bf16[136,2048]{1,0:T(8,128)(2,1)S(1)}, u32[]{:S(2)}, u32[]{:S(2)}) %collective-permute-start.14) | collective-permute-done | bytes 557088 | tf_op jit(solution)/shard_map/ppermute | solution.py:38
  180.6 1.9 collective-permute-start.20
  182.6 3.4 %collective-permute-start.19 = (bf16[64,2048]{1,0:T(8,128)(2,1)S(1)}, bf16[64,2048]{1,0:T(8,128)(2,1)S(1)}, u32[]{:S(2)}, u32[]{:S(2)}) collective-permute-start(bf16[64,2048]{1,0:T(8,128)(2,1)S(1)} %slice.6), channel_id=1, source_target_pairs={{0,4},{4,8},{8,12},{12,16},{16,20},{20,24},{24,28},{28,32},{32,36}... | collective-permute-start | bytes 786440 | tf_op jit(solution)/shard_map/ppermute | solution.py:38
  186.0 5.5 %slopes.3.refs_8_ = bf16[768,512]{1,0:T(8,128)(2,1)} custom-call(bf16[128,2176]{1,0:T(8,128)(2,1)} %get-tuple-element.91.refs_0_.refs_4_, bf16[128,2176]{1,0:T(8,128)(2,1)} %copy-done.2, bf16[128,2176]{1,0:T(8,128)(2,1)} %copy-done.1, bf16[128,2176]{1,0:T(8,128)(2,1)} %copy-done.3, bf16[128,2176]{1,0:T(8,128)(2,1)} %get-tuple-element.91.refs_0_.refs_4_, ...), custom_call_target="tpu_custom_call" | custom-call | flops 1610612736 | bytes 6029312 | tf_op jit(solution)/shard_map/slopes/pallas_call | solution.py:263
  191.5 0.7 copy-done.25
  192.2 4.4 %select.22 = (bf16[96,2176]{1,0:T(8,128)(2,1)}, bf16[96,2176]{1,0:T(8,128)(2,1)}, bf16[96,2176]{1,0:T(8,128)(2,1)}, bf16[96,2176]{1,0:T(8,128)(2,1)}) custom-call(s32[4]{0:T(128)} %pad_add_fusion.home_ref, bf16[136,2048]{1,0:T(8,128)(2,1)} %copy-done.21, bf16[136,2048]{1,0:T(8,128)(2,1)} %copy-done.20, bf16[136,2048]{1,0:T(8,128)(2,1)} %copy-done.12, ...), custom_call_target="tpu_custom_call" | custom-call | flops 1006632960 | bytes 4358144 | tf_op jit(solution)/shard_map/select/pallas_call | solution.py:217
  196.7 5.1 %collective-permute-start.23 = (bf16[96,2176]{1,0:T(8,128)(2,1)}, bf16[96,2176]{1,0:T(8,128)(2,1)S(1)}, u32[]{:S(2)}, u32[]{:S(2)}) collective-permute-start(bf16[96,2176]{1,0:T(8,128)(2,1)} %get-tuple-element.102), channel_id=1, source_target_pairs={{0,1},{1,0},{2,3},{3,2},{4,5},{5,4},{6,7},{7,6},{8,9},{9,8},{10,11... | collective-permute-start | bytes 1253384 | tf_op jit(solution)/shard_map/ppermute | solution.py:45
  201.7 1.9 collective-permute-start.24
  203.7 3.5 %collective-permute-start.25 = (bf16[96,2176]{1,0:T(8,128)(2,1)}, bf16[96,2176]{1,0:T(8,128)(2,1)S(1)}, u32[]{:S(2)}, u32[]{:S(2)}) collective-permute-start(bf16[96,2176]{1,0:T(8,128)(2,1)} %get-tuple-element.104), channel_id=1, source_target_pairs={{0,3},{1,2},{2,1},{3,0},{4,7},{5,6},{6,5},{7,4},{8,11},{9,10},{10,... | collective-permute-start | bytes 1253384 | tf_op jit(solution)/shard_map/ppermute | solution.py:45
  207.2 6.6 %collective-permute-start.26 = (bf16[2,112,768]{2,1,0:T(8,128)(2,1)S(1)}, bf16[2,112,768]{2,1,0:T(8,128)(2,1)S(1)}, u32[]{:S(2)}, u32[]{:S(2)}) collective-permute-start(bf16[2,112,768]{2,1,0:T(8,128)(2,1)S(1)} %copy-done.24), channel_id=1, source_target_pairs={{0,32},{4,36},{8,40},{12,44},{16,48},{20,52},{24,56},{28,60},{32,0... | collective-permute-start | bytes 1032200 | tf_op jit(solution)/shard_map/ppermute | solution.py:38
  213.8 4.5 %slopes.5.refs_9_ = bf16[768,320]{1,0:T(8,128)(2,1)} custom-call(bf16[80,2176]{1,0:T(8,128)(2,1)} %get-tuple-element.105.refs_0_.refs_4_, bf16[80,2176]{1,0:T(8,128)(2,1)} %copy-done.8, bf16[80,2176]{1,0:T(8,128)(2,1)} %copy-done.7, bf16[80,2176]{1,0:T(8,128)(2,1)} %copy-done.9, bf16[80,2176]{1,0:T(8,128)(2,1)} %get-tuple-element.105.refs_0_.refs_4_, ...), custom_call_target="tpu_custom_call" | custom-call | flops 1006632960 | bytes 4947968 | tf_op jit(solution)/shard_map/slopes/pallas_call | solution.py:263
  218.4 7.7 %partial.1.early_ref = f32[8,768,256]{2,1,0:T(8,128)} custom-call(bf16[128,2176]{1,0:T(8,128)(2,1)} %get-tuple-element.91.refs_0_.refs_4_, bf16[128,2176]{1,0:T(8,128)(2,1)} %copy-done.2, bf16[128,2176]{1,0:T(8,128)(2,1)} %copy-done.1, bf16[128,2176]{1,0:T(8,128)(2,1)} %copy-done.3, bf16[80,2176]{1,0:T(8,128)(2,1)} %get-tuple-element.105.refs_0_.refs_4_, ...), custom_call_target="tpu_custom_call" | custom-call | flops 2617245696 | bytes 10977280 | tf_op jit(solution)/shard_map/partial/pallas_call | solution.py:295
  226.1 0.7 copy-done.4
  226.8 0.2 copy-done.5
  227.0 0.1 copy-done.6
  227.1 4.8 %slopes.4.slopes_ref = bf16[768,384]{1,0:T(8,128)(2,1)} custom-call(bf16[96,2176]{1,0:T(8,128)(2,1)} %get-tuple-element.101.refs_0_.refs_4_, bf16[96,2176]{1,0:T(8,128)(2,1)} %copy-done.4, bf16[96,2176]{1,0:T(8,128)(2,1)} %copy-done.5, bf16[96,2176]{1,0:T(8,128)(2,1)} %copy-done.6, bf16[96,2176]{1,0:T(8,128)(2,1)} %get-tuple-element.101.refs_0_.refs_4_, ...), custom_call_target="tpu_custom_call" | custom-call | flops 1207959552 | bytes 5308416 | tf_op jit(solution)/shard_map/slopes/pallas_call | solution.py:263
  232.0 6.4 %gradient.1 = bf16[8,768,256]{2,1,0:T(8,128)(2,1)} custom-call(f32[8,768,256]{2,1,0:T(8,128)} %partial.1.early_ref, bf16[768,384]{1,0:T(8,128)(2,1)} %slopes.4.slopes_ref, bf16[96,2176]{1,0:T(8,128)(2,1)} %get-tuple-element.101.refs_0_.refs_4_, bf16[96,2176]{1,0:T(8,128)(2,1)} %copy-done.4, bf16[96,2176]{1,0:T(8,128)(2,1)} %copy-done.5, ...), custom_call_target="tpu_custom_call" | custom-call | flops 1207959552 | bytes 11599872 | tf_op jit(solution)/shard_map/gradient/pallas_call | solution.py:324
  238.4 9.0 %collective-permute-done.26.far_a = bf16[2,112,768]{2,1,0:T(8,128)(2,1)S(1)} collective-permute-done((bf16[2,112,768]{2,1,0:T(8,128)(2,1)S(1)}, bf16[2,112,768]{2,1,0:T(8,128)(2,1)S(1)}, u32[]{:S(2)}, u32[]{:S(2)}) %collective-permute-start.26) | collective-permute-done | bytes 344096 | tf_op jit(solution)/shard_map/ppermute | solution.py:38
  247.4 0.8 copy-done.11
  248.2 6.5 %all-to-all-start = ((bf16[8,768,256]{2,1,0:T(8,128)(2,1)}), bf16[8,768,256]{2,1,0:T(8,128)(2,1)S(1)}, u32[]{:S(2)}, u32[]{:S(2)}) async-start(bf16[8,768,256]{2,1,0:T(8,128)(2,1)} %gradient.1), calls=%async_computation | async-start | bytes 6291456 | tf_op jit(solution)/shard_map/all_to_all | solution.py:424
  254.7 7.5 %collective-permute-start.27 = (bf16[2,144,768]{2,1,0:T(8,128)(2,1)}, bf16[2,144,768]{2,1,0:T(8,128)(2,1)}, u32[]{:S(2)}, u32[]{:S(2)}) collective-permute-start(bf16[2,144,768]{2,1,0:T(8,128)(2,1)} %get-tuple-element.115), channel_id=1, source_target_pairs={{0,32},{4,36},{8,40},{12,44},{16,48},{20,52},{24,56},{28,60},{32,0... | collective-permute-start | bytes 1327112 | tf_op jit(solution)/shard_map/ppermute | solution.py:38
  262.1 35.1 %collective-permute-done.27.far_b = bf16[2,144,768]{2,1,0:T(8,128)(2,1)} collective-permute-done((bf16[2,144,768]{2,1,0:T(8,128)(2,1)}, bf16[2,144,768]{2,1,0:T(8,128)(2,1)}, u32[]{:S(2)}, u32[]{:S(2)}) %collective-permute-start.27) | collective-permute-done | bytes 442400 | tf_op jit(solution)/shard_map/ppermute | solution.py:38
  297.2 1.6 copy-done
  298.9 4.9 %adam.1 = (bf16[256,768]{1,0:T(8,128)(2,1)}, f32[256,768]{1,0:T(8,128)}, f32[256,768]{1,0:T(8,128)}) custom-call(s32[1]{0:T(128)} %get-tuple-element.120.flag_ref, bf16[8,768,256]{2,1,0:T(8,128)(2,1)} %copy-done, bf16[256,768]{1,0:T(8,128)(2,1)} %broadcast_select_fusion.weight_ref, f32[256,768]{1,0:T(8,128)} %bitcast.21, f32[256,768]{1,0:T(8,128)} %bitcast.23, ...), custom_call_target="tpu_custom_call" | custom-call | flops 5898240 | bytes 7864320 | tf_op jit(solution)/shard_map/adam/pallas_call | solution.py:109
  (69 shorter events, 0.2 us)
Async XLA Ops:
  7.2 178.8 %all-gather.2.cloned.1.call-start = ((), (), s32[]{:S(2)}) async-start(), calls=%async_computation.1 | async-start | bytes 3538944 | tf_op jit(solution)/shard_map/all_gather | solution.py:395
  9.7 109.2 %copy-start.10 = (bf16[136,2048]{1,0:T(8,128)(2,1)}, bf16[136,2048]{1,0:T(8,128)(2,1)S(1)}, u32[]{:S(2)}) copy-start(bf16[136,2048]{1,0:T(8,128)(2,1)S(1)} %pad_maximum_fusion.refs_0_) | copy-start | bytes 1671172
  9.7 65.1 %collective-permute-start.1 = (bf16[136,2048]{1,0:T(8,128)(2,1)S(1)}, bf16[136,2048]{1,0:T(8,128)(2,1)S(1)}, u32[]{:S(2)}, u32[]{:S(2)}) collective-permute-start(bf16[136,2048]{1,0:T(8,128)(2,1)S(1)} %pad_maximum_fusion.refs_0_), channel_id=1, source_target_pairs={{0,60},{4,0},{8,4},{12,8},{16,12},{20,16},{24,20},{28,24},{32,28},... | collective-permute-start | bytes 1671176 | tf_op jit(solution)/shard_map/ppermute | solution.py:38
  21.7 53.1 %collective-permute-start = (bf16[136,2048]{1,0:T(8,128)(2,1)S(1)}, bf16[136,2048]{1,0:T(8,128)(2,1)S(1)}, u32[]{:S(2)}, u32[]{:S(2)}) collective-permute-start(bf16[136,2048]{1,0:T(8,128)(2,1)S(1)} %pad_maximum_fusion.refs_0_), channel_id=1, source_target_pairs={{0,4},{4,8},{8,12},{12,16},{16,20},{20,24},{24,28},{28,32},{32,36}... | collective-permute-start | bytes 1671176 | tf_op jit(solution)/shard_map/ppermute | solution.py:38
  23.6 51.2 %collective-permute-start.2 = (bf16[256,768]{1,0:T(8,128)(2,1)}, bf16[256,768]{1,0:T(8,128)(2,1)S(1)}, u32[]{:S(2)}, u32[]{:S(2)}) collective-permute-start(bf16[256,768]{1,0:T(8,128)(2,1)} %bitcast.24), channel_id=1, source_target_pairs={{0,32},{4,36},{8,40},{12,44},{16,48},{20,52},{24,56},{28,60},{32,0... | collective-permute-start | bytes 1179656 | tf_op jit(solution)/shard_map/ppermute | solution.py:38
  74.8 44.1 %copy-start.14 = (bf16[136,2048]{1,0:T(8,128)(2,1)}, bf16[136,2048]{1,0:T(8,128)(2,1)S(1)}, u32[]{:S(2)}) copy-start(bf16[136,2048]{1,0:T(8,128)(2,1)S(1)} %collective-permute-done.1.refs_1_) | copy-start | bytes 1671172
  74.8 44.1 %copy-start.15 = (bf16[136,2048]{1,0:T(8,128)(2,1)}, bf16[136,2048]{1,0:T(8,128)(2,1)S(1)}, u32[]{:S(2)}) copy-start(bf16[136,2048]{1,0:T(8,128)(2,1)S(1)} %collective-permute-done.refs_2_) | copy-start | bytes 1671172
  76.9 15.1 %collective-permute-start.3 = (bf16[136,2048]{1,0:T(8,128)(2,1)S(1)}, bf16[136,2048]{1,0:T(8,128)(2,1)S(1)}, u32[]{:S(2)}, u32[]{:S(2)}) collective-permute-start(bf16[136,2048]{1,0:T(8,128)(2,1)S(1)} %collective-permute-done.refs_2_), channel_id=1, source_target_pairs={{0,4},{4,8},{8,12},{12,16},{16,20},{20,24},{24,28},{28,32},{32,36}... | collective-permute-start | bytes 1671176 | tf_op jit(solution)/shard_map/ppermute | solution.py:38
  78.8 14.1 %collective-permute-start.4 = (bf16[136,2048]{1,0:T(8,128)(2,1)S(1)}, bf16[136,2048]{1,0:T(8,128)(2,1)S(1)}, u32[]{:S(2)}, u32[]{:S(2)}) collective-permute-start(bf16[136,2048]{1,0:T(8,128)(2,1)S(1)} %collective-permute-done.1.refs_1_), channel_id=1, source_target_pairs={{0,60},{4,0},{8,4},{12,8},{16,12},{20,16},{24,20},{28,24},{32,28},... | collective-permute-start | bytes 1671176 | tf_op jit(solution)/shard_map/ppermute | solution.py:38
  92.1 16.8 %copy-start.18 = (bf16[136,2048]{1,0:T(8,128)(2,1)}, bf16[136,2048]{1,0:T(8,128)(2,1)S(1)}, u32[]{:S(2)}) copy-start(bf16[136,2048]{1,0:T(8,128)(2,1)S(1)} %collective-permute-done.3.refs_4_) | copy-start | bytes 1671172
  93.0 17.8 %copy-start.19 = (bf16[136,2048]{1,0:T(8,128)(2,1)}, bf16[136,2048]{1,0:T(8,128)(2,1)S(1)}, u32[]{:S(2)}) copy-start(bf16[136,2048]{1,0:T(8,128)(2,1)S(1)} %collective-permute-done.4.refs_3_) | copy-start | bytes 1671172
  93.0 15.1 %collective-permute-start.5 = (bf16[136,2048]{1,0:T(8,128)(2,1)S(1)}, bf16[136,2048]{1,0:T(8,128)(2,1)}, u32[]{:S(2)}, u32[]{:S(2)}) collective-permute-start(bf16[136,2048]{1,0:T(8,128)(2,1)S(1)} %collective-permute-done.3.refs_4_), channel_id=1, source_target_pairs={{0,4},{4,8},{8,12},{12,16},{16,20},{20,24},{24,28},{28,32},{32,36}... | collective-permute-start | bytes 1671176 | tf_op jit(solution)/shard_map/ppermute | solution.py:38
  94.9 13.9 %collective-permute-start.6 = (bf16[136,2048]{1,0:T(8,128)(2,1)S(1)}, bf16[136,2048]{1,0:T(8,128)(2,1)}, u32[]{:S(2)}, u32[]{:S(2)}) collective-permute-start(bf16[136,2048]{1,0:T(8,128)(2,1)S(1)} %collective-permute-done.4.refs_3_), channel_id=1, source_target_pairs={{0,60},{4,0},{8,4},{12,8},{16,12},{20,16},{24,20},{28,24},{32,28},... | collective-permute-start | bytes 1671176 | tf_op jit(solution)/shard_map/ppermute | solution.py:38
  108.8 15.9 %collective-permute-start.7 = (bf16[136,2048]{1,0:T(8,128)(2,1)}, bf16[136,2048]{1,0:T(8,128)(2,1)S(1)}, u32[]{:S(2)}, u32[]{:S(2)}) collective-permute-start(bf16[136,2048]{1,0:T(8,128)(2,1)} %collective-permute-done.5.refs_6_), channel_id=1, source_target_pairs={{0,4},{4,8},{8,12},{12,16},{16,20},{20,24},{24,28},{28,32},{32,36}... | collective-permute-start | bytes 1671176 | tf_op jit(solution)/shard_map/ppermute | solution.py:38
  110.7 14.0 %collective-permute-start.8 = (bf16[136,2048]{1,0:T(8,128)(2,1)}, bf16[136,2048]{1,0:T(8,128)(2,1)S(1)}, u32[]{:S(2)}, u32[]{:S(2)}) collective-permute-start(bf16[136,2048]{1,0:T(8,128)(2,1)} %collective-permute-done.6.refs_5_), channel_id=1, source_target_pairs={{0,60},{4,0},{8,4},{12,8},{16,12},{20,16},{24,20},{28,24},{32,28},... | collective-permute-start | bytes 1671176 | tf_op jit(solution)/shard_map/ppermute | solution.py:38
  124.8 31.9 %copy-start.16 = (bf16[136,2048]{1,0:T(8,128)(2,1)}, bf16[136,2048]{1,0:T(8,128)(2,1)S(1)}, u32[]{:S(2)}) copy-start(bf16[136,2048]{1,0:T(8,128)(2,1)S(1)} %collective-permute-done.7.refs_1_) | copy-start | bytes 1671172
  124.8 31.8 %copy-start.17 = (bf16[136,2048]{1,0:T(8,128)(2,1)}, bf16[136,2048]{1,0:T(8,128)(2,1)S(1)}, u32[]{:S(2)}) copy-start(bf16[136,2048]{1,0:T(8,128)(2,1)S(1)} %collective-permute-done.8.refs_0_) | copy-start | bytes 1671172
  124.8 12.5 %collective-permute-start.9 = (bf16[136,2048]{1,0:T(8,128)(2,1)S(1)}, bf16[136,2048]{1,0:T(8,128)(2,1)S(1)}, u32[]{:S(2)}, u32[]{:S(2)}) collective-permute-start(bf16[136,2048]{1,0:T(8,128)(2,1)S(1)} %collective-permute-done.7.refs_1_), channel_id=1, source_target_pairs={{0,4},{4,8},{8,12},{12,16},{16,20},{20,24},{24,28},{28,32},{32,36}... | collective-permute-start | bytes 1671176 | tf_op jit(solution)/shard_map/ppermute | solution.py:38
  126.7 11.6 %collective-permute-start.10 = (bf16[136,2048]{1,0:T(8,128)(2,1)S(1)}, bf16[136,2048]{1,0:T(8,128)(2,1)S(1)}, u32[]{:S(2)}, u32[]{:S(2)}) collective-permute-start(bf16[136,2048]{1,0:T(8,128)(2,1)S(1)} %collective-permute-done.8.refs_0_), channel_id=1, source_target_pairs={{0,60},{4,0},{8,4},{12,8},{16,12},{20,16},{24,20},{28,24},{32,28},... | collective-permute-start | bytes 1671176 | tf_op jit(solution)/shard_map/ppermute | solution.py:38
  131.3 29.0 %collective-permute-start.13 = (bf16[128,2176]{1,0:T(8,128)(2,1)}, bf16[128,2176]{1,0:T(8,128)(2,1)S(1)}, u32[]{:S(2)}, u32[]{:S(2)}) collective-permute-start(bf16[128,2176]{1,0:T(8,128)(2,1)} %get-tuple-element.77), channel_id=1, source_target_pairs={{0,2},{1,3},{2,0},{3,1},{4,6},{5,7},{6,4},{7,5},{8,10},{9,11},{10,... | collective-permute-start | bytes 1671176 | tf_op jit(solution)/shard_map/ppermute | solution.py:45
  137.3 19.3 %copy-start.22 = (bf16[136,2048]{1,0:T(8,128)(2,1)}, bf16[136,2048]{1,0:T(8,128)(2,1)S(1)}, u32[]{:S(2)}) copy-start(bf16[136,2048]{1,0:T(8,128)(2,1)S(1)} %collective-permute-done.9.refs_3_) | copy-start | bytes 1671172
  138.3 18.3 %copy-start.23 = (bf16[136,2048]{1,0:T(8,128)(2,1)}, bf16[136,2048]{1,0:T(8,128)(2,1)S(1)}, u32[]{:S(2)}) copy-start(bf16[136,2048]{1,0:T(8,128)(2,1)S(1)} %collective-permute-done.10.refs_2_) | copy-start | bytes 1671172
  138.3 22.0 %collective-permute-start.11 = (bf16[136,2048]{1,0:T(8,128)(2,1)S(1)}, bf16[136,2048]{1,0:T(8,128)(2,1)S(1)}, u32[]{:S(2)}, u32[]{:S(2)}) collective-permute-start(bf16[136,2048]{1,0:T(8,128)(2,1)S(1)} %collective-permute-done.9.refs_3_), channel_id=1, source_target_pairs={{0,4},{4,8},{8,12},{12,16},{16,20},{20,24},{24,28},{28,32},{32,36}... | collective-permute-start | bytes 1671176 | tf_op jit(solution)/shard_map/ppermute | solution.py:38
  141.3 19.1 %collective-permute-start.12 = (bf16[136,2048]{1,0:T(8,128)(2,1)S(1)}, bf16[136,2048]{1,0:T(8,128)(2,1)S(1)}, u32[]{:S(2)}, u32[]{:S(2)}) collective-permute-start(bf16[136,2048]{1,0:T(8,128)(2,1)S(1)} %collective-permute-done.10.refs_2_), channel_id=1, source_target_pairs={{0,60},{4,0},{8,4},{12,8},{16,12},{20,16},{24,20},{28,24},{32,28},... | collective-permute-start | bytes 1671176 | tf_op jit(solution)/shard_map/ppermute | solution.py:38
  145.5 22.7 %collective-permute-start.16 = (bf16[128,2176]{1,0:T(8,128)(2,1)}, bf16[128,2176]{1,0:T(8,128)(2,1)S(1)}, u32[]{:S(2)}, u32[]{:S(2)}) collective-permute-start(bf16[128,2176]{1,0:T(8,128)(2,1)} %get-tuple-element.84), channel_id=1, source_target_pairs={{0,1},{1,0},{2,3},{3,2},{4,5},{5,4},{6,7},{7,6},{8,9},{9,8},{10,11... | collective-permute-start | bytes 1671176 | tf_op jit(solution)/shard_map/ppermute | solution.py:45
  153.6 18.0 %collective-permute-start.17 = (bf16[128,2176]{1,0:T(8,128)(2,1)}, bf16[128,2176]{1,0:T(8,128)(2,1)S(1)}, u32[]{:S(2)}, u32[]{:S(2)}) collective-permute-start(bf16[128,2176]{1,0:T(8,128)(2,1)} %get-tuple-element.85), channel_id=1, source_target_pairs={{0,3},{1,2},{2,1},{3,0},{4,7},{5,6},{6,5},{7,4},{8,11},{9,10},{10,... | collective-permute-start | bytes 1671176 | tf_op jit(solution)/shard_map/ppermute | solution.py:45
  160.3 25.6 %copy-start.1 = (bf16[128,2176]{1,0:T(8,128)(2,1)}, bf16[128,2176]{1,0:T(8,128)(2,1)S(1)}, u32[]{:S(2)}) copy-start(bf16[128,2176]{1,0:T(8,128)(2,1)S(1)} %collective-permute-done.13.refs_2_.refs_6_) | copy-start | bytes 1671172
  160.4 22.2 %copy-start.20 = (bf16[136,2048]{1,0:T(8,128)(2,1)}, bf16[136,2048]{1,0:T(8,128)(2,1)S(1)}, u32[]{:S(2)}) copy-start(bf16[136,2048]{1,0:T(8,128)(2,1)S(1)} %collective-permute-done.11.refs_1_) | copy-start | bytes 1671172
  160.4 22.1 %copy-start.21 = (bf16[136,2048]{1,0:T(8,128)(2,1)}, bf16[136,2048]{1,0:T(8,128)(2,1)S(1)}, u32[]{:S(2)}) copy-start(bf16[136,2048]{1,0:T(8,128)(2,1)S(1)} %collective-permute-done.12.refs_0_) | copy-start | bytes 1671172
  160.4 16.6 %collective-permute-start.15 = (bf16[136,2048]{1,0:T(8,128)(2,1)S(1)}, bf16[136,2048]{1,0:T(8,128)(2,1)S(1)}, u32[]{:S(2)}, u32[]{:S(2)}) collective-permute-start(bf16[136,2048]{1,0:T(8,128)(2,1)S(1)} %collective-permute-done.12.refs_0_), channel_id=1, source_target_pairs={{0,60},{4,0},{8,4},{12,8},{16,12},{20,16},{24,20},{28,24},{32,28},... | collective-permute-start | bytes 1671176 | tf_op jit(solution)/shard_map/ppermute | solution.py:38
  164.0 16.5 %collective-permute-start.14 = (bf16[136,2048]{1,0:T(8,128)(2,1)S(1)}, bf16[136,2048]{1,0:T(8,128)(2,1)S(1)}, u32[]{:S(2)}, u32[]{:S(2)}) collective-permute-start(bf16[136,2048]{1,0:T(8,128)(2,1)S(1)} %collective-permute-done.11.refs_1_), channel_id=1, source_target_pairs={{0,4},{4,8},{8,12},{12,16},{16,20},{20,24},{24,28},{28,32},{32,36}... | collective-permute-start | bytes 1671176 | tf_op jit(solution)/shard_map/ppermute | solution.py:38
  166.0 11.0 %collective-permute-start.18 = (bf16[80,2176]{1,0:T(8,128)(2,1)}, bf16[80,2176]{1,0:T(8,128)(2,1)S(1)}, u32[]{:S(2)}, u32[]{:S(2)}) collective-permute-start(bf16[80,2176]{1,0:T(8,128)(2,1)} %get-tuple-element.86), channel_id=1, source_target_pairs={{0,2},{1,3},{2,0},{3,1},{4,6},{5,7},{6,4},{7,5},{8,10},{9,11},{10,... | collective-permute-start | bytes 1044488 | tf_op jit(solution)/shard_map/ppermute | solution.py:45
  168.2 17.8 %copy-start.2 = (bf16[128,2176]{1,0:T(8,128)(2,1)}, bf16[128,2176]{1,0:T(8,128)(2,1)S(1)}, u32[]{:S(2)}) copy-start(bf16[128,2176]{1,0:T(8,128)(2,1)S(1)} %collective-permute-done.16.refs_1_.refs_5_) | copy-start | bytes 1671172
  168.2 23.3 %collective-permute-start.21 = (bf16[80,2176]{1,0:T(8,128)(2,1)}, bf16[80,2176]{1,0:T(8,128)(2,1)S(1)}, u32[]{:S(2)}, u32[]{:S(2)}) collective-permute-start(bf16[80,2176]{1,0:T(8,128)(2,1)} %get-tuple-element.97), channel_id=1, source_target_pairs={{0,1},{1,0},{2,3},{3,2},{4,5},{5,4},{6,7},{7,6},{8,9},{9,8},{10,11... | collective-permute-start | bytes 1044488 | tf_op jit(solution)/shard_map/ppermute | solution.py:45
  171.6 14.4 %copy-start.3 = (bf16[128,2176]{1,0:T(8,128)(2,1)}, bf16[128,2176]{1,0:T(8,128)(2,1)S(1)}, u32[]{:S(2)}) copy-start(bf16[128,2176]{1,0:T(8,128)(2,1)S(1)} %collective-permute-done.17.refs_3_.refs_7_) | copy-start | bytes 1671172
  171.6 19.9 %collective-permute-start.22 = (bf16[80,2176]{1,0:T(8,128)(2,1)}, bf16[80,2176]{1,0:T(8,128)(2,1)S(1)}, u32[]{:S(2)}, u32[]{:S(2)}) collective-permute-start(bf16[80,2176]{1,0:T(8,128)(2,1)} %get-tuple-element.98), channel_id=1, source_target_pairs={{0,3},{1,2},{2,1},{3,0},{4,7},{5,6},{6,5},{7,4},{8,11},{9,10},{10,... | collective-permute-start | bytes 1044488 | tf_op jit(solution)/shard_map/ppermute | solution.py:45
  177.0 14.5 %copy-start.7 = (bf16[80,2176]{1,0:T(8,128)(2,1)}, bf16[80,2176]{1,0:T(8,128)(2,1)S(1)}, u32[]{:S(2)}) copy-start(bf16[80,2176]{1,0:T(8,128)(2,1)S(1)} %collective-permute-done.18.refs_2_.refs_6_) | copy-start | bytes 1044484
  177.0 5.5 %copy-start.12 = (bf16[136,2048]{1,0:T(8,128)(2,1)}, bf16[136,2048]{1,0:T(8,128)(2,1)S(1)}, u32[]{:S(2)}) copy-start(bf16[136,2048]{1,0:T(8,128)(2,1)S(1)} %collective-permute-done.15.refs_2_) | copy-start | bytes 1671172
  180.5 2.0 copy-start.13
  180.6 11.0 %collective-permute-start.20 = (bf16[72,2048]{1,0:T(8,128)(2,1)S(1)}, bf16[72,2048]{1,0:T(8,128)(2,1)}, u32[]{:S(2)}, u32[]{:S(2)}) collective-permute-start(bf16[72,2048]{1,0:T(8,128)(2,1)S(1)} %slice.7), channel_id=1, source_target_pairs={{0,60},{4,0},{8,4},{12,8},{16,12},{20,16},{24,20},{28,24},{32,28},... | collective-permute-start | bytes 884744 | tf_op jit(solution)/shard_map/ppermute | solution.py:38
  182.6 9.0 %collective-permute-start.19 = (bf16[64,2048]{1,0:T(8,128)(2,1)S(1)}, bf16[64,2048]{1,0:T(8,128)(2,1)S(1)}, u32[]{:S(2)}, u32[]{:S(2)}) collective-permute-start(bf16[64,2048]{1,0:T(8,128)(2,1)S(1)} %slice.6), channel_id=1, source_target_pairs={{0,4},{4,8},{8,12},{12,16},{16,20},{20,24},{24,28},{28,32},{32,36}... | collective-permute-start | bytes 786440 | tf_op jit(solution)/shard_map/ppermute | solution.py:38
  191.5 15.7 %copy-start.24 = (bf16[2,112,768]{2,1,0:T(8,128)(2,1)S(1)}, bf16[2,112,768]{2,1,0:T(8,128)(2,1)}, u32[]{:S(2)}) copy-start(bf16[2,112,768]{2,1,0:T(8,128)(2,1)} %get-tuple-element.112) | copy-start | bytes 1032196
  191.5 22.4 %copy-start.8 = (bf16[80,2176]{1,0:T(8,128)(2,1)}, bf16[80,2176]{1,0:T(8,128)(2,1)S(1)}, u32[]{:S(2)}) copy-start(bf16[80,2176]{1,0:T(8,128)(2,1)S(1)} %collective-permute-done.21.refs_1_.refs_5_) | copy-start | bytes 1044484
  191.5 22.3 %copy-start.9 = (bf16[80,2176]{1,0:T(8,128)(2,1)}, bf16[80,2176]{1,0:T(8,128)(2,1)S(1)}, u32[]{:S(2)}) copy-start(bf16[80,2176]{1,0:T(8,128)(2,1)S(1)} %collective-permute-done.22.refs_3_.refs_7_) | copy-start | bytes 1044484
  191.5 0.7 copy-start.25
  196.7 29.4 %collective-permute-start.23 = (bf16[96,2176]{1,0:T(8,128)(2,1)}, bf16[96,2176]{1,0:T(8,128)(2,1)S(1)}, u32[]{:S(2)}, u32[]{:S(2)}) collective-permute-start(bf16[96,2176]{1,0:T(8,128)(2,1)} %get-tuple-element.102), channel_id=1, source_target_pairs={{0,1},{1,0},{2,3},{3,2},{4,5},{5,4},{6,7},{7,6},{8,9},{9,8},{10,11... | collective-permute-start | bytes 1253384 | tf_op jit(solution)/shard_map/ppermute | solution.py:45
  201.7 24.4 %collective-permute-start.24 = (bf16[96,2176]{1,0:T(8,128)(2,1)}, bf16[96,2176]{1,0:T(8,128)(2,1)S(1)}, u32[]{:S(2)}, u32[]{:S(2)}) collective-permute-start(bf16[96,2176]{1,0:T(8,128)(2,1)} %get-tuple-element.103), channel_id=1, source_target_pairs={{0,2},{1,3},{2,0},{3,1},{4,6},{5,7},{6,4},{7,5},{8,10},{9,11},{10,... | collective-permute-start | bytes 1253384 | tf_op jit(solution)/shard_map/ppermute | solution.py:45
  203.7 22.5 %collective-permute-start.25 = (bf16[96,2176]{1,0:T(8,128)(2,1)}, bf16[96,2176]{1,0:T(8,128)(2,1)S(1)}, u32[]{:S(2)}, u32[]{:S(2)}) collective-permute-start(bf16[96,2176]{1,0:T(8,128)(2,1)} %get-tuple-element.104), channel_id=1, source_target_pairs={{0,3},{1,2},{2,1},{3,0},{4,7},{5,6},{6,5},{7,4},{8,11},{9,10},{10,... | collective-permute-start | bytes 1253384 | tf_op jit(solution)/shard_map/ppermute | solution.py:45
  207.2 40.2 %collective-permute-start.26 = (bf16[2,112,768]{2,1,0:T(8,128)(2,1)S(1)}, bf16[2,112,768]{2,1,0:T(8,128)(2,1)S(1)}, u32[]{:S(2)}, u32[]{:S(2)}) collective-permute-start(bf16[2,112,768]{2,1,0:T(8,128)(2,1)S(1)} %copy-done.24), channel_id=1, source_target_pairs={{0,32},{4,36},{8,40},{12,44},{16,48},{20,52},{24,56},{28,60},{32,0... | collective-permute-start | bytes 1032200 | tf_op jit(solution)/shard_map/ppermute | solution.py:38
  226.1 0.8 copy-start.4
  226.1 0.9 copy-start.5
  226.1 1.0 copy-start.6
  247.4 0.8 copy-start.11
  248.2 49.0 %all-to-all-start = ((bf16[8,768,256]{2,1,0:T(8,128)(2,1)}), bf16[8,768,256]{2,1,0:T(8,128)(2,1)S(1)}, u32[]{:S(2)}, u32[]{:S(2)}) async-start(bf16[8,768,256]{2,1,0:T(8,128)(2,1)} %gradient.1), calls=%async_computation | async-start | bytes 6291456 | tf_op jit(solution)/shard_map/all_to_all | solution.py:424
  254.7 42.6 %collective-permute-start.27 = (bf16[2,144,768]{2,1,0:T(8,128)(2,1)}, bf16[2,144,768]{2,1,0:T(8,128)(2,1)}, u32[]{:S(2)}, u32[]{:S(2)}) collective-permute-start(bf16[2,144,768]{2,1,0:T(8,128)(2,1)} %get-tuple-element.115), channel_id=1, source_target_pairs={{0,32},{4,36},{8,40},{12,44},{16,48},{20,52},{24,56},{28,60},{32,0... | collective-permute-start | bytes 1327112 | tf_op jit(solution)/shard_map/ppermute | solution.py:38
  297.2 1.6 copy-start
Sparse Core Ops, SparseCore 0:
  77.0 76.3 all-gather.1

commit v5 on v4

--- a/solution.py
+++ b/solution.py
@@ -26,7 +26,7 @@
 TILE = 512
 PICK_TILE = 1024
 INV_ROOT = 1.0 / math.sqrt(D)
-CUTS = (7 * SHARD // 16, 9 * SHARD // 16)
+AHEAD = 3 * SHARD // 16
 VMEM_LIMIT = 56 * 1024 * 1024
 
 
@@ -36,6 +36,10 @@
 
 def shift_z(block, distance):
     return lax.ppermute(block, "z", [(i, (i + distance) % NZ) for i in range(NZ)])
+
+
+def traded(flag, block):
+    return lax.cond(flag == 1, lambda own: shift_z(own, NZ // 2), lambda own: own, block)
 
 
 def swap_xc(block, dx, dc):
@@ -61,12 +65,13 @@
 
 def cast_moments(one, two):
     step = FF // 2
+    cuts = (AHEAD, SHARD - AHEAD)
     return pl.pallas_call(
         cast_kernel,
-        out_shape=[jax.ShapeDtypeStruct((2, rows, FF), jnp.bfloat16) for rows in CUTS],
+        out_shape=[jax.ShapeDtypeStruct((2, rows, FF), jnp.bfloat16) for rows in cuts],
         grid=(FF // step,),
         in_specs=[pl.BlockSpec((SHARD, step), lambda i: (0, i))] * 2,
-        out_specs=[pl.BlockSpec((2, rows, step), lambda i: (0, 0, i)) for rows in CUTS],
+        out_specs=[pl.BlockSpec((2, rows, step), lambda i: (0, 0, i)) for rows in cuts],
         compiler_params=pltpu.CompilerParams(vmem_limit_bytes=VMEM_LIMIT),
         cost_estimate=pl.CostEstimate(
             flops=2 * SHARD * FF, bytes_accessed=12 * SHARD * FF, transcendentals=0
@@ -82,8 +87,7 @@
         total = total + parts_ref[i].astype(jnp.float32)
     gradient = total.T
     swapped = flag_ref[0] == 1
-    rows = gradient.shape[0]
-    rest = rows - far_a.shape[1]
+    rest = gradient.shape[0] - far_a.shape[1]
     low = jnp.concatenate([far_a[...], far_b[:, :rest]], axis=1).astype(jnp.float32)
     high = far_b[:, rest:].astype(jnp.float32)
     far = jnp.where(pl.program_id(0) == 0, low, high)
@@ -105,7 +109,6 @@
 def adam(flag, parts, weight, one, two, far):
     step = SHARD // 2
     plain = pl.BlockSpec((step, FF), lambda i: (i, 0))
-    whole = [pl.BlockSpec(f.shape, lambda i: (0, 0, 0)) for f in far]
     return pl.pallas_call(
         adam_kernel,
         out_shape=[
@@ -117,7 +120,7 @@
         in_specs=[pl.BlockSpec(memory_space=pltpu.SMEM)]
         + [pl.BlockSpec((parts.shape[0], FF, step), lambda i: (0, 0, i))]
         + [plain, plain, plain]
-        + whole,
+        + [pl.BlockSpec(f.shape, lambda i: (0, 0, 0)) for f in far],
         out_specs=[plain] * 3,
         compiler_params=pltpu.CompilerParams(vmem_limit_bytes=VMEM_LIMIT),
         cost_estimate=pl.CostEstimate(
@@ -240,8 +243,9 @@
     )(homes, *flat)
 
 
-def slopes_kernel(*refs):
-    pieces, gains, weight_ref, readout_ref, out_ref, total = refs[:4], refs[4:8], *refs[8:]
+def slopes_kernel(n_pieces, *refs):
+    pieces, gains = refs[:n_pieces], refs[n_pieces : 2 * n_pieces]
+    weight_ref, readout_ref, out_ref, total = refs[2 * n_pieces :]
     step, steps = pl.program_id(0), pl.num_programs(0)
     rows = jnp.concatenate([p[...] for p in pieces], axis=0)
     product = jnp.dot(rows, weight_ref[...], preferred_element_type=jnp.float32)
@@ -258,10 +262,10 @@
 
 
 def slopes_of(pieces, weight_full, readout_row):
-    rows = 4 * pieces[0].shape[0]
+    rows = sum(p.shape[0] for p in pieces)
     step = D // 2
     return pl.pallas_call(
-        slopes_kernel,
+        functools.partial(slopes_kernel, len(pieces)),
         out_shape=jax.ShapeDtypeStruct((FF, rows), jnp.bfloat16),
         grid=(2,),
         in_specs=[pl.BlockSpec((p.shape[0], step), lambda j: (0, j)) for p in pieces]
@@ -281,20 +285,21 @@
     )(*pieces, *pieces, weight_full, readout_row)
 
 
-def partial_kernel(n_pieces, *refs):
+def gradient_kernel(n_pieces, *refs):
     pieces, slopes, out_ref = refs[:n_pieces], refs[n_pieces:-1], refs[-1]
     down = jnp.concatenate([s[...] for s in slopes], axis=1)
     rows = jnp.concatenate([p[...] for p in pieces], axis=0)
     total = jnp.dot(down, rows, preferred_element_type=jnp.float32)
+    total = (total * INV_ROOT).astype(jnp.bfloat16)
     for i in range(TILE // SHARD):
         out_ref[i] = total[:, i * SHARD : (i + 1) * SHARD]
 
 
-def partial_gradient(pieces, slopes):
+def gradient_parts(pieces, slopes):
     rows = sum(p.shape[0] for p in pieces)
     return pl.pallas_call(
-        functools.partial(partial_kernel, len(pieces)),
-        out_shape=jax.ShapeDtypeStruct((D // SHARD, FF, SHARD), jnp.float32),
+        functools.partial(gradient_kernel, len(pieces)),
+        out_shape=jax.ShapeDtypeStruct((D // SHARD, FF, SHARD), jnp.bfloat16),
         grid=(D // TILE,),
         in_specs=[pl.BlockSpec((p.shape[0], TILE), lambda j: (0, j)) for p in pieces]
         + [pl.BlockSpec(s.shape, lambda j: (0, 0)) for s in slopes],
@@ -302,40 +307,11 @@
         compiler_params=pltpu.CompilerParams(vmem_limit_bytes=VMEM_LIMIT),
         cost_estimate=pl.CostEstimate(
             flops=2 * rows * D * FF,
-            bytes_accessed=2 * rows * (D + FF) + 4 * D * FF,
+            bytes_accessed=2 * (rows * (D + FF) + D * FF),
             transcendentals=0,
         ),
-        name="partial",
+        name="gradient",
     )(*pieces, *slopes)
-
-
-def gradient_kernel(n_pieces, early_ref, slopes_ref, *refs):
-    pieces, out_ref = refs[:n_pieces], refs[n_pieces]
-    rows = jnp.concatenate([p[...] for p in pieces], axis=0)
-    late = jnp.dot(slopes_ref[...], rows, preferred_element_type=jnp.float32)
-    for i in range(TILE // SHARD):
-        part = late[:, i * SHARD : (i + 1) * SHARD] + early_ref[i]
-        out_ref[i] = (part * INV_ROOT).astype(jnp.bfloat16)
-
-
-def gradient_parts(early, pieces, slopes):
-    rows = slopes.shape[1]
-    shards = pl.BlockSpec((TILE // SHARD, FF, SHARD), lambda j: (j, 0, 0))
-    return pl.pallas_call(
-        functools.partial(gradient_kernel, len(pieces)),
-        out_shape=jax.ShapeDtypeStruct((D // SHARD, FF, SHARD), jnp.bfloat16),
-        grid=(D // TILE,),
-        in_specs=[shards, pl.BlockSpec(slopes.shape, lambda j: (0, 0))]
-        + [pl.BlockSpec((p.shape[0], TILE), lambda j: (0, j)) for p in pieces],
-        out_specs=shards,
-        compiler_params=pltpu.CompilerParams(vmem_limit_bytes=VMEM_LIMIT),
-        cost_estimate=pl.CostEstimate(
-            flops=2 * rows * D * FF,
-            bytes_accessed=2 * rows * (D + FF) + 6 * D * FF,
-            transcendentals=0,
-        ),
-        name="gradient",
-    )(early, slopes, *pieces)
 
 
 def body(
@@ -358,14 +334,13 @@
     facts = jnp.concatenate([routes.astype(jnp.bfloat16).T, factor.T], axis=1)
     facts = jnp.pad(facts, ((0, 0), (0, D - 2 * TOK)))
     block = jnp.concatenate([activations, facts], axis=0)
-    weight_own = weights[0]
-    weight_far = shift_z(weight_own, NZ // 2)
+    weight_now = traded(my_flag, weights[0])
     moments = cast_moments(moment_one[0], moment_two[0])
     readout_row = lax.dynamic_index_in_dim(readout, resident, 0).astype(jnp.float32)
 
     blocks = {0: (block,)}
     fwd = bwd = block
-    picked, pieces, slopes, far = [], [], [], []
+    picked, pieces = [], []
 
     def pick(group):
         picked.append(select([[blocks[o] for o in part] for part in group], homes))
@@ -378,49 +353,51 @@
     for k in range(1, NZ // 2):
         fwd = shift_z(fwd, 1)
         bwd = shift_z(bwd, -1)
-        beside = {
-            1: (moments, weight_far, readout_row),
-            4: picked[-1:],
-            6: pieces[0][2:3] if pieces else (),
-            7: pieces[0][1:2] + pieces[0][3:] + pieces[1][2:3] if len(pieces) > 1 else (),
-        }.get(k, ())
-        if k == 6:
-            beside = (beside, picked[1])
+        if k == 1:
+            beside = [weight_now, readout_row, *moments]
+        elif k == 3:
+            beside = [ahead]
+        elif k == 4:
+            beside = [picked[0]]
+        elif k == 6:
+            beside = [pieces[0][1], pieces[0][2], picked[1]]
+        elif k == 7:
+            beside = [pieces[0][3], pieces[1][2]]
+        else:
+            beside = []
         fwd, bwd, beside = lax.optimization_barrier((fwd, bwd, beside))
         blocks[-k] = (fwd,)
         blocks[k] = (bwd,)
         if k == 1:
-            moments, weight_far, readout_row = beside
-            weight_now = jnp.where(my_flag == 1, weight_far, weight_own)
+            weight_now, readout_row, *moments = beside
             weight_full = lax.all_gather(weight_now, ("y", "h"), axis=0, tiled=True)
+            ahead = shift_z(moments[0], NZ // 2)
         elif k == 3:
+            (ahead,) = beside
             pick(GROUPS[0])
         elif k == 4:
-            picked[-1] = beside[0]
+            (picked[0],) = beside
             exchange()
         elif k == 5:
             pick(GROUPS[1])
         elif k == 6:
-            (pieces[0][2],), picked[1] = beside
+            pieces[0][1], pieces[0][2], picked[1] = beside
             exchange()
         elif k == 7:
-            pieces[0][1], pieces[0][3], pieces[1][2] = beside
+            pieces[0][3], pieces[1][2] = beside
     last = (shift_z(fwd[: TOK // 2], 1), shift_z(bwd[TOK // 2 :], -1))
-    slopes = [slopes_of(pieces[0], weight_full, readout_row)]
     rest = [pieces[1][1], pieces[1][3]]
-    last, moments, slopes, rest = lax.optimization_barrier((last, moments, slopes, rest))
+    last, rest = lax.optimization_barrier((last, rest))
     pieces[1][1], pieces[1][3] = rest
     blocks[8] = last
-    far = [shift_z(m, NZ // 2) for m in moments]
     pick(GROUPS[2])
     exchange()
-    slopes.append(slopes_of(pieces[1], weight_full, readout_row))
-    early = partial_gradient(pieces[0] + pieces[1], slopes)
-    late = slopes_of(pieces[2], weight_full, readout_row)
-    late, early = lax.optimization_barrier((late, early))
-
-    parts = gradient_parts(early, pieces[2], late)
-    parts, far[0] = lax.optimization_barrier((parts, far[0]))
+    slopes = slopes_of(pieces[0] + pieces[1], weight_full, readout_row)
+    slopes, pieces[2] = lax.optimization_barrier((slopes, pieces[2]))
+    slopes = [slopes, slopes_of(pieces[2], weight_full, readout_row)]
+    parts = gradient_parts([p for group in pieces for p in group], slopes)
+    parts, moment_rest = lax.optimization_barrier((parts, moments[1]))
+    behind = traded(my_flag, moment_rest)
     received = lax.all_to_all(parts, ("y", "h"), split_axis=0, concat_axis=0, tiled=True)
     updated, first, second = adam(
         my_flag.reshape(1),
@@ -428,7 +405,7 @@
         weight_now,
         moment_one[0],
         moment_two[0],
-        far,
+        (ahead, behind),
     )
     return (updated[None], first[None], second[None])
 

time: 315 us -> 319 us (1.013)
  the two profiles are of different devices: /device:TPU:1 before, /device:TPU:7 now
where the time goes in v5:
time: 319 us; the launch traced here: 318 us
  starting transfers between devices  134 us (42%)
  waiting for transfers between devices  115 us (36%)
  Pallas kernels  41.6 us (13%)
  between operations  17.9 us (6%)
  local copies, waits for them, and re-layouts  5.48 us (2%)
  other arithmetic  4.52 us (1%)
    ppermute x19, waiting for transfers between devices, shift_z(): lax.ppermute(block, 'z', [(i, (i + distance) % NZ) for i in range(NZ)])  100 us
    ppermute x19, starting transfers between devices, shift_z(): lax.ppermute(block, 'z', [(i, (i + distance) % NZ) for i in range(NZ)])  83.3 us
    ppermute x9, starting transfers between devices, swap_xc(): return lax.ppermute(block, ('x', 'c'), pairs)  43.6 us
    pallas_call x3, Pallas kernels, select(): pl.pallas_call(functools.partial(select_kernel, cuts), out_shape=[jax.Sha...  14.1 us
    ppermute x9, waiting for transfers between devices, swap_xc(): return lax.ppermute(block, ('x', 'c'), pairs)  14.1 us
    pallas_call x2, Pallas kernels, slopes_of(): pl.pallas_call(functools.partial(slopes_kernel, len(pieces)), out_shape=j...  12.3 us
    pallas_call x1, Pallas kernels, gradient_parts(): pl.pallas_call(functools.partial(gradient_kernel, len(pieces)), out_shape...  8.19 us
    all_to_all x1, starting transfers between devices, body(): lax.all_to_all(parts, ('y', 'h'), split_axis=0, concat_axis=0, tiled=True)  6.89 us
  transfers between devices with their start and end apart: 30, of which 10 were waited for; matrix products, arithmetic and copies ran while one was open for 1% of the time, Pallas kernels for 7%

profile of v5, /device:TPU:7, one launch (start us, length us, event | category | flops | bytes accessed | tf_op | source)
XLA Modules:
  0.0 317.9 jit_solution(1231042731534433586)
XLA Ops:
  7.2 0.0 all-gather.2.cloned.1.call-start
  7.2 0.7 convert_bitcast_fusion
  7.9 0.7 fusion.3
  8.6 0.0 copy-start.3
  8.6 1.1 pad_maximum_fusion.refs_0_
  9.8 3.5 %collective-permute-start.2 = (bf16[136,2048]{1,0:T(8,128)(2,1)S(1)}, bf16[136,2048]{1,0:T(8,128)(2,1)S(1)}, u32[]{:S(2)}, u32[]{:S(2)}) collective-permute-start(bf16[136,2048]{1,0:T(8,128)(2,1)S(1)} %pad_maximum_fusion.refs_0_), channel_id=1, source_target_pairs={{0,4},{4,8},{8,12},{12,16},{16,20},{20,24},{24,28},{28,32},{32,36}... | collective-permute-start | bytes 1671176 | tf_op jit(solution)/shard_map/ppermute | solution.py:38
  13.3 9.5 %collective-permute-start.3 = (bf16[136,2048]{1,0:T(8,128)(2,1)S(1)}, bf16[136,2048]{1,0:T(8,128)(2,1)S(1)}, u32[]{:S(2)}, u32[]{:S(2)}) collective-permute-start(bf16[136,2048]{1,0:T(8,128)(2,1)S(1)} %pad_maximum_fusion.refs_0_), channel_id=1, source_target_pairs={{0,60},{4,0},{8,4},{12,8},{16,12},{20,16},{24,20},{28,24},{32,28},... | collective-permute-start | bytes 1671176 | tf_op jit(solution)/shard_map/ppermute | solution.py:38
  22.8 2.2 cast.1
  25.0 0.7 fusion.4
  27.0 33.8 %conditional.2 = (bf16[256,768]{1,0:T(8,128)(2,1)S(1)}) conditional(s32[]{:T(128)} %bitcast.2, bf16[256,768]{1,0:T(8,128)(2,1)S(1)} %bitcast.19, bf16[256,768]{1,0:T(8,128)(2,1)S(1)} %bitcast.20), branch_computations={%region_0.1_spmd, %region_1.2_spmd} | conditional | bytes 2359344 | solution.py:42
  27.0 8.9 %collective-permute-start = (bf16[256,768]{1,0:T(8,128)(2,1)S(1)}, bf16[256,768]{1,0:T(8,128)(2,1)S(1)}, u32[]{:S(2)}, u32[]{:S(2)}) collective-permute-start(bf16[256,768]{1,0:T(8,128)(2,1)S(1)} %param.1), channel_id=1, source_target_pairs={{0,32},{4,36},{8,40},{12,44},{16,48},{20,52},{24,56},{28,60},{32,0... | collective-permute-start | bytes 1179656 | tf_op jit(solution)/shard_map/cond/branch_1_fun/ppermute | solution.py:38
  35.9 24.8 %collective-permute-done = bf16[256,768]{1,0:T(8,128)(2,1)S(1)} collective-permute-done((bf16[256,768]{1,0:T(8,128)(2,1)S(1)}, bf16[256,768]{1,0:T(8,128)(2,1)S(1)}, u32[]{:S(2)}, u32[]{:S(2)}) %collective-permute-start) | collective-permute-done | bytes 393248 | tf_op jit(solution)/shard_map/cond/branch_1_fun/ppermute | solution.py:38
  60.8 1.3 dynamic-slice_convert_fusion.refs_17_.refs_9_
  62.2 0.0 all-gather.2.cloned.1.call-update
  62.2 1.9 collective-permute-start.4
  64.1 4.6 %collective-permute-start.5 = (bf16[136,2048]{1,0:T(8,128)(2,1)S(1)}, bf16[136,2048]{1,0:T(8,128)(2,1)S(1)}, u32[]{:S(2)}, u32[]{:S(2)}) collective-permute-start(bf16[136,2048]{1,0:T(8,128)(2,1)S(1)} %collective-permute-done.3.refs_1_), channel_id=1, source_target_pairs={{0,60},{4,0},{8,4},{12,8},{16,12},{20,16},{24,20},{28,24},{32,28},... | collective-permute-start | bytes 1671176 | tf_op jit(solution)/shard_map/ppermute | solution.py:38
  68.7 8.5 %collective-permute-done.4.refs_4_ = bf16[136,2048]{1,0:T(8,128)(2,1)S(1)} collective-permute-done((bf16[136,2048]{1,0:T(8,128)(2,1)S(1)}, bf16[136,2048]{1,0:T(8,128)(2,1)S(1)}, u32[]{:S(2)}, u32[]{:S(2)}) %collective-permute-start.4) | collective-permute-done | bytes 557088 | tf_op jit(solution)/shard_map/ppermute | solution.py:38
  77.2 3.6 %collective-permute-done.5.refs_3_ = bf16[136,2048]{1,0:T(8,128)(2,1)S(1)} collective-permute-done((bf16[136,2048]{1,0:T(8,128)(2,1)S(1)}, bf16[136,2048]{1,0:T(8,128)(2,1)S(1)}, u32[]{:S(2)}, u32[]{:S(2)}) %collective-permute-start.5) | collective-permute-done | bytes 557088 | tf_op jit(solution)/shard_map/ppermute | solution.py:38
  80.9 3.1 collective-permute-start.6
  84.0 3.4 %collective-permute-start.7 = (bf16[136,2048]{1,0:T(8,128)(2,1)S(1)}, bf16[136,2048]{1,0:T(8,128)(2,1)}, u32[]{:S(2)}, u32[]{:S(2)}) collective-permute-start(bf16[136,2048]{1,0:T(8,128)(2,1)S(1)} %collective-permute-done.5.refs_3_), channel_id=1, source_target_pairs={{0,60},{4,0},{8,4},{12,8},{16,12},{20,16},{24,20},{28,24},{32,28},... | collective-permute-start | bytes 1671176 | tf_op jit(solution)/shard_map/ppermute | solution.py:38
  87.4 10.8 %collective-permute-start.8 = (bf16[2,48,768]{2,1,0:T(8,128)(2,1)}, bf16[2,48,768]{2,1,0:T(8,128)(2,1)}, u32[]{:S(2)}, u32[]{:S(2)}) collective-permute-start(bf16[2,48,768]{2,1,0:T(8,128)(2,1)} %get-tuple-element.78), channel_id=1, source_target_pairs={{0,32},{4,36},{8,40},{12,44},{16,48},{20,52},{24,56},{28,60},{32,0... | collective-permute-start | bytes 442376 | tf_op jit(solution)/shard_map/ppermute | solution.py:38
  98.2 16.5 %collective-permute-done.8.far_a = bf16[2,48,768]{2,1,0:T(8,128)(2,1)} collective-permute-done((bf16[2,48,768]{2,1,0:T(8,128)(2,1)}, bf16[2,48,768]{2,1,0:T(8,128)(2,1)}, u32[]{:S(2)}, u32[]{:S(2)}) %collective-permute-start.8) | collective-permute-done | bytes 147488 | tf_op jit(solution)/shard_map/ppermute | solution.py:38
  114.7 1.9 collective-permute-start.10
  116.7 4.1 %collective-permute-start.9 = (bf16[136,2048]{1,0:T(8,128)(2,1)}, bf16[136,2048]{1,0:T(8,128)(2,1)S(1)}, u32[]{:S(2)}, u32[]{:S(2)}) collective-permute-start(bf16[136,2048]{1,0:T(8,128)(2,1)} %collective-permute-done.6.refs_6_), channel_id=1, source_target_pairs={{0,4},{4,8},{8,12},{12,16},{16,20},{20,24},{24,28},{28,32},{32,36}... | collective-permute-start | bytes 1671176 | tf_op jit(solution)/shard_map/ppermute | solution.py:38
  122.7 0.7 pad_add_fusion.home_ref
  123.3 5.9 %select.20 = (bf16[128,2176]{1,0:T(8,128)(2,1)}, bf16[128,2176]{1,0:T(8,128)(2,1)}, bf16[128,2176]{1,0:T(8,128)(2,1)}, bf16[128,2176]{1,0:T(8,128)(2,1)}) custom-call(s32[4]{0:T(128)} %pad_add_fusion.home_ref, bf16[136,2048]{1,0:T(8,128)(2,1)} %copy-done.13, bf16[136,2048]{1,0:T(8,128)(2,1)} %copy-done.18, bf16[136,2048]{1,0:T(8,128)(2,1)} %copy-done.17, ...), custom_call_target="tpu_custom_call" | custom-call | flops 1879048192 | bytes 5996544 | tf_op jit(solution)/shard_map/select/pallas_call | solution.py:220
  129.3 3.4 %collective-permute-start.11 = (bf16[136,2048]{1,0:T(8,128)(2,1)S(1)}, bf16[136,2048]{1,0:T(8,128)(2,1)S(1)}, u32[]{:S(2)}, u32[]{:S(2)}) collective-permute-start(bf16[136,2048]{1,0:T(8,128)(2,1)S(1)} %collective-permute-done.9.refs_1_), channel_id=1, source_target_pairs={{0,4},{4,8},{8,12},{12,16},{16,20},{20,24},{24,28},{28,32},{32,36}... | collective-permute-start | bytes 1671176 | tf_op jit(solution)/shard_map/ppermute | solution.py:38
  132.7 3.1 collective-permute-start.12
  135.8 8.8 %collective-permute-start.15 = (bf16[128,2176]{1,0:T(8,128)(2,1)}, bf16[128,2176]{1,0:T(8,128)(2,1)S(1)}, u32[]{:S(2)}, u32[]{:S(2)}) collective-permute-start(bf16[128,2176]{1,0:T(8,128)(2,1)} %get-tuple-element.90), channel_id=1, source_target_pairs={{0,1},{1,0},{2,3},{3,2},{4,5},{5,4},{6,7},{7,6},{8,9},{9,8},{10,11... | collective-permute-start | bytes 1671176 | tf_op jit(solution)/shard_map/ppermute | solution.py:49
  144.6 1.9 collective-permute-start.16
  146.5 3.4 %collective-permute-start.13 = (bf16[136,2048]{1,0:T(8,128)(2,1)S(1)}, bf16[136,2048]{1,0:T(8,128)(2,1)S(1)}, u32[]{:S(2)}, u32[]{:S(2)}) collective-permute-start(bf16[136,2048]{1,0:T(8,128)(2,1)S(1)} %collective-permute-done.11.refs_3_), channel_id=1, source_target_pairs={{0,4},{4,8},{8,12},{12,16},{16,20},{20,24},{24,28},{28,32},{32,36}... | collective-permute-start | bytes 1671176 | tf_op jit(solution)/shard_map/ppermute | solution.py:38
  150.0 3.1 collective-permute-start.14
  153.0 4.1 %collective-permute-start.19 = (bf16[128,2176]{1,0:T(8,128)(2,1)}, bf16[128,2176]{1,0:T(8,128)(2,1)S(1)}, u32[]{:S(2)}, u32[]{:S(2)}) collective-permute-start(bf16[128,2176]{1,0:T(8,128)(2,1)} %get-tuple-element.100), channel_id=1, source_target_pairs={{0,3},{1,2},{2,1},{3,0},{4,7},{5,6},{6,5},{7,4},{8,11},{9,10},{10,... | collective-permute-start | bytes 1671176 | tf_op jit(solution)/shard_map/ppermute | solution.py:49
  157.2 3.8 %select.21 = (bf16[80,2176]{1,0:T(8,128)(2,1)}, bf16[80,2176]{1,0:T(8,128)(2,1)}, bf16[80,2176]{1,0:T(8,128)(2,1)}, bf16[80,2176]{1,0:T(8,128)(2,1)}) custom-call(s32[4]{0:T(128)} %pad_add_fusion.home_ref, bf16[136,2048]{1,0:T(8,128)(2,1)} %copy-done.19, bf16[136,2048]{1,0:T(8,128)(2,1)} %copy-done.20, bf16[136,2048]{1,0:T(8,128)(2,1)} %copy-done.26, ...), custom_call_target="tpu_custom_call" | custom-call | flops 671088640 | bytes 3538944 | tf_op jit(solution)/shard_map/select/pallas_call | solution.py:220
  161.0 3.3 %collective-permute-start.17 = (bf16[136,2048]{1,0:T(8,128)(2,1)S(1)}, bf16[136,2048]{1,0:T(8,128)(2,1)S(1)}, u32[]{:S(2)}, u32[]{:S(2)}) collective-permute-start(bf16[136,2048]{1,0:T(8,128)(2,1)S(1)} %collective-permute-done.13.refs_1_), channel_id=1, source_target_pairs={{0,4},{4,8},{8,12},{12,16},{16,20},{20,24},{24,28},{28,32},{32,36}... | collective-permute-start | bytes 1671176 | tf_op jit(solution)/shard_map/ppermute | solution.py:38
  164.4 3.2 collective-permute-start.18
  167.6 8.4 %collective-permute-start.20 = (bf16[80,2176]{1,0:T(8,128)(2,1)}, bf16[80,2176]{1,0:T(8,128)(2,1)S(1)}, u32[]{:S(2)}, u32[]{:S(2)}) collective-permute-start(bf16[80,2176]{1,0:T(8,128)(2,1)} %get-tuple-element.101), channel_id=1, source_target_pairs={{0,2},{1,3},{2,0},{3,1},{4,6},{5,7},{6,4},{7,5},{8,10},{9,11},{10,... | collective-permute-start | bytes 1044488 | tf_op jit(solution)/shard_map/ppermute | solution.py:49
  175.9 3.9 %collective-permute-start.23 = (bf16[80,2176]{1,0:T(8,128)(2,1)}, bf16[80,2176]{1,0:T(8,128)(2,1)S(1)}, u32[]{:S(2)}, u32[]{:S(2)}) collective-permute-start(bf16[80,2176]{1,0:T(8,128)(2,1)} %get-tuple-element.106), channel_id=1, source_target_pairs={{0,1},{1,0},{2,3},{3,2},{4,5},{5,4},{6,7},{7,6},{8,9},{9,8},{10,11... | collective-permute-start | bytes 1044488 | tf_op jit(solution)/shard_map/ppermute | solution.py:49
  179.8 1.9 collective-permute-start.24
  181.8 0.8 collective-permute-done.20.refs_6_.refs_14_
  182.6 2.1 collective-permute-start.22
  184.7 3.9 %collective-permute-start.21 = (bf16[64,2048]{1,0:T(8,128)(2,1)S(1)}, bf16[64,2048]{1,0:T(8,128)(2,1)S(1)}, u32[]{:S(2)}, u32[]{:S(2)}) collective-permute-start(bf16[64,2048]{1,0:T(8,128)(2,1)S(1)} %slice.6), channel_id=1, source_target_pairs={{0,4},{4,8},{8,12},{12,16},{16,20},{20,24},{24,28},{28,32},{32,36}... | collective-permute-start | bytes 786440 | tf_op jit(solution)/shard_map/ppermute | solution.py:38
  188.7 3.6 %collective-permute-done.24.refs_7_.refs_15_ = bf16[80,2176]{1,0:T(8,128)(2,1)S(1)} collective-permute-done((bf16[80,2176]{1,0:T(8,128)(2,1)}, bf16[80,2176]{1,0:T(8,128)(2,1)S(1)}, u32[]{:S(2)}, u32[]{:S(2)}) %collective-permute-start.24) | collective-permute-done | bytes 348192 | tf_op jit(solution)/shard_map/ppermute | solution.py:49
  192.3 0.7 collective-permute-done.21.refs_4_
  193.1 0.7 copy-done.28
  193.8 0.7 copy-done.27
  194.5 4.5 %select.22 = (bf16[96,2176]{1,0:T(8,128)(2,1)}, bf16[96,2176]{1,0:T(8,128)(2,1)}, bf16[96,2176]{1,0:T(8,128)(2,1)}, bf16[96,2176]{1,0:T(8,128)(2,1)}) custom-call(s32[4]{0:T(128)} %pad_add_fusion.home_ref, bf16[136,2048]{1,0:T(8,128)(2,1)} %copy-done.24, bf16[136,2048]{1,0:T(8,128)(2,1)} %copy-done.23, bf16[136,2048]{1,0:T(8,128)(2,1)} %copy-done.14, ...), custom_call_target="tpu_custom_call" | custom-call | flops 1006632960 | bytes 4358144 | tf_op jit(solution)/shard_map/select/pallas_call | solution.py:220
  199.0 7.0 %collective-permute-start.25 = (bf16[96,2176]{1,0:T(8,128)(2,1)}, bf16[96,2176]{1,0:T(8,128)(2,1)S(1)}, u32[]{:S(2)}, u32[]{:S(2)}) collective-permute-start(bf16[96,2176]{1,0:T(8,128)(2,1)} %get-tuple-element.116), channel_id=1, source_target_pairs={{0,1},{1,0},{2,3},{3,2},{4,5},{5,4},{6,7},{7,6},{8,9},{9,8},{10,11... | collective-permute-start | bytes 1253384 | tf_op jit(solution)/shard_map/ppermute | solution.py:49
  206.0 5.8 %collective-permute-start.26 = (bf16[96,2176]{1,0:T(8,128)(2,1)}, bf16[96,2176]{1,0:T(8,128)(2,1)S(1)}, u32[]{:S(2)}, u32[]{:S(2)}) collective-permute-start(bf16[96,2176]{1,0:T(8,128)(2,1)} %get-tuple-element.117), channel_id=1, source_target_pairs={{0,2},{1,3},{2,0},{3,1},{4,6},{5,7},{6,4},{7,5},{8,10},{9,11},{10,... | collective-permute-start | bytes 1253384 | tf_op jit(solution)/shard_map/ppermute | solution.py:49
  211.8 1.9 collective-permute-start.27
  213.7 0.0 all-gather.2.cloned.1.call-done.refs_16_.refs_8_
  213.7 7.5 %slopes.2.refs_12_ = bf16[768,832]{1,0:T(8,128)(2,1)} custom-call(bf16[128,2176]{1,0:T(8,128)(2,1)} %get-tuple-element.85.refs_0_.refs_8_, bf16[128,2176]{1,0:T(8,128)(2,1)} %copy-done.4, bf16[128,2176]{1,0:T(8,128)(2,1)} %copy-done.5, bf16[128,2176]{1,0:T(8,128)(2,1)} %copy-done.6, bf16[80,2176]{1,0:T(8,128)(2,1)} %get-tuple-element.103.refs_4_.refs_12_, ...), custom_call_target="tpu_custom_call" | custom-call | flops 2617245696 | bytes 7831552 | tf_op jit(solution)/shard_map/slopes/pallas_call | solution.py:267
  221.3 0.7 collective-permute-done.26.refs_2_.refs_6_.refs_10_
  222.0 9.0 %collective-permute-done.27.refs_3_.refs_7_.refs_11_ = bf16[96,2176]{1,0:T(8,128)(2,1)S(1)} collective-permute-done((bf16[96,2176]{1,0:T(8,128)(2,1)}, bf16[96,2176]{1,0:T(8,128)(2,1)S(1)}, u32[]{:S(2)}, u32[]{:S(2)}) %collective-permute-start.27) | collective-permute-done | bytes 417824 | tf_op jit(solution)/shard_map/ppermute | solution.py:49
  230.9 0.7 copy-done.9
  231.7 4.8 %slopes.3.refs_13_ = bf16[768,384]{1,0:T(8,128)(2,1)} custom-call(bf16[96,2176]{1,0:T(8,128)(2,1)} %get-tuple-element.119.refs_0_.refs_4_.refs_8_, bf16[96,2176]{1,0:T(8,128)(2,1)} %copy-done.7, bf16[96,2176]{1,0:T(8,128)(2,1)} %copy-done.8, bf16[96,2176]{1,0:T(8,128)(2,1)} %copy-done.9, bf16[96,2176]{1,0:T(8,128)(2,1)} %get-tuple-element.119.refs_0_.refs_4_.refs_8_, ...), custom_call_target="tpu_custom_call" | custom-call | flops 1207959552 | bytes 5308416 | tf_op jit(solution)/shard_map/slopes/pallas_call | solution.py:267
  236.5 8.2 %gradient.1 = bf16[8,768,256]{2,1,0:T(8,128)(2,1)} custom-call(bf16[128,2176]{1,0:T(8,128)(2,1)} %get-tuple-element.85.refs_0_.refs_8_, bf16[128,2176]{1,0:T(8,128)(2,1)} %copy-done.4, bf16[128,2176]{1,0:T(8,128)(2,1)} %copy-done.5, bf16[128,2176]{1,0:T(8,128)(2,1)} %copy-done.6, bf16[80,2176]{1,0:T(8,128)(2,1)} %get-tuple-element.103.refs_4_.refs_12_, ...), custom_call_target="tpu_custom_call" | custom-call | flops 3825205248 | bytes 9994240 | tf_op jit(solution)/shard_map/gradient/pallas_call | solution.py:300
  244.7 6.9 %all-to-all-start = ((bf16[8,768,256]{2,1,0:T(8,128)(2,1)}), bf16[8,768,256]{2,1,0:T(8,128)(2,1)S(1)}, u32[]{:S(2)}, u32[]{:S(2)}) async-start(bf16[8,768,256]{2,1,0:T(8,128)(2,1)} %gradient.1), calls=%async_computation | async-start | bytes 6291456 | tf_op jit(solution)/shard_map/all_to_all | solution.py:401
  251.6 53.1 %conditional.3 = (bf16[2,208,768]{2,1,0:T(8,128)(2,1)}) conditional(s32[]{:T(128)} %bitcast.2, bf16[2,208,768]{2,1,0:T(8,128)(2,1)} %get-tuple-element.127, bf16[2,208,768]{2,1,0:T(8,128)(2,1)} %get-tuple-element.127), branch_computations={%region_2.3_spmd, %region_3.4_spmd} | conditional | bytes 3833904 | solution.py:42
  251.6 6.1 %collective-permute-start.1 = (bf16[2,208,768]{2,1,0:T(8,128)(2,1)}, bf16[2,208,768]{2,1,0:T(8,128)(2,1)S(1)}, u32[]{:S(2)}, u32[]{:S(2)}) collective-permute-start(bf16[2,208,768]{2,1,0:T(8,128)(2,1)} %param.3), channel_id=1, source_target_pairs={{0,32},{4,36},{8,40},{12,44},{16,48},{20,52},{24,56},{28,60},{32,0... | collective-permute-start | bytes 1916936 | tf_op jit(solution)/shard_map/cond/branch_1_fun/ppermute | solution.py:38
  257.7 46.1 %collective-permute-done.1 = bf16[2,208,768]{2,1,0:T(8,128)(2,1)S(1)} collective-permute-done((bf16[2,208,768]{2,1,0:T(8,128)(2,1)}, bf16[2,208,768]{2,1,0:T(8,128)(2,1)S(1)}, u32[]{:S(2)}, u32[]{:S(2)}) %collective-permute-start.1) | collective-permute-done | bytes 639008 | tf_op jit(solution)/shard_map/cond/branch_1_fun/ppermute | solution.py:38
  303.8 0.8 copy.15
  304.7 1.6 copy-done
  306.3 4.8 %adam.1 = (bf16[256,768]{1,0:T(8,128)(2,1)}, f32[256,768]{1,0:T(8,128)}, f32[256,768]{1,0:T(8,128)}) custom-call(s32[1]{0:T(128)} %get-tuple-element.132.flag_ref, bf16[8,768,256]{2,1,0:T(8,128)(2,1)} %copy-done, bf16[256,768]{1,0:T(8,128)(2,1)S(1)} %copy-done.2, f32[256,768]{1,0:T(8,128)} %bitcast.22, f32[256,768]{1,0:T(8,128)} %bitcast.24, ...), custom_call_target="tpu_custom_call" | custom-call | flops 5898240 | bytes 7864320 | tf_op jit(solution)/shard_map/adam/pallas_call | solution.py:112
  (76 shorter events, 0.2 us)
Async XLA Ops:
  7.2 206.6 %all-gather.2.cloned.1.call-start = ((), (), s32[]{:S(2)}) async-start(), calls=%async_computation.1 | async-start | bytes 3538944 | tf_op jit(solution)/shard_map/all_gather | solution.py:373
  8.6 16.4 %copy-start.16 = (s32[64]{0:T(128)S(1)}, s32[64]{0:T(128)}, u32[]{:S(2)}) copy-start(s32[64]{0:T(128)} %param.21) | copy-start | bytes 772
  8.6 18.4 %copy-start.3 = (bf16[1,256,768]{2,1,0:T(8,128)(2,1)S(1)}, bf16[1,256,768]{2,1,0:T(8,128)(2,1)}, u32[]{:S(2)}) copy-start(bf16[1,256,768]{2,1,0:T(8,128)(2,1)} %param.18) | copy-start | bytes 1179652
  9.8 52.5 %copy-start.13 = (bf16[136,2048]{1,0:T(8,128)(2,1)}, bf16[136,2048]{1,0:T(8,128)(2,1)S(1)}, u32[]{:S(2)}) copy-start(bf16[136,2048]{1,0:T(8,128)(2,1)S(1)} %pad_maximum_fusion.refs_0_) | copy-start | bytes 1671172
  9.8 52.4 %collective-permute-start.2 = (bf16[136,2048]{1,0:T(8,128)(2,1)S(1)}, bf16[136,2048]{1,0:T(8,128)(2,1)S(1)}, u32[]{:S(2)}, u32[]{:S(2)}) collective-permute-start(bf16[136,2048]{1,0:T(8,128)(2,1)S(1)} %pad_maximum_fusion.refs_0_), channel_id=1, source_target_pairs={{0,4},{4,8},{8,12},{12,16},{16,20},{20,24},{24,28},{28,32},{32,36}... | collective-permute-start | bytes 1671176 | tf_op jit(solution)/shard_map/ppermute | solution.py:38
  13.3 48.8 %collective-permute-start.3 = (bf16[136,2048]{1,0:T(8,128)(2,1)S(1)}, bf16[136,2048]{1,0:T(8,128)(2,1)S(1)}, u32[]{:S(2)}, u32[]{:S(2)}) collective-permute-start(bf16[136,2048]{1,0:T(8,128)(2,1)S(1)} %pad_maximum_fusion.refs_0_), channel_id=1, source_target_pairs={{0,60},{4,0},{8,4},{12,8},{16,12},{20,16},{24,20},{28,24},{32,28},... | collective-permute-start | bytes 1671176 | tf_op jit(solution)/shard_map/ppermute | solution.py:38
  27.0 33.7 %collective-permute-start = (bf16[256,768]{1,0:T(8,128)(2,1)S(1)}, bf16[256,768]{1,0:T(8,128)(2,1)S(1)}, u32[]{:S(2)}, u32[]{:S(2)}) collective-permute-start(bf16[256,768]{1,0:T(8,128)(2,1)S(1)} %param.1), channel_id=1, source_target_pairs={{0,32},{4,36},{8,40},{12,44},{16,48},{20,52},{24,56},{28,60},{32,0... | collective-permute-start | bytes 1179656 | tf_op jit(solution)/shard_map/cond/branch_1_fun/ppermute | solution.py:38
  60.8 1.4 copy-start.1
  62.1 61.2 %copy-start.17 = (bf16[136,2048]{1,0:T(8,128)(2,1)}, bf16[136,2048]{1,0:T(8,128)(2,1)S(1)}, u32[]{:S(2)}) copy-start(bf16[136,2048]{1,0:T(8,128)(2,1)S(1)} %collective-permute-done.2.refs_2_) | copy-start | bytes 1671172
  62.2 61.2 %copy-start.18 = (bf16[136,2048]{1,0:T(8,128)(2,1)}, bf16[136,2048]{1,0:T(8,128)(2,1)S(1)}, u32[]{:S(2)}) copy-start(bf16[136,2048]{1,0:T(8,128)(2,1)S(1)} %collective-permute-done.3.refs_1_) | copy-start | bytes 1671172
  62.2 15.0 %collective-permute-start.4 = (bf16[136,2048]{1,0:T(8,128)(2,1)S(1)}, bf16[136,2048]{1,0:T(8,128)(2,1)S(1)}, u32[]{:S(2)}, u32[]{:S(2)}) collective-permute-start(bf16[136,2048]{1,0:T(8,128)(2,1)S(1)} %collective-permute-done.2.refs_2_), channel_id=1, source_target_pairs={{0,4},{4,8},{8,12},{12,16},{16,20},{20,24},{24,28},{28,32},{32,36}... | collective-permute-start | bytes 1671176 | tf_op jit(solution)/shard_map/ppermute | solution.py:38
  64.1 16.7 %collective-permute-start.5 = (bf16[136,2048]{1,0:T(8,128)(2,1)S(1)}, bf16[136,2048]{1,0:T(8,128)(2,1)S(1)}, u32[]{:S(2)}, u32[]{:S(2)}) collective-permute-start(bf16[136,2048]{1,0:T(8,128)(2,1)S(1)} %collective-permute-done.3.refs_1_), channel_id=1, source_target_pairs={{0,60},{4,0},{8,4},{12,8},{16,12},{20,16},{24,20},{28,24},{32,28},... | collective-permute-start | bytes 1671176 | tf_op jit(solution)/shard_map/ppermute | solution.py:38
  77.2 37.5 %copy-start.21 = (bf16[136,2048]{1,0:T(8,128)(2,1)}, bf16[136,2048]{1,0:T(8,128)(2,1)S(1)}, u32[]{:S(2)}) copy-start(bf16[136,2048]{1,0:T(8,128)(2,1)S(1)} %collective-permute-done.4.refs_4_) | copy-start | bytes 1671172
  80.9 42.5 %copy-start.22 = (bf16[136,2048]{1,0:T(8,128)(2,1)}, bf16[136,2048]{1,0:T(8,128)(2,1)S(1)}, u32[]{:S(2)}) copy-start(bf16[136,2048]{1,0:T(8,128)(2,1)S(1)} %collective-permute-done.5.refs_3_) | copy-start | bytes 1671172
  80.9 33.9 %collective-permute-start.6 = (bf16[136,2048]{1,0:T(8,128)(2,1)S(1)}, bf16[136,2048]{1,0:T(8,128)(2,1)}, u32[]{:S(2)}, u32[]{:S(2)}) collective-permute-start(bf16[136,2048]{1,0:T(8,128)(2,1)S(1)} %collective-permute-done.4.refs_4_), channel_id=1, source_target_pairs={{0,4},{4,8},{8,12},{12,16},{16,20},{20,24},{24,28},{28,32},{32,36}... | collective-permute-start | bytes 1671176 | tf_op jit(solution)/shard_map/ppermute | solution.py:38
  84.0 30.8 %collective-permute-start.7 = (bf16[136,2048]{1,0:T(8,128)(2,1)S(1)}, bf16[136,2048]{1,0:T(8,128)(2,1)}, u32[]{:S(2)}, u32[]{:S(2)}) collective-permute-start(bf16[136,2048]{1,0:T(8,128)(2,1)S(1)} %collective-permute-done.5.refs_3_), channel_id=1, source_target_pairs={{0,60},{4,0},{8,4},{12,8},{16,12},{20,16},{24,20},{28,24},{32,28},... | collective-permute-start | bytes 1671176 | tf_op jit(solution)/shard_map/ppermute | solution.py:38
  87.4 27.4 %collective-permute-start.8 = (bf16[2,48,768]{2,1,0:T(8,128)(2,1)}, bf16[2,48,768]{2,1,0:T(8,128)(2,1)}, u32[]{:S(2)}, u32[]{:S(2)}) collective-permute-start(bf16[2,48,768]{2,1,0:T(8,128)(2,1)} %get-tuple-element.78), channel_id=1, source_target_pairs={{0,32},{4,36},{8,40},{12,44},{16,48},{20,52},{24,56},{28,60},{32,0... | collective-permute-start | bytes 442376 | tf_op jit(solution)/shard_map/ppermute | solution.py:38
  114.7 14.5 %collective-permute-start.10 = (bf16[136,2048]{1,0:T(8,128)(2,1)}, bf16[136,2048]{1,0:T(8,128)(2,1)S(1)}, u32[]{:S(2)}, u32[]{:S(2)}) collective-permute-start(bf16[136,2048]{1,0:T(8,128)(2,1)} %collective-permute-done.7.refs_5_), channel_id=1, source_target_pairs={{0,60},{4,0},{8,4},{12,8},{16,12},{20,16},{24,20},{28,24},{32,28},... | collective-permute-start | bytes 1671176 | tf_op jit(solution)/shard_map/ppermute | solution.py:38
  116.7 12.6 %collective-permute-start.9 = (bf16[136,2048]{1,0:T(8,128)(2,1)}, bf16[136,2048]{1,0:T(8,128)(2,1)S(1)}, u32[]{:S(2)}, u32[]{:S(2)}) collective-permute-start(bf16[136,2048]{1,0:T(8,128)(2,1)} %collective-permute-done.6.refs_6_), channel_id=1, source_target_pairs={{0,4},{4,8},{8,12},{12,16},{16,20},{20,24},{24,28},{28,32},{32,36}... | collective-permute-start | bytes 1671176 | tf_op jit(solution)/shard_map/ppermute | solution.py:38
  129.3 27.9 %copy-start.19 = (bf16[136,2048]{1,0:T(8,128)(2,1)}, bf16[136,2048]{1,0:T(8,128)(2,1)S(1)}, u32[]{:S(2)}) copy-start(bf16[136,2048]{1,0:T(8,128)(2,1)S(1)} %collective-permute-done.10.refs_0_) | copy-start | bytes 1671172
  129.3 27.9 %copy-start.20 = (bf16[136,2048]{1,0:T(8,128)(2,1)}, bf16[136,2048]{1,0:T(8,128)(2,1)S(1)}, u32[]{:S(2)}) copy-start(bf16[136,2048]{1,0:T(8,128)(2,1)S(1)} %collective-permute-done.9.refs_1_) | copy-start | bytes 1671172
  129.3 17.2 %collective-permute-start.11 = (bf16[136,2048]{1,0:T(8,128)(2,1)S(1)}, bf16[136,2048]{1,0:T(8,128)(2,1)S(1)}, u32[]{:S(2)}, u32[]{:S(2)}) collective-permute-start(bf16[136,2048]{1,0:T(8,128)(2,1)S(1)} %collective-permute-done.9.refs_1_), channel_id=1, source_target_pairs={{0,4},{4,8},{8,12},{12,16},{16,20},{20,24},{24,28},{28,32},{32,36}... | collective-permute-start | bytes 1671176 | tf_op jit(solution)/shard_map/ppermute | solution.py:38
  132.7 13.9 %collective-permute-start.12 = (bf16[136,2048]{1,0:T(8,128)(2,1)S(1)}, bf16[136,2048]{1,0:T(8,128)(2,1)S(1)}, u32[]{:S(2)}, u32[]{:S(2)}) collective-permute-start(bf16[136,2048]{1,0:T(8,128)(2,1)S(1)} %collective-permute-done.10.refs_0_), channel_id=1, source_target_pairs={{0,60},{4,0},{8,4},{12,8},{16,12},{20,16},{24,20},{28,24},{32,28},... | collective-permute-start | bytes 1671176 | tf_op jit(solution)/shard_map/ppermute | solution.py:38
  135.8 25.2 %collective-permute-start.15 = (bf16[128,2176]{1,0:T(8,128)(2,1)}, bf16[128,2176]{1,0:T(8,128)(2,1)S(1)}, u32[]{:S(2)}, u32[]{:S(2)}) collective-permute-start(bf16[128,2176]{1,0:T(8,128)(2,1)} %get-tuple-element.90), channel_id=1, source_target_pairs={{0,1},{1,0},{2,3},{3,2},{4,5},{5,4},{6,7},{7,6},{8,9},{9,8},{10,11... | collective-permute-start | bytes 1671176 | tf_op jit(solution)/shard_map/ppermute | solution.py:49
  144.6 16.4 %collective-permute-start.16 = (bf16[128,2176]{1,0:T(8,128)(2,1)}, bf16[128,2176]{1,0:T(8,128)(2,1)S(1)}, u32[]{:S(2)}, u32[]{:S(2)}) collective-permute-start(bf16[128,2176]{1,0:T(8,128)(2,1)} %get-tuple-element.91), channel_id=1, source_target_pairs={{0,2},{1,3},{2,0},{3,1},{4,6},{5,7},{6,4},{7,5},{8,10},{9,11},{10,... | collective-permute-start | bytes 1671176 | tf_op jit(solution)/shard_map/ppermute | solution.py:49
  146.5 10.7 %copy-start.25 = (bf16[136,2048]{1,0:T(8,128)(2,1)}, bf16[136,2048]{1,0:T(8,128)(2,1)S(1)}, u32[]{:S(2)}) copy-start(bf16[136,2048]{1,0:T(8,128)(2,1)S(1)} %collective-permute-done.11.refs_3_) | copy-start | bytes 1671172
  146.5 10.7 %copy-start.26 = (bf16[136,2048]{1,0:T(8,128)(2,1)}, bf16[136,2048]{1,0:T(8,128)(2,1)S(1)}, u32[]{:S(2)}) copy-start(bf16[136,2048]{1,0:T(8,128)(2,1)S(1)} %collective-permute-done.12.refs_2_) | copy-start | bytes 1671172
  146.5 14.5 %collective-permute-start.13 = (bf16[136,2048]{1,0:T(8,128)(2,1)S(1)}, bf16[136,2048]{1,0:T(8,128)(2,1)S(1)}, u32[]{:S(2)}, u32[]{:S(2)}) collective-permute-start(bf16[136,2048]{1,0:T(8,128)(2,1)S(1)} %collective-permute-done.11.refs_3_), channel_id=1, source_target_pairs={{0,4},{4,8},{8,12},{12,16},{16,20},{20,24},{24,28},{28,32},{32,36}... | collective-permute-start | bytes 1671176 | tf_op jit(solution)/shard_map/ppermute | solution.py:38
  150.0 11.0 %collective-permute-start.14 = (bf16[136,2048]{1,0:T(8,128)(2,1)S(1)}, bf16[136,2048]{1,0:T(8,128)(2,1)S(1)}, u32[]{:S(2)}, u32[]{:S(2)}) collective-permute-start(bf16[136,2048]{1,0:T(8,128)(2,1)S(1)} %collective-permute-done.12.refs_2_), channel_id=1, source_target_pairs={{0,60},{4,0},{8,4},{12,8},{16,12},{20,16},{24,20},{28,24},{32,28},... | collective-permute-start | bytes 1671176 | tf_op jit(solution)/shard_map/ppermute | solution.py:38
  153.0 26.8 %collective-permute-start.19 = (bf16[128,2176]{1,0:T(8,128)(2,1)}, bf16[128,2176]{1,0:T(8,128)(2,1)S(1)}, u32[]{:S(2)}, u32[]{:S(2)}) collective-permute-start(bf16[128,2176]{1,0:T(8,128)(2,1)} %get-tuple-element.100), channel_id=1, source_target_pairs={{0,3},{1,2},{2,1},{3,0},{4,7},{5,6},{6,5},{7,4},{8,11},{9,10},{10,... | collective-permute-start | bytes 1671176 | tf_op jit(solution)/shard_map/ppermute | solution.py:49
  161.0 38.0 %copy-start.4 = (bf16[128,2176]{1,0:T(8,128)(2,1)}, bf16[128,2176]{1,0:T(8,128)(2,1)S(1)}, u32[]{:S(2)}) copy-start(bf16[128,2176]{1,0:T(8,128)(2,1)S(1)} %collective-permute-done.15.refs_1_.refs_9_) | copy-start | bytes 1671172
  161.0 38.0 %copy-start.5 = (bf16[128,2176]{1,0:T(8,128)(2,1)}, bf16[128,2176]{1,0:T(8,128)(2,1)S(1)}, u32[]{:S(2)}) copy-start(bf16[128,2176]{1,0:T(8,128)(2,1)S(1)} %collective-permute-done.16.refs_2_.refs_10_) | copy-start | bytes 1671172
  161.0 32.1 %copy-start.23 = (bf16[136,2048]{1,0:T(8,128)(2,1)}, bf16[136,2048]{1,0:T(8,128)(2,1)S(1)}, u32[]{:S(2)}) copy-start(bf16[136,2048]{1,0:T(8,128)(2,1)S(1)} %collective-permute-done.13.refs_1_) | copy-start | bytes 1671172
  161.0 32.0 %copy-start.24 = (bf16[136,2048]{1,0:T(8,128)(2,1)}, bf16[136,2048]{1,0:T(8,128)(2,1)S(1)}, u32[]{:S(2)}) copy-start(bf16[136,2048]{1,0:T(8,128)(2,1)S(1)} %collective-permute-done.14.refs_0_) | copy-start | bytes 1671172
  161.0 21.5 %collective-permute-start.17 = (bf16[136,2048]{1,0:T(8,128)(2,1)S(1)}, bf16[136,2048]{1,0:T(8,128)(2,1)S(1)}, u32[]{:S(2)}, u32[]{:S(2)}) collective-permute-start(bf16[136,2048]{1,0:T(8,128)(2,1)S(1)} %collective-permute-done.13.refs_1_), channel_id=1, source_target_pairs={{0,4},{4,8},{8,12},{12,16},{16,20},{20,24},{24,28},{28,32},{32,36}... | collective-permute-start | bytes 1671176 | tf_op jit(solution)/shard_map/ppermute | solution.py:38
  164.4 18.2 %collective-permute-start.18 = (bf16[136,2048]{1,0:T(8,128)(2,1)S(1)}, bf16[136,2048]{1,0:T(8,128)(2,1)S(1)}, u32[]{:S(2)}, u32[]{:S(2)}) collective-permute-start(bf16[136,2048]{1,0:T(8,128)(2,1)S(1)} %collective-permute-done.14.refs_0_), channel_id=1, source_target_pairs={{0,60},{4,0},{8,4},{12,8},{16,12},{20,16},{24,20},{28,24},{32,28},... | collective-permute-start | bytes 1671176 | tf_op jit(solution)/shard_map/ppermute | solution.py:38
  167.6 15.0 %collective-permute-start.20 = (bf16[80,2176]{1,0:T(8,128)(2,1)}, bf16[80,2176]{1,0:T(8,128)(2,1)S(1)}, u32[]{:S(2)}, u32[]{:S(2)}) collective-permute-start(bf16[80,2176]{1,0:T(8,128)(2,1)} %get-tuple-element.101), channel_id=1, source_target_pairs={{0,2},{1,3},{2,0},{3,1},{4,6},{5,7},{6,4},{7,5},{8,10},{9,11},{10,... | collective-permute-start | bytes 1044488 | tf_op jit(solution)/shard_map/ppermute | solution.py:49
  175.9 12.7 %collective-permute-start.23 = (bf16[80,2176]{1,0:T(8,128)(2,1)}, bf16[80,2176]{1,0:T(8,128)(2,1)S(1)}, u32[]{:S(2)}, u32[]{:S(2)}) collective-permute-start(bf16[80,2176]{1,0:T(8,128)(2,1)} %get-tuple-element.106), channel_id=1, source_target_pairs={{0,1},{1,0},{2,3},{3,2},{4,5},{5,4},{6,7},{7,6},{8,9},{9,8},{10,11... | collective-permute-start | bytes 1044488 | tf_op jit(solution)/shard_map/ppermute | solution.py:49
  179.8 19.2 %copy-start.6 = (bf16[128,2176]{1,0:T(8,128)(2,1)}, bf16[128,2176]{1,0:T(8,128)(2,1)S(1)}, u32[]{:S(2)}) copy-start(bf16[128,2176]{1,0:T(8,128)(2,1)S(1)} %collective-permute-done.19.refs_3_.refs_11_) | copy-start | bytes 1671172
  179.8 12.5 %collective-permute-start.24 = (bf16[80,2176]{1,0:T(8,128)(2,1)}, bf16[80,2176]{1,0:T(8,128)(2,1)S(1)}, u32[]{:S(2)}, u32[]{:S(2)}) collective-permute-start(bf16[80,2176]{1,0:T(8,128)(2,1)} %get-tuple-element.107), channel_id=1, source_target_pairs={{0,3},{1,2},{2,1},{3,0},{4,7},{5,6},{6,5},{7,4},{8,11},{9,10},{10,... | collective-permute-start | bytes 1044488 | tf_op jit(solution)/shard_map/ppermute | solution.py:49
  182.6 16.5 %copy-start.10 = (bf16[80,2176]{1,0:T(8,128)(2,1)}, bf16[80,2176]{1,0:T(8,128)(2,1)S(1)}, u32[]{:S(2)}) copy-start(bf16[80,2176]{1,0:T(8,128)(2,1)S(1)} %collective-permute-done.20.refs_6_.refs_14_) | copy-start | bytes 1044484
  182.6 10.5 %copy-start.15 = (bf16[136,2048]{1,0:T(8,128)(2,1)}, bf16[136,2048]{1,0:T(8,128)(2,1)S(1)}, u32[]{:S(2)}) copy-start(bf16[136,2048]{1,0:T(8,128)(2,1)S(1)} %collective-permute-done.17.refs_3_) | copy-start | bytes 1671172
  182.6 10.5 %copy-start.14 = (bf16[136,2048]{1,0:T(8,128)(2,1)}, bf16[136,2048]{1,0:T(8,128)(2,1)S(1)}, u32[]{:S(2)}) copy-start(bf16[136,2048]{1,0:T(8,128)(2,1)S(1)} %collective-permute-done.18.refs_2_) | copy-start | bytes 1671172
  182.6 10.5 %collective-permute-start.22 = (bf16[72,2048]{1,0:T(8,128)(2,1)S(1)}, bf16[72,2048]{1,0:T(8,128)(2,1)S(1)}, u32[]{:S(2)}, u32[]{:S(2)}) collective-permute-start(bf16[72,2048]{1,0:T(8,128)(2,1)S(1)} %slice.7), channel_id=1, source_target_pairs={{0,60},{4,0},{8,4},{12,8},{16,12},{20,16},{24,20},{28,24},{32,28},... | collective-permute-start | bytes 884744 | tf_op jit(solution)/shard_map/ppermute | solution.py:38
  184.7 8.3 %collective-permute-start.21 = (bf16[64,2048]{1,0:T(8,128)(2,1)S(1)}, bf16[64,2048]{1,0:T(8,128)(2,1)S(1)}, u32[]{:S(2)}, u32[]{:S(2)}) collective-permute-start(bf16[64,2048]{1,0:T(8,128)(2,1)S(1)} %slice.6), channel_id=1, source_target_pairs={{0,4},{4,8},{8,12},{12,16},{16,20},{20,24},{24,28},{28,32},{32,36}... | collective-permute-start | bytes 786440 | tf_op jit(solution)/shard_map/ppermute | solution.py:38
  188.7 10.3 %copy-start.11 = (bf16[80,2176]{1,0:T(8,128)(2,1)}, bf16[80,2176]{1,0:T(8,128)(2,1)S(1)}, u32[]{:S(2)}) copy-start(bf16[80,2176]{1,0:T(8,128)(2,1)S(1)} %collective-permute-done.23.refs_5_.refs_13_) | copy-start | bytes 1044484
  192.3 6.7 %copy-start.12 = (bf16[80,2176]{1,0:T(8,128)(2,1)}, bf16[80,2176]{1,0:T(8,128)(2,1)S(1)}, u32[]{:S(2)}) copy-start(bf16[80,2176]{1,0:T(8,128)(2,1)S(1)} %collective-permute-done.24.refs_7_.refs_15_) | copy-start | bytes 1044484
  193.1 0.7 copy-start.28
  193.8 0.7 copy-start.27
  199.0 22.2 %collective-permute-start.25 = (bf16[96,2176]{1,0:T(8,128)(2,1)}, bf16[96,2176]{1,0:T(8,128)(2,1)S(1)}, u32[]{:S(2)}, u32[]{:S(2)}) collective-permute-start(bf16[96,2176]{1,0:T(8,128)(2,1)} %get-tuple-element.116), channel_id=1, source_target_pairs={{0,1},{1,0},{2,3},{3,2},{4,5},{5,4},{6,7},{7,6},{8,9},{9,8},{10,11... | collective-permute-start | bytes 1253384 | tf_op jit(solution)/shard_map/ppermute | solution.py:49
  206.0 16.0 %collective-permute-start.26 = (bf16[96,2176]{1,0:T(8,128)(2,1)}, bf16[96,2176]{1,0:T(8,128)(2,1)S(1)}, u32[]{:S(2)}, u32[]{:S(2)}) collective-permute-start(bf16[96,2176]{1,0:T(8,128)(2,1)} %get-tuple-element.117), channel_id=1, source_target_pairs={{0,2},{1,3},{2,0},{3,1},{4,6},{5,7},{6,4},{7,5},{8,10},{9,11},{10,... | collective-permute-start | bytes 1253384 | tf_op jit(solution)/shard_map/ppermute | solution.py:49
  211.8 19.2 %collective-permute-start.27 = (bf16[96,2176]{1,0:T(8,128)(2,1)}, bf16[96,2176]{1,0:T(8,128)(2,1)S(1)}, u32[]{:S(2)}, u32[]{:S(2)}) collective-permute-start(bf16[96,2176]{1,0:T(8,128)(2,1)} %get-tuple-element.118), channel_id=1, source_target_pairs={{0,3},{1,2},{2,1},{3,0},{4,7},{5,6},{6,5},{7,4},{8,11},{9,10},{10,... | collective-permute-start | bytes 1253384 | tf_op jit(solution)/shard_map/ppermute | solution.py:49
  221.2 9.7 %copy-start.7 = (bf16[96,2176]{1,0:T(8,128)(2,1)}, bf16[96,2176]{1,0:T(8,128)(2,1)S(1)}, u32[]{:S(2)}) copy-start(bf16[96,2176]{1,0:T(8,128)(2,1)S(1)} %collective-permute-done.25.refs_1_.refs_5_.refs_9_) | copy-start | bytes 1253380
  222.0 9.0 %copy-start.8 = (bf16[96,2176]{1,0:T(8,128)(2,1)}, bf16[96,2176]{1,0:T(8,128)(2,1)S(1)}, u32[]{:S(2)}) copy-start(bf16[96,2176]{1,0:T(8,128)(2,1)S(1)} %collective-permute-done.26.refs_2_.refs_6_.refs_10_) | copy-start | bytes 1253380
  230.9 0.8 copy-start.9
  244.7 60.0 %all-to-all-start = ((bf16[8,768,256]{2,1,0:T(8,128)(2,1)}), bf16[8,768,256]{2,1,0:T(8,128)(2,1)S(1)}, u32[]{:S(2)}, u32[]{:S(2)}) async-start(bf16[8,768,256]{2,1,0:T(8,128)(2,1)} %gradient.1), calls=%async_computation | async-start | bytes 6291456 | tf_op jit(solution)/shard_map/all_to_all | solution.py:401
  251.6 54.7 %copy-start.2 = (bf16[256,768]{1,0:T(8,128)(2,1)S(1)}, bf16[256,768]{1,0:T(8,128)(2,1)}, u32[]{:S(2)}) copy-start(bf16[256,768]{1,0:T(8,128)(2,1)} %copy-done.1) | copy-start | bytes 1179652
  251.6 52.2 %collective-permute-start.1 = (bf16[2,208,768]{2,1,0:T(8,128)(2,1)}, bf16[2,208,768]{2,1,0:T(8,128)(2,1)S(1)}, u32[]{:S(2)}, u32[]{:S(2)}) collective-permute-start(bf16[2,208,768]{2,1,0:T(8,128)(2,1)} %param.3), channel_id=1, source_target_pairs={{0,32},{4,36},{8,40},{12,44},{16,48},{20,52},{24,56},{28,60},{32,0... | collective-permute-start | bytes 1916936 | tf_op jit(solution)/shard_map/cond/branch_1_fun/ppermute | solution.py:38
  304.7 1.6 copy-start
Sparse Core Ops, SparseCore 0:
  62.3 76.3 all-gather.1

commit v6 on v5

--- a/solution.py
+++ b/solution.py
@@ -22,11 +22,11 @@
 META = 8
 WIDE = D + 128
 RELS = ((0, 0), (0, 1), (1, 0), (1, 1))
-GROUPS = (((0, 1, -1, 2, -2, 3, -3),), ((4, -4, 5, -5),), ((6, -6, 7, -7, 8),))
+BATCH = 8
 TILE = 512
 PICK_TILE = 1024
 INV_ROOT = 1.0 / math.sqrt(D)
-AHEAD = 3 * SHARD // 16
+AHEAD = 5 * SHARD // 16
 VMEM_LIMIT = 56 * 1024 * 1024
 
 
@@ -163,47 +163,30 @@
     return jnp.concatenate(selects, axis=0), totals
 
 
-def select_kernel(cuts, home_ref, *refs):
-    n_in = sum(sum(cut) for cut in cuts)
-    ins, outs, plans = refs[:n_in], refs[n_in : n_in + 4], refs[n_in + 4 : -1]
-    gain_ref = refs[-1]
+def select_kernel(home_ref, tokens_ref, *refs):
+    outs, plan, gain_ref = refs[:4], refs[4], refs[5]
+    rows = outs[0].shape[0]
     step = pl.program_id(0)
 
     @pl.when(step == 0)
     def _():
         homes = [home_ref[i].astype(jnp.float32) for i in range(4)]
-        at = row = 0
-        for cut, plan in zip(cuts, plans):
-            facts = []
-            for n in cut:
-                tail = ins[at + n - 1]
-                found = tail[tail.shape[0] - META :, 0 : 2 * TOK].astype(jnp.float32)
-                facts.append((found[:, :TOK], found[:, TOK:]))
-                at += n
-            rows = rows_of(len(cut))
-            chosen, totals = pick_plan(homes, facts, rows)
-            plan[...] = chosen
-            for i in range(4):
-                gain_ref[i, row : row + rows, :] = jnp.broadcast_to(
-                    totals[i], (rows, WIDE - D)
-                ).astype(jnp.bfloat16)
-            row += rows
+        facts = []
+        for b in range(BATCH):
+            found = tokens_ref[b, TOK:, 0 : 2 * TOK].astype(jnp.float32)
+            facts.append((found[:, :TOK], found[:, TOK:]))
+        chosen, totals = pick_plan(homes, facts, rows)
+        plan[...] = chosen
+        for i in range(4):
+            gain_ref[i] = jnp.broadcast_to(totals[i], (rows, WIDE - D)).astype(jnp.bfloat16)
 
     @pl.when(step < D // PICK_TILE)
     def _():
-        at = row = 0
-        for cut, plan in zip(cuts, plans):
-            parts = []
-            for n in cut:
-                parts += [r[0 : TOK // n, :] for r in ins[at : at + n]]
-                at += n
-            rows = rows_of(len(cut))
-            picked = jnp.dot(
-                plan[...], jnp.concatenate(parts, axis=0), preferred_element_type=jnp.float32
-            ).astype(jnp.bfloat16)
-            for i in range(4):
-                outs[i][row : row + rows, :] = picked[i * rows : (i + 1) * rows]
-            row += rows
+        source = jnp.concatenate([tokens_ref[b, :TOK, :] for b in range(BATCH)], axis=0)
+        picked = jnp.dot(plan[...], source, preferred_element_type=jnp.float32)
+        picked = picked.astype(jnp.bfloat16)
+        for i in range(4):
+            outs[i][...] = picked[i * rows : (i + 1) * rows]
 
     @pl.when(step == D // PICK_TILE)
     def _():
@@ -211,36 +194,34 @@
             outs[i][:, 0 : WIDE - D] = gain_ref[i]
 
 
-def select(products, homes):
-    cuts = tuple(tuple(len(b) for b in blocks) for blocks in products)
-    sizes = [rows_of(len(blocks)) for blocks in products]
-    rows = sum(sizes)
-    flat = [a for blocks in products for b in blocks for a in b]
+def select(tokens, batch, homes):
+    rows = rows_of(BATCH)
     last = D // PICK_TILE - 1
     return pl.pallas_call(
-        functools.partial(select_kernel, cuts),
+        select_kernel,
         out_shape=[jax.ShapeDtypeStruct((rows, WIDE), jnp.bfloat16)] * 4,
         grid=(D // PICK_TILE + 1,),
-        in_specs=[pl.BlockSpec(memory_space=pltpu.SMEM)]
-        + [
-            pl.BlockSpec((a.shape[0], PICK_TILE), lambda j: (0, jnp.minimum(j, last))) for a in flat
+        in_specs=[
+            pl.BlockSpec(memory_space=pltpu.SMEM),
+            pl.BlockSpec(
+                (BATCH, TOK + META, PICK_TILE), lambda j: (batch, 0, jnp.minimum(j, last))
+            ),
         ],
         out_specs=[pl.BlockSpec((rows, PICK_TILE), lambda j: (0, j))] * 4,
         scratch_shapes=[
-            pltpu.VMEM((4 * size, len(blocks) * TOK), jnp.bfloat16)
-            for size, blocks in zip(sizes, products)
-        ]
-        + [pltpu.VMEM((4, rows, WIDE - D), jnp.bfloat16)],
+            pltpu.VMEM((4 * rows, BATCH * TOK), jnp.bfloat16),
+            pltpu.VMEM((4, rows, WIDE - D), jnp.bfloat16),
+        ],
         compiler_params=pltpu.CompilerParams(
             vmem_limit_bytes=VMEM_LIMIT, dimension_semantics=("arbitrary",)
         ),
         cost_estimate=pl.CostEstimate(
-            flops=sum(8 * s * len(b) * TOK * D for s, b in zip(sizes, products)),
-            bytes_accessed=2 * D * (sum(a.shape[0] for a in flat) + 4 * rows),
+            flops=8 * rows * BATCH * TOK * D,
+            bytes_accessed=2 * D * (BATCH * (TOK + META) + 4 * rows),
             transcendentals=0,
         ),
         name="select",
-    )(homes, *flat)
+    )(homes, tokens)
 
 
 def slopes_kernel(n_pieces, *refs):
@@ -334,70 +315,35 @@
     facts = jnp.concatenate([routes.astype(jnp.bfloat16).T, factor.T], axis=1)
     facts = jnp.pad(facts, ((0, 0), (0, D - 2 * TOK)))
     block = jnp.concatenate([activations, facts], axis=0)
+    tokens = lax.all_gather(block, "z", axis=0, tiled=False)
+
     weight_now = traded(my_flag, weights[0])
+    weight_full = lax.all_to_all(
+        jnp.broadcast_to(weight_now[None], (NY * NH, SHARD, FF)),
+        ("y", "h"),
+        split_axis=0,
+        concat_axis=0,
+        tiled=True,
+    ).reshape(D, FF)
+    readout_row = lax.dynamic_index_in_dim(readout, resident, 0).astype(jnp.float32)
     moments = cast_moments(moment_one[0], moment_two[0])
-    readout_row = lax.dynamic_index_in_dim(readout, resident, 0).astype(jnp.float32)
-
-    blocks = {0: (block,)}
-    fwd = bwd = block
-    picked, pieces = [], []
-
-    def pick(group):
-        picked.append(select([[blocks[o] for o in part] for part in group], homes))
-
-    def exchange():
+    tokens, weight_full, readout_row, moments = lax.optimization_barrier(
+        (tokens, weight_full, readout_row, moments)
+    )
+
+    pieces = []
+    for batch in range(NZ // BATCH):
+        picked = select(tokens, batch, homes)
         pieces.append(
-            [p if rel == (0, 0) else swap_xc(p, *rel) for p, rel in zip(picked[-1], RELS)]
+            [p if rel == (0, 0) else swap_xc(p, *rel) for p, rel in zip(picked, RELS)]
         )
-
-    for k in range(1, NZ // 2):
-        fwd = shift_z(fwd, 1)
-        bwd = shift_z(bwd, -1)
-        if k == 1:
-            beside = [weight_now, readout_row, *moments]
-        elif k == 3:
-            beside = [ahead]
-        elif k == 4:
-            beside = [picked[0]]
-        elif k == 6:
-            beside = [pieces[0][1], pieces[0][2], picked[1]]
-        elif k == 7:
-            beside = [pieces[0][3], pieces[1][2]]
-        else:
-            beside = []
-        fwd, bwd, beside = lax.optimization_barrier((fwd, bwd, beside))
-        blocks[-k] = (fwd,)
-        blocks[k] = (bwd,)
-        if k == 1:
-            weight_now, readout_row, *moments = beside
-            weight_full = lax.all_gather(weight_now, ("y", "h"), axis=0, tiled=True)
-            ahead = shift_z(moments[0], NZ // 2)
-        elif k == 3:
-            (ahead,) = beside
-            pick(GROUPS[0])
-        elif k == 4:
-            (picked[0],) = beside
-            exchange()
-        elif k == 5:
-            pick(GROUPS[1])
-        elif k == 6:
-            pieces[0][1], pieces[0][2], picked[1] = beside
-            exchange()
-        elif k == 7:
-            pieces[0][3], pieces[1][2] = beside
-    last = (shift_z(fwd[: TOK // 2], 1), shift_z(bwd[TOK // 2 :], -1))
-    rest = [pieces[1][1], pieces[1][3]]
-    last, rest = lax.optimization_barrier((last, rest))
-    pieces[1][1], pieces[1][3] = rest
-    blocks[8] = last
-    pick(GROUPS[2])
-    exchange()
-    slopes = slopes_of(pieces[0] + pieces[1], weight_full, readout_row)
-    slopes, pieces[2] = lax.optimization_barrier((slopes, pieces[2]))
-    slopes = [slopes, slopes_of(pieces[2], weight_full, readout_row)]
-    parts = gradient_parts([p for group in pieces for p in group], slopes)
-    parts, moment_rest = lax.optimization_barrier((parts, moments[1]))
-    behind = traded(my_flag, moment_rest)
+    ahead = shift_z(moments[0], NZ // 2)
+    slopes = slopes_of(pieces[0], weight_full, readout_row)
+    slopes, pieces[1] = lax.optimization_barrier((slopes, pieces[1]))
+    slopes = [slopes, slopes_of(pieces[1], weight_full, readout_row)]
+    parts = gradient_parts(pieces[0] + pieces[1], slopes)
+    parts, ahead, moment_rest = lax.optimization_barrier((parts, ahead, moments[1]))
+    behind = shift_z(moment_rest, NZ // 2)
     received = lax.all_to_all(parts, ("y", "h"), split_axis=0, concat_axis=0, tiled=True)
     updated, first, second = adam(
         my_flag.reshape(1),

time: 319 us -> 306 us (0.959)
  the two profiles are of different devices: /device:TPU:7 before, /device:TPU:1 now
where the time goes in v6:
time: 306 us; the launch traced here: 305 us
  waiting for transfers between devices  190 us (62%)
  starting transfers between devices  44.9 us (15%)
  Pallas kernels  39.9 us (13%)
  between operations  17.4 us (6%)
  local copies, waits for them, and re-layouts  7.68 us (3%)
  other arithmetic  5.2 us (2%)
    all_gather x1, waiting for transfers between devices, body(): tokens = lax.all_gather(block, 'z', axis=0, tiled=False)  97.1 us
    ppermute x2, waiting for transfers between devices, shift_z(): lax.ppermute(block, 'z', [(i, (i + distance) % NZ) for i in range(NZ)])  52.5 us
    ppermute x6, waiting for transfers between devices, swap_xc(): return lax.ppermute(block, ('x', 'c'), pairs)  23.9 us
    all_to_all x1, waiting for transfers between devices, body(): lax.all_to_all(jnp.broadcast_to(weight_now[None], (NY * NH, SHARD, FF)),...  16.7 us
    ppermute x6, starting transfers between devices, swap_xc(): return lax.ppermute(block, ('x', 'c'), pairs)  15.8 us
    ppermute x2, starting transfers between devices, shift_z(): lax.ppermute(block, 'z', [(i, (i + distance) % NZ) for i in range(NZ)])  14.9 us
    pallas_call x2, Pallas kernels, select(): pl.pallas_call(select_kernel, out_shape=[jax.ShapeDtypeStruct((rows, WIDE...  13 us
    pallas_call x2, Pallas kernels, slopes_of(): pl.pallas_call(functools.partial(slopes_kernel, len(pieces)), out_shape=j...  11.8 us
  transfers between devices with their start and end apart: 11, of which 6 were waited for; matrix products, arithmetic and copies ran while one was open for 2% of the time, Pallas kernels for 9%

profile of v6, /device:TPU:1, one launch (start us, length us, event | category | flops | bytes accessed | tf_op | source)
XLA Modules:
  0.0 305.3 jit_solution(15953401379763576553)
XLA Ops:
  7.2 0.0 all-gather.3.cloned.1.call-start
  7.2 1.0 copy.15
  8.2 0.7 convert_bitcast_fusion
  8.9 0.7 fusion.3
  9.6 1.9 pad_maximum_fusion
  11.5 0.0 all-gather.3.cloned.1.call-update
  11.5 1.5 fusion.4
  13.7 1.8 broadcast_in_dim.16
  15.5 7.5 %all-to-all-start = ((bf16[8,256,768]{2,1,0:T(8,128)(2,1)}), bf16[8,256,768]{2,1,0:T(8,128)(2,1)S(1)}, u32[]{:S(2)}, u32[]{:S(2)}) async-start(bf16[8,256,768]{2,1,0:T(8,128)(2,1)} %broadcast_in_dim.16), calls=%async_computation | async-start | bytes 6291456 | tf_op jit(solution)/shard_map/all_to_all | solution.py:321
  23.0 2.2 cast.1
  27.8 0.6 pad_add_fusion.home_ref
  28.4 1.3 dynamic-slice_convert_fusion.refs_9_
  29.7 16.7 %all-to-all-done = bf16[8,256,768]{2,1,0:T(8,128)(2,1)S(1)} async-done(((bf16[8,256,768]{2,1,0:T(8,128)(2,1)}), bf16[8,256,768]{2,1,0:T(8,128)(2,1)S(1)}, u32[]{:S(2)}, u32[]{:S(2)}) %all-to-all-start) | async-done | bytes 3145760 | tf_op jit(solution)/shard_map/all_to_all | solution.py:321
  46.4 0.0 copy-start
  46.4 97.1 %all-gather.3.cloned.1.call-done = bf16[2176,2048]{1,0:T(8,128)(2,1)} async-done(((bf16[136,2048]{1,0:T(8,128)(2,1)}), bf16[2176,2048]{1,0:T(8,128)(2,1)}) %all-gather.3.cloned.1.call-update) | async-done | bytes 8912912 | tf_op jit(solution)/shard_map/all_gather | solution.py:318
  143.4 6.5 %select.19 = (bf16[144,2176]{1,0:T(8,128)(2,1)}, bf16[144,2176]{1,0:T(8,128)(2,1)}, bf16[144,2176]{1,0:T(8,128)(2,1)}, bf16[144,2176]{1,0:T(8,128)(2,1)}) custom-call(s32[4]{0:T(128)} %pad_add_fusion.home_ref, bf16[16,136,2048]{2,1,0:T(8,128)(2,1)} %bitcast.29), custom_call_target="tpu_custom_call" | custom-call | flops 2415919104 | bytes 6815744 | tf_op jit(solution)/shard_map/select/pallas_call | solution.py:200
  149.9 0.0 copy-done
  149.9 2.3 collective-permute-start.1
  152.3 1.9 collective-permute-start.2
  154.2 0.0 copy-start.8
  154.2 3.7 %collective-permute-start.3 = (bf16[144,2176]{1,0:T(8,128)(2,1)}, bf16[144,2176]{1,0:T(8,128)(2,1)S(1)}, u32[]{:S(2)}, u32[]{:S(2)}) collective-permute-start(bf16[144,2176]{1,0:T(8,128)(2,1)} %get-tuple-element.40), channel_id=1, source_target_pairs={{0,3},{1,2},{2,1},{3,0},{4,7},{5,6},{6,5},{7,4},{8,11},{9,10},{10,... | collective-permute-start | bytes 1880072 | tf_op jit(solution)/shard_map/ppermute | solution.py:49
  158.0 6.5 %select.20 = (bf16[144,2176]{1,0:T(8,128)(2,1)}, bf16[144,2176]{1,0:T(8,128)(2,1)}, bf16[144,2176]{1,0:T(8,128)(2,1)}, bf16[144,2176]{1,0:T(8,128)(2,1)}) custom-call(s32[4]{0:T(128)} %pad_add_fusion.home_ref, bf16[16,136,2048]{2,1,0:T(8,128)(2,1)} %bitcast.30), custom_call_target="tpu_custom_call" | custom-call | flops 2415919104 | bytes 6815744 | tf_op jit(solution)/shard_map/select/pallas_call | solution.py:200
  164.5 2.1 collective-permute-start.4
  166.6 1.9 collective-permute-start.5
  168.5 0.0 collective-permute-done.1.refs_1_.refs_5_
  168.5 0.0 copy-start.2
  168.5 3.9 %collective-permute-start.6 = (bf16[144,2176]{1,0:T(8,128)(2,1)}, bf16[144,2176]{1,0:T(8,128)(2,1)S(1)}, u32[]{:S(2)}, u32[]{:S(2)}) collective-permute-start(bf16[144,2176]{1,0:T(8,128)(2,1)} %get-tuple-element.46), channel_id=1, source_target_pairs={{0,3},{1,2},{2,1},{3,0},{4,7},{5,6},{6,5},{7,4},{8,11},{9,10},{10,... | collective-permute-start | bytes 1880072 | tf_op jit(solution)/shard_map/ppermute | solution.py:49
  172.4 0.0 collective-permute-done.2.refs_2_.refs_6_
  172.4 0.0 copy-done.8
  172.4 0.0 copy-start.3
  172.4 7.5 %collective-permute-start.7 = (bf16[2,80,768]{2,1,0:T(8,128)(2,1)S(1)}, bf16[2,80,768]{2,1,0:T(8,128)(2,1)}, u32[]{:S(2)}, u32[]{:S(2)}) collective-permute-start(bf16[2,80,768]{2,1,0:T(8,128)(2,1)S(1)} %copy-done.8), channel_id=1, source_target_pairs={{0,32},{4,36},{8,40},{12,44},{16,48},{20,52},{24,56},{28,60},{32,0... | collective-permute-start | bytes 737288 | tf_op jit(solution)/shard_map/ppermute | solution.py:38
  179.9 4.2 %collective-permute-done.3.refs_3_.refs_7_ = bf16[144,2176]{1,0:T(8,128)(2,1)S(1)} collective-permute-done((bf16[144,2176]{1,0:T(8,128)(2,1)}, bf16[144,2176]{1,0:T(8,128)(2,1)S(1)}, u32[]{:S(2)}, u32[]{:S(2)}) %collective-permute-start.3) | collective-permute-done | bytes 626720 | tf_op jit(solution)/shard_map/ppermute | solution.py:49
  184.1 0.0 copy-start.4
  184.1 0.0 copy-done.2
  184.1 0.0 copy-done.3
  184.1 0.8 copy-done.4
  185.0 5.9 %slopes.2.refs_8_ = bf16[768,576]{1,0:T(8,128)(2,1)} custom-call(bf16[144,2176]{1,0:T(8,128)(2,1)} %get-tuple-element.37.refs_0_.refs_4_, bf16[144,2176]{1,0:T(8,128)(2,1)} %copy-done.2, bf16[144,2176]{1,0:T(8,128)(2,1)} %copy-done.3, bf16[144,2176]{1,0:T(8,128)(2,1)} %copy-done.4, bf16[144,2176]{1,0:T(8,128)(2,1)} %get-tuple-element.37.refs_0_.refs_4_, ...), custom_call_target="tpu_custom_call" | custom-call | flops 1811939328 | bytes 6389760 | tf_op jit(solution)/shard_map/slopes/pallas_call | solution.py:248
  190.8 0.0 collective-permute-done.4.refs_1_.refs_5_
  190.8 0.0 copy-start.5
  190.9 6.2 %collective-permute-done.5.refs_2_.refs_6_ = bf16[144,2176]{1,0:T(8,128)(2,1)S(1)} collective-permute-done((bf16[144,2176]{1,0:T(8,128)(2,1)}, bf16[144,2176]{1,0:T(8,128)(2,1)S(1)}, u32[]{:S(2)}, u32[]{:S(2)}) %collective-permute-start.5) | collective-permute-done | bytes 626720 | tf_op jit(solution)/shard_map/ppermute | solution.py:49
  197.0 0.0 copy-start.6
  197.0 13.5 %collective-permute-done.6.refs_3_.refs_7_ = bf16[144,2176]{1,0:T(8,128)(2,1)S(1)} collective-permute-done((bf16[144,2176]{1,0:T(8,128)(2,1)}, bf16[144,2176]{1,0:T(8,128)(2,1)S(1)}, u32[]{:S(2)}, u32[]{:S(2)}) %collective-permute-start.6) | collective-permute-done | bytes 626720 | tf_op jit(solution)/shard_map/ppermute | solution.py:49
  210.5 0.0 copy-start.7
  210.5 0.0 copy-done.5
  210.5 0.0 copy-done.6
  210.5 0.9 copy-done.7
  211.4 5.9 %slopes.3.refs_9_ = bf16[768,576]{1,0:T(8,128)(2,1)} custom-call(bf16[144,2176]{1,0:T(8,128)(2,1)} %get-tuple-element.47.refs_0_.refs_4_, bf16[144,2176]{1,0:T(8,128)(2,1)} %copy-done.5, bf16[144,2176]{1,0:T(8,128)(2,1)} %copy-done.6, bf16[144,2176]{1,0:T(8,128)(2,1)} %copy-done.7, bf16[144,2176]{1,0:T(8,128)(2,1)} %get-tuple-element.47.refs_0_.refs_4_, ...), custom_call_target="tpu_custom_call" | custom-call | flops 1811939328 | bytes 6389760 | tf_op jit(solution)/shard_map/slopes/pallas_call | solution.py:248
  217.3 8.1 %gradient.1 = bf16[8,768,256]{2,1,0:T(8,128)(2,1)} custom-call(bf16[144,2176]{1,0:T(8,128)(2,1)} %get-tuple-element.37.refs_0_.refs_4_, bf16[144,2176]{1,0:T(8,128)(2,1)} %copy-done.2, bf16[144,2176]{1,0:T(8,128)(2,1)} %copy-done.3, bf16[144,2176]{1,0:T(8,128)(2,1)} %copy-done.4, bf16[144,2176]{1,0:T(8,128)(2,1)} %get-tuple-element.47.refs_0_.refs_4_, ...), custom_call_target="tpu_custom_call" | custom-call | flops 3623878656 | bytes 9633792 | tf_op jit(solution)/shard_map/gradient/pallas_call | solution.py:281
  225.5 0.0 collective-permute-done.7.far_a
  225.5 6.7 %all-to-all-start.1 = ((bf16[8,768,256]{2,1,0:T(8,128)(2,1)}), bf16[8,768,256]{2,1,0:T(8,128)(2,1)S(1)}, u32[]{:S(2)}, u32[]{:S(2)}) async-start(bf16[8,768,256]{2,1,0:T(8,128)(2,1)} %gradient.1), calls=%async_computation.1 | async-start | bytes 6291456 | tf_op jit(solution)/shard_map/all_to_all | solution.py:347
  232.1 7.4 %collective-permute-start.8 = (bf16[2,176,768]{2,1,0:T(8,128)(2,1)}, bf16[2,176,768]{2,1,0:T(8,128)(2,1)}, u32[]{:S(2)}, u32[]{:S(2)}) collective-permute-start(bf16[2,176,768]{2,1,0:T(8,128)(2,1)} %get-tuple-element.56), channel_id=1, source_target_pairs={{0,32},{4,36},{8,40},{12,44},{16,48},{20,52},{24,56},{28,60},{32,0... | collective-permute-start | bytes 1622024 | tf_op jit(solution)/shard_map/ppermute | solution.py:38
  239.6 52.4 %collective-permute-done.8.far_b = bf16[2,176,768]{2,1,0:T(8,128)(2,1)} collective-permute-done((bf16[2,176,768]{2,1,0:T(8,128)(2,1)}, bf16[2,176,768]{2,1,0:T(8,128)(2,1)}, u32[]{:S(2)}, u32[]{:S(2)}) %collective-permute-start.8) | collective-permute-done | bytes 540704 | tf_op jit(solution)/shard_map/ppermute | solution.py:38
  292.0 0.0 all-to-all-done.1.parts_ref
  292.0 0.0 copy-start.1
  292.0 1.6 copy-done.1
  293.6 4.8 %adam.1 = (bf16[256,768]{1,0:T(8,128)(2,1)}, f32[256,768]{1,0:T(8,128)}, f32[256,768]{1,0:T(8,128)}) custom-call(s32[1]{0:T(128)} %get-tuple-element.61.flag_ref, bf16[8,768,256]{2,1,0:T(8,128)(2,1)} %copy-done.1, bf16[256,768]{1,0:T(8,128)(2,1)S(1)} %get-tuple-element.64.weight_ref, f32[256,768]{1,0:T(8,128)} %bitcast.26, f32[256,768]{1,0:T(8,128)} %bitcast.28, ...), custom_call_target="tpu_custom_call" | custom-call | flops 5898240 | bytes 7864320 | tf_op jit(solution)/shard_map/adam/pallas_call | solution.py:112
  (2 shorter events, 0.0 us)
Async XLA Ops:
  7.2 136.3 %all-gather.3.cloned.1.call-start = ((), (), s32[]{:S(2)}) async-start(), calls=%async_computation.2 | async-start | bytes 9469952 | tf_op jit(solution)/shard_map/all_gather | solution.py:318
  15.5 30.9 %all-to-all-start = ((bf16[8,256,768]{2,1,0:T(8,128)(2,1)}), bf16[8,256,768]{2,1,0:T(8,128)(2,1)S(1)}, u32[]{:S(2)}, u32[]{:S(2)}) async-start(bf16[8,256,768]{2,1,0:T(8,128)(2,1)} %broadcast_in_dim.16), calls=%async_computation | async-start | bytes 6291456 | tf_op jit(solution)/shard_map/all_to_all | solution.py:321
  46.4 103.6 %copy-start = (bf16[8,256,768]{2,1,0:T(8,128)(2,1)}, bf16[8,256,768]{2,1,0:T(8,128)(2,1)S(1)}, u32[]{:S(2)}) copy-start(bf16[8,256,768]{2,1,0:T(8,128)(2,1)S(1)} %all-to-all-done) | copy-start | bytes 9437188
  149.9 18.6 %collective-permute-start.1 = (bf16[144,2176]{1,0:T(8,128)(2,1)}, bf16[144,2176]{1,0:T(8,128)(2,1)S(1)}, u32[]{:S(2)}, u32[]{:S(2)}) collective-permute-start(bf16[144,2176]{1,0:T(8,128)(2,1)} %get-tuple-element.38), channel_id=1, source_target_pairs={{0,1},{1,0},{2,3},{3,2},{4,5},{5,4},{6,7},{7,6},{8,9},{9,8},{10,11... | collective-permute-start | bytes 1880072 | tf_op jit(solution)/shard_map/ppermute | solution.py:49
  152.3 20.1 %collective-permute-start.2 = (bf16[144,2176]{1,0:T(8,128)(2,1)}, bf16[144,2176]{1,0:T(8,128)(2,1)S(1)}, u32[]{:S(2)}, u32[]{:S(2)}) collective-permute-start(bf16[144,2176]{1,0:T(8,128)(2,1)} %get-tuple-element.39), channel_id=1, source_target_pairs={{0,2},{1,3},{2,0},{3,1},{4,6},{5,7},{6,4},{7,5},{8,10},{9,11},{10,... | collective-permute-start | bytes 1880072 | tf_op jit(solution)/shard_map/ppermute | solution.py:49
  154.2 18.2 %copy-start.8 = (bf16[2,80,768]{2,1,0:T(8,128)(2,1)S(1)}, bf16[2,80,768]{2,1,0:T(8,128)(2,1)}, u32[]{:S(2)}) copy-start(bf16[2,80,768]{2,1,0:T(8,128)(2,1)} %get-tuple-element.52) | copy-start | bytes 737284
  154.2 29.9 %collective-permute-start.3 = (bf16[144,2176]{1,0:T(8,128)(2,1)}, bf16[144,2176]{1,0:T(8,128)(2,1)S(1)}, u32[]{:S(2)}, u32[]{:S(2)}) collective-permute-start(bf16[144,2176]{1,0:T(8,128)(2,1)} %get-tuple-element.40), channel_id=1, source_target_pairs={{0,3},{1,2},{2,1},{3,0},{4,7},{5,6},{6,5},{7,4},{8,11},{9,10},{10,... | collective-permute-start | bytes 1880072 | tf_op jit(solution)/shard_map/ppermute | solution.py:49
  164.5 26.3 %collective-permute-start.4 = (bf16[144,2176]{1,0:T(8,128)(2,1)}, bf16[144,2176]{1,0:T(8,128)(2,1)S(1)}, u32[]{:S(2)}, u32[]{:S(2)}) collective-permute-start(bf16[144,2176]{1,0:T(8,128)(2,1)} %get-tuple-element.44), channel_id=1, source_target_pairs={{0,1},{1,0},{2,3},{3,2},{4,5},{5,4},{6,7},{7,6},{8,9},{9,8},{10,11... | collective-permute-start | bytes 1880072 | tf_op jit(solution)/shard_map/ppermute | solution.py:49
  166.6 30.5 %collective-permute-start.5 = (bf16[144,2176]{1,0:T(8,128)(2,1)}, bf16[144,2176]{1,0:T(8,128)(2,1)S(1)}, u32[]{:S(2)}, u32[]{:S(2)}) collective-permute-start(bf16[144,2176]{1,0:T(8,128)(2,1)} %get-tuple-element.45), channel_id=1, source_target_pairs={{0,2},{1,3},{2,0},{3,1},{4,6},{5,7},{6,4},{7,5},{8,10},{9,11},{10,... | collective-permute-start | bytes 1880072 | tf_op jit(solution)/shard_map/ppermute | solution.py:49
  168.5 15.6 %copy-start.2 = (bf16[144,2176]{1,0:T(8,128)(2,1)}, bf16[144,2176]{1,0:T(8,128)(2,1)S(1)}, u32[]{:S(2)}) copy-start(bf16[144,2176]{1,0:T(8,128)(2,1)S(1)} %collective-permute-done.1.refs_1_.refs_5_) | copy-start | bytes 1880068
  168.5 42.0 %collective-permute-start.6 = (bf16[144,2176]{1,0:T(8,128)(2,1)}, bf16[144,2176]{1,0:T(8,128)(2,1)S(1)}, u32[]{:S(2)}, u32[]{:S(2)}) collective-permute-start(bf16[144,2176]{1,0:T(8,128)(2,1)} %get-tuple-element.46), channel_id=1, source_target_pairs={{0,3},{1,2},{2,1},{3,0},{4,7},{5,6},{6,5},{7,4},{8,11},{9,10},{10,... | collective-permute-start | bytes 1880072 | tf_op jit(solution)/shard_map/ppermute | solution.py:49
  172.4 11.7 %copy-start.3 = (bf16[144,2176]{1,0:T(8,128)(2,1)}, bf16[144,2176]{1,0:T(8,128)(2,1)S(1)}, u32[]{:S(2)}) copy-start(bf16[144,2176]{1,0:T(8,128)(2,1)S(1)} %collective-permute-done.2.refs_2_.refs_6_) | copy-start | bytes 1880068
  172.4 53.0 %collective-permute-start.7 = (bf16[2,80,768]{2,1,0:T(8,128)(2,1)S(1)}, bf16[2,80,768]{2,1,0:T(8,128)(2,1)}, u32[]{:S(2)}, u32[]{:S(2)}) collective-permute-start(bf16[2,80,768]{2,1,0:T(8,128)(2,1)S(1)} %copy-done.8), channel_id=1, source_target_pairs={{0,32},{4,36},{8,40},{12,44},{16,48},{20,52},{24,56},{28,60},{32,0... | collective-permute-start | bytes 737288 | tf_op jit(solution)/shard_map/ppermute | solution.py:38
  184.1 0.8 copy-start.4
  190.8 19.7 %copy-start.5 = (bf16[144,2176]{1,0:T(8,128)(2,1)}, bf16[144,2176]{1,0:T(8,128)(2,1)S(1)}, u32[]{:S(2)}) copy-start(bf16[144,2176]{1,0:T(8,128)(2,1)S(1)} %collective-permute-done.4.refs_1_.refs_5_) | copy-start | bytes 1880068
  197.0 13.5 %copy-start.6 = (bf16[144,2176]{1,0:T(8,128)(2,1)}, bf16[144,2176]{1,0:T(8,128)(2,1)S(1)}, u32[]{:S(2)}) copy-start(bf16[144,2176]{1,0:T(8,128)(2,1)S(1)} %collective-permute-done.5.refs_2_.refs_6_) | copy-start | bytes 1880068
  210.5 0.9 copy-start.7
  225.5 66.5 %all-to-all-start.1 = ((bf16[8,768,256]{2,1,0:T(8,128)(2,1)}), bf16[8,768,256]{2,1,0:T(8,128)(2,1)S(1)}, u32[]{:S(2)}, u32[]{:S(2)}) async-start(bf16[8,768,256]{2,1,0:T(8,128)(2,1)} %gradient.1), calls=%async_computation.1 | async-start | bytes 6291456 | tf_op jit(solution)/shard_map/all_to_all | solution.py:347
  232.1 59.9 %collective-permute-start.8 = (bf16[2,176,768]{2,1,0:T(8,128)(2,1)}, bf16[2,176,768]{2,1,0:T(8,128)(2,1)}, u32[]{:S(2)}, u32[]{:S(2)}) collective-permute-start(bf16[2,176,768]{2,1,0:T(8,128)(2,1)} %get-tuple-element.56), channel_id=1, source_target_pairs={{0,32},{4,36},{8,40},{12,44},{16,48},{20,52},{24,56},{28,60},{32,0... | collective-permute-start | bytes 1622024 | tf_op jit(solution)/shard_map/ppermute | solution.py:38
  292.0 1.6 copy-start.1
Sparse Core Ops, SparseCore 0:
  11.6 131.7 all-gather.2

commit v7 on v6

--- a/solution.py
+++ b/solution.py
@@ -26,7 +26,7 @@
 TILE = 512
 PICK_TILE = 1024
 INV_ROOT = 1.0 / math.sqrt(D)
-AHEAD = 5 * SHARD // 16
+AHEAD = SHARD // 2
 VMEM_LIMIT = 56 * 1024 * 1024
 
 
@@ -87,10 +87,7 @@
         total = total + parts_ref[i].astype(jnp.float32)
     gradient = total.T
     swapped = flag_ref[0] == 1
-    rest = gradient.shape[0] - far_a.shape[1]
-    low = jnp.concatenate([far_a[...], far_b[:, :rest]], axis=1).astype(jnp.float32)
-    high = far_b[:, rest:].astype(jnp.float32)
-    far = jnp.where(pl.program_id(0) == 0, low, high)
+    far = jnp.where(pl.program_id(0) == 0, far_a[...], far_b[...]).astype(jnp.float32)
     first_now = jnp.where(swapped, far[0], one_ref[...])
     second_now = jnp.where(swapped, far[1], two_ref[...])
     first = beta_one * first_now + (1.0 - beta_one) * gradient

time: 306 us -> 293 us (0.958)
  waiting for transfers between devices: 190 us -> 173 us
  starting transfers between devices: 44.9 us -> 48.2 us
    ppermute x2, waiting for transfers between devices: 52.5 us -> 38.2 us  [shift_z(): lax.ppermute(block, 'z', [(i, (i + distance) % NZ) for i in range(NZ)])]
    ppermute x2, starting transfers between devices: 14.9 us -> 18.2 us  [shift_z(): lax.ppermute(block, 'z', [(i, (i + distance) % NZ) for i in range(NZ)])]
  transfers between devices with their start and end apart: 11 -> 11, of which waited for: 6 -> 6; matrix products, arithmetic and copies ran while one was open for 2% -> 2% of each run, Pallas kernels for 9% -> 10%
where the time goes in v7:
time: 293 us; the launch traced here: 291 us
  waiting for transfers between devices  173 us (59%)
  starting transfers between devices  48.2 us (16%)
  Pallas kernels  39.8 us (14%)
  between operations  17.5 us (6%)
  local copies, waits for them, and re-layouts  7.69 us (3%)
  other arithmetic  5.2 us (2%)
    all_gather x1, waiting for transfers between devices, body(): tokens = lax.all_gather(block, 'z', axis=0, tiled=False)  95.4 us
    ppermute x2, waiting for transfers between devices, shift_z(): lax.ppermute(block, 'z', [(i, (i + distance) % NZ) for i in range(NZ)])  38.2 us
    ppermute x6, waiting for transfers between devices, swap_xc(): return lax.ppermute(block, ('x', 'c'), pairs)  22.6 us
    ppermute x2, starting transfers between devices, shift_z(): lax.ppermute(block, 'z', [(i, (i + distance) % NZ) for i in range(NZ)])  18.2 us
    all_to_all x1, waiting for transfers between devices, body(): lax.all_to_all(jnp.broadcast_to(weight_now[None], (NY * NH, SHARD, FF)),...  16.6 us
    ppermute x6, starting transfers between devices, swap_xc(): return lax.ppermute(block, ('x', 'c'), pairs)  15.8 us
    pallas_call x2, Pallas kernels, select(): pl.pallas_call(select_kernel, out_shape=[jax.ShapeDtypeStruct((rows, WIDE...  13 us
    pallas_call x2, Pallas kernels, slopes_of(): pl.pallas_call(functools.partial(slopes_kernel, len(pieces)), out_shape=j...  11.8 us
  transfers between devices with their start and end apart: 11, of which 6 were waited for; matrix products, arithmetic and copies ran while one was open for 2% of the time, Pallas kernels for 10%

profile of v7, /device:TPU:1, one launch (start us, length us, event | category | flops | bytes accessed | tf_op | source)
XLA Modules:
  0.0 291.3 jit_solution(8895888596673111277)
XLA Ops:
  7.2 0.0 all-gather.3.cloned.1.call-start
  7.2 1.0 copy.15
  8.2 0.7 convert_bitcast_fusion
  8.9 0.7 fusion.3
  9.6 1.9 pad_maximum_fusion
  11.5 0.0 all-gather.3.cloned.1.call-update
  11.5 1.5 fusion.4
  13.7 1.8 broadcast_in_dim.16
  15.5 7.5 %all-to-all-start = ((bf16[8,256,768]{2,1,0:T(8,128)(2,1)}), bf16[8,256,768]{2,1,0:T(8,128)(2,1)S(1)}, u32[]{:S(2)}, u32[]{:S(2)}) async-start(bf16[8,256,768]{2,1,0:T(8,128)(2,1)} %broadcast_in_dim.16), calls=%async_computation | async-start | bytes 6291456 | tf_op jit(solution)/shard_map/all_to_all | solution.py:318
  23.0 2.2 cast.1
  27.8 0.6 pad_add_fusion.home_ref
  28.4 1.3 dynamic-slice_convert_fusion.refs_9_
  29.7 16.6 %all-to-all-done = bf16[8,256,768]{2,1,0:T(8,128)(2,1)S(1)} async-done(((bf16[8,256,768]{2,1,0:T(8,128)(2,1)}), bf16[8,256,768]{2,1,0:T(8,128)(2,1)S(1)}, u32[]{:S(2)}, u32[]{:S(2)}) %all-to-all-start) | async-done | bytes 3145760 | tf_op jit(solution)/shard_map/all_to_all | solution.py:318
  46.4 0.0 copy-start
  46.4 95.4 %all-gather.3.cloned.1.call-done = bf16[2176,2048]{1,0:T(8,128)(2,1)} async-done(((bf16[136,2048]{1,0:T(8,128)(2,1)}), bf16[2176,2048]{1,0:T(8,128)(2,1)}) %all-gather.3.cloned.1.call-update) | async-done | bytes 8912912 | tf_op jit(solution)/shard_map/all_gather | solution.py:315
  141.8 6.5 %select.19 = (bf16[144,2176]{1,0:T(8,128)(2,1)}, bf16[144,2176]{1,0:T(8,128)(2,1)}, bf16[144,2176]{1,0:T(8,128)(2,1)}, bf16[144,2176]{1,0:T(8,128)(2,1)}) custom-call(s32[4]{0:T(128)} %pad_add_fusion.home_ref, bf16[16,136,2048]{2,1,0:T(8,128)(2,1)} %bitcast.29), custom_call_target="tpu_custom_call" | custom-call | flops 2415919104 | bytes 6815744 | tf_op jit(solution)/shard_map/select/pallas_call | solution.py:197
  148.3 0.0 copy-done
  148.3 2.4 collective-permute-start.1
  150.6 1.9 collective-permute-start.2
  152.6 0.0 copy-start.8
  152.6 3.7 %collective-permute-start.3 = (bf16[144,2176]{1,0:T(8,128)(2,1)}, bf16[144,2176]{1,0:T(8,128)(2,1)S(1)}, u32[]{:S(2)}, u32[]{:S(2)}) collective-permute-start(bf16[144,2176]{1,0:T(8,128)(2,1)} %get-tuple-element.40), channel_id=1, source_target_pairs={{0,3},{1,2},{2,1},{3,0},{4,7},{5,6},{6,5},{7,4},{8,11},{9,10},{10,... | collective-permute-start | bytes 1880072 | tf_op jit(solution)/shard_map/ppermute | solution.py:49
  156.3 6.5 %select.20 = (bf16[144,2176]{1,0:T(8,128)(2,1)}, bf16[144,2176]{1,0:T(8,128)(2,1)}, bf16[144,2176]{1,0:T(8,128)(2,1)}, bf16[144,2176]{1,0:T(8,128)(2,1)}) custom-call(s32[4]{0:T(128)} %pad_add_fusion.home_ref, bf16[16,136,2048]{2,1,0:T(8,128)(2,1)} %bitcast.30), custom_call_target="tpu_custom_call" | custom-call | flops 2415919104 | bytes 6815744 | tf_op jit(solution)/shard_map/select/pallas_call | solution.py:197
  162.8 2.1 collective-permute-start.4
  164.9 1.9 collective-permute-start.5
  166.8 0.0 collective-permute-done.1.refs_1_.refs_5_
  166.8 0.0 copy-start.2
  166.9 3.9 %collective-permute-start.6 = (bf16[144,2176]{1,0:T(8,128)(2,1)}, bf16[144,2176]{1,0:T(8,128)(2,1)S(1)}, u32[]{:S(2)}, u32[]{:S(2)}) collective-permute-start(bf16[144,2176]{1,0:T(8,128)(2,1)} %get-tuple-element.46), channel_id=1, source_target_pairs={{0,3},{1,2},{2,1},{3,0},{4,7},{5,6},{6,5},{7,4},{8,11},{9,10},{10,... | collective-permute-start | bytes 1880072 | tf_op jit(solution)/shard_map/ppermute | solution.py:49
  170.7 0.0 collective-permute-done.2.refs_2_.refs_6_
  170.7 0.0 copy-done.8
  170.8 0.0 copy-start.3
  170.8 9.1 %collective-permute-start.7 = (bf16[2,128,768]{2,1,0:T(8,128)(2,1)S(1)}, bf16[2,128,768]{2,1,0:T(8,128)(2,1)}, u32[]{:S(2)}, u32[]{:S(2)}) collective-permute-start(bf16[2,128,768]{2,1,0:T(8,128)(2,1)S(1)} %copy-done.8), channel_id=1, source_target_pairs={{0,32},{4,36},{8,40},{12,44},{16,48},{20,52},{24,56},{28,60},{32,0... | collective-permute-start | bytes 1179656 | tf_op jit(solution)/shard_map/ppermute | solution.py:38
  179.9 2.5 collective-permute-done.3.refs_3_.refs_7_
  182.4 0.0 copy-start.4
  182.4 0.0 copy-done.2
  182.4 0.0 copy-done.3
  182.4 0.8 copy-done.4
  183.3 5.9 %slopes.2.refs_8_ = bf16[768,576]{1,0:T(8,128)(2,1)} custom-call(bf16[144,2176]{1,0:T(8,128)(2,1)} %get-tuple-element.37.refs_0_.refs_4_, bf16[144,2176]{1,0:T(8,128)(2,1)} %copy-done.2, bf16[144,2176]{1,0:T(8,128)(2,1)} %copy-done.3, bf16[144,2176]{1,0:T(8,128)(2,1)} %copy-done.4, bf16[144,2176]{1,0:T(8,128)(2,1)} %get-tuple-element.37.refs_0_.refs_4_, ...), custom_call_target="tpu_custom_call" | custom-call | flops 1811939328 | bytes 6389760 | tf_op jit(solution)/shard_map/slopes/pallas_call | solution.py:245
  189.2 0.0 collective-permute-done.4.refs_1_.refs_5_
  189.2 0.0 copy-start.5
  189.2 6.2 %collective-permute-done.5.refs_2_.refs_6_ = bf16[144,2176]{1,0:T(8,128)(2,1)S(1)} collective-permute-done((bf16[144,2176]{1,0:T(8,128)(2,1)}, bf16[144,2176]{1,0:T(8,128)(2,1)S(1)}, u32[]{:S(2)}, u32[]{:S(2)}) %collective-permute-start.5) | collective-permute-done | bytes 626720 | tf_op jit(solution)/shard_map/ppermute | solution.py:49
  195.4 0.0 copy-start.6
  195.4 13.9 %collective-permute-done.6.refs_3_.refs_7_ = bf16[144,2176]{1,0:T(8,128)(2,1)S(1)} collective-permute-done((bf16[144,2176]{1,0:T(8,128)(2,1)}, bf16[144,2176]{1,0:T(8,128)(2,1)S(1)}, u32[]{:S(2)}, u32[]{:S(2)}) %collective-permute-start.6) | collective-permute-done | bytes 626720 | tf_op jit(solution)/shard_map/ppermute | solution.py:49
  209.3 0.0 copy-start.7
  209.3 0.0 copy-done.5
  209.3 0.0 copy-done.6
  209.3 0.9 copy-done.7
  210.1 5.9 %slopes.3.refs_9_ = bf16[768,576]{1,0:T(8,128)(2,1)} custom-call(bf16[144,2176]{1,0:T(8,128)(2,1)} %get-tuple-element.47.refs_0_.refs_4_, bf16[144,2176]{1,0:T(8,128)(2,1)} %copy-done.5, bf16[144,2176]{1,0:T(8,128)(2,1)} %copy-done.6, bf16[144,2176]{1,0:T(8,128)(2,1)} %copy-done.7, bf16[144,2176]{1,0:T(8,128)(2,1)} %get-tuple-element.47.refs_0_.refs_4_, ...), custom_call_target="tpu_custom_call" | custom-call | flops 1811939328 | bytes 6389760 | tf_op jit(solution)/shard_map/slopes/pallas_call | solution.py:245
  216.1 8.1 %gradient.1 = bf16[8,768,256]{2,1,0:T(8,128)(2,1)} custom-call(bf16[144,2176]{1,0:T(8,128)(2,1)} %get-tuple-element.37.refs_0_.refs_4_, bf16[144,2176]{1,0:T(8,128)(2,1)} %copy-done.2, bf16[144,2176]{1,0:T(8,128)(2,1)} %copy-done.3, bf16[144,2176]{1,0:T(8,128)(2,1)} %copy-done.4, bf16[144,2176]{1,0:T(8,128)(2,1)} %get-tuple-element.47.refs_0_.refs_4_, ...), custom_call_target="tpu_custom_call" | custom-call | flops 3623878656 | bytes 9633792 | tf_op jit(solution)/shard_map/gradient/pallas_call | solution.py:278
  224.2 0.0 collective-permute-done.7.far_a
  224.2 6.7 %all-to-all-start.1 = ((bf16[8,768,256]{2,1,0:T(8,128)(2,1)}), bf16[8,768,256]{2,1,0:T(8,128)(2,1)S(1)}, u32[]{:S(2)}, u32[]{:S(2)}) async-start(bf16[8,768,256]{2,1,0:T(8,128)(2,1)} %gradient.1), calls=%async_computation.1 | async-start | bytes 6291456 | tf_op jit(solution)/shard_map/all_to_all | solution.py:344
  230.9 9.1 %collective-permute-start.8 = (bf16[2,128,768]{2,1,0:T(8,128)(2,1)}, bf16[2,128,768]{2,1,0:T(8,128)(2,1)}, u32[]{:S(2)}, u32[]{:S(2)}) collective-permute-start(bf16[2,128,768]{2,1,0:T(8,128)(2,1)} %get-tuple-element.56), channel_id=1, source_target_pairs={{0,32},{4,36},{8,40},{12,44},{16,48},{20,52},{24,56},{28,60},{32,0... | collective-permute-start | bytes 1179656 | tf_op jit(solution)/shard_map/ppermute | solution.py:38
  240.0 38.2 %collective-permute-done.8.far_b = bf16[2,128,768]{2,1,0:T(8,128)(2,1)} collective-permute-done((bf16[2,128,768]{2,1,0:T(8,128)(2,1)}, bf16[2,128,768]{2,1,0:T(8,128)(2,1)}, u32[]{:S(2)}, u32[]{:S(2)}) %collective-permute-start.8) | collective-permute-done | bytes 393248 | tf_op jit(solution)/shard_map/ppermute | solution.py:38
  278.2 0.0 all-to-all-done.1.parts_ref
  278.2 0.0 copy-start.1
  278.2 1.6 copy-done.1
  279.8 4.7 %adam.1 = (bf16[256,768]{1,0:T(8,128)(2,1)}, f32[256,768]{1,0:T(8,128)}, f32[256,768]{1,0:T(8,128)}) custom-call(s32[1]{0:T(128)} %get-tuple-element.61.flag_ref, bf16[8,768,256]{2,1,0:T(8,128)(2,1)} %copy-done.1, bf16[256,768]{1,0:T(8,128)(2,1)S(1)} %get-tuple-element.64.weight_ref, f32[256,768]{1,0:T(8,128)} %bitcast.26, f32[256,768]{1,0:T(8,128)} %bitcast.28, ...), custom_call_target="tpu_custom_call" | custom-call | flops 5898240 | bytes 7864320 | tf_op jit(solution)/shard_map/adam/pallas_call | solution.py:109
  (2 shorter events, 0.0 us)
Async XLA Ops:
  7.2 134.6 %all-gather.3.cloned.1.call-start = ((), (), s32[]{:S(2)}) async-start(), calls=%async_computation.2 | async-start | bytes 9469952 | tf_op jit(solution)/shard_map/all_gather | solution.py:315
  15.5 30.9 %all-to-all-start = ((bf16[8,256,768]{2,1,0:T(8,128)(2,1)}), bf16[8,256,768]{2,1,0:T(8,128)(2,1)S(1)}, u32[]{:S(2)}, u32[]{:S(2)}) async-start(bf16[8,256,768]{2,1,0:T(8,128)(2,1)} %broadcast_in_dim.16), calls=%async_computation | async-start | bytes 6291456 | tf_op jit(solution)/shard_map/all_to_all | solution.py:318
  46.4 101.9 %copy-start = (bf16[8,256,768]{2,1,0:T(8,128)(2,1)}, bf16[8,256,768]{2,1,0:T(8,128)(2,1)S(1)}, u32[]{:S(2)}) copy-start(bf16[8,256,768]{2,1,0:T(8,128)(2,1)S(1)} %all-to-all-done) | copy-start | bytes 9437188
  148.3 18.6 %collective-permute-start.1 = (bf16[144,2176]{1,0:T(8,128)(2,1)}, bf16[144,2176]{1,0:T(8,128)(2,1)S(1)}, u32[]{:S(2)}, u32[]{:S(2)}) collective-permute-start(bf16[144,2176]{1,0:T(8,128)(2,1)} %get-tuple-element.38), channel_id=1, source_target_pairs={{0,1},{1,0},{2,3},{3,2},{4,5},{5,4},{6,7},{7,6},{8,9},{9,8},{10,11... | collective-permute-start | bytes 1880072 | tf_op jit(solution)/shard_map/ppermute | solution.py:49
  150.6 20.1 %collective-permute-start.2 = (bf16[144,2176]{1,0:T(8,128)(2,1)}, bf16[144,2176]{1,0:T(8,128)(2,1)S(1)}, u32[]{:S(2)}, u32[]{:S(2)}) collective-permute-start(bf16[144,2176]{1,0:T(8,128)(2,1)} %get-tuple-element.39), channel_id=1, source_target_pairs={{0,2},{1,3},{2,0},{3,1},{4,6},{5,7},{6,4},{7,5},{8,10},{9,11},{10,... | collective-permute-start | bytes 1880072 | tf_op jit(solution)/shard_map/ppermute | solution.py:49
  152.6 18.2 %copy-start.8 = (bf16[2,128,768]{2,1,0:T(8,128)(2,1)S(1)}, bf16[2,128,768]{2,1,0:T(8,128)(2,1)}, u32[]{:S(2)}) copy-start(bf16[2,128,768]{2,1,0:T(8,128)(2,1)} %get-tuple-element.52) | copy-start | bytes 1179652
  152.6 29.9 %collective-permute-start.3 = (bf16[144,2176]{1,0:T(8,128)(2,1)}, bf16[144,2176]{1,0:T(8,128)(2,1)S(1)}, u32[]{:S(2)}, u32[]{:S(2)}) collective-permute-start(bf16[144,2176]{1,0:T(8,128)(2,1)} %get-tuple-element.40), channel_id=1, source_target_pairs={{0,3},{1,2},{2,1},{3,0},{4,7},{5,6},{6,5},{7,4},{8,11},{9,10},{10,... | collective-permute-start | bytes 1880072 | tf_op jit(solution)/shard_map/ppermute | solution.py:49
  162.8 26.3 %collective-permute-start.4 = (bf16[144,2176]{1,0:T(8,128)(2,1)}, bf16[144,2176]{1,0:T(8,128)(2,1)S(1)}, u32[]{:S(2)}, u32[]{:S(2)}) collective-permute-start(bf16[144,2176]{1,0:T(8,128)(2,1)} %get-tuple-element.44), channel_id=1, source_target_pairs={{0,1},{1,0},{2,3},{3,2},{4,5},{5,4},{6,7},{7,6},{8,9},{9,8},{10,11... | collective-permute-start | bytes 1880072 | tf_op jit(solution)/shard_map/ppermute | solution.py:49
  164.9 30.5 %collective-permute-start.5 = (bf16[144,2176]{1,0:T(8,128)(2,1)}, bf16[144,2176]{1,0:T(8,128)(2,1)S(1)}, u32[]{:S(2)}, u32[]{:S(2)}) collective-permute-start(bf16[144,2176]{1,0:T(8,128)(2,1)} %get-tuple-element.45), channel_id=1, source_target_pairs={{0,2},{1,3},{2,0},{3,1},{4,6},{5,7},{6,4},{7,5},{8,10},{9,11},{10,... | collective-permute-start | bytes 1880072 | tf_op jit(solution)/shard_map/ppermute | solution.py:49
  166.8 15.6 %copy-start.2 = (bf16[144,2176]{1,0:T(8,128)(2,1)}, bf16[144,2176]{1,0:T(8,128)(2,1)S(1)}, u32[]{:S(2)}) copy-start(bf16[144,2176]{1,0:T(8,128)(2,1)S(1)} %collective-permute-done.1.refs_1_.refs_5_) | copy-start | bytes 1880068
  166.9 42.4 %collective-permute-start.6 = (bf16[144,2176]{1,0:T(8,128)(2,1)}, bf16[144,2176]{1,0:T(8,128)(2,1)S(1)}, u32[]{:S(2)}, u32[]{:S(2)}) collective-permute-start(bf16[144,2176]{1,0:T(8,128)(2,1)} %get-tuple-element.46), channel_id=1, source_target_pairs={{0,3},{1,2},{2,1},{3,0},{4,7},{5,6},{6,5},{7,4},{8,11},{9,10},{10,... | collective-permute-start | bytes 1880072 | tf_op jit(solution)/shard_map/ppermute | solution.py:49
  170.8 11.7 %copy-start.3 = (bf16[144,2176]{1,0:T(8,128)(2,1)}, bf16[144,2176]{1,0:T(8,128)(2,1)S(1)}, u32[]{:S(2)}) copy-start(bf16[144,2176]{1,0:T(8,128)(2,1)S(1)} %collective-permute-done.2.refs_2_.refs_6_) | copy-start | bytes 1880068
  170.8 53.4 %collective-permute-start.7 = (bf16[2,128,768]{2,1,0:T(8,128)(2,1)S(1)}, bf16[2,128,768]{2,1,0:T(8,128)(2,1)}, u32[]{:S(2)}, u32[]{:S(2)}) collective-permute-start(bf16[2,128,768]{2,1,0:T(8,128)(2,1)S(1)} %copy-done.8), channel_id=1, source_target_pairs={{0,32},{4,36},{8,40},{12,44},{16,48},{20,52},{24,56},{28,60},{32,0... | collective-permute-start | bytes 1179656 | tf_op jit(solution)/shard_map/ppermute | solution.py:38
  182.4 0.8 copy-start.4
  189.2 20.1 %copy-start.5 = (bf16[144,2176]{1,0:T(8,128)(2,1)}, bf16[144,2176]{1,0:T(8,128)(2,1)S(1)}, u32[]{:S(2)}) copy-start(bf16[144,2176]{1,0:T(8,128)(2,1)S(1)} %collective-permute-done.4.refs_1_.refs_5_) | copy-start | bytes 1880068
  195.4 13.9 %copy-start.6 = (bf16[144,2176]{1,0:T(8,128)(2,1)}, bf16[144,2176]{1,0:T(8,128)(2,1)S(1)}, u32[]{:S(2)}) copy-start(bf16[144,2176]{1,0:T(8,128)(2,1)S(1)} %collective-permute-done.5.refs_2_.refs_6_) | copy-start | bytes 1880068
  209.3 0.9 copy-start.7
  224.2 54.0 %all-to-all-start.1 = ((bf16[8,768,256]{2,1,0:T(8,128)(2,1)}), bf16[8,768,256]{2,1,0:T(8,128)(2,1)S(1)}, u32[]{:S(2)}, u32[]{:S(2)}) async-start(bf16[8,768,256]{2,1,0:T(8,128)(2,1)} %gradient.1), calls=%async_computation.1 | async-start | bytes 6291456 | tf_op jit(solution)/shard_map/all_to_all | solution.py:344
  230.9 47.3 %collective-permute-start.8 = (bf16[2,128,768]{2,1,0:T(8,128)(2,1)}, bf16[2,128,768]{2,1,0:T(8,128)(2,1)}, u32[]{:S(2)}, u32[]{:S(2)}) collective-permute-start(bf16[2,128,768]{2,1,0:T(8,128)(2,1)} %get-tuple-element.56), channel_id=1, source_target_pairs={{0,32},{4,36},{8,40},{12,44},{16,48},{20,52},{24,56},{28,60},{32,0... | collective-permute-start | bytes 1179656 | tf_op jit(solution)/shard_map/ppermute | solution.py:38
  278.2 1.6 copy-start.1
Sparse Core Ops, SparseCore 0:
  11.6 130.0 all-gather.2

commit v8 on v7

--- a/solution.py
+++ b/solution.py
@@ -26,7 +26,7 @@
 TILE = 512
 PICK_TILE = 1024
 INV_ROOT = 1.0 / math.sqrt(D)
-AHEAD = SHARD // 2
+AHEAD = 9 * SHARD // 16
 VMEM_LIMIT = 56 * 1024 * 1024
 
 
@@ -87,7 +87,9 @@
         total = total + parts_ref[i].astype(jnp.float32)
     gradient = total.T
     swapped = flag_ref[0] == 1
-    far = jnp.where(pl.program_id(0) == 0, far_a[...], far_b[...]).astype(jnp.float32)
+    far = jnp.concatenate([far_a[...], far_b[...]], axis=1)
+    rows = gradient.shape[0]
+    far = jnp.where(pl.program_id(0) == 0, far[:, :rows], far[:, rows:]).astype(jnp.float32)
     first_now = jnp.where(swapped, far[0], one_ref[...])
     second_now = jnp.where(swapped, far[1], two_ref[...])
     first = beta_one * first_now + (1.0 - beta_one) * gradient

time: 293 us -> 294 us (level)
    ppermute x6, starting transfers between devices: 15.8 us -> 30.4 us  [swap_xc(): return lax.ppermute(block, ('x', 'c'), pairs)]
    ppermute x2, starting transfers between devices: 18.2 us -> 3.83 us  [shift_z(): lax.ppermute(block, 'z', [(i, (i + distance) % NZ) for i in range(NZ)])]
    ppermute x6, waiting for transfers between devices: 22.6 us -> 30 us  [swap_xc(): return lax.ppermute(block, ('x', 'c'), pairs)]
    ppermute x2, waiting for transfers between devices: 38.2 us -> 32.3 us  [shift_z(): lax.ppermute(block, 'z', [(i, (i + distance) % NZ) for i in range(NZ)])]
    all_to_all x1, waiting for transfers between devices: 0.01 us -> 5.31 us  [body(): lax.all_to_all(parts, ('y', 'h'), split_axis=0, concat_axis=0, tiled=True)]
    all_gather x1, waiting for transfers between devices: 95.4 us -> 90.5 us  [body(): tokens = lax.all_gather(block, 'z', axis=0, tiled=False)]
  transfers between devices with their start and end apart: 11 -> 11, of which waited for: 6 -> 7; matrix products, arithmetic and copies ran while one was open for 2% -> 2% of each run, Pallas kernels for 10% -> 10%
where the time goes in v8:
time: 294 us; the launch traced here: 293 us
  waiting for transfers between devices  175 us (60%)
  starting transfers between devices  48.1 us (16%)
  Pallas kernels  39.8 us (14%)
  between operations  17.4 us (6%)
  local copies, waits for them, and re-layouts  7.68 us (3%)
  other arithmetic  5.25 us (2%)
    all_gather x1, waiting for transfers between devices, body(): tokens = lax.all_gather(block, 'z', axis=0, tiled=False)  90.5 us
    ppermute x2, waiting for transfers between devices, shift_z(): lax.ppermute(block, 'z', [(i, (i + distance) % NZ) for i in range(NZ)])  32.3 us
    ppermute x6, starting transfers between devices, swap_xc(): return lax.ppermute(block, ('x', 'c'), pairs)  30.4 us
    ppermute x6, waiting for transfers between devices, swap_xc(): return lax.ppermute(block, ('x', 'c'), pairs)  30 us
    all_to_all x1, waiting for transfers between devices, body(): lax.all_to_all(jnp.broadcast_to(weight_now[None], (NY * NH, SHARD, FF)),...  16.7 us
    pallas_call x2, Pallas kernels, select(): pl.pallas_call(select_kernel, out_shape=[jax.ShapeDtypeStruct((rows, WIDE...  13 us
    pallas_call x2, Pallas kernels, slopes_of(): pl.pallas_call(functools.partial(slopes_kernel, len(pieces)), out_shape=j...  11.8 us
    pallas_call x1, Pallas kernels, gradient_parts(): pl.pallas_call(functools.partial(gradient_kernel, len(pieces)), out_shape...  8.13 us
  transfers between devices with their start and end apart: 11, of which 7 were waited for; matrix products, arithmetic and copies ran while one was open for 2% of the time, Pallas kernels for 10%

profile of v8, /device:TPU:1, one launch (start us, length us, event | category | flops | bytes accessed | tf_op | source)
XLA Modules:
  0.0 293.0 jit_solution(12047384512037583336)
XLA Ops:
  7.2 0.0 all-gather.3.cloned.1.call-start
  7.2 1.0 copy.15
  8.2 0.7 convert_bitcast_fusion
  8.9 0.7 fusion.3
  9.6 1.9 pad_maximum_fusion
  11.5 0.0 all-gather.3.cloned.1.call-update
  11.5 1.5 fusion.4
  13.6 1.8 broadcast_in_dim.16
  15.5 7.5 %all-to-all-start = ((bf16[8,256,768]{2,1,0:T(8,128)(2,1)}), bf16[8,256,768]{2,1,0:T(8,128)(2,1)S(1)}, u32[]{:S(2)}, u32[]{:S(2)}) async-start(bf16[8,256,768]{2,1,0:T(8,128)(2,1)} %broadcast_in_dim.16), calls=%async_computation | async-start | bytes 6291456 | tf_op jit(solution)/shard_map/all_to_all | solution.py:320
  23.0 2.1 cast.1
  27.7 0.7 pad_add_fusion.home_ref
  28.4 1.3 dynamic-slice_convert_fusion.refs_9_
  29.7 16.7 %all-to-all-done = bf16[8,256,768]{2,1,0:T(8,128)(2,1)S(1)} async-done(((bf16[8,256,768]{2,1,0:T(8,128)(2,1)}), bf16[8,256,768]{2,1,0:T(8,128)(2,1)S(1)}, u32[]{:S(2)}, u32[]{:S(2)}) %all-to-all-start) | async-done | bytes 3145760 | tf_op jit(solution)/shard_map/all_to_all | solution.py:320
  46.3 0.0 copy-start
  46.3 90.5 %all-gather.3.cloned.1.call-done = bf16[2176,2048]{1,0:T(8,128)(2,1)} async-done(((bf16[136,2048]{1,0:T(8,128)(2,1)}), bf16[2176,2048]{1,0:T(8,128)(2,1)}) %all-gather.3.cloned.1.call-update) | async-done | bytes 8912912 | tf_op jit(solution)/shard_map/all_gather | solution.py:317
  136.9 6.5 %select.19 = (bf16[144,2176]{1,0:T(8,128)(2,1)}, bf16[144,2176]{1,0:T(8,128)(2,1)}, bf16[144,2176]{1,0:T(8,128)(2,1)}, bf16[144,2176]{1,0:T(8,128)(2,1)}) custom-call(s32[4]{0:T(128)} %pad_add_fusion.home_ref, bf16[16,136,2048]{2,1,0:T(8,128)(2,1)} %bitcast.29), custom_call_target="tpu_custom_call" | custom-call | flops 2415919104 | bytes 6815744 | tf_op jit(solution)/shard_map/select/pallas_call | solution.py:199
  143.4 0.0 copy-done
  143.4 2.4 collective-permute-start.1
  145.7 18.1 %collective-permute-start.2 = (bf16[144,2176]{1,0:T(8,128)(2,1)}, bf16[144,2176]{1,0:T(8,128)(2,1)S(1)}, u32[]{:S(2)}, u32[]{:S(2)}) collective-permute-start(bf16[144,2176]{1,0:T(8,128)(2,1)} %get-tuple-element.39), channel_id=1, source_target_pairs={{0,2},{1,3},{2,0},{3,1},{4,6},{5,7},{6,4},{7,5},{8,10},{9,11},{10,... | collective-permute-start | bytes 1880072 | tf_op jit(solution)/shard_map/ppermute | solution.py:49
  163.8 0.0 copy-start.8
  163.8 2.1 collective-permute-start.3
  165.9 6.5 %select.20 = (bf16[144,2176]{1,0:T(8,128)(2,1)}, bf16[144,2176]{1,0:T(8,128)(2,1)}, bf16[144,2176]{1,0:T(8,128)(2,1)}, bf16[144,2176]{1,0:T(8,128)(2,1)}) custom-call(s32[4]{0:T(128)} %pad_add_fusion.home_ref, bf16[16,136,2048]{2,1,0:T(8,128)(2,1)} %bitcast.30), custom_call_target="tpu_custom_call" | custom-call | flops 2415919104 | bytes 6815744 | tf_op jit(solution)/shard_map/select/pallas_call | solution.py:199
  172.4 2.3 collective-permute-start.4
  174.7 3.4 %collective-permute-start.5 = (bf16[144,2176]{1,0:T(8,128)(2,1)}, bf16[144,2176]{1,0:T(8,128)(2,1)S(1)}, u32[]{:S(2)}, u32[]{:S(2)}) collective-permute-start(bf16[144,2176]{1,0:T(8,128)(2,1)} %get-tuple-element.45), channel_id=1, source_target_pairs={{0,2},{1,3},{2,0},{3,1},{4,6},{5,7},{6,4},{7,5},{8,10},{9,11},{10,... | collective-permute-start | bytes 1880072 | tf_op jit(solution)/shard_map/ppermute | solution.py:49
  178.1 0.0 collective-permute-done.1.refs_1_.refs_5_
  178.1 0.0 copy-start.2
  178.1 2.2 collective-permute-start.6
  180.4 0.0 collective-permute-done.2.refs_2_.refs_6_
  180.4 0.0 copy-done.8
  180.4 0.0 copy-start.3
  180.4 1.9 collective-permute-start.7
  182.3 9.7 %collective-permute-done.3.refs_3_.refs_7_ = bf16[144,2176]{1,0:T(8,128)(2,1)S(1)} collective-permute-done((bf16[144,2176]{1,0:T(8,128)(2,1)}, bf16[144,2176]{1,0:T(8,128)(2,1)S(1)}, u32[]{:S(2)}, u32[]{:S(2)}) %collective-permute-start.3) | collective-permute-done | bytes 626720 | tf_op jit(solution)/shard_map/ppermute | solution.py:49
  192.1 0.0 copy-start.4
  192.1 0.0 copy-done.2
  192.1 0.0 copy-done.3
  192.1 0.8 copy-done.4
  192.9 5.9 %slopes.2.refs_8_ = bf16[768,576]{1,0:T(8,128)(2,1)} custom-call(bf16[144,2176]{1,0:T(8,128)(2,1)} %get-tuple-element.37.refs_0_.refs_4_, bf16[144,2176]{1,0:T(8,128)(2,1)} %copy-done.2, bf16[144,2176]{1,0:T(8,128)(2,1)} %copy-done.3, bf16[144,2176]{1,0:T(8,128)(2,1)} %copy-done.4, bf16[144,2176]{1,0:T(8,128)(2,1)} %get-tuple-element.37.refs_0_.refs_4_, ...), custom_call_target="tpu_custom_call" | custom-call | flops 1811939328 | bytes 6389760 | tf_op jit(solution)/shard_map/slopes/pallas_call | solution.py:247
  198.8 0.0 collective-permute-done.4.refs_1_.refs_5_
  198.8 0.0 copy-start.5
  198.8 6.6 %collective-permute-done.5.refs_2_.refs_6_ = bf16[144,2176]{1,0:T(8,128)(2,1)S(1)} collective-permute-done((bf16[144,2176]{1,0:T(8,128)(2,1)}, bf16[144,2176]{1,0:T(8,128)(2,1)S(1)}, u32[]{:S(2)}, u32[]{:S(2)}) %collective-permute-start.5) | collective-permute-done | bytes 626720 | tf_op jit(solution)/shard_map/ppermute | solution.py:49
  205.4 0.0 copy-start.6
  205.4 13.7 %collective-permute-done.6.refs_3_.refs_7_ = bf16[144,2176]{1,0:T(8,128)(2,1)S(1)} collective-permute-done((bf16[144,2176]{1,0:T(8,128)(2,1)}, bf16[144,2176]{1,0:T(8,128)(2,1)S(1)}, u32[]{:S(2)}, u32[]{:S(2)}) %collective-permute-start.6) | collective-permute-done | bytes 626720 | tf_op jit(solution)/shard_map/ppermute | solution.py:49
  219.1 0.0 copy-start.7
  219.1 0.0 copy-done.5
  219.1 0.0 copy-done.6
  219.1 0.9 copy-done.7
  220.0 5.9 %slopes.3.refs_9_ = bf16[768,576]{1,0:T(8,128)(2,1)} custom-call(bf16[144,2176]{1,0:T(8,128)(2,1)} %get-tuple-element.47.refs_0_.refs_4_, bf16[144,2176]{1,0:T(8,128)(2,1)} %copy-done.5, bf16[144,2176]{1,0:T(8,128)(2,1)} %copy-done.6, bf16[144,2176]{1,0:T(8,128)(2,1)} %copy-done.7, bf16[144,2176]{1,0:T(8,128)(2,1)} %get-tuple-element.47.refs_0_.refs_4_, ...), custom_call_target="tpu_custom_call" | custom-call | flops 1811939328 | bytes 6389760 | tf_op jit(solution)/shard_map/slopes/pallas_call | solution.py:247
  225.9 8.1 %gradient.1 = bf16[8,768,256]{2,1,0:T(8,128)(2,1)} custom-call(bf16[144,2176]{1,0:T(8,128)(2,1)} %get-tuple-element.37.refs_0_.refs_4_, bf16[144,2176]{1,0:T(8,128)(2,1)} %copy-done.2, bf16[144,2176]{1,0:T(8,128)(2,1)} %copy-done.3, bf16[144,2176]{1,0:T(8,128)(2,1)} %copy-done.4, bf16[144,2176]{1,0:T(8,128)(2,1)} %get-tuple-element.47.refs_0_.refs_4_, ...), custom_call_target="tpu_custom_call" | custom-call | flops 3623878656 | bytes 9633792 | tf_op jit(solution)/shard_map/gradient/pallas_call | solution.py:280
  234.0 0.0 collective-permute-done.7.far_a
  234.0 6.4 %all-to-all-start.1 = ((bf16[8,768,256]{2,1,0:T(8,128)(2,1)}), bf16[8,768,256]{2,1,0:T(8,128)(2,1)S(1)}, u32[]{:S(2)}, u32[]{:S(2)}) async-start(bf16[8,768,256]{2,1,0:T(8,128)(2,1)} %gradient.1), calls=%async_computation.1 | async-start | bytes 6291456 | tf_op jit(solution)/shard_map/all_to_all | solution.py:346
  240.4 1.9 collective-permute-start.8
  242.3 32.3 %collective-permute-done.8.far_b = bf16[2,112,768]{2,1,0:T(8,128)(2,1)} collective-permute-done((bf16[2,112,768]{2,1,0:T(8,128)(2,1)}, bf16[2,112,768]{2,1,0:T(8,128)(2,1)}, u32[]{:S(2)}, u32[]{:S(2)}) %collective-permute-start.8) | collective-permute-done | bytes 344096 | tf_op jit(solution)/shard_map/ppermute | solution.py:38
  274.6 5.3 %all-to-all-done.1.parts_ref = bf16[8,768,256]{2,1,0:T(8,128)(2,1)S(1)} async-done(((bf16[8,768,256]{2,1,0:T(8,128)(2,1)}), bf16[8,768,256]{2,1,0:T(8,128)(2,1)S(1)}, u32[]{:S(2)}, u32[]{:S(2)}) %all-to-all-start.1) | async-done | bytes 3145760 | tf_op jit(solution)/shard_map/all_to_all | solution.py:346
  279.9 0.0 copy-start.1
  279.9 1.6 copy-done.1
  281.5 4.7 %adam.1 = (bf16[256,768]{1,0:T(8,128)(2,1)}, f32[256,768]{1,0:T(8,128)}, f32[256,768]{1,0:T(8,128)}) custom-call(s32[1]{0:T(128)} %get-tuple-element.61.flag_ref, bf16[8,768,256]{2,1,0:T(8,128)(2,1)} %copy-done.1, bf16[256,768]{1,0:T(8,128)(2,1)S(1)} %get-tuple-element.64.weight_ref, f32[256,768]{1,0:T(8,128)} %bitcast.26, f32[256,768]{1,0:T(8,128)} %bitcast.28, ...), custom_call_target="tpu_custom_call" | custom-call | flops 5898240 | bytes 7864320 | tf_op jit(solution)/shard_map/adam/pallas_call | solution.py:111
  (2 shorter events, 0.0 us)
Async XLA Ops:
  7.2 129.7 %all-gather.3.cloned.1.call-start = ((), (), s32[]{:S(2)}) async-start(), calls=%async_computation.2 | async-start | bytes 9469952 | tf_op jit(solution)/shard_map/all_gather | solution.py:317
  15.5 30.9 %all-to-all-start = ((bf16[8,256,768]{2,1,0:T(8,128)(2,1)}), bf16[8,256,768]{2,1,0:T(8,128)(2,1)S(1)}, u32[]{:S(2)}, u32[]{:S(2)}) async-start(bf16[8,256,768]{2,1,0:T(8,128)(2,1)} %broadcast_in_dim.16), calls=%async_computation | async-start | bytes 6291456 | tf_op jit(solution)/shard_map/all_to_all | solution.py:320
  46.3 97.0 %copy-start = (bf16[8,256,768]{2,1,0:T(8,128)(2,1)}, bf16[8,256,768]{2,1,0:T(8,128)(2,1)S(1)}, u32[]{:S(2)}) copy-start(bf16[8,256,768]{2,1,0:T(8,128)(2,1)S(1)} %all-to-all-done) | copy-start | bytes 9437188
  143.4 34.7 %collective-permute-start.1 = (bf16[144,2176]{1,0:T(8,128)(2,1)}, bf16[144,2176]{1,0:T(8,128)(2,1)S(1)}, u32[]{:S(2)}, u32[]{:S(2)}) collective-permute-start(bf16[144,2176]{1,0:T(8,128)(2,1)} %get-tuple-element.38), channel_id=1, source_target_pairs={{0,1},{1,0},{2,3},{3,2},{4,5},{5,4},{6,7},{7,6},{8,9},{9,8},{10,11... | collective-permute-start | bytes 1880072 | tf_op jit(solution)/shard_map/ppermute | solution.py:49
  145.7 34.6 %collective-permute-start.2 = (bf16[144,2176]{1,0:T(8,128)(2,1)}, bf16[144,2176]{1,0:T(8,128)(2,1)S(1)}, u32[]{:S(2)}, u32[]{:S(2)}) collective-permute-start(bf16[144,2176]{1,0:T(8,128)(2,1)} %get-tuple-element.39), channel_id=1, source_target_pairs={{0,2},{1,3},{2,0},{3,1},{4,6},{5,7},{6,4},{7,5},{8,10},{9,11},{10,... | collective-permute-start | bytes 1880072 | tf_op jit(solution)/shard_map/ppermute | solution.py:49
  163.8 16.6 %copy-start.8 = (bf16[2,144,768]{2,1,0:T(8,128)(2,1)S(1)}, bf16[2,144,768]{2,1,0:T(8,128)(2,1)}, u32[]{:S(2)}) copy-start(bf16[2,144,768]{2,1,0:T(8,128)(2,1)} %get-tuple-element.52) | copy-start | bytes 1327108
  163.8 28.2 %collective-permute-start.3 = (bf16[144,2176]{1,0:T(8,128)(2,1)}, bf16[144,2176]{1,0:T(8,128)(2,1)S(1)}, u32[]{:S(2)}, u32[]{:S(2)}) collective-permute-start(bf16[144,2176]{1,0:T(8,128)(2,1)} %get-tuple-element.40), channel_id=1, source_target_pairs={{0,3},{1,2},{2,1},{3,0},{4,7},{5,6},{6,5},{7,4},{8,11},{9,10},{10,... | collective-permute-start | bytes 1880072 | tf_op jit(solution)/shard_map/ppermute | solution.py:49
  172.4 26.4 %collective-permute-start.4 = (bf16[144,2176]{1,0:T(8,128)(2,1)}, bf16[144,2176]{1,0:T(8,128)(2,1)S(1)}, u32[]{:S(2)}, u32[]{:S(2)}) collective-permute-start(bf16[144,2176]{1,0:T(8,128)(2,1)} %get-tuple-element.44), channel_id=1, source_target_pairs={{0,1},{1,0},{2,3},{3,2},{4,5},{5,4},{6,7},{7,6},{8,9},{9,8},{10,11... | collective-permute-start | bytes 1880072 | tf_op jit(solution)/shard_map/ppermute | solution.py:49
  174.7 30.7 %collective-permute-start.5 = (bf16[144,2176]{1,0:T(8,128)(2,1)}, bf16[144,2176]{1,0:T(8,128)(2,1)S(1)}, u32[]{:S(2)}, u32[]{:S(2)}) collective-permute-start(bf16[144,2176]{1,0:T(8,128)(2,1)} %get-tuple-element.45), channel_id=1, source_target_pairs={{0,2},{1,3},{2,0},{3,1},{4,6},{5,7},{6,4},{7,5},{8,10},{9,11},{10,... | collective-permute-start | bytes 1880072 | tf_op jit(solution)/shard_map/ppermute | solution.py:49
  178.1 14.0 %copy-start.2 = (bf16[144,2176]{1,0:T(8,128)(2,1)}, bf16[144,2176]{1,0:T(8,128)(2,1)S(1)}, u32[]{:S(2)}) copy-start(bf16[144,2176]{1,0:T(8,128)(2,1)S(1)} %collective-permute-done.1.refs_1_.refs_5_) | copy-start | bytes 1880068
  178.1 41.0 %collective-permute-start.6 = (bf16[144,2176]{1,0:T(8,128)(2,1)}, bf16[144,2176]{1,0:T(8,128)(2,1)S(1)}, u32[]{:S(2)}, u32[]{:S(2)}) collective-permute-start(bf16[144,2176]{1,0:T(8,128)(2,1)} %get-tuple-element.46), channel_id=1, source_target_pairs={{0,3},{1,2},{2,1},{3,0},{4,7},{5,6},{6,5},{7,4},{8,11},{9,10},{10,... | collective-permute-start | bytes 1880072 | tf_op jit(solution)/shard_map/ppermute | solution.py:49
  180.4 11.7 %copy-start.3 = (bf16[144,2176]{1,0:T(8,128)(2,1)}, bf16[144,2176]{1,0:T(8,128)(2,1)S(1)}, u32[]{:S(2)}) copy-start(bf16[144,2176]{1,0:T(8,128)(2,1)S(1)} %collective-permute-done.2.refs_2_.refs_6_) | copy-start | bytes 1880068
  180.4 53.6 %collective-permute-start.7 = (bf16[2,144,768]{2,1,0:T(8,128)(2,1)S(1)}, bf16[2,144,768]{2,1,0:T(8,128)(2,1)}, u32[]{:S(2)}, u32[]{:S(2)}) collective-permute-start(bf16[2,144,768]{2,1,0:T(8,128)(2,1)S(1)} %copy-done.8), channel_id=1, source_target_pairs={{0,32},{4,36},{8,40},{12,44},{16,48},{20,52},{24,56},{28,60},{32,0... | collective-permute-start | bytes 1327112 | tf_op jit(solution)/shard_map/ppermute | solution.py:38
  192.1 0.8 copy-start.4
  198.8 20.3 %copy-start.5 = (bf16[144,2176]{1,0:T(8,128)(2,1)}, bf16[144,2176]{1,0:T(8,128)(2,1)S(1)}, u32[]{:S(2)}) copy-start(bf16[144,2176]{1,0:T(8,128)(2,1)S(1)} %collective-permute-done.4.refs_1_.refs_5_) | copy-start | bytes 1880068
  205.4 13.7 %copy-start.6 = (bf16[144,2176]{1,0:T(8,128)(2,1)}, bf16[144,2176]{1,0:T(8,128)(2,1)S(1)}, u32[]{:S(2)}) copy-start(bf16[144,2176]{1,0:T(8,128)(2,1)S(1)} %collective-permute-done.5.refs_2_.refs_6_) | copy-start | bytes 1880068
  219.1 0.9 copy-start.7
  234.0 45.8 %all-to-all-start.1 = ((bf16[8,768,256]{2,1,0:T(8,128)(2,1)}), bf16[8,768,256]{2,1,0:T(8,128)(2,1)S(1)}, u32[]{:S(2)}, u32[]{:S(2)}) async-start(bf16[8,768,256]{2,1,0:T(8,128)(2,1)} %gradient.1), calls=%async_computation.1 | async-start | bytes 6291456 | tf_op jit(solution)/shard_map/all_to_all | solution.py:346
  240.4 34.2 %collective-permute-start.8 = (bf16[2,112,768]{2,1,0:T(8,128)(2,1)}, bf16[2,112,768]{2,1,0:T(8,128)(2,1)}, u32[]{:S(2)}, u32[]{:S(2)}) collective-permute-start(bf16[2,112,768]{2,1,0:T(8,128)(2,1)} %get-tuple-element.56), channel_id=1, source_target_pairs={{0,32},{4,36},{8,40},{12,44},{16,48},{20,52},{24,56},{28,60},{32,0... | collective-permute-start | bytes 1032200 | tf_op jit(solution)/shard_map/ppermute | solution.py:38
  279.9 1.6 copy-start.1
Sparse Core Ops, SparseCore 0:
  11.6 125.2 all-gather.2
